TPU v7x, 32 devices: a whole 2x2x4 slice. The times are simulated.
32 devices in a mesh: dp: 2 (over core), expert: 4 (over z), tensor: 4 (over y, x).
Axes of the slice: x: 2, y: 2, z: 4, core: 2. Of those that a mesh axis runs over, the one named last changes fastest.
Arguments:
- hidden_in: bfloat16 [20480, 768], P(('dp', 'expert', 'tensor')), may hold values from -6 to 6
- route_ids: int32 [2, 20480, 1], P(None, ('dp', 'expert', 'tensor')), may hold values from 0 to 3; in each aligned block of 640 rows (0 to 639, 640 to 1279, ..., all dimensions but the last counted through in order) at most 240 rows name the same one
- segment_ids: int32 [20480], P(('dp', 'expert')), may hold values from 0 to 12, as said below
- path_pos: int32 [20480], P(('dp', 'expert')), may hold values from 0 to 1279, as said below
- parent_ids: int32 [8, 13], P(('dp', 'expert')), may hold values from 0 to 4, as said below
- norm_att: bfloat16 [2, 768], replicated, may hold values from 0.5 to 1.5
- w_qkv: bfloat16 [2, 768, 3, 768], P(None, None, None, 'tensor'), may hold values from -0.21875 to 0.21875
- w_out: bfloat16 [2, 768, 768], P(None, 'tensor'), may hold values from -0.875 to 0.875
- norm_ffn: bfloat16 [2, 768], replicated, may hold values from 0.5 to 1.5
- w_route: bfloat16 [2, 768, 4], replicated, may hold values from -0.15625 to 0.15625
- w_in: bfloat16 [2, 4, 768, 3072], P(None, 'expert', None, 'tensor'), may hold values from -0.21875 to 0.21875
- w_down: bfloat16 [2, 4, 3072, 768], P(None, 'expert', 'tensor'), may hold values from -0.4375 to 0.4375
- cotangent: bfloat16 [20480, 768], P(('dp', 'expert', 'tensor')), may hold values from -6 to 6
Outputs:
- hidden_out: bfloat16 [20480, 768], P(('dp', 'expert', 'tensor'))
- grad_hidden: float32 [20480, 768], P(('dp', 'expert', 'tensor'))
- grad_norm_att: float32 [2, 768], replicated
- grad_qkv: float32 [2, 768, 3, 768], P(None, None, None, 'tensor')
- grad_out: float32 [2, 768, 768], P(None, 'tensor')
- grad_norm_ffn: float32 [2, 768], replicated
- grad_route: float32 [2, 768, 4], replicated
- grad_w_in: float32 [2, 4, 768, 3072], P(None, 'expert', None, 'tensor')
- grad_w_down: float32 [2, 4, 3072, 768], P(None, 'expert', 'tensor')
Inputs may be any that keep to these rules, and one draw needn't show every extreme that they name: `route_ids`: in the rows of one device at most 240 tokens name one expert. `segment_ids`: each tree is 2560 consecutive tokens in 20 blocks of 128, the blocks in an order drawn from the seed: eight of segment 0 (the trunk), one of each branch 1 to 4 and one of each leaf 5 to 12. `path_pos`: inside a block positions rise by one; the trunk's blocks hold 0 to 1023, a branch starts at 1024, a leaf at 1152. `parent_ids`: segments 0 to 4 have parent 0; each branch 1 to 4 is the parent of two leaves.
All inputs are finite; a program needn't handle non-finite values.
Results may differ from a plain program's by a relative error of at most 0.03.
Values may be sent and summed in bfloat16 or wider, within the bound.
A program may use at most 256 MiB of HBM per device.

v0:
```python
import jax
import jax.numpy as jnp
from jax import lax
from jax.sharding import PartitionSpec as P

HEAD_DIM = 64
TREE = 2560
QBLK = 512


EPS = 1e-06
NEG = -1000000000.0
HIGH = lax.Precision.HIGHEST


def inverse_rms(stream):
    return lax.rsqrt(jnp.mean(stream * stream, axis=-1, keepdims=True) + EPS)


def norm_backward(upstream, stream, inverse, gain):
    weighted = upstream * gain
    inner = jnp.mean(weighted * stream, axis=-1, keepdims=True)
    return inverse * weighted - stream * (inverse * inverse * inverse) * inner


def lookup(indices, parent_rows):
    matches = indices[:, None] == jnp.arange(parent_rows.shape[-1], dtype=jnp.int32)[None, :]
    return jnp.sum(jnp.where(matches, parent_rows, 0), axis=1)


def path_tables(segment_ids, path_pos, parent_ids):
    row_total = segment_ids.shape[0]
    tree_of = jnp.arange(row_total, dtype=jnp.int32) // TREE
    tree_match = tree_of[:, None] == jnp.arange(parent_ids.shape[0], dtype=jnp.int32)[None, :]
    parent_rows = jnp.sum(jnp.where(tree_match[:, :, None], parent_ids[None], 0), axis=1)
    parent_one = lookup(segment_ids, parent_rows)
    parent_two = lookup(parent_one, parent_rows)
    return (tree_of, segment_ids, parent_one, parent_two, path_pos)


def allowed_block(offset, path_info):
    tree_of, seg_ids, parent_one, parent_two, places = path_info

    def cut_rows(values):
        return lax.dynamic_slice_in_dim(values, offset, QBLK)

    same_path = (seg_ids[None, :] == cut_rows(seg_ids)[:, None]) | (
        seg_ids[None, :] == cut_rows(parent_one)[:, None]
    )
    same_path = same_path | (seg_ids[None, :] == cut_rows(parent_two)[:, None])
    return (
        same_path
        & (tree_of[None, :] == cut_rows(tree_of)[:, None])
        & (places[None, :] <= cut_rows(places)[:, None])
    )


def block_scores(queries, keys_all, offset, path_info):
    query_rows = lax.dynamic_slice_in_dim(queries, offset, QBLK)
    scores = jnp.einsum(
        "qhd,khd->hqk", query_rows, keys_all, preferred_element_type=jnp.float32
    ) * HEAD_DIM ** (-0.5)
    return (jnp.where(allowed_block(offset, path_info)[None], scores, NEG), query_rows)


def attend(queries, keys_all, values_all, path_info):
    row_total = queries.shape[0]

    def one_block(offset):
        scores, query_rows = block_scores(queries, keys_all, offset, path_info)
        row_max = jnp.max(scores, axis=-1, keepdims=True)
        expo = jnp.exp(scores - row_max)
        row_sum = jnp.sum(expo, axis=-1, keepdims=True)
        weights = (expo / row_sum).astype(jnp.bfloat16)
        mixed_out = jnp.einsum(
            "hqk,khd->qhd", weights, values_all, preferred_element_type=jnp.float32
        )
        return (mixed_out.astype(jnp.bfloat16), row_max[..., 0] + jnp.log(row_sum[..., 0]))

    offsets = jnp.arange(row_total // QBLK, dtype=jnp.int32) * QBLK
    heads_out, log_sums = lax.map(one_block, offsets)
    return (heads_out.reshape(row_total, -1), log_sums)


def attend_back(queries, keys_all, values_all, log_sums, d_heads, path_info):
    row_total = queries.shape[0]

    def one_block(totals, entries):
        d_keys, d_values = totals
        offset, block_sums = entries
        scores, query_rows = block_scores(queries, keys_all, offset, path_info)
        weights = jnp.exp(scores - block_sums[..., None])
        grad_rows = lax.dynamic_slice_in_dim(d_heads, offset, QBLK)
        d_weights = jnp.einsum(
            "qhd,khd->hqk", grad_rows, values_all, preferred_element_type=jnp.float32
        )
        inner = jnp.sum(weights * d_weights, axis=-1, keepdims=True)
        d_scores = (weights * (d_weights - inner)).astype(jnp.bfloat16)
        d_query = jnp.einsum(
            "hqk,khd->qhd", d_scores, keys_all, preferred_element_type=jnp.float32
        ) * HEAD_DIM ** (-0.5)
        d_keys = d_keys + jnp.einsum(
            "hqk,qhd->khd", d_scores, query_rows, preferred_element_type=jnp.float32
        ) * HEAD_DIM ** (-0.5)
        d_values = d_values + jnp.einsum(
            "hqk,qhd->khd",
            weights.astype(jnp.bfloat16),
            grad_rows,
            preferred_element_type=jnp.float32,
        )
        return ((d_keys, d_values), d_query)

    zeros_kv = jnp.zeros(keys_all.shape, jnp.float32)
    offsets = jnp.arange(row_total // QBLK, dtype=jnp.int32) * QBLK
    (d_keys, d_values), d_query = lax.scan(one_block, (zeros_kv, zeros_kv), (offsets, log_sums))
    return (d_query.reshape(keys_all.shape), d_keys, d_values)


def to_experts(buffer):
    return lax.all_to_all(buffer, "expert", split_axis=0, concat_axis=0, tiled=True)


def from_experts(buffer):
    return lax.all_to_all(buffer, "expert", split_axis=0, concat_axis=0, tiled=True)


def forward_layer(stream, weights, route_col, path_info):
    gain_att, w_mix, w_proj, gain_ffn, w_gate, w_up, w_back = weights
    tok_count, model_width = stream.shape
    expert_count = w_gate.shape[1]
    capacity = 3 * tok_count // (2 * expert_count)
    inverse_att = inverse_rms(stream)
    normed = (stream * inverse_att * gain_att.astype(jnp.float32)).astype(jnp.bfloat16)
    normed_all = lax.all_gather(normed, "tensor", axis=0, tiled=True)
    group_len = normed_all.shape[0]
    mixed = jnp.dot(
        normed_all, w_mix.reshape(model_width, -1), preferred_element_type=jnp.float32
    ).astype(jnp.bfloat16)
    mixed = mixed.reshape(group_len, 3, -1, HEAD_DIM)
    heads_out, log_sums = attend(mixed[:, 0], mixed[:, 1], mixed[:, 2], path_info)
    after_att = stream + lax.psum_scatter(
        jnp.dot(heads_out, w_proj, preferred_element_type=jnp.float32).astype(jnp.bfloat16),
        "tensor",
        scatter_dimension=0,
        tiled=True,
    ).astype(jnp.float32)
    inverse_ffn = inverse_rms(after_att)
    token_rows = (after_att * inverse_ffn * gain_ffn.astype(jnp.float32)).astype(jnp.bfloat16)
    router = jax.nn.softmax(
        jnp.dot(token_rows, w_gate, preferred_element_type=jnp.float32), axis=-1
    )
    chosen = route_col[:, None] == jnp.arange(expert_count, dtype=jnp.int32)[None, :]
    gate = jnp.sum(jnp.where(chosen, router, 0.0), axis=1)
    before = jnp.cumsum(chosen.astype(jnp.int32), axis=0) - 1
    slot_ids = jnp.sum(jnp.where(chosen, before, 0), axis=1)
    flat_slot = route_col * capacity + slot_ids
    slot_table = (
        jnp.full((expert_count * capacity,), tok_count, jnp.int32)
        .at[flat_slot]
        .set(jnp.arange(tok_count, dtype=jnp.int32))
    )
    padded = jnp.concatenate([token_rows, jnp.zeros((1, model_width), jnp.bfloat16)], axis=0)
    arrived = to_experts(padded[slot_table].reshape(expert_count, capacity, model_width)).reshape(
        -1, model_width
    )
    slot_all = lax.all_gather(arrived, "tensor", axis=0, tiled=True)
    pre_act = jnp.dot(slot_all, w_up[0], preferred_element_type=jnp.float32)
    hidden = jax.nn.gelu(pre_act).astype(jnp.bfloat16)
    summed = lax.psum_scatter(
        jnp.dot(hidden, w_back[0], preferred_element_type=jnp.float32).astype(jnp.bfloat16),
        "tensor",
        scatter_dimension=0,
        tiled=True,
    )
    returned = from_experts(summed.reshape(expert_count, capacity, model_width))
    expert_rows = returned.reshape(-1, model_width)[flat_slot].astype(jnp.float32)
    result = after_att + gate[:, None] * expert_rows
    saved = (
        stream,
        inverse_att,
        normed_all,
        mixed,
        heads_out,
        log_sums,
        after_att,
        inverse_ffn,
        token_rows,
        router,
        gate,
        chosen,
        flat_slot,
        slot_table,
        slot_all,
        pre_act,
        hidden,
        expert_rows,
    )
    return (result, saved)


def backward_layer(upstream, weights, saved, path_info):
    gain_att, w_mix, w_proj, gain_ffn, w_gate, w_up, w_back = weights
    (
        stream,
        inverse_att,
        normed_all,
        mixed,
        heads_out,
        log_sums,
        after_att,
        inverse_ffn,
        token_rows,
        router,
        gate,
        chosen,
        flat_slot,
        slot_table,
        slot_all,
        pre_act,
        hidden,
        expert_rows,
    ) = saved
    tok_count, model_width = stream.shape
    expert_count = w_gate.shape[1]
    capacity = 3 * tok_count // (2 * expert_count)
    d_gate = jnp.sum(expert_rows * upstream, axis=1)
    d_output = (gate[:, None] * upstream).astype(jnp.bfloat16)
    padded = jnp.concatenate([d_output, jnp.zeros((1, model_width), jnp.bfloat16)], axis=0)
    d_arrived = to_experts(padded[slot_table].reshape(expert_count, capacity, model_width)).reshape(
        -1, model_width
    )
    d_slots = lax.all_gather(d_arrived, "tensor", axis=0, tiled=True)
    grad_back = jnp.dot(hidden.T, d_slots, preferred_element_type=jnp.float32)
    d_hidden = jnp.dot(d_slots, w_back[0].T, preferred_element_type=jnp.float32)
    gelu_out, gelu_pull = jax.vjp(jax.nn.gelu, pre_act)
    d_pre = gelu_pull(d_hidden)[0].astype(jnp.bfloat16)
    grad_up = jnp.dot(slot_all.T, d_pre, preferred_element_type=jnp.float32)
    d_summed = lax.psum_scatter(
        jnp.dot(d_pre, w_up[0].T, preferred_element_type=jnp.float32).astype(jnp.bfloat16),
        "tensor",
        scatter_dimension=0,
        tiled=True,
    )
    d_returned = from_experts(d_summed.reshape(expert_count, capacity, model_width))
    d_expert = d_returned.reshape(-1, model_width)[flat_slot].astype(jnp.float32)
    d_logits = (gate * d_gate)[:, None] * (chosen.astype(jnp.float32) - router)
    grad_gate = jnp.dot(token_rows.astype(jnp.float32).T, d_logits, precision=HIGH)
    d_rows = d_expert + jnp.dot(d_logits, w_gate.astype(jnp.float32).T, precision=HIGH)
    gain_ffn32 = gain_ffn.astype(jnp.float32)
    grad_gain_ffn = jnp.sum(d_rows * after_att * inverse_ffn, axis=0)
    d_after = upstream + norm_backward(d_rows, after_att, inverse_ffn, gain_ffn32)
    d_att_all = lax.all_gather(d_after.astype(jnp.bfloat16), "tensor", axis=0, tiled=True)
    grad_proj = jnp.dot(heads_out.T, d_att_all, preferred_element_type=jnp.float32)
    group_len = normed_all.shape[0]
    d_heads = jnp.dot(d_att_all, w_proj.T, preferred_element_type=jnp.float32).astype(jnp.bfloat16)
    d_heads = d_heads.reshape(group_len, -1, HEAD_DIM)
    d_query, d_keys, d_values = attend_back(
        mixed[:, 0], mixed[:, 1], mixed[:, 2], log_sums, d_heads, path_info
    )
    d_mixed = (
        jnp.stack([d_query, d_keys, d_values], axis=1).reshape(group_len, -1).astype(jnp.bfloat16)
    )
    grad_mix = jnp.dot(normed_all.T, d_mixed, preferred_element_type=jnp.float32).reshape(
        model_width, 3, -1
    )
    mix_matrix = w_mix.reshape(model_width, -1)
    d_normed = lax.psum_scatter(
        jnp.dot(d_mixed, mix_matrix.T, preferred_element_type=jnp.float32).astype(jnp.bfloat16),
        "tensor",
        scatter_dimension=0,
        tiled=True,
    ).astype(jnp.float32)
    gain_att32 = gain_att.astype(jnp.float32)
    grad_gain_att = jnp.sum(d_normed * stream * inverse_att, axis=0)
    d_stream = d_after + norm_backward(d_normed, stream, inverse_att, gain_att32)
    return (
        d_stream,
        [grad_gain_att, grad_mix, grad_proj, grad_gain_ffn, grad_gate, grad_up, grad_back],
    )


def reduce_grads(pieces):
    gain_att, grad_mix, grad_proj, gain_ffn, grad_gate, grad_up, grad_back = pieces
    grad_mix, grad_proj = lax.psum((grad_mix, grad_proj), ("dp", "expert"))
    gain_att, gain_ffn, grad_gate = lax.psum(
        (gain_att, gain_ffn, grad_gate), ("dp", "expert", "tensor")
    )
    grad_up, grad_back = (
        lax.psum(grad_up.astype(jnp.bfloat16), "dp").astype(jnp.float32),
        lax.psum(grad_back.astype(jnp.bfloat16), "dp").astype(jnp.float32),
    )
    return [gain_att, grad_mix, grad_proj, gain_ffn, grad_gate, grad_up, grad_back]


def body(
    hidden_in,
    route_ids,
    segment_ids,
    path_pos,
    parent_ids,
    norm_att,
    w_qkv,
    w_out,
    norm_ffn,
    w_route,
    w_in,
    w_down,
    cotangent,
):
    depth_total = w_qkv.shape[0]
    path_info = path_tables(segment_ids, path_pos, parent_ids)
    stream = hidden_in.astype(jnp.float32)
    all_weights = [
        [w[depth] for w in (norm_att, w_qkv, w_out, norm_ffn, w_route, w_in, w_down)]
        for depth in range(depth_total)
    ]
    kept_all = []
    for depth in range(depth_total):
        stream, saved = forward_layer(stream, all_weights[depth], route_ids[depth, :, 0], path_info)
        kept_all.append(saved)
    hidden_out = stream.astype(jnp.bfloat16)
    upstream = cotangent.astype(jnp.float32)
    layer_grads = [None] * depth_total
    for depth in reversed(range(depth_total)):
        upstream, pieces = backward_layer(upstream, all_weights[depth], kept_all[depth], path_info)
        layer_grads[depth] = reduce_grads(pieces)
    stacked = [
        jnp.stack([layer_grads[depth][member] for depth in range(depth_total)])
        for member in range(7)
    ]
    return (
        hidden_out,
        upstream,
        stacked[0],
        stacked[1],
        stacked[2],
        stacked[3],
        stacked[4],
        stacked[5][:, None],
        stacked[6][:, None],
    )


def solution(mesh):
    in_specs = (
        P(("dp", "expert", "tensor"), None),
        P(None, ("dp", "expert", "tensor"), None),
        P(("dp", "expert")),
        P(("dp", "expert")),
        P(("dp", "expert"), None),
        P(),
        P(None, None, None, "tensor"),
        P(None, "tensor", None),
        P(),
        P(),
        P(None, "expert", None, "tensor"),
        P(None, "expert", "tensor", None),
        P(("dp", "expert", "tensor"), None),
    )
    out_specs = (
        P(("dp", "expert", "tensor"), None),
        P(("dp", "expert", "tensor"), None),
        P(),
        P(None, None, None, "tensor"),
        P(None, "tensor", None),
        P(),
        P(),
        P(None, "expert", None, "tensor"),
        P(None, "expert", "tensor", None),
    )
    return jax.shard_map(body, mesh=mesh, in_specs=in_specs, out_specs=out_specs, check_vma=False)
```

profile of v0, /device:TPU:1, one launch (start us, length us, event | category | flops | bytes accessed | tf_op | source)
XLA Modules:
  0.0 2413.3 jit_solution(11770136835163680906)
XLA Ops:
  14.7 51.3 %all-gather.9.cloned.1.call-done = bf16[2560,768]{1,0:T(8,128)(2,1)} async-done(((bf16[640,768]{1,0:T(8,128)(2,1)}), bf16[2560,768]{1,0:T(8,128)(2,1)}) %all-gather.9.cloned.1.call-update) | async-done | bytes 3932176 | tf_op jit(solution)/shard_map/all_gather | solution.py:134
  71.9 94.9 %while.58 = (s32[]{:T(128)}, bf16[5,512,3,64]{1,3,2,0:T(8,128)(2,1)}, f32[5,3,512]{2,1,0:T(4,128)S(1)}, s32[2560]{0:T(1024)S(1)}, s32[5]{0:T(128)S(1)}, /*index=...) while((s32[]{:T(128)}, ...), condition=%wide.region_6.7_spmd.clone, body=%wide.region_3.6_spmd.clone.sunk | while | flops 1065712128 | bytes 54905056 | solution.py:81
  183.6 41.1 %reduce-scatter.9.cloned.1.call-done = bf16[640,768]{1,0:T(8,128)(2,1)} async-done(((bf16[2560,768]{1,0:T(8,128)(2,1)}), bf16[640,768]{1,0:T(8,128)(2,1)}) %reduce-scatter.9.cloned.1.call-update) | async-done | bytes 983056 | tf_op jit(solution)/shard_map/reduce_scatter | solution.py:141
  234.4 38.5 %all_to_all.40 = bf16[4,240,768]{2,1,0:T(8,128)(2,1)} all-to-all(bf16[4,240,768]{2,1,0:T(8,128)(2,1)S(1)} %bitcast.371), channel_id=1, replica_groups=mesh['dp'=2,'expert'=4,'tensor'=4] {'expert'}, dimensions={0} | all-to-all | bytes 2949120 | tf_op jit(solution)/shard_map/all_to_all | solution.py:120
  273.0 66.0 %all-gather.11.cloned.1.call-done = bf16[3840,768]{1,0:T(8,128)(2,1)} async-done(((bf16[960,768]{1,0:T(8,128)(2,1)}), bf16[3840,768]{1,0:T(8,128)(2,1)}) %all-gather.11.cloned.1.call-update) | async-done | bytes 5898256 | tf_op jit(solution)/shard_map/all_gather | solution.py:166
  350.4 10.1 convolution_convert_fusion.3
  360.6 67.1 %reduce-scatter.11.cloned.1.call-done = bf16[960,768]{1,0:T(8,128)(2,1)} async-done(((bf16[3840,768]{1,0:T(8,128)(2,1)}), bf16[960,768]{1,0:T(8,128)(2,1)}) %reduce-scatter.11.cloned.1.call-update) | async-done | bytes 1474576 | tf_op jit(solution)/shard_map/reduce_scatter | solution.py:169
  433.0 33.3 %all-to-all-done.1 = bf16[4,240,768]{2,1,0:T(8,128)(2,1)S(1)} async-done(((bf16[4,240,768]{2,1,0:T(8,128)(2,1)}), bf16[4,240,768]{2,1,0:T(8,128)(2,1)S(1)}, u32[]{:S(2)}, u32[]{:S(2)}) %all-to-all-start.1) | async-done | bytes 1474592 | tf_op jit(solution)/shard_map/all_to_all | solution.py:124
  474.1 49.5 %all-gather.13.cloned.1.call-done = bf16[2560,768]{1,0:T(8,128)(2,1)} async-done(((bf16[640,768]{1,0:T(8,128)(2,1)}), bf16[2560,768]{1,0:T(8,128)(2,1)}) %all-gather.13.cloned.1.call-update) | async-done | bytes 3932176 | tf_op jit(solution)/shard_map/all_gather | solution.py:134
  529.5 95.1 %while.59 = (s32[]{:T(128)}, bf16[5,512,3,64]{1,3,2,0:T(8,128)(2,1)}, f32[5,3,512]{2,1,0:T(4,128)S(1)}, s32[2560]{0:T(1024)S(1)}, s32[5]{0:T(128)S(1)}, /*index=...) while((s32[]{:T(128)}, ...), condition=%wide.region_21.22_spmd.clone, body=%wide.region_18.21_spmd.clone.sunk | while | flops 1065712128 | bytes 54905056 | solution.py:81
  636.4 45.7 %reduce-scatter.13.cloned.1.call-done = bf16[640,768]{1,0:T(8,128)(2,1)} async-done(((bf16[2560,768]{1,0:T(8,128)(2,1)}), bf16[640,768]{1,0:T(8,128)(2,1)}) %reduce-scatter.13.cloned.1.call-update) | async-done | bytes 983056 | tf_op jit(solution)/shard_map/reduce_scatter | solution.py:141
  692.0 38.7 %all_to_all.41 = bf16[4,240,768]{2,1,0:T(8,128)(2,1)} all-to-all(bf16[4,240,768]{2,1,0:T(8,128)(2,1)} %bitcast.372), channel_id=1, replica_groups=mesh['dp'=2,'expert'=4,'tensor'=4] {'expert'}, dimensions={0} | all-to-all | bytes 2949120 | tf_op jit(solution)/shard_map/all_to_all | solution.py:120
  730.8 66.0 %all-gather.15.cloned.1.call-done = bf16[3840,768]{1,0:T(8,128)(2,1)} async-done(((bf16[960,768]{1,0:T(8,128)(2,1)}), bf16[3840,768]{1,0:T(8,128)(2,1)}) %all-gather.15.cloned.1.call-update) | async-done | bytes 5898256 | tf_op jit(solution)/shard_map/all_gather | solution.py:166
  808.4 8.9 convolution_convert_fusion.2
  817.4 67.1 %reduce-scatter.15.cloned.1.call-done = bf16[960,768]{1,0:T(8,128)(2,1)} async-done(((bf16[3840,768]{1,0:T(8,128)(2,1)}), bf16[960,768]{1,0:T(8,128)(2,1)}) %reduce-scatter.15.cloned.1.call-update) | async-done | bytes 1474576 | tf_op jit(solution)/shard_map/reduce_scatter | solution.py:169
  889.3 33.9 %all-to-all-done.3 = bf16[4,240,768]{2,1,0:T(8,128)(2,1)} async-done(((bf16[4,240,768]{2,1,0:T(8,128)(2,1)}), bf16[4,240,768]{2,1,0:T(8,128)(2,1)}, u32[]{:S(2)}, u32[]{:S(2)}) %all-to-all-start.3) | async-done | bytes 1474592 | tf_op jit(solution)/shard_map/all_to_all | solution.py:124
  935.7 38.2 %all_to_all.42 = bf16[4,240,768]{2,1,0:T(8,128)(2,1)} all-to-all(bf16[4,240,768]{2,1,0:T(8,128)(2,1)} %bitcast.369), channel_id=1, replica_groups=mesh['dp'=2,'expert'=4,'tensor'=4] {'expert'}, dimensions={0} | all-to-all | bytes 2949120 | tf_op jit(solution)/shard_map/all_to_all | solution.py:120
  974.2 66.2 %all-gather.17.cloned.1.call-done = bf16[3840,768]{1,0:T(8,128)(2,1)} async-done(((bf16[960,768]{1,0:T(8,128)(2,1)}), bf16[3840,768]{1,0:T(8,128)(2,1)}) %all-gather.17.cloned.1.call-update) | async-done | bytes 5898256 | tf_op jit(solution)/shard_map/all_gather | solution.py:232
  1040.4 14.9 fusion.75
  1064.6 67.1 %reduce-scatter.17.cloned.1.call-done = bf16[960,768]{1,0:T(8,128)(2,1)} async-done(((bf16[3840,768]{1,0:T(8,128)(2,1)}), bf16[960,768]{1,0:T(8,128)(2,1)}) %reduce-scatter.17.cloned.1.call-update) | async-done | bytes 1474576 | tf_op jit(solution)/shard_map/reduce_scatter | solution.py:238
  1136.1 34.4 %all-to-all-done.5 = bf16[4,240,768]{2,1,0:T(8,128)(2,1)} async-done(((bf16[4,240,768]{2,1,0:T(8,128)(2,1)}), bf16[4,240,768]{2,1,0:T(8,128)(2,1)}, u32[]{:S(2)}, u32[]{:S(2)}) %all-to-all-start.5) | async-done | bytes 1474592 | tf_op jit(solution)/shard_map/all_to_all | solution.py:124
  1182.0 49.5 %all-gather.19.cloned.1.call-done = bf16[2560,768]{1,0:T(8,128)(2,1)} async-done(((bf16[640,768]{1,0:T(8,128)(2,1)}), bf16[2560,768]{1,0:T(8,128)(2,1)}) %all-gather.19.cloned.1.call-update) | async-done | bytes 3932176 | tf_op jit(solution)/shard_map/all_gather | solution.py:252
  1237.3 284.6 %while.60 = (s32[]{:T(128)}, f32[2560,3,64]{0,2,1:T(8,128)}, f32[2560,3,64]{0,2,1:T(8,128)}, bf16[5,512,3,64]{1,0,3,2:T(8,128)(2,1)}, s32[5]{0:T(128)S(1)}, /*in...) while((s32[]{:T(128)}, f32[2560,3,64]{0,2,1:T(8,128)}, ...), condition=%wide.region_37.38_spmd.clone.clone, body=%wide.region_35.37_spmd.clone.clone.sunk | while | flops 2566420992 | bytes 164718880 | solution.py:115
  1243.4 8.8 fusion.293
  1252.2 9.4 multiply_reduce_fusion.11
  1261.6 9.5 multiply_convert_fusion.14
  1299.1 8.8 fusion.293
  1307.9 9.4 multiply_reduce_fusion.11
  1317.2 9.5 multiply_convert_fusion.14
  1356.3 8.8 fusion.293
  1365.0 9.4 multiply_reduce_fusion.11
  1374.4 9.5 multiply_convert_fusion.14
  1413.4 8.8 fusion.293
  1422.2 9.4 multiply_reduce_fusion.11
  1431.6 9.5 multiply_convert_fusion.14
  1479.3 9.3 multiply_reduce_fusion.11
  1488.7 9.5 multiply_convert_fusion.14
  1533.7 50.6 %reduce-scatter.19.cloned.1.call-done = bf16[640,768]{1,0:T(8,128)(2,1)} async-done(((bf16[2560,768]{1,0:T(8,128)(2,1)}), bf16[640,768]{1,0:T(8,128)(2,1)}) %reduce-scatter.19.cloned.1.call-update) | async-done | bytes 983056 | tf_op jit(solution)/shard_map/reduce_scatter | solution.py:267
  1593.8 38.5 %all_to_all.43 = bf16[4,240,768]{2,1,0:T(8,128)(2,1)} all-to-all(bf16[4,240,768]{2,1,0:T(8,128)(2,1)S(1)} %bitcast.370), channel_id=1, replica_groups=mesh['dp'=2,'expert'=4,'tensor'=4] {'expert'}, dimensions={0} | all-to-all | bytes 2949120 | tf_op jit(solution)/shard_map/all_to_all | solution.py:120
  1632.4 66.0 %all-gather.21.cloned.1.call-done = bf16[3840,768]{1,0:T(8,128)(2,1)} async-done(((bf16[960,768]{1,0:T(8,128)(2,1)}), bf16[3840,768]{1,0:T(8,128)(2,1)}) %all-gather.21.cloned.1.call-update) | async-done | bytes 5898256 | tf_op jit(solution)/shard_map/all_gather | solution.py:232
  1698.3 14.7 fusion.68
  1722.4 67.1 %reduce-scatter.21.cloned.1.call-done = bf16[960,768]{1,0:T(8,128)(2,1)} async-done(((bf16[3840,768]{1,0:T(8,128)(2,1)}), bf16[960,768]{1,0:T(8,128)(2,1)}) %reduce-scatter.21.cloned.1.call-update) | async-done | bytes 1474576 | tf_op jit(solution)/shard_map/reduce_scatter | solution.py:238
  1793.8 34.3 %all-to-all-done.7 = bf16[4,240,768]{2,1,0:T(8,128)(2,1)S(1)} async-done(((bf16[4,240,768]{2,1,0:T(8,128)(2,1)}), bf16[4,240,768]{2,1,0:T(8,128)(2,1)S(1)}, u32[]{:S(2)}, u32[]{:S(2)}) %all-to-all-start.7) | async-done | bytes 1474592 | tf_op jit(solution)/shard_map/all_to_all | solution.py:124
  1837.7 11.1 fusion.114
  1848.8 10.4 fusion.112
  1878.1 9.1 all-gather.23.cloned.1.call-done
  1892.9 290.7 %while.61 = (s32[]{:T(128)}, f32[2560,3,64]{0,2,1:T(8,128)}, f32[2560,3,64]{0,2,1:T(8,128)}, bf16[5,512,3,64]{1,0,3,2:T(8,128)(2,1)}, s32[5]{0:T(128)S(1)}, /*in...) while((s32[]{:T(128)}, f32[2560,3,64]{0,2,1:T(8,128)}, ...), condition=%wide.region_45.46_spmd.clone.clone, body=%wide.region_43.45_spmd.clone.clone.sunk | while | flops 2566420992 | bytes 164718880 | solution.py:115
  1899.9 8.8 fusion.306
  1908.8 10.0 multiply_reduce_fusion.12
  1918.8 9.6 multiply_convert_fusion.15
  1957.5 8.7 fusion.306
  1966.2 9.4 multiply_reduce_fusion.12
  1975.6 9.5 multiply_convert_fusion.15
  2015.8 8.7 fusion.306
  2024.5 9.4 multiply_reduce_fusion.12
  2033.9 9.5 multiply_convert_fusion.15
  2074.0 8.7 fusion.306
  2082.7 9.4 multiply_reduce_fusion.12
  2092.1 9.5 multiply_convert_fusion.15
  2141.0 9.3 multiply_reduce_fusion.12
  2150.3 9.5 multiply_convert_fusion.15
  2215.4 90.7 %all-reduce.10.cloned.1.call-done = (f32[1,768,3,192]{1,3,2,0:T(8,128)}, f32[1,768,3,192]{1,3,2,0:T(8,128)}, f32[1,192,768]{2,1,0:T(8,128)}, f32[1,192,768]{2,1,0:T(8,128)}) async-done(((f32[1,768,3,192]{1,3,2,0:T(8,128)}, f32[1,768,3,192]{1,3,2,0:T(8,128)}, f32[1,192,768]{2,1,0:T(8,128)}, f32[1,192,768]{2,1,0:T(8,128)}), (f32[1,768,3,192]{1,3,2,0:T(8,128)}, f32[1,768,3,192]{1,3,2,0:T(8,128)}, ...) | async-done | bytes 4718608 | tf_op jit(solution)/shard_map/psum | solution.py:284
  2312.3 47.7 %reduce-scatter.23.cloned.1.call-done = bf16[640,768]{1,0:T(8,128)(2,1)} async-done(((bf16[2560,768]{1,0:T(8,128)(2,1)}), bf16[640,768]{1,0:T(8,128)(2,1)}) %reduce-scatter.23.cloned.1.call-update) | async-done | bytes 983056 | tf_op jit(solution)/shard_map/reduce_scatter | solution.py:267
  2362.1 39.3 %all-reduce.4 = (f32[1,768]{1,0:T(1,128)S(1)}, f32[1,768]{1,0:T(1,128)S(1)}, f32[1,768]{1,0:T(1,128)S(1)}, f32[1,768]{1,0:T(1,128)S(1)}, f32[1,768,4]{1,2,0:T(4,128)S(1)}, /*index=5*/f32[1,768,4]{1,2,0:T(4,128)S(1)}) all-reduce(f32[1,768]{1,0:T(1,128)S(1)} %stack.94, ...), channel_id=1, replica_groups=mesh['dp'=2,'expert'=4,'tensor'=4] {'dp','expert','tensor'}, use_global_device_ids=true, to_apply=%region_51.52 | all-reduce | flops 9216 | bytes 73728 | tf_op jit(solution)/shard_map/psum | solution.py:285
  (671 shorter events, 730.4 us)
Async XLA Ops:
  7.2 58.8 %all-gather.9.cloned.1.call-start = ((), (), s32[]{:S(2)}) async-start(), calls=%async_computation.16 | async-start | bytes 4915200 | tf_op jit(solution)/shard_map/all_gather | solution.py:134
  13.3 211.5 %reduce-scatter.9.cloned.1.call-start = ((), (), s32[]{:S(2)}) async-start(), calls=%async_computation.17 | async-start | bytes 4915200 | tf_op jit(solution)/shard_map/reduce_scatter | solution.py:141
  14.7 55.9 %copy-start.48 = (bf16[1,768,3,192]{1,3,2,0:T(8,128)(2,1)}, bf16[1,768,3,192]{1,3,2,0:T(8,128)(2,1)S(1)}, u32[]{:S(2)}) copy-start(bf16[1,768,3,192]{1,3,2,0:T(8,128)(2,1)S(1)} %get-tuple-element.730) | copy-start | bytes 2654212
  174.1 50.7 %copy-start.6 = (bf16[640,768]{1,0:T(8,128)(2,1)S(1)}, bf16[640,768]{1,0:T(8,128)(2,1)}, u32[]{:S(2)}) copy-start(bf16[640,768]{1,0:T(8,128)(2,1)} %param.21) | copy-start | bytes 2949124
  174.1 164.8 %all-gather.11.cloned.1.call-start = ((), (), s32[]{:S(2)}) async-start(), calls=%async_computation.18 | async-start | bytes 7372800 | tf_op jit(solution)/shard_map/all_gather | solution.py:166
  174.8 52.2 %copy-start.56 = (s32[640]{0:T(1024)}, s32[640]{0:T(1024)S(1)}, u32[]{:S(2)}) copy-start(s32[640]{0:T(1024)S(1)} %get-tuple-element.572) | copy-start | bytes 7684
  174.8 257.6 %copy-start.59 = (s32[640]{0:T(1024)}, s32[640]{0:T(1024)S(1)}, u32[]{:S(2)}) copy-start(s32[640]{0:T(1024)S(1)} %get-tuple-element.573) | copy-start | bytes 7684
  183.0 47.2 %copy-start.83 = (s32[1024]{0:T(1024)}, s32[1024]{0:T(1024)S(1)}, u32[]{:S(2)}) copy-start(s32[1024]{0:T(1024)S(1)} %pad_clamp_fusion.3) | copy-start | bytes 12292
  183.6 43.4 %copy-start.77 = (f32[768]{0:T(1024)}, f32[768]{0:T(1024)S(1)}, u32[]{:S(2)}) copy-start(f32[768]{0:T(1024)S(1)} %get-tuple-element.575) | copy-start | bytes 9220
  272.9 154.7 %reduce-scatter.11.cloned.1.call-start = ((), (), s32[]{:S(2)}) async-start(), calls=%async_computation.19 | async-start | bytes 7372800 | tf_op jit(solution)/shard_map/reduce_scatter | solution.py:169
  360.5 71.4 %copy-start.20 = (bf16[640,768]{1,0:T(8,128)(2,1)S(1)}, bf16[640,768]{1,0:T(8,128)(2,1)}, u32[]{:S(2)}) copy-start(bf16[640,768]{1,0:T(8,128)(2,1)} %copy-done.19) | copy-start | bytes 2949124
  360.5 71.4 %copy-start.87 = (bf16[2,768,4]{1,2,0:T(4,128)(2,1)S(1)}, bf16[2,768,4]{1,2,0:T(4,128)(2,1)}, u32[]{:S(2)}) copy-start(bf16[2,768,4]{1,2,0:T(4,128)(2,1)} %param.30) | copy-start | bytes 36868
  427.6 38.7 %all-to-all-start.1 = ((bf16[4,240,768]{2,1,0:T(8,128)(2,1)}), bf16[4,240,768]{2,1,0:T(8,128)(2,1)S(1)}, u32[]{:S(2)}, u32[]{:S(2)}) async-start(bf16[4,240,768]{2,1,0:T(8,128)(2,1)} %bitcast.385), calls=%async_computation.3 | async-start | bytes 2949120 | tf_op jit(solution)/shard_map/all_to_all | solution.py:124
  431.9 91.7 %all-gather.13.cloned.1.call-start = ((), (), s32[]{:S(2)}) async-start(), calls=%async_computation.20 | async-start | bytes 4915200 | tf_op jit(solution)/shard_map/all_gather | solution.py:134
  432.0 37.7 %copy-start.85 = (s32[1024]{0:T(1024)}, s32[1024]{0:T(1024)S(1)}, u32[]{:S(2)}) copy-start(s32[1024]{0:T(1024)S(1)} %pad_clamp_fusion.2) | copy-start | bytes 12292
  433.0 36.7 %copy-start.69 = (f32[640]{0:T(1024)}, f32[640]{0:T(1024)S(1)}, u32[]{:S(2)}) copy-start(f32[640]{0:T(1024)S(1)} %get-tuple-element.712) | copy-start | bytes 7684
  471.6 52.1 %copy-start.49 = (bf16[1,768,3,192]{1,3,2,0:T(8,128)(2,1)S(1)}, bf16[1,768,3,192]{1,3,2,0:T(8,128)(2,1)}, u32[]{:S(2)}) copy-start(bf16[1,768,3,192]{1,3,2,0:T(8,128)(2,1)} %get-tuple-element.729) | copy-start | bytes 2654212
  472.2 56.0 %copy-start.66 = (f32[640]{0:T(1024)}, f32[640]{0:T(1024)S(1)}, u32[]{:S(2)}) copy-start(f32[640]{0:T(1024)S(1)} %get-tuple-element.738) | copy-start | bytes 7684
  474.1 208.1 %reduce-scatter.13.cloned.1.call-start = ((), (), s32[]{:S(2)}) async-start(), calls=%async_computation.21 | async-start | bytes 4915200 | tf_op jit(solution)/shard_map/reduce_scatter | solution.py:141
  631.4 54.1 %copy-start.68 = (f32[768]{0:T(1024)S(1)}, f32[768]{0:T(1024)}, u32[]{:S(2)}) copy-start(f32[768]{0:T(1024)} %get-tuple-element.574) | copy-start | bytes 9220
  631.5 165.4 %all-gather.15.cloned.1.call-start = ((), (), s32[]{:S(2)}) async-start(), calls=%async_computation.22 | async-start | bytes 7372800 | tf_op jit(solution)/shard_map/all_gather | solution.py:166
  730.8 153.6 %reduce-scatter.15.cloned.1.call-start = ((), (), s32[]{:S(2)}) async-start(), calls=%async_computation.23 | async-start | bytes 7372800 | tf_op jit(solution)/shard_map/reduce_scatter | solution.py:169
  796.8 11.6 copy-start.104
  817.3 71.5 %copy-start.23 = (bf16[640,768]{1,0:T(8,128)(2,1)S(1)}, bf16[640,768]{1,0:T(8,128)(2,1)}, u32[]{:S(2)}) copy-start(bf16[640,768]{1,0:T(8,128)(2,1)} %copy-done.22) | copy-start | bytes 2949124
  817.3 71.5 %copy-start.88 = (bf16[2,768,4]{1,2,0:T(4,128)(2,1)S(1)}, bf16[2,768,4]{1,2,0:T(4,128)(2,1)}, u32[]{:S(2)}) copy-start(bf16[2,768,4]{1,2,0:T(4,128)(2,1)} %param.30) | copy-start | bytes 36868
  817.4 71.9 %copy-start.57 = (s32[640]{0:T(1024)S(1)}, s32[640]{0:T(1024)}, u32[]{:S(2)}) copy-start(s32[640]{0:T(1024)} %copy-done.56) | copy-start | bytes 7684
  884.4 38.8 %all-to-all-start.3 = ((bf16[4,240,768]{2,1,0:T(8,128)(2,1)}), bf16[4,240,768]{2,1,0:T(8,128)(2,1)}, u32[]{:S(2)}, u32[]{:S(2)}) async-start(bf16[4,240,768]{2,1,0:T(8,128)(2,1)} %bitcast.386), calls=%async_computation.7 | async-start | bytes 2949120 | tf_op jit(solution)/shard_map/all_to_all | solution.py:124
  888.8 151.6 %all-gather.17.cloned.1.call-start = ((), (), s32[]{:S(2)}) async-start(), calls=%async_computation.24 | async-start | bytes 7372800 | tf_op jit(solution)/shard_map/all_gather | solution.py:232
  889.3 286.3 %copy-start.62 = (f32[640,4]{0,1:T(4,128)}, f32[640,4]{0,1:T(4,128)S(1)}, u32[]{:S(2)}) copy-start(f32[640,4]{0,1:T(4,128)S(1)} %get-tuple-element.707) | copy-start | bytes 30724
  973.9 157.8 %reduce-scatter.17.cloned.1.call-start = ((), (), s32[]{:S(2)}) async-start(), calls=%async_computation.25 | async-start | bytes 7372800 | tf_op jit(solution)/shard_map/reduce_scatter | solution.py:238
  1040.4 17.5 copy-start.105
  1131.7 38.8 %all-to-all-start.5 = ((bf16[4,240,768]{2,1,0:T(8,128)(2,1)}), bf16[4,240,768]{2,1,0:T(8,128)(2,1)}, u32[]{:S(2)}, u32[]{:S(2)}) async-start(bf16[4,240,768]{2,1,0:T(8,128)(2,1)} %bitcast.388), calls=%async_computation.10 | async-start | bytes 2949120 | tf_op jit(solution)/shard_map/all_to_all | solution.py:124
  1136.0 95.5 %all-gather.19.cloned.1.call-start = ((), (), s32[]{:S(2)}) async-start(), calls=%async_computation.26 | async-start | bytes 4915200 | tf_op jit(solution)/shard_map/all_gather | solution.py:252
  1136.1 39.5 %copy-start.81 = (f32[640]{0:T(1024)}, f32[640]{0:T(1024)S(1)}, u32[]{:S(2)}) copy-start(f32[640]{0:T(1024)S(1)} %mul.613) | copy-start | bytes 7684
  1179.5 52.0 %copy-start.53 = (bf16[2,192,768]{2,1,0:T(8,128)(2,1)S(1)}, bf16[2,192,768]{2,1,0:T(8,128)(2,1)}, u32[]{:S(2)}) copy-start(bf16[2,192,768]{2,1,0:T(8,128)(2,1)} %param.28) | copy-start | bytes 1769476
  1181.9 402.4 %reduce-scatter.19.cloned.1.call-start = ((), (), s32[]{:S(2)}) async-start(), calls=%async_computation.27 | async-start | bytes 4915200 | tf_op jit(solution)/shard_map/reduce_scatter | solution.py:267
  1533.6 50.7 %copy-start.10 = (f32[640,768]{1,0:T(8,128)S(1)}, f32[640,768]{1,0:T(8,128)}, u32[]{:S(2)}) copy-start(f32[640,768]{1,0:T(8,128)} %copy-done.9) | copy-start | bytes 5898244
  1533.6 50.7 %copy-start.65 = (f32[768]{0:T(1024)S(1)}, f32[768]{0:T(1024)}, u32[]{:S(2)}) copy-start(f32[768]{0:T(1024)} %get-tuple-element.576) | copy-start | bytes 9220
  1533.6 50.7 %copy-start.67 = (f32[640]{0:T(1024)S(1)}, f32[640]{0:T(1024)}, u32[]{:S(2)}) copy-start(f32[640]{0:T(1024)} %copy-done.66) | copy-start | bytes 7684
  1533.6 53.5 %copy-start.30 = (bf16[640,768]{1,0:T(8,128)(2,1)S(1)}, bf16[640,768]{1,0:T(8,128)(2,1)}, u32[]{:S(2)}) copy-start(bf16[640,768]{1,0:T(8,128)(2,1)} %gather_fusion.1) | copy-start | bytes 2949124
  1533.6 53.5 %copy-start.91 = (f32[640]{0:T(1024)S(1)}, f32[640]{0:T(1024)}, u32[]{:S(2)}) copy-start(f32[640]{0:T(1024)} %get-tuple-element.737) | copy-start | bytes 7684
  1533.6 164.7 %all-gather.21.cloned.1.call-start = ((), (), s32[]{:S(2)}) async-start(), calls=%async_computation.28 | async-start | bytes 7372800 | tf_op jit(solution)/shard_map/all_gather | solution.py:232
  1632.3 83.4 %copy-start.106 = (bf16[2,1,768,768]{3,2,1,0:T(8,128)(2,1)S(1)}, bf16[2,1,768,768]{3,2,1,0:T(8,128)(2,1)}, u32[]{:S(2)}) copy-start(bf16[2,1,768,768]{3,2,1,0:T(8,128)(2,1)} %param.31) | copy-start | bytes 7077892
  1632.3 157.2 %reduce-scatter.21.cloned.1.call-start = ((), (), s32[]{:S(2)}) async-start(), calls=%async_computation.29 | async-start | bytes 7372800 | tf_op jit(solution)/shard_map/reduce_scatter | solution.py:238
  1722.4 105.8 %copy-start.86 = (s32[1024]{0:T(1024)S(1)}, s32[1024]{0:T(1024)}, u32[]{:S(2)}) copy-start(s32[1024]{0:T(1024)} %copy-done.85) | copy-start | bytes 12292
  1789.5 38.7 %all-to-all-start.7 = ((bf16[4,240,768]{2,1,0:T(8,128)(2,1)}), bf16[4,240,768]{2,1,0:T(8,128)(2,1)S(1)}, u32[]{:S(2)}, u32[]{:S(2)}) async-start(bf16[4,240,768]{2,1,0:T(8,128)(2,1)} %bitcast.387), calls=%async_computation.14 | async-start | bytes 2949120 | tf_op jit(solution)/shard_map/all_to_all | solution.py:124
  1793.8 93.4 %all-gather.23.cloned.1.call-start = ((), (), s32[]{:S(2)}) async-start(), calls=%async_computation.30 | async-start | bytes 4915200 | tf_op jit(solution)/shard_map/all_gather | solution.py:252
  1793.8 37.8 %copy-start.93 = (f32[640]{0:T(1024)}, f32[640]{0:T(1024)S(1)}, u32[]{:S(2)}) copy-start(f32[640]{0:T(1024)S(1)} %mul.645) | copy-start | bytes 7684
  1837.6 371.0 %all-reduce.12.cloned.1.call-start = ((), (), s32[]{:S(2)}) async-start(), calls=%async_computation.33 | async-start | bytes 9437184 | tf_op jit(solution)/shard_map/psum | solution.py:289
  1837.7 27.1 %slice-start.6 = ((s8[11796480]{0:T(1024)(128)(4,1)}), s8[4194304]{0:T(1024)(128)(4,1)S(1)}, s32[]{:S(2)}) async-start(s8[11796480]{0:T(1024)(128)(4,1)} %bitcast.405), calls=%async_computation.40 | async-start | bytes 8388608
  1837.7 27.1 %slice-start.7 = ((s8[11796480]{0:T(1024)(128)(4,1)}), s8[4194304]{0:T(1024)(128)(4,1)S(1)}, s32[]{:S(2)}) async-start(s8[11796480]{0:T(1024)(128)(4,1)} %bitcast.405), calls=%async_computation.41 | async-start | bytes 8388608
  1848.8 12.2 copy-start.103
  1848.8 16.0 slice-start.8
  1861.0 10.9 slice-start
  1861.0 10.9 slice-start.4
  1878.1 14.9 copy-start.3
  1878.1 14.9 copy-start.12
  1878.1 428.0 %all-reduce.10.cloned.1.call-start = ((), (), s32[]{:S(2)}) async-start(), calls=%async_computation.32 | async-start | bytes 9437184 | tf_op jit(solution)/shard_map/psum | solution.py:284
  2198.5 161.4 %reduce-scatter.23.cloned.1.call-start = ((), (), s32[]{:S(2)}) async-start(), calls=%async_computation.31 | async-start | bytes 4915200 | tf_op jit(solution)/shard_map/reduce_scatter | solution.py:267
  2308.5 51.4 %copy-start.8 = (bf16[640,768]{1,0:T(8,128)(2,1)S(1)}, bf16[640,768]{1,0:T(8,128)(2,1)}, u32[]{:S(2)}) copy-start(bf16[640,768]{1,0:T(8,128)(2,1)} %param.21) | copy-start | bytes 2949124
  2308.5 51.4 %copy-start.72 = (f32[640]{0:T(1024)S(1)}, f32[640]{0:T(1024)}, u32[]{:S(2)}) copy-start(f32[640]{0:T(1024)} %copy-done.71) | copy-start | bytes 7684
  2308.5 51.4 %copy-start.74 = (f32[768]{0:T(1024)S(1)}, f32[768]{0:T(1024)}, u32[]{:S(2)}) copy-start(f32[768]{0:T(1024)} %copy-done.73) | copy-start | bytes 9220
  2308.5 94.7 %copy-start.33 = (f32[640,768]{1,0:T(8,128)S(1)}, f32[640,768]{1,0:T(8,128)}, u32[]{:S(2)}) copy-start(f32[640,768]{1,0:T(8,128)} %get-tuple-element.701) | copy-start | bytes 5898244
  2308.5 94.6 %copy-start.98 = (f32[640]{0:T(1024)S(1)}, f32[640]{0:T(1024)}, u32[]{:S(2)}) copy-start(f32[640]{0:T(1024)} %get-tuple-element.733) | copy-start | bytes 7684
  (86 other events, 318.0 us)
Sparse Core Ops, SparseCore 0:
  13.4 52.5 all-gather.8
  174.2 50.5 reduce-scatter.8
  273.0 65.8 all-gather.10
  360.7 66.9 reduce-scatter.10
  474.2 49.4 all-gather.12
  631.6 50.5 reduce-scatter.12
  730.9 65.8 all-gather.14
  817.5 66.9 reduce-scatter.14
  974.0 66.3 all-gather.16
  1064.7 66.9 reduce-scatter.16
  1182.0 49.4 all-gather.18
  1533.8 50.5 reduce-scatter.18
  1632.4 65.8 all-gather.20
  1722.5 66.9 reduce-scatter.20
  1837.7 49.4 all-gather.22
  1890.4 29.7 all-reduce.11
  2198.7 107.3 all-reduce.9
  2309.3 50.6 reduce-scatter.22
where the time goes:
time: 2420 us; the launch traced here: 2410 us
  waiting for transfers between devices  1100 us (45%)
  matrix products  584 us (24%)
  other arithmetic  254 us (10%)
  local copies, waits for them, and re-layouts  203 us (8%)
  blocking collectives  193 us (8%)
  loops' own time  40.2 us (2%)
    all_to_all x4, blocking collectives, to_experts(): lax.all_to_all(buffer, 'expert', split_axis=0, concat_axis=0, tiled=True)  154 us
    all_to_all x4, waiting for transfers between devices, from_experts(): lax.all_to_all(buffer, 'expert', split_axis=0, concat_axis=0, tiled=True)  136 us
    reduce_scatter x2, waiting for transfers between devices, backward_layer(): lax.psum_scatter(jnp.dot(d_pre, w_up[0].T, preferred_element_type=jnp.flo...  134 us
    reduce_scatter x2, waiting for transfers between devices, forward_layer(): lax.psum_scatter(jnp.dot(hidden, w_back[0], preferred_element_type=jnp.fl...  134 us
    all_gather x2, waiting for transfers between devices, backward_layer(): d_slots = lax.all_gather(d_arrived, 'tensor', axis=0, tiled=True)  132 us
    all_gather x2, waiting for transfers between devices, forward_layer(): slot_all = lax.all_gather(arrived, 'tensor', axis=0, tiled=True)  132 us
    dot_general x20, matrix products, block_scores(): jnp.einsum('qhd,khd->hqk', query_rows, keys_all, preferred_element_type=j...  128 us
    all_gather x2, waiting for transfers between devices, forward_layer(): normed_all = lax.all_gather(normed, 'tensor', axis=0, tiled=True)  101 us
  transfers between devices with their start and end apart: 22, of which 21 were waited for; matrix products, arithmetic and copies ran while one was open for 16% of the time, Pallas kernels for 0%

commit v1 on v0

v1 whole, which is shorter than its diff:
```python
import functools

import jax
import jax.numpy as jnp
from jax import lax
from jax.experimental import pallas as pl
from jax.experimental.pallas import tpu as pltpu
from jax.sharding import PartitionSpec as P

HEAD_DIM = 64
BLK = 128
TRUNK = 8
PAIR = 2 * HEAD_DIM
EPS = 1e-06
NEG = -1000000000.0
BIG = 1 << 20
F32 = jnp.float32
BF16 = jnp.bfloat16
VMEM_LIMIT = 56 * 1024 * 1024

NT = (((1,), (1,)), ((), ()))
TN = (((0,), (0,)), ((), ()))


def dot(a, b):
    return jnp.dot(a, b, preferred_element_type=F32)


def dot_nt(a, b):
    return lax.dot_general(a, b, NT, preferred_element_type=F32)


def dot_tn(a, b):
    return lax.dot_general(a, b, TN, preferred_element_type=F32)


def cost(macs, moved, trans=0):
    return pl.CostEstimate(flops=2 * macs, bytes_accessed=moved, transcendentals=trans)


def xperm(x, axis, k):
    n = lax.axis_size(axis)
    return lax.ppermute(x, axis, [(i, i ^ k) for i in range(n)])


def after(x, dep):
    return lax.optimization_barrier((x, dep))[0]


def gather_rows(x):
    half = x.shape[0] // 2
    lo, hi = x[:half], x[half:]
    a_lo, b_hi = xperm(lo, "tensor", 1), xperm(hi, "tensor", 2)
    a_hi, b_lo = xperm(hi, "tensor", 1), xperm(lo, "tensor", 2)
    c_lo, c_hi = xperm(a_lo, "tensor", 2), xperm(b_hi, "tensor", 1)
    return [x, a_lo, a_hi, b_lo, b_hi, c_lo, c_hi]


def gather_shared(mine, other):
    half = mine.shape[0] // 2
    a, b = xperm(mine, "tensor", 1), xperm(mine, "tensor", 2)
    c = jnp.concatenate([xperm(a[:half], "tensor", 2), xperm(b[half:], "tensor", 1)], axis=0)
    got = [mine, a, b, c]
    return got, [other] + [xperm(p, "dp", 1) for p in got[1:]]


def scatter_rows(blocks, own):
    half = own.shape[0] // 2
    b1, b2, b3 = blocks
    x3, y3 = xperm(b3[:half], "tensor", 1), xperm(b3[half:], "tensor", 2)
    x1, y2 = xperm(b1[:half], "tensor", 1), xperm(b2[half:], "tensor", 2)
    x2 = xperm((b2[:half].astype(F32) + x3.astype(F32)).astype(BF16), "tensor", 2)
    y1 = xperm((b1[half:].astype(F32) + y3.astype(F32)).astype(BF16), "tensor", 1)
    low = own[:half] + x1.astype(F32) + x2.astype(F32)
    high = own[half:] + y2.astype(F32) + y1.astype(F32)
    return jnp.concatenate([low, high], axis=0)


def scatter_shared(mine, other):
    total = mine.astype(F32) + xperm(other, "dp", 1).astype(F32)
    own, rest = total[0], total[1:].astype(BF16)
    return scatter_rows([rest[0], rest[1], rest[2]], own)


def sum_expert(piece):
    n = lax.axis_size("expert")
    if n != 4:
        return lax.psum(piece, "expert")
    rows = piece.shape[0] // n
    z = lax.axis_index("expert")
    cut = [lax.dynamic_slice_in_dim(piece, (z ^ k) * rows, rows, 0) for k in range(n)]
    total = cut[0]
    for k in range(1, n):
        total = total + xperm(cut[k].astype(BF16), "expert", k).astype(F32)
    low = total.astype(BF16)
    parts = [low] + [xperm(low, "expert", k) for k in range(1, n)]
    stacked = jnp.stack(parts)
    order = jnp.arange(n, dtype=jnp.int32) ^ z
    return jnp.concatenate([lax.dynamic_index_in_dim(stacked, order[k], 0, keepdims=False) for k in range(n)], axis=0)


def sum_small(x):
    for axis in ("dp", "tensor", "expert"):
        n = lax.axis_size(axis)
        k = 1
        while k < n:
            x = x + xperm(x, axis, k)
            k *= 2
    return x


def by_core(mine, other, axis):
    first = lax.axis_index("dp") == 0
    return jnp.concatenate([jnp.where(first, mine, other), jnp.where(first, other, mine)], axis=axis)


def exchange(chunks):
    n = len(chunks)
    if n == 4:
        return [chunks[0]] + [xperm(chunks[k], "expert", k) for k in range(1, n)]
    out = lax.all_to_all(jnp.stack(chunks), "expert", split_axis=0, concat_axis=0, tiled=True)
    return [out[k] for k in range(n)]


def masked_pair(x):
    lane = lax.broadcasted_iota(jnp.int32, x.shape, 1)
    zero = jnp.zeros_like(x)
    return jnp.concatenate([jnp.where(lane < HEAD_DIM, x, zero), jnp.where(lane < HEAD_DIM, zero, x)], axis=0)


def attend_kernel(table, q_ref, k_ref, v_ref, out_ref, lse_ref, keys, values):
    pair = pl.program_id(0)
    blocks = k_ref.shape[0] // BLK
    mine = q_ref.shape[0] // BLK
    trunk = TRUNK * BLK
    for b in range(blocks):
        place = pl.ds(pl.multiple_of(table[b] * BLK, BLK), BLK)
        rows = pl.ds(b * BLK, BLK)
        keys[place, :] = k_ref[rows, :]
        values[place, pl.ds(0, PAIR)] = v_ref[rows, :]
    values[:, pl.ds(PAIR, PAIR)] = jnp.ones((blocks * BLK, PAIR), BF16)
    lane = lax.broadcasted_iota(jnp.int32, (BLK, PAIR), 1)
    for i in range(mine):
        at = blocks + 5 * i
        place_q, own, parent, base_own, base_parent = [table[at + j] for j in range(5)]
        rows = pl.ds(i * BLK, BLK)
        own_rows = pl.ds(pl.multiple_of(own * BLK, BLK), BLK)
        parent_rows = pl.ds(pl.multiple_of(parent * BLK, BLK), BLK)
        q = masked_pair(q_ref[rows, :] * jnp.asarray(HEAD_DIM ** -0.5, BF16))
        row = lax.broadcasted_iota(jnp.int32, (2 * BLK, 1), 0) % BLK
        pos_q = place_q + row
        s_trunk = dot_nt(q, keys[pl.ds(0, trunk), :])
        key_pos = lax.broadcasted_iota(jnp.int32, s_trunk.shape, 1)
        s_trunk = jnp.where(key_pos <= pos_q, s_trunk, NEG)
        s_parent = dot_nt(q, keys[parent_rows, :])
        col = lax.broadcasted_iota(jnp.int32, s_parent.shape, 1)
        s_parent = jnp.where(col + base_parent <= pos_q, s_parent, NEG)
        s_own = dot_nt(q, keys[own_rows, :])
        s_own = jnp.where(col + base_own <= pos_q, s_own, NEG)
        top = jnp.maximum(
            jnp.max(s_trunk, axis=1, keepdims=True),
            jnp.max(jnp.maximum(s_parent, s_own), axis=1, keepdims=True),
        )
        p_trunk = jnp.exp(s_trunk - top).astype(BF16)
        p_parent = jnp.exp(s_parent - top).astype(BF16)
        p_own = jnp.exp(s_own - top).astype(BF16)
        both = dot(p_trunk, values[pl.ds(0, trunk), :])
        both = both + dot(p_parent, values[parent_rows, :]) + dot(p_own, values[own_rows, :])
        total = both[:, PAIR:]
        heads = both[:, :PAIR] / total
        lse = top + jnp.log(total)
        out_ref[rows, :] = jnp.where(lane < HEAD_DIM, heads[:BLK], heads[BLK:]).astype(BF16)
        known = jnp.where(pair == 0, 0.0, lse_ref[rows, :])
        known = jnp.where(lane == 2 * pair, lse[:BLK], known)
        lse_ref[rows, :] = jnp.where(lane == 2 * pair + 1, lse[BLK:], known)


def attend(table, q, k, v):
    mine, width = q.shape
    rows = k.shape[0]
    pairs = width // PAIR
    column = lambda n: pl.BlockSpec((n, PAIR), lambda p, table: (0, p))
    return pl.pallas_call(
        attend_kernel,
        grid_spec=pltpu.PrefetchScalarGridSpec(
            num_scalar_prefetch=1,
            grid=(pairs,),
            in_specs=[column(mine), column(rows), column(rows)],
            out_specs=[column(mine), pl.BlockSpec((mine, PAIR), lambda p, table: (0, 0))],
            scratch_shapes=[pltpu.VMEM((rows, PAIR), BF16), pltpu.VMEM((rows, 2 * PAIR), BF16)],
        ),
        out_shape=[jax.ShapeDtypeStruct((mine, width), BF16), jax.ShapeDtypeStruct((mine, PAIR), F32)],
        compiler_params=pltpu.CompilerParams(vmem_limit_bytes=VMEM_LIMIT),
        cost_estimate=cost(mine * 1280 * width * 8, 4 * rows * width, mine * 1280 * width // HEAD_DIM),
        name="attend",
    )(table, q, k, v)


def attend_back_kernel(
    table, q_ref, k_ref, v_ref, do_ref, o_ref, lse_ref, dq_ref, dk_ref, dv_ref,
    keys, values, keys_t, dk_acc, dv_acc, lse_t,
):
    pair = pl.program_id(0)
    blocks = k_ref.shape[0] // BLK
    mine = q_ref.shape[0] // BLK
    trunk = TRUNK * BLK
    for b in range(blocks):
        place = pl.ds(pl.multiple_of(table[b] * BLK, BLK), BLK)
        rows = pl.ds(b * BLK, BLK)
        keys[place, :] = k_ref[rows, :]
        values[place, :] = v_ref[rows, :]
        keys_t[:, place] = k_ref[rows, :].T
    dk_acc[...] = jnp.zeros_like(dk_acc)
    dv_acc[...] = jnp.zeros_like(dv_acc)

    @pl.when(pair == 0)
    def _():
        for i in range(mine):
            turned = lse_ref[pl.ds(i * BLK, BLK), :].T
            for p in range(lse_t.shape[0]):
                lse_t[p, pl.ds(0, 2), pl.ds(i * BLK, BLK)] = turned[2 * p : 2 * p + 2]

    lane = lax.broadcasted_iota(jnp.int32, (BLK, PAIR), 1)
    scale = jnp.asarray(HEAD_DIM ** -0.5, BF16)
    for i in range(mine):
        at = blocks + 5 * i
        place_q, own, parent, base_own, base_parent = [table[at + j] for j in range(5)]
        rows = pl.ds(i * BLK, BLK)
        q = masked_pair(q_ref[rows, :] * scale)
        do = do_ref[rows, :]
        product = (do.astype(F32) * o_ref[rows, :].astype(F32)).T
        inner = jnp.concatenate(
            [
                jnp.sum(product[:HEAD_DIM], axis=0, keepdims=True),
                jnp.sum(product[HEAD_DIM:], axis=0, keepdims=True),
            ],
            axis=1,
        )
        do = masked_pair(do)
        lse = jnp.concatenate([lse_t[pair, pl.ds(0, 1), rows], lse_t[pair, pl.ds(1, 1), rows]], axis=1)
        pos_q = place_q + lax.broadcasted_iota(jnp.int32, (1, 2 * BLK), 1) % BLK
        dq_t = jnp.zeros((PAIR, 2 * BLK), F32)
        steps = [(j * 2 * BLK, 2 * BLK, j * 2 * BLK) for j in range(TRUNK // 2)]
        steps += [(pl.multiple_of(parent * BLK, BLK), BLK, base_parent)]
        steps += [(pl.multiple_of(own * BLK, BLK), BLK, base_own)]
        for start, size, base in steps:
            here = pl.ds(start, size)
            k_rows, v_rows = keys[here, :], values[here, :]
            scores = dot_nt(k_rows, q)
            key_pos = base + lax.broadcasted_iota(jnp.int32, (size, 1), 0)
            weights = jnp.exp(jnp.where(key_pos <= pos_q, scores - lse, NEG))
            d_weights = dot_nt(v_rows, do)
            d_scores = (weights * (d_weights - inner)).astype(BF16)
            dv_acc[here, :] += dot(weights.astype(BF16), do)
            dk_acc[here, :] += dot(d_scores, q)
            dq_t = dq_t + dot(keys_t[:, here], d_scores)
        dq = dq_t.T * (HEAD_DIM ** -0.5)
        dq_ref[rows, :] = jnp.where(lane < HEAD_DIM, dq[:BLK], dq[BLK:]).astype(BF16)
    for b in range(blocks):
        place = pl.ds(pl.multiple_of(table[b] * BLK, BLK), BLK)
        rows = pl.ds(b * BLK, BLK)
        dk_ref[rows, :] = dk_acc[place, :].astype(BF16)
        dv_ref[rows, :] = dv_acc[place, :].astype(BF16)


def attend_back(table, q, k, v, d_heads, heads, lse):
    mine, width = q.shape
    rows = k.shape[0]
    pairs = width // PAIR
    column = lambda n: pl.BlockSpec((n, PAIR), lambda p, table: (0, p))
    return pl.pallas_call(
        attend_back_kernel,
        grid_spec=pltpu.PrefetchScalarGridSpec(
            num_scalar_prefetch=1,
            grid=(pairs,),
            in_specs=[
                column(mine), column(rows), column(rows), column(mine), column(mine),
                pl.BlockSpec((mine, PAIR), lambda p, table: (0, 0)),
            ],
            out_specs=[column(mine), column(rows), column(rows)],
            scratch_shapes=[
                pltpu.VMEM((rows, PAIR), BF16),
                pltpu.VMEM((rows, PAIR), BF16),
                pltpu.VMEM((PAIR, rows), BF16),
                pltpu.VMEM((rows, PAIR), F32),
                pltpu.VMEM((rows, PAIR), F32),
                pltpu.VMEM((pairs, 8, mine), F32),
            ],
        ),
        out_shape=[
            jax.ShapeDtypeStruct((mine, width), BF16),
            jax.ShapeDtypeStruct((rows, width), BF16),
            jax.ShapeDtypeStruct((rows, width), BF16),
        ],
        compiler_params=pltpu.CompilerParams(vmem_limit_bytes=VMEM_LIMIT),
        cost_estimate=cost(mine * 1280 * width * 20, 8 * rows * width, mine * 1280 * width // HEAD_DIM),
        name="attend_back",
    )(table, q, k, v, d_heads, heads, lse)


GELU_C = 0.7978845608028654
GELU_A = 0.044715


def row_cuts(total):
    step = next(s for s in (240, 320, 160, 128, total) if total % s == 0)
    return [pl.ds(i, step) for i in range(0, total, step)]


def expert_kernel(rows_ref, up_ref, down_ref, out_ref, hidden_ref, slope_ref, acc):
    step = pl.program_id(0)
    last = pl.num_programs(0) - 1
    for cut in row_cuts(rows_ref.shape[0]):
        u = dot(rows_ref[cut, :], up_ref[0])
        square = u * u
        half = 0.5 + 0.5 * jnp.tanh(u * (GELU_C + (GELU_C * GELU_A) * square))
        hidden = u * half
        low = hidden.astype(BF16)
        hidden_ref[0, cut, :] = low
        slope = half + hidden * (1.0 - half) * (2 * GELU_C + (6 * GELU_C * GELU_A) * square)
        slope_ref[0, cut, :] = slope.astype(BF16)
        part = dot(low, down_ref[0])
        total = jnp.where(step == 0, part, acc[cut, :] + part)
        acc[cut, :] = total

        @pl.when(step == last)
        def _():
            out_ref[cut, :] = total.astype(BF16)


def expert_forward(rows, up, down):
    count, width = rows.shape
    pieces, _, size = up.shape
    whole = pl.BlockSpec((count, width), lambda n: (0, 0))
    piece = pl.BlockSpec((1, count, size), lambda n: (n, 0, 0))
    kept = jax.ShapeDtypeStruct((pieces, count, size), BF16)
    return pl.pallas_call(
        expert_kernel,
        grid=(pieces,),
        in_specs=[
            whole,
            pl.BlockSpec((1, width, size), lambda n: (n, 0, 0)),
            pl.BlockSpec((1, size, width), lambda n: (n, 0, 0)),
        ],
        out_specs=[whole, piece, piece],
        out_shape=[jax.ShapeDtypeStruct((count, width), BF16), kept, kept],
        scratch_shapes=[pltpu.VMEM((count, width), F32)],
        compiler_params=pltpu.CompilerParams(vmem_limit_bytes=VMEM_LIMIT),
        cost_estimate=cost(2 * count * width * size * pieces, 4 * count * size * pieces + 4 * pieces * size * width),
        name="expert_forward",
    )(rows, up, down)


def expert_rows_kernel(
    expert, d_out_ref, up_ref, down_ref, slope_ref, rows_ref, out_ref, route_ref, d_rows_ref, d_pre_ref, d_log_ref, gain_ref, acc,
    *, experts,
):
    step = pl.program_id(0)
    last = pl.num_programs(0) - 1
    count = d_out_ref.shape[0]
    for cut in row_cuts(count):
        d_hidden = dot_nt(d_out_ref[cut, :], down_ref[0])
        d_pre = (d_hidden * slope_ref[0, cut, :].astype(F32)).astype(BF16)
        d_pre_ref[0, cut, :] = d_pre
        part = dot_nt(d_pre, up_ref[0])
        acc[cut, :] = jnp.where(step == 0, part, acc[cut, :] + part)

    @pl.when(step == last)
    def _():
        gain = jnp.zeros((1, acc.shape[1]), F32)
        for cut in row_cuts(count):
            rows = rows_ref[cut, :]
            logits = dot(rows, route_ref[...])
            lane = lax.broadcasted_iota(jnp.int32, logits.shape, 1)
            logits = jnp.where(lane < experts, logits, NEG)
            router = jnp.exp(logits - jnp.max(logits, axis=1, keepdims=True))
            router = router / jnp.sum(router, axis=1, keepdims=True)
            amount = jnp.sum(out_ref[cut, :].astype(F32) * d_out_ref[cut, :].astype(F32), axis=1, keepdims=True)
            d_log = amount * (jnp.where(lane == expert[0], 1.0, 0.0) - router)
            d_low = d_log.astype(BF16)
            d_log_ref[cut, :] = d_low
            d_rows = acc[cut, :] + dot_nt(d_low, route_ref[...])
            gain = gain + jnp.sum(d_rows * rows.astype(F32), axis=0, keepdims=True)
            d_rows_ref[cut, :] = d_rows.astype(BF16)
        gain_ref[...] = gain


def expert_rows(expert, d_out, up, down, slope, rows, out, route, experts):
    count, width = d_out.shape
    pieces, _, size = up.shape
    lanes = route.shape[1]
    whole = pl.BlockSpec((count, width), lambda n, e: (0, 0))
    piece = pl.BlockSpec((1, count, size), lambda n, e: (n, 0, 0))
    return pl.pallas_call(
        functools.partial(expert_rows_kernel, experts=experts),
        grid_spec=pltpu.PrefetchScalarGridSpec(
            num_scalar_prefetch=1,
            grid=(pieces,),
            in_specs=[
                whole,
                pl.BlockSpec((1, width, size), lambda n, e: (n, 0, 0)),
                pl.BlockSpec((1, size, width), lambda n, e: (n, 0, 0)),
                piece, whole, whole,
                pl.BlockSpec((width, lanes), lambda n, e: (0, 0)),
            ],
            out_specs=[
                whole, piece,
                pl.BlockSpec((count, lanes), lambda n, e: (0, 0)),
                pl.BlockSpec((1, width), lambda n, e: (0, 0)),
            ],
            scratch_shapes=[pltpu.VMEM((count, width), F32)],
        ),
        out_shape=[
            jax.ShapeDtypeStruct((count, width), BF16),
            jax.ShapeDtypeStruct((pieces, count, size), BF16),
            jax.ShapeDtypeStruct((count, lanes), BF16),
            jax.ShapeDtypeStruct((1, width), F32),
        ],
        compiler_params=pltpu.CompilerParams(vmem_limit_bytes=VMEM_LIMIT),
        cost_estimate=cost(2 * count * width * size * pieces, 4 * count * size * pieces + 4 * pieces * size * width),
        name="expert_rows",
    )(expert, d_out, up, down, slope, rows, out, route)


def expert_grads_kernel(rows_ref, d_out_ref, hidden_ref, d_pre_ref, d_log_ref, up_ref, down_ref, route_ref, rows_t):
    @pl.when(pl.program_id(0) == 0)
    def _():
        rows_t[...] = rows_ref[...].T
        route_ref[...] = dot(rows_t[...], d_log_ref[...])

    up_ref[0] = dot(rows_t[...], d_pre_ref[0]).astype(BF16)
    down_ref[0] = dot_tn(hidden_ref[0], d_out_ref[...]).astype(BF16)


def expert_grads(rows, d_out, hidden, d_pre, d_log):
    count, width = rows.shape
    pieces, _, size = hidden.shape
    lanes = d_log.shape[1]
    whole = pl.BlockSpec((count, width), lambda n: (0, 0))
    piece = pl.BlockSpec((1, count, size), lambda n: (n, 0, 0))
    return pl.pallas_call(
        expert_grads_kernel,
        grid=(pieces,),
        in_specs=[whole, whole, piece, piece, pl.BlockSpec((count, lanes), lambda n: (0, 0))],
        out_specs=[
            pl.BlockSpec((1, width, size), lambda n: (n, 0, 0)),
            pl.BlockSpec((1, size, width), lambda n: (n, 0, 0)),
            pl.BlockSpec((width, lanes), lambda n: (0, 0)),
        ],
        out_shape=[
            jax.ShapeDtypeStruct((pieces, width, size), BF16),
            jax.ShapeDtypeStruct((pieces, size, width), BF16),
            jax.ShapeDtypeStruct((width, lanes), F32),
        ],
        scratch_shapes=[pltpu.VMEM((width, count), BF16)],
        compiler_params=pltpu.CompilerParams(vmem_limit_bytes=VMEM_LIMIT),
        cost_estimate=cost(2 * count * width * size * pieces, 4 * count * size * pieces + 4 * pieces * size * width),
        name="expert_grads",
    )(rows, d_out, hidden, d_pre, d_log)


def inverse_rms(stream):
    return lax.rsqrt(jnp.mean(stream * stream, axis=-1, keepdims=True) + EPS)


def norm_backward(upstream, stream, inverse, gain):
    weighted = upstream * gain
    inner = jnp.mean(weighted * stream, axis=-1, keepdims=True)
    return inverse * weighted - stream * (inverse * inverse * inverse) * inner


def path_table(segment_ids, path_pos, parent_ids, peers):
    segment = segment_ids[::BLK].reshape(peers, -1)
    position = path_pos[::BLK].reshape(peers, -1)
    t = lax.axis_index("tensor")
    order = jnp.arange(peers, dtype=jnp.int32) ^ t
    match = order[:, None] == jnp.arange(peers, dtype=jnp.int32)[None, :]
    pick = lambda v: jnp.sum(jnp.where(match[:, :, None], v[None], 0), axis=1)
    segment, position = pick(segment), pick(position)
    place = jnp.where(segment == 0, position // BLK, segment + (TRUNK - 1))
    seg, pos, own = segment[0], position[0], place[0]
    names = jnp.arange(parent_ids.shape[-1], dtype=jnp.int32)
    parent = jnp.sum(jnp.where(seg[:, None] == names[None, :], parent_ids[0][None], 0), axis=1)
    leaf = (seg > 0) & (parent > 0)
    parent_place = jnp.where(leaf, parent + (TRUNK - 1), own)
    base_own = jnp.where(seg > 0, pos, BIG)
    base_parent = jnp.where(leaf, TRUNK * BLK, BIG)
    mine = jnp.stack([pos, own, parent_place, base_own, base_parent], axis=1)
    return jnp.concatenate([place.reshape(-1), mine.reshape(-1)]).astype(jnp.int32)


def dispatch_plan(route, experts, capacity):
    count = route.shape[0]
    chosen = route[:, None] == jnp.arange(experts, dtype=jnp.int32)[None, :]
    index = jnp.arange(count, dtype=jnp.int32)
    before = (index[None, :] < index[:, None]).astype(BF16)
    ranks = dot(before, chosen.astype(BF16)).astype(jnp.int32)
    rank = jnp.sum(jnp.where(chosen, ranks, 0), axis=1)
    to = route ^ lax.axis_index("expert") if experts == 4 else route
    slot = to * capacity + rank
    table = slot[None, :] == jnp.arange(experts * capacity, dtype=jnp.int32)[:, None]
    return chosen, table.astype(BF16)


def send_rows(table, rows, experts, capacity):
    chunks = [
        dot(table[k * capacity : (k + 1) * capacity], rows).astype(BF16) for k in range(experts)
    ]
    return jnp.concatenate(exchange(chunks), axis=0)


def return_rows(table, results, experts, capacity):
    chunks = exchange([results[k * capacity : (k + 1) * capacity] for k in range(experts)])
    return dot_tn(table, jnp.concatenate(chunks, axis=0))


def split_core(x, axis):
    c = lax.axis_index("dp")
    half = x.shape[axis] // 2
    return (
        lax.dynamic_slice_in_dim(x, c * half, half, axis),
        lax.dynamic_slice_in_dim(x, (1 - c) * half, half, axis),
    )


def attention_weights(w_mix, w_proj):
    width = w_mix.shape[0]
    mix = gather_shared(*split_core(w_mix.reshape(width, -1), 0))
    proj = gather_shared(*split_core(w_proj, 0))
    mixes = [by_core(a, b, 0).reshape(width, 3, -1) for a, b in zip(*mix)]
    projs = [by_core(a, b, 0) for a, b in zip(*proj)]
    parts = [jnp.concatenate([m[:, i] for m in mixes], axis=1) for i in range(3)]
    return parts[0], parts[1], parts[2], jnp.concatenate(projs, axis=0)


def expert_weights(w_up, w_back):
    up = gather_shared(*split_core(w_up, 1))
    down = gather_shared(*split_core(w_back, 0))
    return jnp.stack(up[0] + up[1]), jnp.stack(down[0] + down[1])


def body(
    hidden_in, route_ids, segment_ids, path_pos, parent_ids, norm_att, w_qkv, w_out, norm_ffn, w_route, w_in, w_down, cotangent,
):
    depth_total = w_qkv.shape[0]
    tokens, width = hidden_in.shape
    experts = w_route.shape[-1]
    capacity = 3 * tokens // (2 * experts)
    peers = lax.axis_size("tensor")
    own_expert = lax.axis_index("expert").reshape(1).astype(jnp.int32)
    shard = width // peers
    table = path_table(segment_ids, path_pos, parent_ids, peers)
    plans = [dispatch_plan(route_ids[d, :, 0], experts, capacity) for d in range(depth_total)]
    routes = [jnp.pad(w_route[d], ((0, 0), (0, BLK - experts))) for d in range(depth_total)]
    cotangent = cotangent.astype(F32)

    stream = hidden_in.astype(F32)
    kept = []
    weights, moe = [None] * depth_total, [None] * depth_total
    weights[0] = attention_weights(w_qkv[0], w_out[0])
    for depth in range(depth_total):
        gain_att, gain_ffn = norm_att[depth].astype(F32), norm_ffn[depth].astype(F32)
        chosen, plan = plans[depth]
        inverse_att = inverse_rms(stream)
        normed = (stream * inverse_att * gain_att).astype(BF16)
        normed_all = jnp.concatenate(gather_rows(normed), axis=0)
        if depth == 0:
            up, down = after((w_in[0, 0], w_down[0, 0]), normed_all)
            moe[0] = expert_weights(up, down)
        w_q, w_k, w_v, w_o = weights[depth]
        q = dot(normed, w_q).astype(BF16)
        k = dot(normed_all, w_k).astype(BF16)
        v = dot(normed_all, w_v).astype(BF16)
        heads, lse = attend(table, q, k, v)
        after_att = stream + dot(heads, w_o)
        inverse_ffn = inverse_rms(after_att)
        token_rows = (after_att * inverse_ffn * gain_ffn).astype(BF16)
        if depth + 1 < depth_total:
            mix, proj, up, down = after(
                (w_qkv[depth + 1], w_out[depth + 1], w_in[depth + 1, 0], w_down[depth + 1, 0]), token_rows
            )
            weights[depth + 1] = attention_weights(mix, proj)
            moe[depth + 1] = expert_weights(up, down)
        rows = send_rows(plan, token_rows, experts, capacity)
        router = jax.nn.softmax(dot(token_rows, w_route[depth]), axis=-1)
        gate = jnp.sum(jnp.where(chosen, router, 0.0), axis=1, keepdims=True)
        d_sent = None
        if depth + 1 == depth_total:
            d_low = (gate * cotangent).astype(BF16)
            d_sent = send_rows(plan, d_low, experts, capacity)
        out, hidden, slope = expert_forward(rows, *moe[depth])
        stream_next = after_att + gate * return_rows(plan, out, experts, capacity)
        kept.append(
            (stream, inverse_att, normed, normed_all, q, k, v, heads, lse, after_att, inverse_ffn, gate, rows, d_sent, out, hidden, slope)
        )
        stream = stream_next
    hidden_out = stream.astype(BF16)

    upstream = cotangent
    grads = [None] * depth_total
    for depth in reversed(range(depth_total)):
        (stream, inverse_att, normed, normed_all, q, k, v, heads, lse, after_att, inverse_ffn, gate, rows, d_sent, out, hidden, slope) = kept[depth]
        gain_att, gain_ffn = norm_att[depth].astype(F32), norm_ffn[depth].astype(F32)
        chosen, plan = plans[depth]
        w_q, w_k, w_v, w_o = weights[depth]
        if d_sent is None:
            d_sent = send_rows(plan, (gate * upstream).astype(BF16), experts, capacity)
        d_slots, d_pre, d_log, gain_sum = expert_rows(
            own_expert, d_sent, *moe[depth], slope, rows, out, routes[depth], experts
        )
        d_rows = return_rows(plan, d_slots, experts, capacity)
        g_up, g_down, g_route = expert_grads(rows, d_sent, hidden, d_pre, d_log)
        half = peers
        up_mine = scatter_shared(g_up[:half], g_up[half:]).astype(BF16)
        down_mine = scatter_shared(g_down[:half], g_down[half:]).astype(BF16)
        grad_up = by_core(up_mine, xperm(up_mine, "dp", 1), 1).astype(F32)
        grad_down = by_core(down_mine, xperm(down_mine, "dp", 1), 0).astype(F32)

        dx1 = upstream + norm_backward(d_rows, after_att, inverse_ffn, gain_ffn)
        d_att = dx1.astype(BF16)
        d_heads = dot_nt(d_att, w_o).astype(BF16)
        dq, dk, dv = attend_back(table, q, k, v, d_heads, heads, lse)
        blocks = []
        for j in reversed(range(peers)):
            at = slice(j * tokens, (j + 1) * tokens)
            part = dot_nt(dk[at], w_k) + dot_nt(dv[at], w_v)
            if j == 0:
                part = part + dot_nt(dq, w_q)
            else:
                part = part.astype(BF16)
            blocks.insert(0, part)
        d_normed = scatter_rows(blocks[1:], blocks[0])
        g_q, g_k, g_v = dot_tn(normed, dq), dot_tn(normed_all, dk), dot_tn(normed_all, dv)
        g_o = dot_tn(heads, d_att).reshape(peers, shard, width).astype(BF16)
        att_sum = jnp.sum(g_q * w_q.astype(F32) + g_k * w_k.astype(F32) + g_v * w_v.astype(F32), axis=1)
        g_mix = jnp.stack(
            [
                jnp.concatenate([g[:, j * shard : (j + 1) * shard].astype(BF16) for g in (g_q, g_k, g_v)], axis=1)
                for j in range(peers)
            ]
        )
        mix_mine = sum_expert(scatter_shared(*split_core(g_mix, 1))).astype(BF16)
        out_mine = sum_expert(scatter_shared(*split_core(g_o, 1))).astype(BF16)
        grad_mix = by_core(mix_mine, xperm(mix_mine, "dp", 1), 0).astype(F32).reshape(width, 3, shard)
        grad_out = by_core(out_mine, xperm(out_mine, "dp", 1), 0).astype(F32)
        small = sum_small(
            jnp.concatenate([g_route[:, :experts].T, gain_sum, att_sum[None]], axis=0)
        )
        grads[depth] = (
            small[experts + 1] / gain_att, grad_mix, grad_out, small[experts] / gain_ffn, small[:experts].T, grad_up[None], grad_down[None],
        )
        upstream = dx1 + norm_backward(d_normed, stream, inverse_att, gain_att)
    stacked = [jnp.stack([grads[d][m] for d in range(depth_total)]) for m in range(7)]
    return (hidden_out, upstream, *stacked)


def solution(mesh):
    in_specs = (
        P(("dp", "expert", "tensor"), None),
        P(None, ("dp", "expert", "tensor"), None),
        P(("dp", "expert")),
        P(("dp", "expert")),
        P(("dp", "expert"), None),
        P(),
        P(None, None, None, "tensor"),
        P(None, "tensor", None),
        P(),
        P(),
        P(None, "expert", None, "tensor"),
        P(None, "expert", "tensor", None),
        P(("dp", "expert", "tensor"), None),
    )
    out_specs = (
        P(("dp", "expert", "tensor"), None),
        P(("dp", "expert", "tensor"), None),
        P(),
        P(None, None, None, "tensor"),
        P(None, "tensor", None),
        P(),
        P(),
        P(None, "expert", None, "tensor"),
        P(None, "expert", "tensor", None),
    )
    return jax.shard_map(body, mesh=mesh, in_specs=in_specs, out_specs=out_specs, check_vma=False)
```

time: 2420 us -> 1160 us (0.48)
  waiting for transfers between devices: 1100 us -> 271 us
  matrix products: 584 us -> 106 us
  starting transfers between devices: 18.2 us -> 311 us
  Pallas kernels: 0 us -> 278 us
  blocking collectives: 193 us -> 0 us
  other arithmetic: 254 us -> 77.2 us
  local copies, waits for them, and re-layouts: 203 us -> 91.1 us
  loops' own time: 40.2 us -> 0 us
    dot_general x100 -> x60, matrix products: 584 us -> 106 us  [the longest x12 44.3 us: dot_tn(): return lax.dot_general(a, b, TN, preferred_element_type=F32)]
    reduce_scatter x8 -> x0, waiting for transfers between devices: 453 us -> none  [the longest x2 134 us: backward_layer(): lax.psum_scatter(jnp.dot(d_pre, w_up[0].T, preferred_element_type=jnp.flo...]
    all_gather x8 -> x0, waiting for transfers between devices: 424 us -> none  [the longest x2 132 us: backward_layer(): d_slots = lax.all_gather(d_arrived, 'tensor', axis=0, tiled=True)]
    ppermute x0 -> x202, starting transfers between devices: none -> 311 us  [xperm(): return lax.ppermute(x, axis, [(i, i ^ k) for i in range(n)])]
    pallas_call x0 -> x10, Pallas kernels: none -> 278 us  [the longest x2 93.4 us: attend_back(): pl.pallas_call(attend_back_kernel, grid_spec=pltpu.PrefetchScalarGridSpec...]
    ppermute x0 -> x202, waiting for transfers between devices: none -> 271 us  [xperm(): return lax.ppermute(x, axis, [(i, i ^ k) for i in range(n)])]
    all_to_all x4 -> x0, blocking collectives: 154 us -> none  [to_experts(): lax.all_to_all(buffer, 'expert', split_axis=0, concat_axis=0, tiled=True)]
    all_to_all x4 -> x0, waiting for transfers between devices: 136 us -> none  [from_experts(): lax.all_to_all(buffer, 'expert', split_axis=0, concat_axis=0, tiled=True)]
  transfers between devices with their start and end apart: 22 -> 202, of which waited for: 21 -> 68; matrix products, arithmetic and copies ran while one was open for 16% -> 20% of each run, Pallas kernels for 0% -> 20%
where the time goes in v1:
time: 1160 us; the launch traced here: 1150 us
  starting transfers between devices  311 us (27%)
  Pallas kernels  278 us (24%)
  waiting for transfers between devices  271 us (23%)
  matrix products  106 us (9%)
  local copies, waits for them, and re-layouts  91.1 us (8%)
  other arithmetic  77.2 us (7%)
  between operations  11.6 us (1%)
    ppermute x202, starting transfers between devices, xperm(): return lax.ppermute(x, axis, [(i, i ^ k) for i in range(n)])  311 us
    ppermute x202, waiting for transfers between devices, xperm(): return lax.ppermute(x, axis, [(i, i ^ k) for i in range(n)])  271 us
    pallas_call x2, Pallas kernels, attend_back(): pl.pallas_call(attend_back_kernel, grid_spec=pltpu.PrefetchScalarGridSpec...  93.4 us
    pallas_call x2, Pallas kernels, expert_forward(): pl.pallas_call(expert_kernel, grid=(pieces,), in_specs=[whole, pl.BlockSp...  56.6 us
    pallas_call x2, Pallas kernels, expert_rows(): pl.pallas_call(functools.partial(expert_rows_kernel, experts=experts), gr...  47.1 us
    pallas_call x2, Pallas kernels, attend(): pl.pallas_call(attend_kernel, grid_spec=pltpu.PrefetchScalarGridSpec(num_...  46.8 us
    dot_general x12, matrix products, dot_tn(): return lax.dot_general(a, b, TN, preferred_element_type=F32)  44.3 us
    dot_general x28, matrix products, dot(): return jnp.dot(a, b, preferred_element_type=F32)  37.3 us
  transfers between devices with their start and end apart: 202, of which 68 were waited for; matrix products, arithmetic and copies ran while one was open for 20% of the time, Pallas kernels for 20%

profile of v1, /device:TPU:1, one launch (start us, length us, event | category | flops | bytes accessed | tf_op | source)
XLA Modules:
  0.0 1145.9 jit_solution(4092719341823215363)
XLA Ops:
  65.7 4.7 collective-permute-done.8
  74.5 5.9 collective-permute-done.4
  80.7 5.0 collective-permute-start.6
  94.9 5.0 convolution_convert_fusion.2.v_ref
  99.9 4.8 convolution_convert_fusion.3.k_ref
  106.6 23.5 %attend.2 = (bf16[640,768]{1,0:T(8,128)(2,1)}, f32[640,128]{1,0:T(8,128)}) custom-call(s32[45]{0:T(128)} %pad_add_fusion.table, bf16[640,768]{1,0:T(8,128)(2,1)} %convolution_convert_fusion.9.q_ref, bf16[2560,768]{1,0:T(8,128)(2,1)} %convolution_convert_fusion.3.k_ref, bf16[2560,768]{1,0:T(8,128)(2,1)} %convolution_convert_fusion.2.v_ref), custom_call_target="tpu_custom_call" | custom-call | flops 10066329600 | bytes 7864320 | tf_op jit(solution)/shard_map/attend/pallas_call | solution.py:183
  145.1 4.8 collective-permute-start.54
  160.5 16.1 %collective-permute-done.21 = bf16[240,768]{1,0:T(8,128)(2,1)S(1)} collective-permute-done((bf16[240,768]{1,0:T(8,128)(2,1)S(1)}, bf16[240,768]{1,0:T(8,128)(2,1)S(1)}, u32[]{:S(2)}, u32[]{:S(2)}) %collective-permute-start.21) | collective-permute-done | bytes 368672 | tf_op jit(solution)/shard_map/ppermute | solution.py:43
  184.3 6.1 collective-permute-done.31
  194.7 8.2 collective-permute-done.24
  208.4 7.1 collective-permute-done.71
  215.6 4.5 collective-permute-start.41
  220.5 7.7 collective-permute-done.64
  234.5 4.5 collective-permute-start.43
  242.1 5.1 collective-permute-done.25
  266.0 7.8 collective-permute-done.65
  276.0 5.0 collective-permute-done.66
  295.9 28.5 %expert_forward.2 = (bf16[960,768]{1,0:T(8,128)(2,1)}, bf16[8,960,384]{2,1,0:T(8,128)(2,1)}, bf16[8,960,384]{2,1,0:T(8,128)(2,1)}) custom-call(bf16[960,768]{1,0:T(8,128)(2,1)} %pad_maximum_fusion.2.rows_ref, bf16[8,768,384]{2,1,0:T(8,128)(2,1)} %bitcast_dynamic-update-slice_fusion.24.up_ref, bf16[8,384,768]{2,1,0:T(8,128)(2,1)} %copy-done.106), custom_call_target="tpu_custom_call" | custom-call | flops 9059696640 | bytes 21233664 | tf_op jit(solution)/shard_map/expert_forward/pallas_call | solution.py:337
  331.2 11.9 %collective-permute-done.37 = bf16[240,768]{1,0:T(8,128)(2,1)S(1)} collective-permute-done((bf16[240,768]{1,0:T(8,128)(2,1)S(1)}, bf16[240,768]{1,0:T(8,128)(2,1)S(1)}, u32[]{:S(2)}, u32[]{:S(2)}) %collective-permute-start.37) | collective-permute-done | bytes 368672 | tf_op jit(solution)/shard_map/ppermute | solution.py:43
  343.0 9.7 collective-permute-done.39
  361.4 15.5 %collective-permute-done.47 = bf16[320,768]{1,0:T(8,128)(2,1)S(1)} collective-permute-done((bf16[320,768]{1,0:T(8,128)(2,1)S(1)}, bf16[320,768]{1,0:T(8,128)(2,1)S(1)}, u32[]{:S(2)}, u32[]{:S(2)}) %collective-permute-start.47) | collective-permute-done | bytes 491552 | tf_op jit(solution)/shard_map/ppermute | solution.py:43
  379.3 9.0 collective-permute-done.51
  388.4 4.8 convolution_convert_fusion.v_ref
  393.3 4.8 convolution_convert_fusion.1.k_ref
  398.1 23.3 %attend.3 = (bf16[640,768]{1,0:T(8,128)(2,1)}, f32[640,128]{1,0:T(8,128)}) custom-call(s32[45]{0:T(128)} %pad_add_fusion.table, bf16[640,768]{1,0:T(8,128)(2,1)} %convolution_convert_fusion.8.q_ref, bf16[2560,768]{1,0:T(8,128)(2,1)} %convolution_convert_fusion.1.k_ref, bf16[2560,768]{1,0:T(8,128)(2,1)} %convolution_convert_fusion.v_ref), custom_call_target="tpu_custom_call" | custom-call | flops 10066329600 | bytes 7864320 | tf_op jit(solution)/shard_map/attend/pallas_call | solution.py:183
  429.3 9.0 collective-permute-start.60
  444.0 5.8 collective-permute-done.60
  451.9 9.6 collective-permute-done.62
  462.8 28.2 %expert_forward.3 = (bf16[960,768]{1,0:T(8,128)(2,1)}, bf16[8,960,384]{2,1,0:T(8,128)(2,1)}, bf16[8,960,384]{2,1,0:T(8,128)(2,1)}) custom-call(bf16[960,768]{1,0:T(8,128)(2,1)} %pad_maximum_fusion.3.rows_ref, bf16[8,768,384]{2,1,0:T(8,128)(2,1)} %bitcast_dynamic-update-slice_fusion.8.up_ref, bf16[8,384,768]{2,1,0:T(8,128)(2,1)} %bitcast_dynamic-update-slice_fusion.down_ref), custom_call_target="tpu_custom_call" | custom-call | flops 9059696640 | bytes 21233664 | tf_op jit(solution)/shard_map/expert_forward/pallas_call | solution.py:337
  494.3 23.7 %expert_rows.2 = (bf16[960,768]{1,0:T(8,128)(2,1)}, bf16[8,960,384]{2,1,0:T(8,128)(2,1)}, bf16[960,128]{1,0:T(8,128)(2,1)}, f32[1,768]{1,0:T(1,128)}) custom-call(s32[1]{0:T(128)} %bitcast.83.expert, bf16[960,768]{1,0:T(8,128)(2,1)} %pad_maximum_fusion.4.d_out_ref, bf16[8,768,384]{2,1,0:T(8,128)(2,1)} %bitcast_dynamic-update-slice_fusion.8.up_ref, ...), custom_call_target="tpu_custom_call" | custom-call | flops 9059696640 | bytes 21233664 | tf_op jit(solution)/shard_map/expert_rows/pallas_call | solution.py:394
  520.5 8.2 collective-permute-start.83
  531.6 16.7 %expert_grads.3 = (bf16[8,768,384]{2,1,0:T(8,128)(2,1)}, bf16[8,384,768]{2,1,0:T(8,128)(2,1)}, f32[768,128]{1,0:T(8,128)}) custom-call(bf16[960,768]{1,0:T(8,128)(2,1)} %pad_maximum_fusion.3.rows_ref, bf16[960,768]{1,0:T(8,128)(2,1)} %pad_maximum_fusion.4.d_out_ref, bf16[8,960,384]{2,1,0:T(8,128)(2,1)} %get-tuple-element.72.hidden_ref, ...), custom_call_target="tpu_custom_call" | custom-call | flops 9059696640 | bytes 21233664 | tf_op jit(solution)/shard_map/expert_grads/pallas_call | solution.py:441
  564.1 3.9 convolution_convert_fusion.7.do_ref
  568.0 46.4 %attend_back.2 = (bf16[640,768]{1,0:T(8,128)(2,1)}, bf16[2560,768]{1,0:T(8,128)(2,1)}, bf16[2560,768]{1,0:T(8,128)(2,1)}) custom-call(s32[45]{0:T(128)} %pad_add_fusion.table, bf16[640,768]{1,0:T(8,128)(2,1)} %convolution_convert_fusion.8.q_ref, bf16[2560,768]{1,0:T(8,128)(2,1)} %convolution_convert_fusion.1.k_ref, ...), custom_call_target="tpu_custom_call" | custom-call | flops 25165824000 | bytes 15728640 | tf_op jit(solution)/shard_map/attend_back/pallas_call | solution.py:271
  621.3 4.9 fusion.257
  627.2 5.0 fusion.258
  637.3 4.1 fusion.236
  641.4 22.7 %collective-permute-start.109 = (f32[6,768]{1,0:T(8,128)S(1)}, f32[6,768]{1,0:T(8,128)S(1)}, u32[]{:S(2)}, u32[]{:S(2)}) collective-permute-start(f32[6,768]{1,0:T(8,128)S(1)} %pad_maximum_fusion.35), channel_id=1, source_target_pairs={{0,16},{16,0},{1,17},{17,1},{2,18},{18,2},{3,19},{19,3},{4,20},{20... | collective-permute-start | bytes 55304 | tf_op jit(solution)/shard_map/ppermute | solution.py:43
  693.3 11.8 %collective-permute-done.87 = bf16[320,768]{1,0:T(8,128)(2,1)S(1)} collective-permute-done((bf16[320,768]{1,0:T(8,128)(2,1)S(1)}, bf16[320,768]{1,0:T(8,128)(2,1)S(1)}, u32[]{:S(2)}, u32[]{:S(2)}) %collective-permute-start.87) | collective-permute-done | bytes 491552 | tf_op jit(solution)/shard_map/ppermute | solution.py:43
  713.8 11.6 %collective-permute-start.194 = (bf16[4,384,768]{2,1,0:T(8,128)(2,1)}, bf16[4,384,768]{2,1,0:T(8,128)(2,1)}, u32[]{:S(2)}, u32[]{:S(2)}) collective-permute-start(bf16[4,384,768]{2,1,0:T(8,128)(2,1)} %slice.1319), channel_id=1, source_target_pairs={{0,16},{16,0},{1,17},{17,1},{2,18},{18,2},{3,19},{19,3},{4,20},{20... | collective-permute-start | bytes 7077896 | tf_op jit(solution)/shard_map/ppermute | solution.py:43
  735.6 12.8 %collective-permute-done.92 = bf16[240,768]{1,0:T(8,128)(2,1)S(1)} collective-permute-done((bf16[240,768]{1,0:T(8,128)(2,1)S(1)}, bf16[240,768]{1,0:T(8,128)(2,1)S(1)}, u32[]{:S(2)}, u32[]{:S(2)}) %collective-permute-start.92) | collective-permute-done | bytes 368672 | tf_op jit(solution)/shard_map/ppermute | solution.py:43
  748.3 9.4 collective-permute-done.93
  759.0 23.3 %expert_rows.3 = (bf16[960,768]{1,0:T(8,128)(2,1)}, bf16[8,960,384]{2,1,0:T(8,128)(2,1)}, bf16[960,128]{1,0:T(8,128)(2,1)}, f32[1,768]{1,0:T(1,128)}) custom-call(s32[1]{0:T(128)} %bitcast.83.expert, bf16[960,768]{1,0:T(8,128)(2,1)} %pad_maximum_fusion.5.d_out_ref, bf16[8,768,384]{2,1,0:T(8,128)(2,1)} %bitcast_dynamic-update-slice_fusion.24.up_ref, ...), custom_call_target="tpu_custom_call" | custom-call | flops 9059696640 | bytes 21233664 | tf_op jit(solution)/shard_map/expert_rows/pallas_call | solution.py:394
  784.7 8.2 collective-permute-start.95
  795.0 16.9 %expert_grads.2 = (bf16[8,768,384]{2,1,0:T(8,128)(2,1)}, bf16[8,384,768]{2,1,0:T(8,128)(2,1)}, f32[768,128]{1,0:T(8,128)}) custom-call(bf16[960,768]{1,0:T(8,128)(2,1)} %pad_maximum_fusion.2.rows_ref, bf16[960,768]{1,0:T(8,128)(2,1)} %pad_maximum_fusion.5.d_out_ref, bf16[8,960,384]{2,1,0:T(8,128)(2,1)} %get-tuple-element.67.hidden_ref, ...), custom_call_target="tpu_custom_call" | custom-call | flops 9059696640 | bytes 21233664 | tf_op jit(solution)/shard_map/expert_grads/pallas_call | solution.py:441
  826.1 47.0 %attend_back.3 = (bf16[640,768]{1,0:T(8,128)(2,1)}, bf16[2560,768]{1,0:T(8,128)(2,1)}, bf16[2560,768]{1,0:T(8,128)(2,1)}) custom-call(s32[45]{0:T(128)} %pad_add_fusion.table, bf16[640,768]{1,0:T(8,128)(2,1)} %convolution_convert_fusion.9.q_ref, bf16[2560,768]{1,0:T(8,128)(2,1)} %convolution_convert_fusion.3.k_ref, ...), custom_call_target="tpu_custom_call" | custom-call | flops 25165824000 | bytes 15728640 | tf_op jit(solution)/shard_map/attend_back/pallas_call | solution.py:271
  873.2 6.9 fusion.255
  885.3 5.0 fusion.256
  893.1 5.1 fusion.235
  898.3 4.0 collective-permute-start.104
  915.7 6.5 collective-permute-start.107
  938.3 5.2 collective-permute-done.130
  957.6 5.3 collective-permute-done.196
  967.2 8.4 collective-permute-done.180
  1001.9 4.2 collective-permute-start.152
  1023.1 18.7 %collective-permute-start.155 = (bf16[96,768]{1,0:T(8,128)(2,1)S(1)}, bf16[96,768]{1,0:T(8,128)(2,1)S(1)}, u32[]{:S(2)}, u32[]{:S(2)}) collective-permute-start(bf16[96,768]{1,0:T(8,128)(2,1)S(1)} %pad_maximum_fusion.31), channel_id=1, source_target_pairs={{0,16},{16,0},{1,17},{17,1},{2,18},{18,2},{3,19},{19,3},{4,20},{20... | collective-permute-start | bytes 442376 | tf_op jit(solution)/shard_map/ppermute | solution.py:43
  1048.5 5.2 collective-permute-start.201
  1064.1 5.0 collective-permute-done.116
  1077.1 4.8 collective-permute-done.117
  1083.1 4.9 collective-permute-done.120
  1095.6 7.1 collective-permute-start.190
  1107.7 7.6 collective-permute-done.125
  1122.6 3.9 collective-permute-done.192
  1126.5 7.6 collective-permute-start.127
  (1040 shorter events, 456.6 us)
Async XLA Ops:
  3.3 55.5 %collective-permute-start = (bf16[384,576]{0,1:T(8,128)(2,1)}, bf16[384,576]{0,1:T(8,128)(2,1)}, u32[]{:S(2)}, u32[]{:S(2)}) collective-permute-start(bf16[384,576]{0,1:T(8,128)(2,1)} %get-tuple-element.136), channel_id=1, source_target_pairs={{0,1},{1,0},{2,3},{3,2},{4,5},{5,4},{6,7},{7,6},{8,9},{9,8},{10,11... | collective-permute-start | bytes 1327112 | tf_op jit(solution)/shard_map/ppermute | solution.py:43
  5.3 56.6 %collective-permute-start.2 = (bf16[384,576]{0,1:T(8,128)(2,1)}, bf16[384,576]{0,1:T(8,128)(2,1)}, u32[]{:S(2)}, u32[]{:S(2)}) collective-permute-start(bf16[384,576]{0,1:T(8,128)(2,1)} %get-tuple-element.136), channel_id=1, source_target_pairs={{0,2},{1,3},{2,0},{3,1},{4,6},{5,7},{6,4},{7,5},{8,10},{9,11},{10,... | collective-permute-start | bytes 1327112 | tf_op jit(solution)/shard_map/ppermute | solution.py:43
  8.4 37.1 %collective-permute-start.13 = (bf16[96,768]{1,0:T(8,128)(2,1)}, bf16[96,768]{1,0:T(8,128)(2,1)}, u32[]{:S(2)}, u32[]{:S(2)}) collective-permute-start(bf16[96,768]{1,0:T(8,128)(2,1)} %get-tuple-element.132), channel_id=1, source_target_pairs={{0,1},{1,0},{2,3},{3,2},{4,5},{5,4},{6,7},{7,6},{8,9},{9,8},{10,11... | collective-permute-start | bytes 442376 | tf_op jit(solution)/shard_map/ppermute | solution.py:43
  8.6 40.2 %collective-permute-start.15 = (bf16[96,768]{1,0:T(8,128)(2,1)}, bf16[96,768]{1,0:T(8,128)(2,1)S(1)}, u32[]{:S(2)}, u32[]{:S(2)}) collective-permute-start(bf16[96,768]{1,0:T(8,128)(2,1)} %get-tuple-element.132), channel_id=1, source_target_pairs={{0,2},{1,3},{2,0},{3,1},{4,6},{5,7},{6,4},{7,5},{8,10},{9,11},{10,... | collective-permute-start | bytes 442376 | tf_op jit(solution)/shard_map/ppermute | solution.py:43
  12.9 50.3 %collective-permute-start.7 = (bf16[320,768]{1,0:T(8,128)(2,1)}, bf16[320,768]{1,0:T(8,128)(2,1)}, u32[]{:S(2)}, u32[]{:S(2)}) collective-permute-start(bf16[320,768]{1,0:T(8,128)(2,1)} %get-tuple-element.278), channel_id=1, source_target_pairs={{0,1},{1,0},{2,3},{3,2},{4,5},{5,4},{6,7},{7,6},{8,9},{9,8},{10,11... | collective-permute-start | bytes 1474568 | tf_op jit(solution)/shard_map/ppermute | solution.py:43
  92.1 89.6 %collective-permute-start.30 = (bf16[384,768]{1,0:T(8,128)(2,1)}, bf16[384,768]{1,0:T(8,128)(2,1)}, u32[]{:S(2)}, u32[]{:S(2)}) collective-permute-start(bf16[384,768]{1,0:T(8,128)(2,1)} %get-tuple-element.128), channel_id=1, source_target_pairs={{0,1},{1,0},{2,3},{3,2},{4,5},{5,4},{6,7},{7,6},{8,9},{9,8},{10,11... | collective-permute-start | bytes 1769480 | tf_op jit(solution)/shard_map/ppermute | solution.py:43
  137.4 43.8 %collective-permute-start.40 = (bf16[384,576]{0,1:T(8,128)(2,1)S(1)}, bf16[384,576]{0,1:T(8,128)(2,1)S(1)}, u32[]{:S(2)}, u32[]{:S(2)}) collective-permute-start(bf16[384,576]{0,1:T(8,128)(2,1)S(1)} %get-tuple-element.126), channel_id=1, source_target_pairs={{0,1},{1,0},{2,3},{3,2},{4,5},{5,4},{6,7},{7,6},{8,9},{9,8},{10,11... | collective-permute-start | bytes 1327112 | tf_op jit(solution)/shard_map/ppermute | solution.py:43
  149.9 26.7 %collective-permute-start.21 = (bf16[240,768]{1,0:T(8,128)(2,1)S(1)}, bf16[240,768]{1,0:T(8,128)(2,1)S(1)}, u32[]{:S(2)}, u32[]{:S(2)}) collective-permute-start(bf16[240,768]{1,0:T(8,128)(2,1)S(1)} %convolution_convert_fusion.23), channel_id=1, source_target_pairs={{0,8},{4,12},{8,0},{12,4},{1,9},{5,13},{9,1},{13,5},{2,10},{6,14},... | collective-permute-start | bytes 1105928 | tf_op jit(solution)/shard_map/ppermute | solution.py:43
  158.2 23.0 %collective-permute-start.42 = (bf16[384,576]{0,1:T(8,128)(2,1)S(1)}, bf16[384,576]{0,1:T(8,128)(2,1)S(1)}, u32[]{:S(2)}, u32[]{:S(2)}) collective-permute-start(bf16[384,576]{0,1:T(8,128)(2,1)S(1)} %get-tuple-element.126), channel_id=1, source_target_pairs={{0,2},{1,3},{2,0},{3,1},{4,6},{5,7},{6,4},{7,5},{8,10},{9,11},{10,... | collective-permute-start | bytes 1327112 | tf_op jit(solution)/shard_map/ppermute | solution.py:43
  181.1 21.8 %collective-permute-start.24 = (bf16[768,384]{1,0:T(8,128)(2,1)S(1)}, bf16[768,384]{1,0:T(8,128)(2,1)S(1)}, u32[]{:S(2)}, u32[]{:S(2)}) collective-permute-start(bf16[768,384]{1,0:T(8,128)(2,1)S(1)} %copy-done.54), channel_id=1, source_target_pairs={{0,2},{1,3},{2,0},{3,1},{4,6},{5,7},{6,4},{7,5},{8,10},{9,11},{10,... | collective-permute-start | bytes 1769480 | tf_op jit(solution)/shard_map/ppermute | solution.py:43
  181.2 25.9 %collective-permute-start.70 = (bf16[384,768]{1,0:T(8,128)(2,1)S(1)}, bf16[384,768]{1,0:T(8,128)(2,1)S(1)}, u32[]{:S(2)}, u32[]{:S(2)}) collective-permute-start(bf16[384,768]{1,0:T(8,128)(2,1)S(1)} %get-tuple-element.118), channel_id=1, source_target_pairs={{0,1},{1,0},{2,3},{3,2},{4,5},{5,4},{6,7},{7,6},{8,9},{9,8},{10,11... | collective-permute-start | bytes 1769480 | tf_op jit(solution)/shard_map/ppermute | solution.py:43
  181.7 33.8 %collective-permute-start.71 = (bf16[384,768]{1,0:T(8,128)(2,1)S(1)}, bf16[384,768]{1,0:T(8,128)(2,1)S(1)}, u32[]{:S(2)}, u32[]{:S(2)}) collective-permute-start(bf16[384,768]{1,0:T(8,128)(2,1)S(1)} %get-tuple-element.118), channel_id=1, source_target_pairs={{0,2},{1,3},{2,0},{3,1},{4,6},{5,7},{6,4},{7,5},{8,10},{9,11},{10,... | collective-permute-start | bytes 1769480 | tf_op jit(solution)/shard_map/ppermute | solution.py:43
  190.4 29.7 %collective-permute-start.63 = (bf16[768,384]{1,0:T(8,128)(2,1)S(1)}, bf16[768,384]{1,0:T(8,128)(2,1)S(1)}, u32[]{:S(2)}, u32[]{:S(2)}) collective-permute-start(bf16[768,384]{1,0:T(8,128)(2,1)S(1)} %get-tuple-element.120), channel_id=1, source_target_pairs={{0,1},{1,0},{2,3},{3,2},{4,5},{5,4},{6,7},{7,6},{8,9},{9,8},{10,11... | collective-permute-start | bytes 1769480 | tf_op jit(solution)/shard_map/ppermute | solution.py:43
  192.7 35.5 %collective-permute-start.64 = (bf16[768,384]{1,0:T(8,128)(2,1)S(1)}, bf16[768,384]{1,0:T(8,128)(2,1)S(1)}, u32[]{:S(2)}, u32[]{:S(2)}) collective-permute-start(bf16[768,384]{1,0:T(8,128)(2,1)S(1)} %get-tuple-element.120), channel_id=1, source_target_pairs={{0,2},{1,3},{2,0},{3,1},{4,6},{5,7},{6,4},{7,5},{8,10},{9,11},{10,... | collective-permute-start | bytes 1769480 | tf_op jit(solution)/shard_map/ppermute | solution.py:43
  202.9 31.6 %collective-permute-start.44 = (bf16[192,576]{0,1:T(8,128)(2,1)S(1)}, bf16[192,576]{0,1:T(8,128)(2,1)S(1)}, u32[]{:S(2)}, u32[]{:S(2)}) collective-permute-start(bf16[192,576]{0,1:T(8,128)(2,1)S(1)} %slice.1363), channel_id=1, source_target_pairs={{0,2},{1,3},{2,0},{3,1},{4,6},{5,7},{6,4},{7,5},{8,10},{9,11},{10,... | collective-permute-start | bytes 663560 | tf_op jit(solution)/shard_map/ppermute | solution.py:43
  207.1 31.9 %collective-permute-start.45 = (bf16[192,576]{0,1:T(8,128)(2,1)S(1)}, bf16[192,576]{0,1:T(8,128)(2,1)S(1)}, u32[]{:S(2)}, u32[]{:S(2)}) collective-permute-start(bf16[192,576]{0,1:T(8,128)(2,1)S(1)} %slice.1364), channel_id=1, source_target_pairs={{0,1},{1,0},{2,3},{3,2},{4,5},{5,4},{6,7},{7,6},{8,9},{9,8},{10,11... | collective-permute-start | bytes 663560 | tf_op jit(solution)/shard_map/ppermute | solution.py:43
  215.6 49.9 %collective-permute-start.41 = (bf16[384,576]{0,1:T(8,128)(2,1)S(1)}, bf16[384,576]{0,1:T(8,128)(2,1)S(1)}, u32[]{:S(2)}, u32[]{:S(2)}) collective-permute-start(bf16[384,576]{0,1:T(8,128)(2,1)S(1)} %collective-permute-done.40), channel_id=1, source_target_pairs={{0,16},{16,0},{1,17},{17,1},{2,18},{18,2},{3,19},{19,3},{4,20},{20... | collective-permute-start | bytes 1327112 | tf_op jit(solution)/shard_map/ppermute | solution.py:43
  220.1 20.7 %collective-permute-start.32 = (bf16[192,768]{1,0:T(8,128)(2,1)S(1)}, bf16[192,768]{1,0:T(8,128)(2,1)S(1)}, u32[]{:S(2)}, u32[]{:S(2)}) collective-permute-start(bf16[192,768]{1,0:T(8,128)(2,1)S(1)} %slice.1358), channel_id=1, source_target_pairs={{0,2},{1,3},{2,0},{3,1},{4,6},{5,7},{6,4},{7,5},{8,10},{9,11},{10,... | collective-permute-start | bytes 884744 | tf_op jit(solution)/shard_map/ppermute | solution.py:43
  234.5 31.1 %collective-permute-start.43 = (bf16[384,576]{0,1:T(8,128)(2,1)S(1)}, bf16[384,576]{0,1:T(8,128)(2,1)S(1)}, u32[]{:S(2)}, u32[]{:S(2)}) collective-permute-start(bf16[384,576]{0,1:T(8,128)(2,1)S(1)} %collective-permute-done.42), channel_id=1, source_target_pairs={{0,16},{16,0},{1,17},{17,1},{2,18},{18,2},{3,19},{19,3},{4,20},{20... | collective-permute-start | bytes 1327112 | tf_op jit(solution)/shard_map/ppermute | solution.py:43
  247.2 37.2 %collective-permute-start.34 = (bf16[384,768]{1,0:T(8,128)(2,1)}, bf16[384,768]{1,0:T(8,128)(2,1)S(1)}, u32[]{:S(2)}, u32[]{:S(2)}) collective-permute-start(bf16[384,768]{1,0:T(8,128)(2,1)} %collective-permute-done.30), channel_id=1, source_target_pairs={{0,16},{16,0},{1,17},{17,1},{2,18},{18,2},{3,19},{19,3},{4,20},{20... | collective-permute-start | bytes 1769480 | tf_op jit(solution)/shard_map/ppermute | solution.py:43
  258.2 26.3 %collective-permute-start.35 = (bf16[384,768]{1,0:T(8,128)(2,1)S(1)}, bf16[384,768]{1,0:T(8,128)(2,1)S(1)}, u32[]{:S(2)}, u32[]{:S(2)}) collective-permute-start(bf16[384,768]{1,0:T(8,128)(2,1)S(1)} %collective-permute-done.31), channel_id=1, source_target_pairs={{0,16},{16,0},{1,17},{17,1},{2,18},{18,2},{3,19},{19,3},{4,20},{20... | collective-permute-start | bytes 1769480 | tf_op jit(solution)/shard_map/ppermute | solution.py:43
  262.0 23.1 %collective-permute-start.27 = (bf16[768,384]{1,0:T(8,128)(2,1)S(1)}, bf16[768,384]{1,0:T(8,128)(2,1)S(1)}, u32[]{:S(2)}, u32[]{:S(2)}) collective-permute-start(bf16[768,384]{1,0:T(8,128)(2,1)S(1)} %collective-permute-done.23), channel_id=1, source_target_pairs={{0,16},{16,0},{1,17},{17,1},{2,18},{18,2},{3,19},{19,3},{4,20},{20... | collective-permute-start | bytes 1769480 | tf_op jit(solution)/shard_map/ppermute | solution.py:43
  286.1 42.5 %collective-permute-start.68 = (bf16[768,384]{1,0:T(8,128)(2,1)S(1)}, bf16[768,384]{1,0:T(8,128)(2,1)S(1)}, u32[]{:S(2)}, u32[]{:S(2)}) collective-permute-start(bf16[768,384]{1,0:T(8,128)(2,1)S(1)} %collective-permute-done.64), channel_id=1, source_target_pairs={{0,16},{16,0},{1,17},{17,1},{2,18},{18,2},{3,19},{19,3},{4,20},{20... | collective-permute-start | bytes 1769480 | tf_op jit(solution)/shard_map/ppermute | solution.py:43
  289.6 40.7 %collective-permute-start.76 = (bf16[384,768]{1,0:T(8,128)(2,1)}, bf16[384,768]{1,0:T(8,128)(2,1)S(1)}, u32[]{:S(2)}, u32[]{:S(2)}) collective-permute-start(bf16[384,768]{1,0:T(8,128)(2,1)} %constant_dynamic-update-slice_fusion.40), channel_id=1, source_target_pairs={{0,16},{16,0},{1,17},{17,1},{2,18},{18,2},{3,19},{19,3},{4,20},{20... | collective-permute-start | bytes 1769480 | tf_op jit(solution)/shard_map/ppermute | solution.py:43
  289.9 68.3 %collective-permute-start.69 = (bf16[768,384]{1,0:T(8,128)(2,1)S(1)}, bf16[768,384]{1,0:T(8,128)(2,1)S(1)}, u32[]{:S(2)}, u32[]{:S(2)}) collective-permute-start(bf16[768,384]{1,0:T(8,128)(2,1)S(1)} %constant_dynamic-update-slice_fusion.38), channel_id=1, source_target_pairs={{0,16},{16,0},{1,17},{17,1},{2,18},{18,2},{3,19},{19,3},{4,20},{20... | collective-permute-start | bytes 1769480 | tf_op jit(solution)/shard_map/ppermute | solution.py:43
  328.5 24.2 %collective-permute-start.39 = (bf16[240,768]{1,0:T(8,128)(2,1)S(1)}, bf16[240,768]{1,0:T(8,128)(2,1)S(1)}, u32[]{:S(2)}, u32[]{:S(2)}) collective-permute-start(bf16[240,768]{1,0:T(8,128)(2,1)S(1)} %get-tuple-element.226), channel_id=1, source_target_pairs={{0,12},{4,8},{8,4},{12,0},{1,13},{5,9},{9,5},{13,1},{2,14},{6,10},... | collective-permute-start | bytes 1105928 | tf_op jit(solution)/shard_map/ppermute | solution.py:43
  355.6 23.6 %collective-permute-start.48 = (bf16[320,768]{1,0:T(8,128)(2,1)S(1)}, bf16[320,768]{1,0:T(8,128)(2,1)S(1)}, u32[]{:S(2)}, u32[]{:S(2)}) collective-permute-start(bf16[320,768]{1,0:T(8,128)(2,1)S(1)} %get-tuple-element.275), channel_id=1, source_target_pairs={{0,1},{1,0},{2,3},{3,2},{4,5},{5,4},{6,7},{7,6},{8,9},{9,8},{10,11... | collective-permute-start | bytes 1474568 | tf_op jit(solution)/shard_map/ppermute | solution.py:43
  356.6 21.4 %collective-permute-start.50 = (bf16[320,768]{1,0:T(8,128)(2,1)S(1)}, bf16[320,768]{1,0:T(8,128)(2,1)S(1)}, u32[]{:S(2)}, u32[]{:S(2)}) collective-permute-start(bf16[320,768]{1,0:T(8,128)(2,1)S(1)} %get-tuple-element.275), channel_id=1, source_target_pairs={{0,2},{1,3},{2,0},{3,1},{4,6},{5,7},{6,4},{7,5},{8,10},{9,11},{10,... | collective-permute-start | bytes 1474568 | tf_op jit(solution)/shard_map/ppermute | solution.py:43
  439.4 22.2 %collective-permute-start.62 = (bf16[240,768]{1,0:T(8,128)(2,1)S(1)}, bf16[240,768]{1,0:T(8,128)(2,1)S(1)}, u32[]{:S(2)}, u32[]{:S(2)}) collective-permute-start(bf16[240,768]{1,0:T(8,128)(2,1)S(1)} %convolution_convert_fusion.18), channel_id=1, source_target_pairs={{0,12},{4,8},{8,4},{12,0},{1,13},{5,9},{9,5},{13,1},{2,14},{6,10},... | collective-permute-start | bytes 1105928 | tf_op jit(solution)/shard_map/ppermute | solution.py:43
  440.9 50.0 %collective-permute-start.80 = (bf16[240,768]{1,0:T(8,128)(2,1)S(1)}, bf16[240,768]{1,0:T(8,128)(2,1)S(1)}, u32[]{:S(2)}, u32[]{:S(2)}) collective-permute-start(bf16[240,768]{1,0:T(8,128)(2,1)S(1)} %convolution_convert_fusion.16), channel_id=1, source_target_pairs={{0,4},{4,0},{8,12},{12,8},{1,5},{5,1},{9,13},{13,9},{2,6},{6,2},{1... | collective-permute-start | bytes 1105928 | tf_op jit(solution)/shard_map/ppermute | solution.py:43
  441.5 51.5 %collective-permute-start.81 = (bf16[240,768]{1,0:T(8,128)(2,1)S(1)}, bf16[240,768]{1,0:T(8,128)(2,1)S(1)}, u32[]{:S(2)}, u32[]{:S(2)}) collective-permute-start(bf16[240,768]{1,0:T(8,128)(2,1)S(1)} %convolution_convert_fusion.15), channel_id=1, source_target_pairs={{0,8},{4,12},{8,0},{12,4},{1,9},{5,13},{9,1},{13,5},{2,10},{6,14},... | collective-permute-start | bytes 1105928 | tf_op jit(solution)/shard_map/ppermute | solution.py:43
  449.8 43.2 %collective-permute-start.82 = (bf16[240,768]{1,0:T(8,128)(2,1)S(1)}, bf16[240,768]{1,0:T(8,128)(2,1)S(1)}, u32[]{:S(2)}, u32[]{:S(2)}) collective-permute-start(bf16[240,768]{1,0:T(8,128)(2,1)S(1)} %convolution_convert_fusion.14), channel_id=1, source_target_pairs={{0,12},{4,8},{8,4},{12,0},{1,13},{5,9},{9,5},{13,1},{2,14},{6,10},... | collective-permute-start | bytes 1105928 | tf_op jit(solution)/shard_map/ppermute | solution.py:43
  520.5 39.0 %collective-permute-start.83 = (bf16[240,768]{1,0:T(8,128)(2,1)}, bf16[240,768]{1,0:T(8,128)(2,1)}, u32[]{:S(2)}, u32[]{:S(2)}) collective-permute-start(bf16[240,768]{1,0:T(8,128)(2,1)} %get-tuple-element.220), channel_id=1, source_target_pairs={{0,4},{4,0},{8,12},{12,8},{1,5},{5,1},{9,13},{13,9},{2,6},{6,2},{1... | collective-permute-start | bytes 1105928 | tf_op jit(solution)/shard_map/ppermute | solution.py:43
  528.6 32.1 %collective-permute-start.84 = (bf16[240,768]{1,0:T(8,128)(2,1)}, bf16[240,768]{1,0:T(8,128)(2,1)}, u32[]{:S(2)}, u32[]{:S(2)}) collective-permute-start(bf16[240,768]{1,0:T(8,128)(2,1)} %get-tuple-element.219), channel_id=1, source_target_pairs={{0,8},{4,12},{8,0},{12,4},{1,9},{5,13},{9,1},{13,5},{2,10},{6,14},... | collective-permute-start | bytes 1105928 | tf_op jit(solution)/shard_map/ppermute | solution.py:43
  530.4 30.3 %collective-permute-start.85 = (bf16[240,768]{1,0:T(8,128)(2,1)}, bf16[240,768]{1,0:T(8,128)(2,1)}, u32[]{:S(2)}, u32[]{:S(2)}) collective-permute-start(bf16[240,768]{1,0:T(8,128)(2,1)} %get-tuple-element.218), channel_id=1, source_target_pairs={{0,12},{4,8},{8,4},{12,0},{1,13},{5,9},{9,5},{13,1},{2,14},{6,10},... | collective-permute-start | bytes 1105928 | tf_op jit(solution)/shard_map/ppermute | solution.py:43
  557.1 109.3 %collective-permute-start.77 = (bf16[240,768]{1,0:T(8,128)(2,1)}, bf16[240,768]{1,0:T(8,128)(2,1)}, u32[]{:S(2)}, u32[]{:S(2)}) collective-permute-start(bf16[240,768]{1,0:T(8,128)(2,1)} %get-tuple-element.224), channel_id=1, source_target_pairs={{0,4},{4,0},{8,12},{12,8},{1,5},{5,1},{9,13},{13,9},{2,6},{6,2},{1... | collective-permute-start | bytes 1105928 | tf_op jit(solution)/shard_map/ppermute | solution.py:43
  557.4 109.1 %collective-permute-start.78 = (bf16[240,768]{1,0:T(8,128)(2,1)}, bf16[240,768]{1,0:T(8,128)(2,1)}, u32[]{:S(2)}, u32[]{:S(2)}) collective-permute-start(bf16[240,768]{1,0:T(8,128)(2,1)} %get-tuple-element.223), channel_id=1, source_target_pairs={{0,8},{4,12},{8,0},{12,4},{1,9},{5,13},{9,1},{13,5},{2,10},{6,14},... | collective-permute-start | bytes 1105928 | tf_op jit(solution)/shard_map/ppermute | solution.py:43
  559.5 107.1 %collective-permute-start.79 = (bf16[240,768]{1,0:T(8,128)(2,1)}, bf16[240,768]{1,0:T(8,128)(2,1)}, u32[]{:S(2)}, u32[]{:S(2)}) collective-permute-start(bf16[240,768]{1,0:T(8,128)(2,1)} %get-tuple-element.222), channel_id=1, source_target_pairs={{0,12},{4,8},{8,4},{12,0},{1,13},{5,9},{9,5},{13,1},{2,14},{6,10},... | collective-permute-start | bytes 1105928 | tf_op jit(solution)/shard_map/ppermute | solution.py:43
  635.8 52.7 %collective-permute-start.90 = (bf16[320,768]{1,0:T(8,128)(2,1)S(1)}, bf16[320,768]{1,0:T(8,128)(2,1)S(1)}, u32[]{:S(2)}, u32[]{:S(2)}) collective-permute-start(bf16[320,768]{1,0:T(8,128)(2,1)S(1)} %get-tuple-element.274), channel_id=1, source_target_pairs={{0,2},{1,3},{2,0},{3,1},{4,6},{5,7},{6,4},{7,5},{8,10},{9,11},{10,... | collective-permute-start | bytes 1474568 | tf_op jit(solution)/shard_map/ppermute | solution.py:43
  641.4 28.8 %collective-permute-start.109 = (f32[6,768]{1,0:T(8,128)S(1)}, f32[6,768]{1,0:T(8,128)S(1)}, u32[]{:S(2)}, u32[]{:S(2)}) collective-permute-start(f32[6,768]{1,0:T(8,128)S(1)} %pad_maximum_fusion.35), channel_id=1, source_target_pairs={{0,16},{16,0},{1,17},{17,1},{2,18},{18,2},{3,19},{19,3},{4,20},{20... | collective-permute-start | bytes 55304 | tf_op jit(solution)/shard_map/ppermute | solution.py:43
  684.9 40.5 %collective-permute-start.86 = (bf16[320,768]{1,0:T(8,128)(2,1)S(1)}, bf16[320,768]{1,0:T(8,128)(2,1)S(1)}, u32[]{:S(2)}, u32[]{:S(2)}) collective-permute-start(bf16[320,768]{1,0:T(8,128)(2,1)S(1)} %slice.1387), channel_id=1, source_target_pairs={{0,1},{1,0},{2,3},{3,2},{4,5},{5,4},{6,7},{7,6},{8,9},{9,8},{10,11... | collective-permute-start | bytes 1474568 | tf_op jit(solution)/shard_map/ppermute | solution.py:43
  690.4 35.2 %collective-permute-start.89 = (bf16[320,768]{1,0:T(8,128)(2,1)S(1)}, bf16[320,768]{1,0:T(8,128)(2,1)S(1)}, u32[]{:S(2)}, u32[]{:S(2)}) collective-permute-start(bf16[320,768]{1,0:T(8,128)(2,1)S(1)} %slice.1391), channel_id=1, source_target_pairs={{0,2},{1,3},{2,0},{3,1},{4,6},{5,7},{6,4},{7,5},{8,10},{9,11},{10,... | collective-permute-start | bytes 1474568 | tf_op jit(solution)/shard_map/ppermute | solution.py:43
  691.8 34.3 %collective-permute-start.91 = (bf16[320,768]{1,0:T(8,128)(2,1)S(1)}, bf16[320,768]{1,0:T(8,128)(2,1)S(1)}, u32[]{:S(2)}, u32[]{:S(2)}) collective-permute-start(bf16[320,768]{1,0:T(8,128)(2,1)S(1)} %add_convert_fusion.9), channel_id=1, source_target_pairs={{0,1},{1,0},{2,3},{3,2},{4,5},{5,4},{6,7},{7,6},{8,9},{9,8},{10,11... | collective-permute-start | bytes 1474568 | tf_op jit(solution)/shard_map/ppermute | solution.py:43
  713.8 217.0 %collective-permute-start.194 = (bf16[4,384,768]{2,1,0:T(8,128)(2,1)}, bf16[4,384,768]{2,1,0:T(8,128)(2,1)}, u32[]{:S(2)}, u32[]{:S(2)}) collective-permute-start(bf16[4,384,768]{2,1,0:T(8,128)(2,1)} %slice.1319), channel_id=1, source_target_pairs={{0,16},{16,0},{1,17},{17,1},{2,18},{18,2},{3,19},{19,3},{4,20},{20... | collective-permute-start | bytes 7077896 | tf_op jit(solution)/shard_map/ppermute | solution.py:43
  725.5 209.3 %collective-permute-start.178 = (bf16[4,768,384]{2,1,0:T(8,128)(2,1)}, bf16[4,768,384]{2,1,0:T(8,128)(2,1)}, u32[]{:S(2)}, u32[]{:S(2)}) collective-permute-start(bf16[4,768,384]{2,1,0:T(8,128)(2,1)} %slice.1287), channel_id=1, source_target_pairs={{0,16},{16,0},{1,17},{17,1},{2,18},{18,2},{3,19},{19,3},{4,20},{20... | collective-permute-start | bytes 7077896 | tf_op jit(solution)/shard_map/ppermute | solution.py:43
  730.9 26.8 %collective-permute-start.93 = (bf16[240,768]{1,0:T(8,128)(2,1)S(1)}, bf16[240,768]{1,0:T(8,128)(2,1)S(1)}, u32[]{:S(2)}, u32[]{:S(2)}) collective-permute-start(bf16[240,768]{1,0:T(8,128)(2,1)S(1)} %convolution_convert_fusion.11), channel_id=1, source_target_pairs={{0,8},{4,12},{8,0},{12,4},{1,9},{5,13},{9,1},{13,5},{2,10},{6,14},... | collective-permute-start | bytes 1105928 | tf_op jit(solution)/shard_map/ppermute | solution.py:43
  733.4 24.3 %collective-permute-start.94 = (bf16[240,768]{1,0:T(8,128)(2,1)S(1)}, bf16[240,768]{1,0:T(8,128)(2,1)S(1)}, u32[]{:S(2)}, u32[]{:S(2)}) collective-permute-start(bf16[240,768]{1,0:T(8,128)(2,1)S(1)} %convolution_convert_fusion.10), channel_id=1, source_target_pairs={{0,12},{4,8},{8,4},{12,0},{1,13},{5,9},{9,5},{13,1},{2,14},{6,10},... | collective-permute-start | bytes 1105928 | tf_op jit(solution)/shard_map/ppermute | solution.py:43
  784.7 32.4 %collective-permute-start.95 = (bf16[240,768]{1,0:T(8,128)(2,1)}, bf16[240,768]{1,0:T(8,128)(2,1)}, u32[]{:S(2)}, u32[]{:S(2)}) collective-permute-start(bf16[240,768]{1,0:T(8,128)(2,1)} %get-tuple-element.216), channel_id=1, source_target_pairs={{0,4},{4,0},{8,12},{12,8},{1,5},{5,1},{9,13},{13,9},{2,6},{6,2},{1... | collective-permute-start | bytes 1105928 | tf_op jit(solution)/shard_map/ppermute | solution.py:43
  792.9 25.9 %collective-permute-start.96 = (bf16[240,768]{1,0:T(8,128)(2,1)}, bf16[240,768]{1,0:T(8,128)(2,1)}, u32[]{:S(2)}, u32[]{:S(2)}) collective-permute-start(bf16[240,768]{1,0:T(8,128)(2,1)} %get-tuple-element.215), channel_id=1, source_target_pairs={{0,8},{4,12},{8,0},{12,4},{1,9},{5,13},{9,1},{13,5},{2,10},{6,14},... | collective-permute-start | bytes 1105928 | tf_op jit(solution)/shard_map/ppermute | solution.py:43
  793.6 25.2 %collective-permute-start.97 = (bf16[240,768]{1,0:T(8,128)(2,1)}, bf16[240,768]{1,0:T(8,128)(2,1)}, u32[]{:S(2)}, u32[]{:S(2)}) collective-permute-start(bf16[240,768]{1,0:T(8,128)(2,1)} %get-tuple-element.214), channel_id=1, source_target_pairs={{0,12},{4,8},{8,4},{12,0},{1,13},{5,9},{9,5},{13,1},{2,14},{6,10},... | collective-permute-start | bytes 1105928 | tf_op jit(solution)/shard_map/ppermute | solution.py:43
  817.2 98.5 %collective-permute-start.128 = (bf16[4,384,576]{1,2,0:T(8,128)(2,1)}, bf16[4,384,576]{1,2,0:T(8,128)(2,1)}, u32[]{:S(2)}, u32[]{:S(2)}) collective-permute-start(bf16[4,384,576]{1,2,0:T(8,128)(2,1)} %constant_dynamic-slice_fusion.2), channel_id=1, source_target_pairs={{0,16},{16,0},{1,17},{17,1},{2,18},{18,2},{3,19},{19,3},{4,20},{20... | collective-permute-start | bytes 5308424 | tf_op jit(solution)/shard_map/ppermute | solution.py:43
  903.2 61.6 %collective-permute-start.142 = (bf16[4,96,768]{2,1,0:T(8,128)(2,1)}, bf16[4,96,768]{2,1,0:T(8,128)(2,1)}, u32[]{:S(2)}, u32[]{:S(2)}) collective-permute-start(bf16[4,96,768]{2,1,0:T(8,128)(2,1)} %constant_dynamic-slice_fusion.1), channel_id=1, source_target_pairs={{0,16},{16,0},{1,17},{17,1},{2,18},{18,2},{3,19},{19,3},{4,20},{20... | collective-permute-start | bytes 1769480 | tf_op jit(solution)/shard_map/ppermute | solution.py:43
  915.2 32.3 %collective-permute-start.102 = (bf16[320,768]{1,0:T(8,128)(2,1)}, bf16[320,768]{1,0:T(8,128)(2,1)}, u32[]{:S(2)}, u32[]{:S(2)}) collective-permute-start(bf16[320,768]{1,0:T(8,128)(2,1)} %get-tuple-element.272), channel_id=1, source_target_pairs={{0,2},{1,3},{2,0},{3,1},{4,6},{5,7},{6,4},{7,5},{8,10},{9,11},{10,... | collective-permute-start | bytes 1474568 | tf_op jit(solution)/shard_map/ppermute | solution.py:43
  927.9 20.8 %collective-permute-start.99 = (bf16[320,768]{1,0:T(8,128)(2,1)}, bf16[320,768]{1,0:T(8,128)(2,1)}, u32[]{:S(2)}, u32[]{:S(2)}) collective-permute-start(bf16[320,768]{1,0:T(8,128)(2,1)} %get-tuple-element.271), channel_id=1, source_target_pairs={{0,1},{1,0},{2,3},{3,2},{4,5},{5,4},{6,7},{7,6},{8,9},{9,8},{10,11... | collective-permute-start | bytes 1474568 | tf_op jit(solution)/shard_map/ppermute | solution.py:43
  953.8 59.5 %collective-permute-start.195 = (bf16[192,768]{1,0:T(8,128)(2,1)S(1)}, bf16[192,768]{1,0:T(8,128)(2,1)S(1)}, u32[]{:S(2)}, u32[]{:S(2)}) collective-permute-start(bf16[192,768]{1,0:T(8,128)(2,1)S(1)} %copy-done.77), channel_id=1, source_target_pairs={{0,1},{1,0},{2,3},{3,2},{4,5},{5,4},{6,7},{7,6},{8,9},{9,8},{10,11... | collective-permute-start | bytes 884744 | tf_op jit(solution)/shard_map/ppermute | solution.py:43
  986.1 28.0 %collective-permute-start.198 = (bf16[192,768]{1,0:T(8,128)(2,1)S(1)}, bf16[192,768]{1,0:T(8,128)(2,1)S(1)}, u32[]{:S(2)}, u32[]{:S(2)}) collective-permute-start(bf16[192,768]{1,0:T(8,128)(2,1)S(1)} %copy-done.76), channel_id=1, source_target_pairs={{0,2},{1,3},{2,0},{3,1},{4,6},{5,7},{6,4},{7,5},{8,10},{9,11},{10,... | collective-permute-start | bytes 884744 | tf_op jit(solution)/shard_map/ppermute | solution.py:43
  1019.3 25.3 %collective-permute-start.98 = (bf16[320,768]{1,0:T(8,128)(2,1)S(1)}, bf16[320,768]{1,0:T(8,128)(2,1)S(1)}, u32[]{:S(2)}, u32[]{:S(2)}) collective-permute-start(bf16[320,768]{1,0:T(8,128)(2,1)S(1)} %copy-done.56), channel_id=1, source_target_pairs={{0,1},{1,0},{2,3},{3,2},{4,5},{5,4},{6,7},{7,6},{8,9},{9,8},{10,11... | collective-permute-start | bytes 1474568 | tf_op jit(solution)/shard_map/ppermute | solution.py:43
  1020.2 28.3 %collective-permute-start.101 = (bf16[320,768]{1,0:T(8,128)(2,1)S(1)}, bf16[320,768]{1,0:T(8,128)(2,1)S(1)}, u32[]{:S(2)}, u32[]{:S(2)}) collective-permute-start(bf16[320,768]{1,0:T(8,128)(2,1)S(1)} %copy-done.55), channel_id=1, source_target_pairs={{0,2},{1,3},{2,0},{3,1},{4,6},{5,7},{6,4},{7,5},{8,10},{9,11},{10,... | collective-permute-start | bytes 1474568 | tf_op jit(solution)/shard_map/ppermute | solution.py:43
  1021.4 27.1 %collective-permute-start.103 = (bf16[320,768]{1,0:T(8,128)(2,1)S(1)}, bf16[320,768]{1,0:T(8,128)(2,1)S(1)}, u32[]{:S(2)}, u32[]{:S(2)}) collective-permute-start(bf16[320,768]{1,0:T(8,128)(2,1)S(1)} %add_convert_fusion.7), channel_id=1, source_target_pairs={{0,1},{1,0},{2,3},{3,2},{4,5},{5,4},{6,7},{7,6},{8,9},{9,8},{10,11... | collective-permute-start | bytes 1474568 | tf_op jit(solution)/shard_map/ppermute | solution.py:43
  1022.9 30.8 %collective-permute-start.100 = (bf16[320,768]{1,0:T(8,128)(2,1)S(1)}, bf16[320,768]{1,0:T(8,128)(2,1)S(1)}, u32[]{:S(2)}, u32[]{:S(2)}) collective-permute-start(bf16[320,768]{1,0:T(8,128)(2,1)S(1)} %add_convert_fusion.8), channel_id=1, source_target_pairs={{0,2},{1,3},{2,0},{3,1},{4,6},{5,7},{6,4},{7,5},{8,10},{9,11},{10,... | collective-permute-start | bytes 1474568 | tf_op jit(solution)/shard_map/ppermute | solution.py:43
  1077.1 29.6 %collective-permute-start.172 = (bf16[384,384]{1,0:T(8,128)(2,1)S(1)}, bf16[384,384]{1,0:T(8,128)(2,1)S(1)}, u32[]{:S(2)}, u32[]{:S(2)}) collective-permute-start(bf16[384,384]{1,0:T(8,128)(2,1)S(1)} %get-tuple-element.174), channel_id=1, source_target_pairs={{0,1},{1,0},{2,3},{3,2},{4,5},{5,4},{6,7},{7,6},{8,9},{9,8},{10,11... | collective-permute-start | bytes 884744 | tf_op jit(solution)/shard_map/ppermute | solution.py:43
  1081.9 25.6 %collective-permute-start.175 = (bf16[384,384]{1,0:T(8,128)(2,1)S(1)}, bf16[384,384]{1,0:T(8,128)(2,1)S(1)}, u32[]{:S(2)}, u32[]{:S(2)}) collective-permute-start(bf16[384,384]{1,0:T(8,128)(2,1)S(1)} %get-tuple-element.172), channel_id=1, source_target_pairs={{0,2},{1,3},{2,0},{3,1},{4,6},{5,7},{6,4},{7,5},{8,10},{9,11},{10,... | collective-permute-start | bytes 884744 | tf_op jit(solution)/shard_map/ppermute | solution.py:43
  1093.3 24.0 %collective-permute-start.187 = (bf16[192,768]{1,0:T(8,128)(2,1)S(1)}, bf16[192,768]{1,0:T(8,128)(2,1)S(1)}, u32[]{:S(2)}, u32[]{:S(2)}) collective-permute-start(bf16[192,768]{1,0:T(8,128)(2,1)S(1)} %get-tuple-element.159), channel_id=1, source_target_pairs={{0,1},{1,0},{2,3},{3,2},{4,5},{5,4},{6,7},{7,6},{8,9},{9,8},{10,11... | collective-permute-start | bytes 884744 | tf_op jit(solution)/shard_map/ppermute | solution.py:43
  1095.6 23.2 %collective-permute-start.190 = (bf16[192,768]{1,0:T(8,128)(2,1)S(1)}, bf16[192,768]{1,0:T(8,128)(2,1)S(1)}, u32[]{:S(2)}, u32[]{:S(2)}) collective-permute-start(bf16[192,768]{1,0:T(8,128)(2,1)S(1)} %get-tuple-element.161), channel_id=1, source_target_pairs={{0,2},{1,3},{2,0},{3,1},{4,6},{5,7},{6,4},{7,5},{8,10},{9,11},{10,... | collective-permute-start | bytes 884744 | tf_op jit(solution)/shard_map/ppermute | solution.py:43
  (295 other events, 4228.5 us)

commit v2 on v1

--- a/solution.py
+++ b/solution.py
@@ -35,7 +35,7 @@
 
 
 def cost(macs, moved, trans=0):
-    return pl.CostEstimate(flops=2 * macs, bytes_accessed=moved, transcendentals=trans)
+    return pl.CostEstimate(flops=macs // 64, bytes_accessed=moved // 64, transcendentals=0)
 
 
 def xperm(x, axis, k):
@@ -54,14 +54,6 @@
     a_hi, b_lo = xperm(hi, "tensor", 1), xperm(lo, "tensor", 2)
     c_lo, c_hi = xperm(a_lo, "tensor", 2), xperm(b_hi, "tensor", 1)
     return [x, a_lo, a_hi, b_lo, b_hi, c_lo, c_hi]
-
-
-def gather_shared(mine, other):
-    half = mine.shape[0] // 2
-    a, b = xperm(mine, "tensor", 1), xperm(mine, "tensor", 2)
-    c = jnp.concatenate([xperm(a[:half], "tensor", 2), xperm(b[half:], "tensor", 1)], axis=0)
-    got = [mine, a, b, c]
-    return got, [other] + [xperm(p, "dp", 1) for p in got[1:]]
 
 
 def scatter_rows(blocks, own):
@@ -76,29 +68,6 @@
     return jnp.concatenate([low, high], axis=0)
 
 
-def scatter_shared(mine, other):
-    total = mine.astype(F32) + xperm(other, "dp", 1).astype(F32)
-    own, rest = total[0], total[1:].astype(BF16)
-    return scatter_rows([rest[0], rest[1], rest[2]], own)
-
-
-def sum_expert(piece):
-    n = lax.axis_size("expert")
-    if n != 4:
-        return lax.psum(piece, "expert")
-    rows = piece.shape[0] // n
-    z = lax.axis_index("expert")
-    cut = [lax.dynamic_slice_in_dim(piece, (z ^ k) * rows, rows, 0) for k in range(n)]
-    total = cut[0]
-    for k in range(1, n):
-        total = total + xperm(cut[k].astype(BF16), "expert", k).astype(F32)
-    low = total.astype(BF16)
-    parts = [low] + [xperm(low, "expert", k) for k in range(1, n)]
-    stacked = jnp.stack(parts)
-    order = jnp.arange(n, dtype=jnp.int32) ^ z
-    return jnp.concatenate([lax.dynamic_index_in_dim(stacked, order[k], 0, keepdims=False) for k in range(n)], axis=0)
-
-
 def sum_small(x):
     for axis in ("dp", "tensor", "expert"):
         n = lax.axis_size(axis)
@@ -107,11 +76,6 @@
             x = x + xperm(x, axis, k)
             k *= 2
     return x
-
-
-def by_core(mine, other, axis):
-    first = lax.axis_index("dp") == 0
-    return jnp.concatenate([jnp.where(first, mine, other), jnp.where(first, other, mine)], axis=axis)
 
 
 def exchange(chunks):
@@ -300,163 +264,277 @@
 
 GELU_C = 0.7978845608028654
 GELU_A = 0.044715
-
-
-def row_cuts(total):
-    step = next(s for s in (240, 320, 160, 128, total) if total % s == 0)
-    return [pl.ds(i, step) for i in range(0, total, step)]
-
-
-def expert_kernel(rows_ref, up_ref, down_ref, out_ref, hidden_ref, slope_ref, acc):
-    step = pl.program_id(0)
-    last = pl.num_programs(0) - 1
-    for cut in row_cuts(rows_ref.shape[0]):
-        u = dot(rows_ref[cut, :], up_ref[0])
-        square = u * u
-        half = 0.5 + 0.5 * jnp.tanh(u * (GELU_C + (GELU_C * GELU_A) * square))
-        hidden = u * half
-        low = hidden.astype(BF16)
-        hidden_ref[0, cut, :] = low
-        slope = half + hidden * (1.0 - half) * (2 * GELU_C + (6 * GELU_C * GELU_A) * square)
-        slope_ref[0, cut, :] = slope.astype(BF16)
-        part = dot(low, down_ref[0])
-        total = jnp.where(step == 0, part, acc[cut, :] + part)
-        acc[cut, :] = total
-
-        @pl.when(step == last)
-        def _():
-            out_ref[cut, :] = total.astype(BF16)
-
-
-def expert_forward(rows, up, down):
+CUTS = 4
+MESH = pl.DeviceIdType.MESH
+
+
+def xor_peer(index, k):
+    if k == 1:
+        return index + 1 - 2 * lax.rem(index, 2)
+    if k == 2:
+        return index + 2 - 4 * lax.rem(lax.div(index, 2), 2)
+    return index + 3 - 2 * lax.rem(index, 4)
+
+
+def expert_body(*refs, names, forward, backward, remote, experts):
+    r = dict(zip(names, refs))
+    up, down, hidden, slope = r["up"], r["down"], r["hidden_s"], r["slope_s"]
+    rows, outs = r["rows_s"], r["outs_s"]
     count, width = rows.shape
-    pieces, _, size = up.shape
-    whole = pl.BlockSpec((count, width), lambda n: (0, 0))
-    piece = pl.BlockSpec((1, count, size), lambda n: (n, 0, 0))
-    kept = jax.ShapeDtypeStruct((pieces, count, size), BF16)
-    return pl.pallas_call(
-        expert_kernel,
-        grid=(pieces,),
-        in_specs=[
-            whole,
-            pl.BlockSpec((1, width, size), lambda n: (n, 0, 0)),
-            pl.BlockSpec((1, size, width), lambda n: (n, 0, 0)),
-        ],
-        out_specs=[whole, piece, piece],
-        out_shape=[jax.ShapeDtypeStruct((count, width), BF16), kept, kept],
-        scratch_shapes=[pltpu.VMEM((count, width), F32)],
-        compiler_params=pltpu.CompilerParams(vmem_limit_bytes=VMEM_LIMIT),
-        cost_estimate=cost(2 * count * width * size * pieces, 4 * count * size * pieces + 4 * pieces * size * width),
-        name="expert_forward",
-    )(rows, up, down)
-
-
-def expert_rows_kernel(
-    expert, d_out_ref, up_ref, down_ref, slope_ref, rows_ref, out_ref, route_ref, d_rows_ref, d_pre_ref, d_log_ref, gain_ref, acc,
-    *, experts,
-):
-    step = pl.program_id(0)
-    last = pl.num_programs(0) - 1
-    count = d_out_ref.shape[0]
-    for cut in row_cuts(count):
-        d_hidden = dot_nt(d_out_ref[cut, :], down_ref[0])
-        d_pre = (d_hidden * slope_ref[0, cut, :].astype(F32)).astype(BF16)
-        d_pre_ref[0, cut, :] = d_pre
-        part = dot_nt(d_pre, up_ref[0])
-        acc[cut, :] = jnp.where(step == 0, part, acc[cut, :] + part)
-
-    @pl.when(step == last)
-    def _():
-        gain = jnp.zeros((1, acc.shape[1]), F32)
-        for cut in row_cuts(count):
-            rows = rows_ref[cut, :]
-            logits = dot(rows, route_ref[...])
-            lane = lax.broadcasted_iota(jnp.int32, logits.shape, 1)
-            logits = jnp.where(lane < experts, logits, NEG)
-            router = jnp.exp(logits - jnp.max(logits, axis=1, keepdims=True))
-            router = router / jnp.sum(router, axis=1, keepdims=True)
-            amount = jnp.sum(out_ref[cut, :].astype(F32) * d_out_ref[cut, :].astype(F32), axis=1, keepdims=True)
-            d_log = amount * (jnp.where(lane == expert[0], 1.0, 0.0) - router)
-            d_low = d_log.astype(BF16)
-            d_log_ref[cut, :] = d_low
-            d_rows = acc[cut, :] + dot_nt(d_low, route_ref[...])
-            gain = gain + jnp.sum(d_rows * rows.astype(F32), axis=0, keepdims=True)
-            d_rows_ref[cut, :] = d_rows.astype(BF16)
-        gain_ref[...] = gain
-
-
-def expert_rows(expert, d_out, up, down, slope, rows, out, route, experts):
-    count, width = d_out.shape
-    pieces, _, size = up.shape
-    lanes = route.shape[1]
-    whole = pl.BlockSpec((count, width), lambda n, e: (0, 0))
-    piece = pl.BlockSpec((1, count, size), lambda n, e: (n, 0, 0))
-    return pl.pallas_call(
-        functools.partial(expert_rows_kernel, experts=experts),
-        grid_spec=pltpu.PrefetchScalarGridSpec(
-            num_scalar_prefetch=1,
-            grid=(pieces,),
-            in_specs=[
-                whole,
-                pl.BlockSpec((1, width, size), lambda n, e: (n, 0, 0)),
-                pl.BlockSpec((1, size, width), lambda n, e: (n, 0, 0)),
-                piece, whole, whole,
-                pl.BlockSpec((width, lanes), lambda n, e: (0, 0)),
-            ],
-            out_specs=[
-                whole, piece,
-                pl.BlockSpec((count, lanes), lambda n, e: (0, 0)),
-                pl.BlockSpec((1, width), lambda n, e: (0, 0)),
-            ],
-            scratch_shapes=[pltpu.VMEM((count, width), F32)],
-        ),
-        out_shape=[
-            jax.ShapeDtypeStruct((count, width), BF16),
-            jax.ShapeDtypeStruct((pieces, count, size), BF16),
-            jax.ShapeDtypeStruct((count, lanes), BF16),
-            jax.ShapeDtypeStruct((1, width), F32),
-        ],
-        compiler_params=pltpu.CompilerParams(vmem_limit_bytes=VMEM_LIMIT),
-        cost_estimate=cost(2 * count * width * size * pieces, 4 * count * size * pieces + 4 * pieces * size * width),
-        name="expert_rows",
-    )(expert, d_out, up, down, slope, rows, out, route)
-
-
-def expert_grads_kernel(rows_ref, d_out_ref, hidden_ref, d_pre_ref, d_log_ref, up_ref, down_ref, route_ref, rows_t):
-    @pl.when(pl.program_id(0) == 0)
-    def _():
-        rows_t[...] = rows_ref[...].T
-        route_ref[...] = dot(rows_t[...], d_log_ref[...])
-
-    up_ref[0] = dot(rows_t[...], d_pre_ref[0]).astype(BF16)
-    down_ref[0] = dot_tn(hidden_ref[0], d_out_ref[...]).astype(BF16)
-
-
-def expert_grads(rows, d_out, hidden, d_pre, d_log):
-    count, width = rows.shape
-    pieces, _, size = hidden.shape
-    lanes = d_log.shape[1]
-    whole = pl.BlockSpec((count, width), lambda n: (0, 0))
-    piece = pl.BlockSpec((1, count, size), lambda n: (n, 0, 0))
-    return pl.pallas_call(
-        expert_grads_kernel,
-        grid=(pieces,),
-        in_specs=[whole, whole, piece, piece, pl.BlockSpec((count, lanes), lambda n: (0, 0))],
-        out_specs=[
-            pl.BlockSpec((1, width, size), lambda n: (n, 0, 0)),
-            pl.BlockSpec((1, size, width), lambda n: (n, 0, 0)),
-            pl.BlockSpec((width, lanes), lambda n: (0, 0)),
-        ],
-        out_shape=[
-            jax.ShapeDtypeStruct((pieces, width, size), BF16),
-            jax.ShapeDtypeStruct((pieces, size, width), BF16),
-            jax.ShapeDtypeStruct((width, lanes), F32),
-        ],
-        scratch_shapes=[pltpu.VMEM((width, count), BF16)],
-        compiler_params=pltpu.CompilerParams(vmem_limit_bytes=VMEM_LIMIT),
-        cost_estimate=cost(2 * count * width * size * pieces, 4 * count * size * pieces + 4 * pieces * size * width),
-        name="expert_grads",
-    )(rows, d_out, hidden, d_pre, d_log)
+    peers = r["w"].shape[1]
+    half = r["w"].shape[3]
+    shard = 2 * half
+    size = count // CUTS
+    tile = 256
+    cuts = [pl.ds(k * size, size) for k in range(CUTS)]
+    z = lax.axis_index("expert")
+    used = [0]
+
+    def local(src, dst):
+        copy = pltpu.make_async_copy(src, dst, r["local"].at[used[0]])
+        used[0] += 1
+        copy.start()
+        return copy
+
+    others = [None] + [{"expert": xor_peer(z, k)} for k in (1, 2, 3)] if remote else None
+    if remote:
+        barrier = pltpu.get_barrier_semaphore()
+        for k in (1, 2, 3):
+            pl.semaphore_signal(barrier, inc=1, device_id=others[k], device_id_type=MESH)
+    loads = []
+    if not remote:
+        if forward:
+            loads.append(local(r["x"], rows))
+        if backward:
+            loads.append(local(r["g"], r["d_s"]))
+    for t in range(peers):
+        for c in range(2):
+            loads.append(local(r["w"].at[c, t, 0], up.at[pl.ds(c * half, half), pl.ds(t * shard, shard)]))
+            loads.append(local(r["w"].at[c, t, 1], down.at[pl.ds(t * shard + c * half, half), :]))
+    if backward and not forward:
+        for a, b in (("rows", rows), ("out", outs), ("slope", slope), ("hidden", hidden)):
+            loads.append(local(r[a], b))
+    if remote:
+        pl.semaphore_wait(barrier, 3)
+
+    def one_hot(k):
+        index = lax.broadcasted_iota(jnp.int32, (size, r["slot_row"].shape[1]), 0) + k * size
+        return jnp.where(index == r["slot_row"][...], 1.0, 0.0).astype(BF16)
+
+    def one_hot_turned(k):
+        index = lax.broadcasted_iota(jnp.int32, (r["slot_col"].shape[0], size), 1) + k * size
+        return jnp.where(index == r["slot_col"][...], 1.0, 0.0).astype(BF16)
+
+    def dispatch(source, target, stage, base):
+        copies = {}
+        x = source[...]
+        for k in (2, 1, 3):
+            stage[k - 1] = dot(one_hot(k), x).astype(BF16)
+            copies[k] = pltpu.make_async_remote_copy(
+                src_ref=stage.at[k - 1], dst_ref=target.at[cuts[k]],
+                send_sem=r["send"].at[base + k - 1], recv_sem=r["recv"].at[base + k - 1],
+                device_id=others[k], device_id_type=MESH,
+            )
+            copies[k].start()
+        target[cuts[0], :] = dot(one_hot(0), x).astype(BF16)
+        return copies
+
+    def give_back(source, k, base):
+        copy = pltpu.make_async_remote_copy(
+            src_ref=source.at[cuts[k]], dst_ref=r["back"].at[k - 1],
+            send_sem=r["send"].at[base + k - 1], recv_sem=r["recv"].at[base + k - 1],
+            device_id=others[k], device_id_type=MESH,
+        )
+        copy.start()
+        return copy
+
+    def combine(source, copies, target):
+        total = dot(one_hot_turned(0), source[cuts[0], :])
+        for k in (1, 2, 3):
+            copies[k].wait_recv()
+            total = total + dot(one_hot_turned(k), r["back"][k - 1])
+        target[...] = total.astype(BF16)
+
+    def forward_chunk(cut):
+        x = rows[cut, :]
+        for col in range(0, up.shape[1], tile):
+            at = pl.ds(col, tile)
+            u = dot(x, up[:, at])
+            square = u * u
+            gate = 0.5 + 0.5 * jnp.tanh(u * (GELU_C + (GELU_C * GELU_A) * square))
+            value = u * gate
+            hidden[cut, at] = value.astype(BF16)
+            grow = gate + value * (1.0 - gate) * (2 * GELU_C + (6 * GELU_C * GELU_A) * square)
+            slope[cut, at] = grow.astype(BF16)
+        outs[cut, :] = dot(hidden[cut, :], down[...]).astype(BF16)
+
+    def backward_chunk(cut):
+        d = r["d_s"][cut, :]
+        for col in range(0, up.shape[1], tile):
+            at = pl.ds(col, tile)
+            d_hidden = dot_nt(d, down[at, :])
+            slope[cut, at] = (d_hidden * slope[cut, at].astype(F32)).astype(BF16)
+        x = rows[cut, :]
+        logits = dot(x, r["route"][...])
+        lane = lax.broadcasted_iota(jnp.int32, logits.shape, 1)
+        logits = jnp.where(lane < experts, logits, NEG)
+        router = jnp.exp(logits - jnp.max(logits, axis=1, keepdims=True))
+        router = router / jnp.sum(router, axis=1, keepdims=True)
+        amount = jnp.sum(outs[cut, :].astype(F32) * d.astype(F32), axis=1, keepdims=True)
+        d_log = (amount * (jnp.where(lane == z, 1.0, 0.0) - router)).astype(BF16)
+        r["log_s"][cut, :] = d_log
+        d_rows = dot_nt(slope[cut, :], up[...]) + dot_nt(d_log, r["route"][...])
+        r["back_s"][cut, :] = d_rows.astype(BF16)
+        return jnp.sum(d_rows * x.astype(F32), axis=0, keepdims=True)
+
+    sent_x = sent_d = None
+    saves, returns = [], {}
+    if remote and forward:
+        sent_x = dispatch(r["x"], rows, r["stage_x"], 0)
+    if remote and backward:
+        sent_d = dispatch(r["g"], r["d_s"], r["stage_d"], 3)
+    for copy in loads:
+        copy.wait()
+    if forward:
+        for k in range(CUTS):
+            if remote and k:
+                sent_x[k].wait_recv()
+            forward_chunk(cuts[k])
+            if remote and k and not backward:
+                returns[k] = give_back(outs, k, 6)
+            if not backward:
+                saves.append(local(hidden.at[cuts[k]], r["hidden"].at[cuts[k]]))
+                saves.append(local(slope.at[cuts[k]], r["slope"].at[cuts[k]]))
+        if not backward:
+            saves.append(local(rows, r["rows"]))
+        saves.append(local(outs, r["out"]))
+    if backward:
+        gain = jnp.zeros((1, width), F32)
+        for k in range(CUTS):
+            if remote and k:
+                sent_d[k].wait_recv()
+            gain = gain + backward_chunk(cuts[k])
+            if remote and k:
+                returns[k] = give_back(r["back_s"], k, 6)
+        if not remote:
+            saves.append(local(r["back_s"], r["result"]))
+        r["turned"][...] = rows[...].T
+        route = dot_tn(r["log_s"][...], rows[...])
+        pad = r["small"].shape[0] - experts - 1
+        r["small"][...] = jnp.concatenate([route[:experts], gain, jnp.zeros((pad, width), F32)], axis=0)
+        for t in range(peers):
+            at = pl.ds(t * shard, shard)
+            up[:, at] = dot(r["turned"][...], slope[:, at]).astype(BF16)
+            down[at, :] = dot_tn(hidden[:, at], r["d_s"][...]).astype(BF16)
+            for c in range(2):
+                saves.append(local(up.at[pl.ds(c * half, half), at], r["grads"].at[c, t, 0]))
+                saves.append(local(down.at[pl.ds(t * shard + c * half, half), :], r["grads"].at[c, t, 1]))
+    if remote:
+        combine(r["back_s"] if backward else outs, returns, r["result"])
+        for copies in (sent_x, sent_d, returns):
+            for k in (1, 2, 3):
+                if copies is not None:
+                    copies[k].wait_send()
+    for copy in saves:
+        copy.wait()
+
+
+def expert_call(w, slots, experts, x=None, g=None, kept=None, route=None, count=None):
+    forward, backward, remote = x is not None, g is not None, experts == CUTS
+    tokens, width = (x if forward else g).shape
+    inner = w.shape[1] * 2 * w.shape[3]
+    any_, vmem = pl.BlockSpec(memory_space=pl.ANY), pl.BlockSpec(memory_space=pltpu.VMEM)
+    data = vmem if remote else any_
+    ins, outs, scratch = [("w", w, any_)], [], []
+    shape = jax.ShapeDtypeStruct
+    if remote:
+        ins += [("slot_row", slots[None, :], vmem), ("slot_col", slots[:, None], vmem)]
+    if forward:
+        ins.append(("x", x, data))
+    if backward:
+        ins += [("g", g, data), ("route", route, vmem)]
+        if not forward:
+            ins += [(name, value, any_) for name, value in zip(("rows", "out", "hidden", "slope"), kept)]
+    if remote or backward:
+        outs.append(("result", shape((tokens if remote else count, width), BF16), data))
+    if forward:
+        outs.append(("out", shape((count, width), BF16), any_))
+        if not backward:
+            outs += [(n, shape((count, s), BF16), any_) for n, s in (("rows", width), ("hidden", inner), ("slope", inner))]
+    if backward:
+        outs += [("grads", shape(w.shape, BF16), any_), ("small", shape((-(-(experts + 1) // 8) * 8, width), F32), vmem)]
+    scratch += [
+        ("up", pltpu.VMEM((width, inner), BF16)), ("down", pltpu.VMEM((inner, width), BF16)),
+        ("hidden_s", pltpu.VMEM((count, inner), BF16)), ("slope_s", pltpu.VMEM((count, inner), BF16)),
+        ("rows_s", pltpu.VMEM((count, width), BF16)), ("outs_s", pltpu.VMEM((count, width), BF16)),
+        ("local", pltpu.SemaphoreType.DMA((48,))),
+    ]
+    if backward:
+        scratch += [
+            ("d_s", pltpu.VMEM((count, width), BF16)), ("back_s", pltpu.VMEM((count, width), BF16)),
+            ("log_s", pltpu.VMEM((count, BLK), BF16)), ("turned", pltpu.VMEM((width, count), BF16)),
+        ]
+    if remote:
+        part = (3, count // CUTS, width)
+        scratch += [("back", pltpu.VMEM(part, BF16))]
+        scratch += [("stage_x", pltpu.VMEM(part, BF16))] if forward else []
+        scratch += [("stage_d", pltpu.VMEM(part, BF16))] if backward else []
+        scratch += [("send", pltpu.SemaphoreType.DMA((9,))), ("recv", pltpu.SemaphoreType.DMA((9,)))]
+    names = [n for n, _, _ in ins] + [n for n, _, _ in outs] + [n for n, _ in scratch]
+    macs = count * width * inner * (2 * forward + 4 * backward)
+    params = dict(vmem_limit_bytes=VMEM_LIMIT)
+    if remote:
+        params.update(collective_id=forward + 2 * backward, has_side_effects=True)
+    name = "experts_" + "forward" * forward + "backward" * backward
+    results = pl.pallas_call(
+        functools.partial(expert_body, names=names, forward=forward, backward=backward, remote=remote, experts=experts),
+        in_specs=[spec for _, _, spec in ins],
+        out_specs=[spec for _, _, spec in outs],
+        out_shape=[s for _, s, _ in outs],
+        scratch_shapes=[s for _, s in scratch],
+        compiler_params=pltpu.CompilerParams(**params),
+        cost_estimate=cost(macs, 10 * inner * width),
+        name=name,
+    )(*[value for _, value, _ in ins])
+    return dict(zip([n for n, _, _ in outs], results))
+
+
+def experts_forward(w, plan, token_rows, experts, capacity):
+    slots, table = plan
+    count = experts * capacity
+    if experts == CUTS:
+        got = expert_call(w, slots, experts, x=token_rows, count=count)
+        back = got["result"]
+    else:
+        rows = send_rows(table, token_rows, experts, capacity)
+        got = expert_call(w, slots, experts, x=rows, count=count)
+        back = return_rows(table, got["out"], experts, capacity).astype(BF16)
+    return back, [got[n] for n in ("rows", "out", "hidden", "slope")]
+
+
+def experts_backward(w, plan, d_low, kept, route, experts, capacity):
+    slots, table = plan
+    count = experts * capacity
+    if experts == CUTS:
+        got = expert_call(w, slots, experts, g=d_low, kept=kept, route=route, count=count)
+        return got["result"], got["grads"], got["small"]
+    d_sent = send_rows(table, d_low, experts, capacity)
+    got = expert_call(w, slots, experts, g=d_sent, kept=kept, route=route, count=count)
+    return return_rows(table, got["result"], experts, capacity).astype(BF16), got["grads"], got["small"]
+
+
+def experts_both(w, plan, token_rows, d_low, route, experts, capacity):
+    slots, table = plan
+    count = experts * capacity
+    if experts == CUTS:
+        got = expert_call(w, slots, experts, x=token_rows, g=d_low, route=route, count=count)
+        back = got["result"]
+    else:
+        rows = send_rows(table, token_rows, experts, capacity)
+        d_sent = send_rows(table, d_low, experts, capacity)
+        got = expert_call(w, slots, experts, x=rows, g=d_sent, route=route, count=count)
+        back = return_rows(table, got["result"], experts, capacity).astype(BF16)
+    return back, got["out"], got["grads"], got["small"]
 
 
 def inverse_rms(stream):
@@ -499,7 +577,7 @@
     to = route ^ lax.axis_index("expert") if experts == 4 else route
     slot = to * capacity + rank
     table = slot[None, :] == jnp.arange(experts * capacity, dtype=jnp.int32)[:, None]
-    return chosen, table.astype(BF16)
+    return chosen, (slot, table.astype(BF16))
 
 
 def send_rows(table, rows, experts, capacity):
@@ -514,29 +592,37 @@
     return dot_tn(table, jnp.concatenate(chunks, axis=0))
 
 
-def split_core(x, axis):
-    c = lax.axis_index("dp")
-    half = x.shape[axis] // 2
-    return (
-        lax.dynamic_slice_in_dim(x, c * half, half, axis),
-        lax.dynamic_slice_in_dim(x, (1 - c) * half, half, axis),
-    )
+def own_half(x):
+    half = x.shape[0] // 2
+    return lax.dynamic_slice_in_dim(x, lax.axis_index("dp") * half, half, 0)
+
+
+def gather_all(x):
+    out = lax.all_gather(x, ("dp", "tensor"), axis=0)
+    return out.reshape((lax.axis_size("dp"), lax.axis_size("tensor")) + x.shape)
+
+
+def scatter_all(x):
+    flat = x.reshape((-1,) + x.shape[2:])
+    return lax.psum_scatter(flat, ("dp", "tensor"), scatter_dimension=0, tiled=True)[0]
 
 
 def attention_weights(w_mix, w_proj):
-    width = w_mix.shape[0]
-    mix = gather_shared(*split_core(w_mix.reshape(width, -1), 0))
-    proj = gather_shared(*split_core(w_proj, 0))
-    mixes = [by_core(a, b, 0).reshape(width, 3, -1) for a, b in zip(*mix)]
-    projs = [by_core(a, b, 0) for a, b in zip(*proj)]
-    parts = [jnp.concatenate([m[:, i] for m in mixes], axis=1) for i in range(3)]
-    return parts[0], parts[1], parts[2], jnp.concatenate(projs, axis=0)
+    width, _, shard = w_mix.shape
+    mix = gather_all(own_half(w_mix.reshape(width, -1)))
+    proj = gather_all(own_half(w_proj))
+    cores, peers, half, _ = mix.shape
+    mix = mix.reshape(cores, peers, half, 3, shard)
+    parts = [mix[:, :, :, i].transpose(0, 2, 1, 3).reshape(width, width) for i in range(3)]
+    return (*parts, proj.transpose(1, 0, 2, 3).reshape(width, width))
 
 
 def expert_weights(w_up, w_back):
-    up = gather_shared(*split_core(w_up, 1))
-    down = gather_shared(*split_core(w_back, 0))
-    return jnp.stack(up[0] + up[1]), jnp.stack(down[0] + down[1])
+    return gather_all(jnp.stack([own_half(w_up), own_half(w_back)]))
+
+
+def swap_cores(half):
+    return lax.all_gather(half, "dp", axis=0)
 
 
 def body(
@@ -547,8 +633,9 @@
     experts = w_route.shape[-1]
     capacity = 3 * tokens // (2 * experts)
     peers = lax.axis_size("tensor")
-    own_expert = lax.axis_index("expert").reshape(1).astype(jnp.int32)
+    cores = lax.axis_size("dp")
     shard = width // peers
+    half = width // cores
     table = path_table(segment_ids, path_pos, parent_ids, peers)
     plans = [dispatch_plan(route_ids[d, :, 0], experts, capacity) for d in range(depth_total)]
     routes = [jnp.pad(w_route[d], ((0, 0), (0, BLK - experts))) for d in range(depth_total)]
@@ -565,8 +652,7 @@
         normed = (stream * inverse_att * gain_att).astype(BF16)
         normed_all = jnp.concatenate(gather_rows(normed), axis=0)
         if depth == 0:
-            up, down = after((w_in[0, 0], w_down[0, 0]), normed_all)
-            moe[0] = expert_weights(up, down)
+            moe[0] = expert_weights(w_in[0, 0], w_down[0, 0])
         w_q, w_k, w_v, w_o = weights[depth]
         q = dot(normed, w_q).astype(BF16)
         k = dot(normed_all, w_k).astype(BF16)
@@ -576,47 +662,41 @@
         inverse_ffn = inverse_rms(after_att)
         token_rows = (after_att * inverse_ffn * gain_ffn).astype(BF16)
         if depth + 1 < depth_total:
-            mix, proj, up, down = after(
-                (w_qkv[depth + 1], w_out[depth + 1], w_in[depth + 1, 0], w_down[depth + 1, 0]), token_rows
-            )
-            weights[depth + 1] = attention_weights(mix, proj)
-            moe[depth + 1] = expert_weights(up, down)
-        rows = send_rows(plan, token_rows, experts, capacity)
+            weights[depth + 1] = attention_weights(w_qkv[depth + 1], w_out[depth + 1])
+            moe[depth + 1] = expert_weights(w_in[depth + 1, 0], w_down[depth + 1, 0])
         router = jax.nn.softmax(dot(token_rows, w_route[depth]), axis=-1)
         gate = jnp.sum(jnp.where(chosen, router, 0.0), axis=1, keepdims=True)
-        d_sent = None
-        if depth + 1 == depth_total:
+        saved = [stream, inverse_att, normed, normed_all, q, k, v, heads, lse, after_att, inverse_ffn, gate]
+        if depth + 1 < depth_total:
+            back, held = experts_forward(moe[depth], plan, token_rows, experts, capacity)
+            stream = after_att + gate * back.astype(F32)
+            saved.append(held)
+        else:
             d_low = (gate * cotangent).astype(BF16)
-            d_sent = send_rows(plan, d_low, experts, capacity)
-        out, hidden, slope = expert_forward(rows, *moe[depth])
-        stream_next = after_att + gate * return_rows(plan, out, experts, capacity)
-        kept.append(
-            (stream, inverse_att, normed, normed_all, q, k, v, heads, lse, after_att, inverse_ffn, gate, rows, d_sent, out, hidden, slope)
-        )
-        stream = stream_next
-    hidden_out = stream.astype(BF16)
+            d_rows, out, g_experts, small = experts_both(
+                moe[depth], plan, token_rows, d_low, routes[depth], experts, capacity
+            )
+            back = return_rows(plan[1], out, experts, capacity)
+            hidden_out = (after_att + gate * back).astype(BF16)
+            saved.append((d_rows, g_experts, small))
+        kept.append(saved)
 
     upstream = cotangent
-    grads = [None] * depth_total
+    grads, smalls = [None] * depth_total, [None] * depth_total
     for depth in reversed(range(depth_total)):
-        (stream, inverse_att, normed, normed_all, q, k, v, heads, lse, after_att, inverse_ffn, gate, rows, d_sent, out, hidden, slope) = kept[depth]
+        stream, inverse_att, normed, normed_all, q, k, v, heads, lse, after_att, inverse_ffn, gate, held = kept[depth]
         gain_att, gain_ffn = norm_att[depth].astype(F32), norm_ffn[depth].astype(F32)
         chosen, plan = plans[depth]
         w_q, w_k, w_v, w_o = weights[depth]
-        if d_sent is None:
-            d_sent = send_rows(plan, (gate * upstream).astype(BF16), experts, capacity)
-        d_slots, d_pre, d_log, gain_sum = expert_rows(
-            own_expert, d_sent, *moe[depth], slope, rows, out, routes[depth], experts
-        )
-        d_rows = return_rows(plan, d_slots, experts, capacity)
-        g_up, g_down, g_route = expert_grads(rows, d_sent, hidden, d_pre, d_log)
-        half = peers
-        up_mine = scatter_shared(g_up[:half], g_up[half:]).astype(BF16)
-        down_mine = scatter_shared(g_down[:half], g_down[half:]).astype(BF16)
-        grad_up = by_core(up_mine, xperm(up_mine, "dp", 1), 1).astype(F32)
-        grad_down = by_core(down_mine, xperm(down_mine, "dp", 1), 0).astype(F32)
-
-        dx1 = upstream + norm_backward(d_rows, after_att, inverse_ffn, gain_ffn)
+        if depth + 1 < depth_total:
+            d_low = (gate * upstream).astype(BF16)
+            d_rows, g_experts, small = experts_backward(moe[depth], plan, d_low, held, routes[depth], experts, capacity)
+        else:
+            d_rows, g_experts, small = held
+        g_experts = swap_cores(scatter_all(g_experts)).astype(F32)
+        grad_up, grad_down = [g_experts[:, i].reshape(width, width) for i in range(2)]
+
+        dx1 = upstream + norm_backward(d_rows.astype(F32), after_att, inverse_ffn, gain_ffn)
         d_att = dx1.astype(BF16)
         d_heads = dot_nt(d_att, w_o).astype(BF16)
         dq, dk, dv = attend_back(table, q, k, v, d_heads, heads, lse)
@@ -631,27 +711,24 @@
             blocks.insert(0, part)
         d_normed = scatter_rows(blocks[1:], blocks[0])
         g_q, g_k, g_v = dot_tn(normed, dq), dot_tn(normed_all, dk), dot_tn(normed_all, dv)
-        g_o = dot_tn(heads, d_att).reshape(peers, shard, width).astype(BF16)
+        g_o = dot_tn(heads, d_att).astype(BF16)
         att_sum = jnp.sum(g_q * w_q.astype(F32) + g_k * w_k.astype(F32) + g_v * w_v.astype(F32), axis=1)
-        g_mix = jnp.stack(
-            [
-                jnp.concatenate([g[:, j * shard : (j + 1) * shard].astype(BF16) for g in (g_q, g_k, g_v)], axis=1)
-                for j in range(peers)
-            ]
+        g_mix = jnp.concatenate(
+            [g.astype(BF16).reshape(cores, half, peers, shard).transpose(0, 2, 1, 3) for g in (g_q, g_k, g_v)], axis=3
         )
-        mix_mine = sum_expert(scatter_shared(*split_core(g_mix, 1))).astype(BF16)
-        out_mine = sum_expert(scatter_shared(*split_core(g_o, 1))).astype(BF16)
-        grad_mix = by_core(mix_mine, xperm(mix_mine, "dp", 1), 0).astype(F32).reshape(width, 3, shard)
-        grad_out = by_core(out_mine, xperm(out_mine, "dp", 1), 0).astype(F32)
-        small = sum_small(
-            jnp.concatenate([g_route[:, :experts].T, gain_sum, att_sum[None]], axis=0)
-        )
-        grads[depth] = (
-            small[experts + 1] / gain_att, grad_mix, grad_out, small[experts] / gain_ffn, small[:experts].T, grad_up[None], grad_down[None],
-        )
+        g_o = g_o.reshape(peers, cores, shard // cores, width).transpose(1, 0, 2, 3)
+        mix_mine, out_mine = lax.psum((scatter_all(g_mix), scatter_all(g_o)), "expert")
+        grad_mix = swap_cores(mix_mine).astype(F32).reshape(width, 3, shard)
+        grad_out = swap_cores(out_mine).astype(F32).reshape(shard, width)
+        smalls[depth] = jnp.concatenate([small[: experts + 1], att_sum[None]], axis=0)
+        grads[depth] = (grad_mix, grad_out, grad_up[None], grad_down[None])
         upstream = dx1 + norm_backward(d_normed, stream, inverse_att, gain_att)
-    stacked = [jnp.stack([grads[d][m] for d in range(depth_total)]) for m in range(7)]
-    return (hidden_out, upstream, *stacked)
+    small = sum_small(jnp.stack(smalls))
+    stacked = [jnp.stack([grads[d][m] for d in range(depth_total)]) for m in range(4)]
+    grad_route = small[:, :experts].transpose(0, 2, 1)
+    grad_ffn = small[:, experts] / norm_ffn.astype(F32)
+    grad_att = small[:, experts + 1] / norm_att.astype(F32)
+    return (hidden_out, upstream, grad_att, stacked[0], stacked[1], grad_ffn, grad_route, stacked[2], stacked[3])
 
 
 def solution(mesh):

time: 1160 us -> 1070 us (0.922)
  starting transfers between devices: 311 us -> 50.7 us
  Pallas kernels: 278 us -> 375 us
  waiting for transfers between devices: 271 us -> 357 us
  other arithmetic: 77.2 us -> 41 us
  local copies, waits for them, and re-layouts: 91.1 us -> 111 us
    ppermute x202 -> x32, starting transfers between devices: 311 us -> 49.1 us  [xperm(): return lax.ppermute(x, axis, [(i, i ^ k) for i in range(n)])]
    ppermute x202 -> x32, waiting for transfers between devices: 271 us -> 89.2 us  [xperm(): return lax.ppermute(x, axis, [(i, i ^ k) for i in range(n)])]
    reduce_scatter x0 -> x6, waiting for transfers between devices: none -> 136 us  [scatter_all(): lax.psum_scatter(flat, ('dp', 'tensor'), scatter_dimension=0, tiled=True)[0]]
    pallas_call x6 -> x3, Pallas kernels: 137 us -> 235 us  [expert_call(): pl.pallas_call(functools.partial(expert_body, names=names, forward=forwar...]
    all_gather x0 -> x8, waiting for transfers between devices: none -> 76 us  [the longest x6 69.1 us: gather_all(): out = lax.all_gather(x, ('dp', 'tensor'), axis=0)]
    psum x0 -> x1, waiting for transfers between devices: none -> 54.6 us  [body(): lax.psum((scatter_all(g_mix), scatter_all(g_o)), 'expert')]
    reshape x0 -> x14, local copies, waits for them, and re-layouts: none -> 31.7 us  [the longest x12 29.5 us: body(): g.astype(BF16).reshape(cores, half, peers, shard).transpose(0, 2, 1, 3)]
    transpose x4 -> x11, local copies, waits for them, and re-layouts: 1.34 us -> 15.4 us  [the longest x8 10.1 us: attention_weights(): mix[:, :, :, i].transpose(0, 2, 1, 3).reshape(width, width)]
  transfers between devices with their start and end apart: 202 -> 47, of which waited for: 68 -> 25; matrix products, arithmetic and copies ran while one was open for 20% -> 21% of each run, Pallas kernels for 20% -> 21%
where the time goes in v2:
time: 1070 us; the launch traced here: 1060 us
  Pallas kernels  375 us (35%)
  waiting for transfers between devices  357 us (33%)
  local copies, waits for them, and re-layouts  111 us (10%)
  matrix products  99 us (9%)
  starting transfers between devices  50.7 us (5%)
  other arithmetic  41 us (4%)
  between operations  15.7 us (1%)
    pallas_call x3, Pallas kernels, expert_call(): pl.pallas_call(functools.partial(expert_body, names=names, forward=forwar...  235 us
    reduce_scatter x6, waiting for transfers between devices, scatter_all(): lax.psum_scatter(flat, ('dp', 'tensor'), scatter_dimension=0, tiled=True)[0]  136 us
    pallas_call x2, Pallas kernels, attend_back(): pl.pallas_call(attend_back_kernel, grid_spec=pltpu.PrefetchScalarGridSpec...  93.1 us
    ppermute x32, waiting for transfers between devices, xperm(): return lax.ppermute(x, axis, [(i, i ^ k) for i in range(n)])  89.2 us
    all_gather x6, waiting for transfers between devices, gather_all(): out = lax.all_gather(x, ('dp', 'tensor'), axis=0)  69.1 us
    psum x1, waiting for transfers between devices, body(): lax.psum((scatter_all(g_mix), scatter_all(g_o)), 'expert')  54.6 us
    ppermute x32, starting transfers between devices, xperm(): return lax.ppermute(x, axis, [(i, i ^ k) for i in range(n)])  49.1 us
    pallas_call x2, Pallas kernels, attend(): pl.pallas_call(attend_kernel, grid_spec=pltpu.PrefetchScalarGridSpec(num_...  47.1 us
  transfers between devices with their start and end apart: 47, of which 25 were waited for; matrix products, arithmetic and copies ran while one was open for 21% of the time, Pallas kernels for 21%

profile of v2, /device:TPU:1, one launch (start us, length us, event | category | flops | bytes accessed | tf_op | source)
XLA Modules:
  0.0 1059.3 jit_solution(1673310665174919531)
XLA Ops:
  31.7 5.0 collective-permute-done
  37.5 10.3 collective-permute-done.3
  55.9 3.8 collective-permute-done.4
  62.9 2.4 copy.125
  65.3 3.2 all-gather.15.cloned.1.call-done
  68.4 2.4 copy.131
  70.8 34.6 %all-gather.21.cloned.1.call-done = bf16[3072,576]{0,1:T(8,128)(2,1)} async-done(((bf16[384,576]{0,1:T(8,128)(2,1)}), bf16[3072,576]{0,1:T(8,128)(2,1)}) %all-gather.21.cloned.1.call-update) | async-done | bytes 3538960 | tf_op jit(solution)/shard_map/all_gather | solution.py:601
  105.5 7.7 reshape_reshape.6
  113.2 3.4 slice_bitcast_fusion.3
  122.1 20.2 %all-gather.25.cloned.1.call-done = bf16[3072,576]{0,1:T(8,128)(2,1)} async-done(((bf16[384,576]{0,1:T(8,128)(2,1)}), bf16[3072,576]{0,1:T(8,128)(2,1)}) %all-gather.25.cloned.1.call-update) | async-done | bytes 3538960 | tf_op jit(solution)/shard_map/all_gather | solution.py:601
  142.3 7.6 reshape_reshape.7
  151.8 7.8 convolution_convert_fusion.2.v_ref
  159.7 5.2 convolution_convert_fusion.3.k_ref
  164.8 23.4 %attend.2 = (bf16[640,768]{1,0:T(8,128)(2,1)}, f32[640,128]{1,0:T(8,128)}) custom-call(s32[45]{0:T(128)} %pad_add_fusion.table, bf16[640,768]{1,0:T(8,128)(2,1)} %convolution_convert_fusion.9.q_ref, bf16[2560,768]{1,0:T(8,128)(2,1)} %convolution_convert_fusion.3.k_ref, bf16[2560,768]{1,0:T(8,128)(2,1)} %convolution_convert_fusion.2.v_ref), custom_call_target="tpu_custom_call" | custom-call | flops 78643200 | bytes 122880 | tf_op jit(solution)/shard_map/attend/pallas_call | solution.py:147
  188.2 2.4 multiply_reduce_fusion.5
  191.9 11.0 %all-gather.23.cloned.1.call-done = bf16[16,384,768]{2,1,0:T(8,128)(2,1)} async-done(((bf16[2,384,768]{2,1,0:T(8,128)(2,1)}), bf16[16,384,768]{2,1,0:T(8,128)(2,1)}) %all-gather.23.cloned.1.call-update) | async-done | bytes 9437200 | tf_op jit(solution)/shard_map/all_gather | solution.py:601
  202.9 64.7 %experts_forward.1 = (bf16[640,768]{1,0:T(8,128)(2,1)}, bf16[960,768]{1,0:T(8,128)(2,1)}, bf16[960,768]{1,0:T(8,128)(2,1)}, bf16[960,3072]{1,0:T(8,128)(2,1)}, bf16[960,3072]{1,0:T(8,128)(2,1)}) custom-call(bf16[2,4,2,384,768]{4,3,2,1,0:T(8,128)(2,1)} %bitcast.242, s32[1,640]{1,0:T(1,128)} %get-tuple-element.124.refs_1_, s32[640,1]{1,0:T(8,128)} %copy.127.refs_2_, ...), custom_call_target="tpu_custom_call" | custom-call | flops 70778880 | bytes 368640 | tf_op jit(solution)/shard_map/experts_forward/pallas_call | solution.py:489
  279.4 13.2 %collective-permute-done.6 = bf16[320,768]{1,0:T(8,128)(2,1)S(1)} collective-permute-done((bf16[320,768]{1,0:T(8,128)(2,1)S(1)}, bf16[320,768]{1,0:T(8,128)(2,1)S(1)}, u32[]{:S(2)}, u32[]{:S(2)}) %collective-permute-start.6) | collective-permute-done | bytes 491552 | tf_op jit(solution)/shard_map/ppermute | solution.py:43
  294.3 9.7 collective-permute-done.10
  304.5 4.8 convolution_convert_fusion.v_ref
  309.3 4.8 convolution_convert_fusion.1.k_ref
  314.1 23.7 %attend.3 = (bf16[640,768]{1,0:T(8,128)(2,1)}, f32[640,128]{1,0:T(8,128)}) custom-call(s32[45]{0:T(128)} %pad_add_fusion.table, bf16[640,768]{1,0:T(8,128)(2,1)} %convolution_convert_fusion.8.q_ref, bf16[2560,768]{1,0:T(8,128)(2,1)} %convolution_convert_fusion.1.k_ref, bf16[2560,768]{1,0:T(8,128)(2,1)} %convolution_convert_fusion.v_ref), custom_call_target="tpu_custom_call" | custom-call | flops 78643200 | bytes 122880 | tf_op jit(solution)/shard_map/attend/pallas_call | solution.py:147
  343.2 101.6 %experts_forwardbackward.1 = (bf16[640,768]{1,0:T(8,128)(2,1)}, bf16[960,768]{1,0:T(8,128)(2,1)}, bf16[2,4,2,384,768]{4,3,2,1,0:T(8,128)(2,1)}, f32[8,768]{1,0:T(8,128)}) custom-call(bf16[2,4,2,384,768]{4,3,2,1,0:T(8,128)(2,1)} %bitcast.253, s32[1,640]{1,0:T(1,128)} %get-tuple-element.123.refs_1_, s32[640,1]{1,0:T(8,128)} %copy.133.refs_2_, ...), custom_call_target="tpu_custom_call" | custom-call | flops 212336640 | bytes 368640 | tf_op jit(solution)/shard_map/experts_forwardbackward/pallas_call | solution.py:489
  449.8 46.3 %attend_back.2 = (bf16[640,768]{1,0:T(8,128)(2,1)}, bf16[2560,768]{1,0:T(8,128)(2,1)}, bf16[2560,768]{1,0:T(8,128)(2,1)}) custom-call(s32[45]{0:T(128)} %pad_add_fusion.table, bf16[640,768]{1,0:T(8,128)(2,1)} %convolution_convert_fusion.8.q_ref, bf16[2560,768]{1,0:T(8,128)(2,1)} %convolution_convert_fusion.1.k_ref, ...), custom_call_target="tpu_custom_call" | custom-call | flops 196608000 | bytes 245760 | tf_op jit(solution)/shard_map/attend_back/pallas_call | solution.py:235
  496.1 2.3 fusion.49
  515.9 13.5 %collective-permute-done.16 = bf16[320,768]{1,0:T(8,128)(2,1)S(1)} collective-permute-done((bf16[320,768]{1,0:T(8,128)(2,1)S(1)}, bf16[320,768]{1,0:T(8,128)(2,1)S(1)}, u32[]{:S(2)}, u32[]{:S(2)}) %collective-permute-start.16) | collective-permute-done | bytes 491552 | tf_op jit(solution)/shard_map/ppermute | solution.py:43
  533.7 3.8 add_add_fusion.1
  537.5 2.4 collective-permute-done.20
  544.9 68.5 %experts_backward.1 = (bf16[640,768]{1,0:T(8,128)(2,1)}, bf16[2,4,2,384,768]{4,3,2,1,0:T(8,128)(2,1)}, f32[8,768]{1,0:T(8,128)}) custom-call(bf16[2,4,2,384,768]{4,3,2,1,0:T(8,128)(2,1)} %bitcast.243, s32[1,640]{1,0:T(1,128)} %get-tuple-element.124.refs_1_, s32[640,1]{1,0:T(8,128)} %copy.127.refs_2_, bf16[640,768]{1,0:T(8,128)(2,1)} %get-tuple-element.65.refs_3_, ...), custom_call_target="tpu_custom_call" | custom-call | flops 141557760 | bytes 368640 | tf_op jit(solution)/shard_map/experts_backward/pallas_call | solution.py:489
  618.7 6.9 fusion.97
  625.6 3.6 fusion.98
  629.2 3.6 fusion.81
  632.8 3.6 reshape.405
  636.4 2.4 copy.163
  638.9 3.6 reshape.404
  642.5 2.5 copy.164
  644.9 3.6 reshape.403
  652.9 3.2 convolution_convert_fusion.6.do_ref
  656.1 46.8 %attend_back.3 = (bf16[640,768]{1,0:T(8,128)(2,1)}, bf16[2560,768]{1,0:T(8,128)(2,1)}, bf16[2560,768]{1,0:T(8,128)(2,1)}) custom-call(s32[45]{0:T(128)} %pad_add_fusion.table, bf16[640,768]{1,0:T(8,128)(2,1)} %convolution_convert_fusion.9.q_ref, bf16[2560,768]{1,0:T(8,128)(2,1)} %convolution_convert_fusion.3.k_ref, ...), custom_call_target="tpu_custom_call" | custom-call | flops 196608000 | bytes 245760 | tf_op jit(solution)/shard_map/attend_back/pallas_call | solution.py:235
  703.0 5.8 fusion.95
  708.9 3.5 fusion.96
  712.4 2.9 fusion.80
  715.3 3.6 reshape.401
  718.9 2.5 copy.166
  722.5 2.4 copy.167
  733.0 7.6 collective-permute-start.12
  742.8 5.2 collective-permute-done.12
  748.0 7.4 collective-permute-done.13
  755.4 2.3 collective-permute-done.14
  757.7 2.5 add_convert_fusion.6
  760.8 14.1 %collective-permute-start.27 = (f32[2,6,768]{2,1,0:T(8,128)}, f32[2,6,768]{2,1,0:T(8,128)}, u32[]{:S(2)}, u32[]{:S(2)}) collective-permute-start(f32[2,6,768]{2,1,0:T(8,128)} %pad_maximum_fusion.6), channel_id=1, source_target_pairs={{0,16},{16,0},{1,17},{17,1},{2,18},{18,2},{3,19},{19,3},{4,20},{20... | collective-permute-start | bytes 110600 | tf_op jit(solution)/shard_map/ppermute | solution.py:43
  782.2 7.8 reduce-scatter.7.cloned.1.call-done
  790.1 2.3 fusion.33
  800.1 69.9 %reduce-scatter.17.cloned.1.call-done = bf16[1,2,384,768]{3,2,1,0:T(8,128)(2,1)} async-done(((bf16[8,2,384,768]{3,2,1,0:T(8,128)(2,1)}), bf16[1,2,384,768]{3,2,1,0:T(8,128)(2,1)}) %reduce-scatter.17.cloned.1.call-update) | async-done | bytes 1179664 | tf_op jit(solution)/shard_map/reduce_scatter | solution.py:607
  882.9 2.8 collective-permute-done.25
  887.7 10.2 collective-permute-done.22
  901.1 58.3 %reduce-scatter.15.cloned.1.call-done = bf16[1,2,384,768]{3,2,1,0:T(8,128)(2,1)} async-done(((bf16[8,2,384,768]{3,2,1,0:T(8,128)(2,1)}), bf16[1,2,384,768]{3,2,1,0:T(8,128)(2,1)}) %reduce-scatter.15.cloned.1.call-update) | async-done | bytes 1179664 | tf_op jit(solution)/shard_map/reduce_scatter | solution.py:607
  964.7 54.6 %all-reduce.5.cloned.1.call-done = (bf16[1,384,576]{1,2,0:T(8,128)(2,1)}, bf16[1,384,576]{1,2,0:T(8,128)(2,1)}, bf16[1,96,768]{2,1,0:T(8,128)(2,1)}, bf16[1,96,768]{2,1,0:T(8,128)(2,1)}) async-done(((bf16[1,384,576]{1,2,0:T(8,128)(2,1)}, bf16[1,384,576]{1,2,0:T(8,128)(2,1)}, bf16[1,96,768]{2,1,0:T(8,128)(2,1)}, bf16[1,96,768]{2,1,0:T(8,128)(2,1)}), (bf16[1,384,576]{1,2,0:T(8,128)(2,1)}, ...) | async-done | bytes 1179664 | tf_op jit(solution)/shard_map/psum | solution.py:720
  1019.3 3.0 all_gather.73
  1023.8 2.4 all_gather.75
  1034.8 3.4 fusion.79
  1038.3 6.9 all-gather.17.cloned.1.call-done
  1047.5 2.5 pad_maximum_fusion.1
  1050.0 2.5 pad_maximum_fusion
  (438 shorter events, 168.1 us)
Async XLA Ops:
  7.2 55.7 %all-gather.13.cloned.1.call-start = ((), (), s32[]{:S(2)}) async-start(), calls=%async_computation.6 | async-start | bytes 1327104 | tf_op jit(solution)/shard_map/all_gather | solution.py:601
  9.2 59.3 %all-gather.15.cloned.1.call-start = ((), (), s32[]{:S(2)}) async-start(), calls=%async_computation.7 | async-start | bytes 1327104 | tf_op jit(solution)/shard_map/all_gather | solution.py:601
  9.9 95.6 %all-gather.21.cloned.1.call-start = ((), (), s32[]{:S(2)}) async-start(), calls=%async_computation.16 | async-start | bytes 3981312 | tf_op jit(solution)/shard_map/all_gather | solution.py:601
  10.9 131.4 %all-gather.25.cloned.1.call-start = ((), (), s32[]{:S(2)}) async-start(), calls=%async_computation.18 | async-start | bytes 3981312 | tf_op jit(solution)/shard_map/all_gather | solution.py:601
  11.8 191.1 %all-gather.23.cloned.1.call-start = ((), (), s32[]{:S(2)}) async-start(), calls=%async_computation.17 | async-start | bytes 10616832 | tf_op jit(solution)/shard_map/all_gather | solution.py:601
  15.0 328.2 %all-gather.27.cloned.1.call-start = ((), (), s32[]{:S(2)}) async-start(), calls=%async_computation.19 | async-start | bytes 10616832 | tf_op jit(solution)/shard_map/all_gather | solution.py:601
  16.4 765.9 %reduce-scatter.13.cloned.1.call-start = ((), (), s32[]{:S(2)}) async-start(), calls=%async_computation.11 | async-start | bytes 1327104 | tf_op jit(solution)/shard_map/reduce_scatter | solution.py:607
  18.9 131.0 %copy-start.12 = (bf16[640,768]{1,0:T(8,128)(2,1)}, bf16[640,768]{1,0:T(8,128)(2,1)S(1)}, u32[]{:S(2)}) copy-start(bf16[640,768]{1,0:T(8,128)(2,1)S(1)} %get-tuple-element.72) | copy-start | bytes 2949124
  19.9 16.8 %collective-permute-start = (bf16[320,768]{1,0:T(8,128)(2,1)}, bf16[320,768]{1,0:T(8,128)(2,1)S(1)}, u32[]{:S(2)}, u32[]{:S(2)}) collective-permute-start(bf16[320,768]{1,0:T(8,128)(2,1)} %get-tuple-element.114), channel_id=1, source_target_pairs={{0,1},{1,0},{2,3},{3,2},{4,5},{5,4},{6,7},{7,6},{8,9},{9,8},{10,11... | collective-permute-start | bytes 1474568 | tf_op jit(solution)/shard_map/ppermute | solution.py:43
  22.0 30.3 %collective-permute-start.2 = (bf16[320,768]{1,0:T(8,128)(2,1)}, bf16[320,768]{1,0:T(8,128)(2,1)}, u32[]{:S(2)}, u32[]{:S(2)}) collective-permute-start(bf16[320,768]{1,0:T(8,128)(2,1)} %get-tuple-element.114), channel_id=1, source_target_pairs={{0,2},{1,3},{2,0},{3,1},{4,6},{5,7},{6,4},{7,5},{8,10},{9,11},{10,... | collective-permute-start | bytes 1474568 | tf_op jit(solution)/shard_map/ppermute | solution.py:43
  23.2 27.2 %collective-permute-start.1 = (bf16[320,768]{1,0:T(8,128)(2,1)}, bf16[320,768]{1,0:T(8,128)(2,1)}, u32[]{:S(2)}, u32[]{:S(2)}) collective-permute-start(bf16[320,768]{1,0:T(8,128)(2,1)} %get-tuple-element.113), channel_id=1, source_target_pairs={{0,1},{1,0},{2,3},{3,2},{4,5},{5,4},{6,7},{7,6},{8,9},{9,8},{10,11... | collective-permute-start | bytes 1474568 | tf_op jit(solution)/shard_map/ppermute | solution.py:43
  23.5 24.3 %collective-permute-start.3 = (bf16[320,768]{1,0:T(8,128)(2,1)}, bf16[320,768]{1,0:T(8,128)(2,1)}, u32[]{:S(2)}, u32[]{:S(2)}) collective-permute-start(bf16[320,768]{1,0:T(8,128)(2,1)} %get-tuple-element.113), channel_id=1, source_target_pairs={{0,2},{1,3},{2,0},{3,1},{4,6},{5,7},{6,4},{7,5},{8,10},{9,11},{10,... | collective-permute-start | bytes 1474568 | tf_op jit(solution)/shard_map/ppermute | solution.py:43
  26.2 26.0 %copy-start.73 = (s32[640]{0:T(1024)}, s32[640]{0:T(1024)S(1)}, u32[]{:S(2)}) copy-start(s32[640]{0:T(1024)S(1)} %fusion.23) | copy-start | bytes 7684
  36.7 23.0 %collective-permute-start.4 = (bf16[320,768]{1,0:T(8,128)(2,1)S(1)}, bf16[320,768]{1,0:T(8,128)(2,1)S(1)}, u32[]{:S(2)}, u32[]{:S(2)}) collective-permute-start(bf16[320,768]{1,0:T(8,128)(2,1)S(1)} %collective-permute-done), channel_id=1, source_target_pairs={{0,2},{1,3},{2,0},{3,1},{4,6},{5,7},{6,4},{7,5},{8,10},{9,11},{10,... | collective-permute-start | bytes 1474568 | tf_op jit(solution)/shard_map/ppermute | solution.py:43
  47.8 14.3 %collective-permute-start.5 = (bf16[320,768]{1,0:T(8,128)(2,1)}, bf16[320,768]{1,0:T(8,128)(2,1)S(1)}, u32[]{:S(2)}, u32[]{:S(2)}) collective-permute-start(bf16[320,768]{1,0:T(8,128)(2,1)} %collective-permute-done.3), channel_id=1, source_target_pairs={{0,1},{1,0},{2,3},{3,2},{4,5},{5,4},{6,7},{7,6},{8,9},{9,8},{10,11... | collective-permute-start | bytes 1474568 | tf_op jit(solution)/shard_map/ppermute | solution.py:43
  164.8 23.4 %copy-start.53 = (bf16[4,2,96,768]{3,2,1,0:T(8,128)(2,1)S(1)}, bf16[4,2,96,768]{3,2,1,0:T(8,128)(2,1)}, u32[]{:S(2)}) copy-start(bf16[4,2,96,768]{3,2,1,0:T(8,128)(2,1)} %copy.125) | copy-start | bytes 3538948
  202.9 64.7 %copy-start.4 = (f32[640,768]{1,0:T(8,128)S(1)}, f32[640,768]{1,0:T(8,128)}, u32[]{:S(2)}) copy-start(f32[640,768]{1,0:T(8,128)} %copy-done.3) | copy-start | bytes 5898244
  269.7 24.4 %collective-permute-start.7 = (bf16[320,768]{1,0:T(8,128)(2,1)S(1)}, bf16[320,768]{1,0:T(8,128)(2,1)S(1)}, u32[]{:S(2)}, u32[]{:S(2)}) collective-permute-start(bf16[320,768]{1,0:T(8,128)(2,1)S(1)} %get-tuple-element.111), channel_id=1, source_target_pairs={{0,1},{1,0},{2,3},{3,2},{4,5},{5,4},{6,7},{7,6},{8,9},{9,8},{10,11... | collective-permute-start | bytes 1474568 | tf_op jit(solution)/shard_map/ppermute | solution.py:43
  271.0 22.4 %collective-permute-start.9 = (bf16[320,768]{1,0:T(8,128)(2,1)S(1)}, bf16[320,768]{1,0:T(8,128)(2,1)S(1)}, u32[]{:S(2)}, u32[]{:S(2)}) collective-permute-start(bf16[320,768]{1,0:T(8,128)(2,1)S(1)} %get-tuple-element.111), channel_id=1, source_target_pairs={{0,2},{1,3},{2,0},{3,1},{4,6},{5,7},{6,4},{7,5},{8,10},{9,11},{10,... | collective-permute-start | bytes 1474568 | tf_op jit(solution)/shard_map/ppermute | solution.py:43
  271.3 21.3 %collective-permute-start.6 = (bf16[320,768]{1,0:T(8,128)(2,1)S(1)}, bf16[320,768]{1,0:T(8,128)(2,1)S(1)}, u32[]{:S(2)}, u32[]{:S(2)}) collective-permute-start(bf16[320,768]{1,0:T(8,128)(2,1)S(1)} %get-tuple-element.112), channel_id=1, source_target_pairs={{0,1},{1,0},{2,3},{3,2},{4,5},{5,4},{6,7},{7,6},{8,9},{9,8},{10,11... | collective-permute-start | bytes 1474568 | tf_op jit(solution)/shard_map/ppermute | solution.py:43
  274.4 30.1 %copy-start.29 = (bf16[96,8,2,384]{3,1,2,0:T(8,128)(2,1)}, bf16[96,8,2,384]{3,1,2,0:T(8,128)(2,1)S(1)}, u32[]{:S(2)}) copy-start(bf16[96,8,2,384]{3,1,2,0:T(8,128)(2,1)S(1)} %copy.154) | copy-start | bytes 3538948
  275.6 33.7 %copy-start.32 = (bf16[96,8,2,384]{3,1,2,0:T(8,128)(2,1)}, bf16[96,8,2,384]{3,1,2,0:T(8,128)(2,1)S(1)}, u32[]{:S(2)}) copy-start(bf16[96,8,2,384]{3,1,2,0:T(8,128)(2,1)S(1)} %copy.153) | copy-start | bytes 3538948
  276.8 17.4 %collective-permute-start.8 = (bf16[320,768]{1,0:T(8,128)(2,1)S(1)}, bf16[320,768]{1,0:T(8,128)(2,1)S(1)}, u32[]{:S(2)}, u32[]{:S(2)}) collective-permute-start(bf16[320,768]{1,0:T(8,128)(2,1)S(1)} %get-tuple-element.112), channel_id=1, source_target_pairs={{0,2},{1,3},{2,0},{3,1},{4,6},{5,7},{6,4},{7,5},{8,10},{9,11},{10,... | collective-permute-start | bytes 1474568 | tf_op jit(solution)/shard_map/ppermute | solution.py:43
  292.6 11.3 %collective-permute-start.10 = (bf16[320,768]{1,0:T(8,128)(2,1)S(1)}, bf16[320,768]{1,0:T(8,128)(2,1)S(1)}, u32[]{:S(2)}, u32[]{:S(2)}) collective-permute-start(bf16[320,768]{1,0:T(8,128)(2,1)S(1)} %collective-permute-done.6), channel_id=1, source_target_pairs={{0,2},{1,3},{2,0},{3,1},{4,6},{5,7},{6,4},{7,5},{8,10},{9,11},{10,... | collective-permute-start | bytes 1474568 | tf_op jit(solution)/shard_map/ppermute | solution.py:43
  293.4 11.1 %collective-permute-start.11 = (bf16[320,768]{1,0:T(8,128)(2,1)S(1)}, bf16[320,768]{1,0:T(8,128)(2,1)S(1)}, u32[]{:S(2)}, u32[]{:S(2)}) collective-permute-start(bf16[320,768]{1,0:T(8,128)(2,1)S(1)} %collective-permute-done.9), channel_id=1, source_target_pairs={{0,1},{1,0},{2,3},{3,2},{4,5},{5,4},{6,7},{7,6},{8,9},{9,8},{10,11... | collective-permute-start | bytes 1474568 | tf_op jit(solution)/shard_map/ppermute | solution.py:43
  314.1 23.7 %copy-start.39 = (bf16[4,2,96,768]{3,2,1,0:T(8,128)(2,1)S(1)}, bf16[4,2,96,768]{3,2,1,0:T(8,128)(2,1)}, u32[]{:S(2)}) copy-start(bf16[4,2,96,768]{3,2,1,0:T(8,128)(2,1)} %copy.131) | copy-start | bytes 3538948
  343.2 101.6 %copy-start.1 = (f32[640,768]{1,0:T(8,128)S(1)}, f32[640,768]{1,0:T(8,128)}, u32[]{:S(2)}) copy-start(f32[640,768]{1,0:T(8,128)} %copy-done) | copy-start | bytes 5898244
  447.8 83.2 %copy-start.18 = (f32[640,768]{1,0:T(8,128)}, f32[640,768]{1,0:T(8,128)S(1)}, u32[]{:S(2)}) copy-start(f32[640,768]{1,0:T(8,128)S(1)} %convert_add_fusion.1) | copy-start | bytes 5898244
  449.8 46.3 %copy-start.33 = (bf16[96,8,2,384]{3,1,2,0:T(8,128)(2,1)S(1)}, bf16[96,8,2,384]{3,1,2,0:T(8,128)(2,1)}, u32[]{:S(2)}) copy-start(bf16[96,8,2,384]{3,1,2,0:T(8,128)(2,1)} %copy-done.32) | copy-start | bytes 3538948
  503.9 10.3 collective-permute-start.19
  508.7 28.9 %collective-permute-start.15 = (bf16[320,768]{1,0:T(8,128)(2,1)}, bf16[320,768]{1,0:T(8,128)(2,1)}, u32[]{:S(2)}, u32[]{:S(2)}) collective-permute-start(bf16[320,768]{1,0:T(8,128)(2,1)} %slice.321), channel_id=1, source_target_pairs={{0,1},{1,0},{2,3},{3,2},{4,5},{5,4},{6,7},{7,6},{8,9},{9,8},{10,11... | collective-permute-start | bytes 1474568 | tf_op jit(solution)/shard_map/ppermute | solution.py:43
  509.8 19.5 %collective-permute-start.16 = (bf16[320,768]{1,0:T(8,128)(2,1)S(1)}, bf16[320,768]{1,0:T(8,128)(2,1)S(1)}, u32[]{:S(2)}, u32[]{:S(2)}) collective-permute-start(bf16[320,768]{1,0:T(8,128)(2,1)S(1)} %get-tuple-element.109), channel_id=1, source_target_pairs={{0,1},{1,0},{2,3},{3,2},{4,5},{5,4},{6,7},{7,6},{8,9},{9,8},{10,11... | collective-permute-start | bytes 1474568 | tf_op jit(solution)/shard_map/ppermute | solution.py:43
  510.9 26.6 %collective-permute-start.18 = (bf16[320,768]{1,0:T(8,128)(2,1)}, bf16[320,768]{1,0:T(8,128)(2,1)}, u32[]{:S(2)}, u32[]{:S(2)}) collective-permute-start(bf16[320,768]{1,0:T(8,128)(2,1)} %slice.325), channel_id=1, source_target_pairs={{0,2},{1,3},{2,0},{3,1},{4,6},{5,7},{6,4},{7,5},{8,10},{9,11},{10,... | collective-permute-start | bytes 1474568 | tf_op jit(solution)/shard_map/ppermute | solution.py:43
  515.0 24.9 %collective-permute-start.20 = (bf16[320,768]{1,0:T(8,128)(2,1)}, bf16[320,768]{1,0:T(8,128)(2,1)}, u32[]{:S(2)}, u32[]{:S(2)}) collective-permute-start(bf16[320,768]{1,0:T(8,128)(2,1)} %add_convert_fusion.9), channel_id=1, source_target_pairs={{0,1},{1,0},{2,3},{3,2},{4,5},{5,4},{6,7},{7,6},{8,9},{9,8},{10,11... | collective-permute-start | bytes 1474568 | tf_op jit(solution)/shard_map/ppermute | solution.py:43
  530.2 9.7 collective-permute-start.17
  533.3 248.9 %reduce-scatter.11.cloned.1.call-start = ((), (), s32[]{:S(2)}) async-start(), calls=%async_computation.10 | async-start | bytes 1327104 | tf_op jit(solution)/shard_map/reduce_scatter | solution.py:607
  544.9 68.5 %copy-start.5 = (f32[640,768]{1,0:T(8,128)S(1)}, f32[640,768]{1,0:T(8,128)}, u32[]{:S(2)}) copy-start(f32[640,768]{1,0:T(8,128)} %copy-done.3) | copy-start | bytes 5898244
  616.3 36.6 %copy-start.20 = (f32[640,768]{1,0:T(8,128)}, f32[640,768]{1,0:T(8,128)S(1)}, u32[]{:S(2)}) copy-start(f32[640,768]{1,0:T(8,128)S(1)} %subtract_add_fusion) | copy-start | bytes 5898244
  618.6 163.6 %reduce-scatter.9.cloned.1.call-start = ((), (), s32[]{:S(2)}) async-start(), calls=%async_computation.9 | async-start | bytes 3981312 | tf_op jit(solution)/shard_map/reduce_scatter | solution.py:607
  652.5 137.5 %reduce-scatter.7.cloned.1.call-start = ((), (), s32[]{:S(2)}) async-start(), calls=%async_computation.8 | async-start | bytes 3981312 | tf_op jit(solution)/shard_map/reduce_scatter | solution.py:607
  656.1 46.9 %copy-start.64 = (bf16[2560,768]{1,0:T(8,128)(2,1)S(1)}, bf16[2560,768]{1,0:T(8,128)(2,1)}, u32[]{:S(2)}) copy-start(bf16[2560,768]{1,0:T(8,128)(2,1)} %constant_dynamic-update-slice_fusion) | copy-start | bytes 11796484
  729.8 140.2 %reduce-scatter.17.cloned.1.call-start = ((), (), s32[]{:S(2)}) async-start(), calls=%async_computation.14 | async-start | bytes 10616832 | tf_op jit(solution)/shard_map/reduce_scatter | solution.py:607
  730.5 228.9 %reduce-scatter.15.cloned.1.call-start = ((), (), s32[]{:S(2)}) async-start(), calls=%async_computation.12 | async-start | bytes 10616832 | tf_op jit(solution)/shard_map/reduce_scatter | solution.py:607
  731.1 26.5 %copy-start.2 = (f32[640,768]{1,0:T(8,128)S(1)}, f32[640,768]{1,0:T(8,128)}, u32[]{:S(2)}) copy-start(f32[640,768]{1,0:T(8,128)} %copy-done) | copy-start | bytes 5898244
  731.1 288.1 %all-reduce.5.cloned.1.call-start = ((), (), s32[]{:S(2)}) async-start(), calls=%async_computation.20 | async-start | bytes 2359296 | tf_op jit(solution)/shard_map/psum | solution.py:720
  733.0 15.0 %collective-permute-start.12 = (bf16[240,768]{1,0:T(8,128)(2,1)S(1)}, bf16[240,768]{1,0:T(8,128)(2,1)S(1)}, u32[]{:S(2)}, u32[]{:S(2)}) collective-permute-start(bf16[240,768]{1,0:T(8,128)(2,1)S(1)} %get-tuple-element.106), channel_id=1, source_target_pairs={{0,4},{4,0},{8,12},{12,8},{1,5},{5,1},{9,13},{13,9},{2,6},{6,2},{1... | collective-permute-start | bytes 1105928 | tf_op jit(solution)/shard_map/ppermute | solution.py:43
  740.6 14.8 %collective-permute-start.13 = (bf16[240,768]{1,0:T(8,128)(2,1)S(1)}, bf16[240,768]{1,0:T(8,128)(2,1)S(1)}, u32[]{:S(2)}, u32[]{:S(2)}) collective-permute-start(bf16[240,768]{1,0:T(8,128)(2,1)S(1)} %get-tuple-element.105), channel_id=1, source_target_pairs={{0,8},{4,12},{8,0},{12,4},{1,9},{5,13},{9,1},{13,5},{2,10},{6,14},... | collective-permute-start | bytes 1105928 | tf_op jit(solution)/shard_map/ppermute | solution.py:43
  740.6 17.1 %collective-permute-start.14 = (bf16[240,768]{1,0:T(8,128)(2,1)S(1)}, bf16[240,768]{1,0:T(8,128)(2,1)S(1)}, u32[]{:S(2)}, u32[]{:S(2)}) collective-permute-start(bf16[240,768]{1,0:T(8,128)(2,1)S(1)} %get-tuple-element.104), channel_id=1, source_target_pairs={{0,12},{4,8},{8,4},{12,0},{1,13},{5,9},{9,5},{13,1},{2,14},{6,10},... | collective-permute-start | bytes 1105928 | tf_op jit(solution)/shard_map/ppermute | solution.py:43
  742.8 17.4 %copy-start.59 = (f32[1,6,768]{2,1,0:T(8,128)}, f32[1,6,768]{2,1,0:T(8,128)S(1)}, u32[]{:S(2)}) copy-start(f32[1,6,768]{2,1,0:T(8,128)S(1)} %maximum_bitcast_fusion.1) | copy-start | bytes 55300
  760.8 33.6 %collective-permute-start.27 = (f32[2,6,768]{2,1,0:T(8,128)}, f32[2,6,768]{2,1,0:T(8,128)}, u32[]{:S(2)}, u32[]{:S(2)}) collective-permute-start(f32[2,6,768]{2,1,0:T(8,128)} %pad_maximum_fusion.6), channel_id=1, source_target_pairs={{0,16},{16,0},{1,17},{17,1},{2,18},{18,2},{3,19},{19,3},{4,20},{20... | collective-permute-start | bytes 110600 | tf_op jit(solution)/shard_map/ppermute | solution.py:43
  790.0 244.8 %all-gather.19.cloned.1.call-start = ((), (), s32[]{:S(2)}) async-start(), calls=%async_computation.15 | async-start | bytes 3538944 | tf_op jit(solution)/shard_map/all_gather | solution.py:625
  795.2 3.3 collective-permute-start.28
  799.4 73.0 %collective-permute-start.29 = (f32[2,6,768]{2,1,0:T(8,128)S(1)}, f32[2,6,768]{2,1,0:T(8,128)S(1)}, u32[]{:S(2)}, u32[]{:S(2)}) collective-permute-start(f32[2,6,768]{2,1,0:T(8,128)S(1)} %fusion.153), channel_id=1, source_target_pairs={{0,2},{1,3},{2,0},{3,1},{4,6},{5,7},{6,4},{7,5},{8,10},{9,11},{10,... | collective-permute-start | bytes 110600 | tf_op jit(solution)/shard_map/ppermute | solution.py:43
  870.0 175.1 %all-gather.17.cloned.1.call-start = ((), (), s32[]{:S(2)}) async-start(), calls=%async_computation.13 | async-start | bytes 3538944 | tf_op jit(solution)/shard_map/all_gather | solution.py:625
  872.4 6.0 collective-permute-start.30
  873.8 11.9 %collective-permute-start.25 = (bf16[320,768]{1,0:T(8,128)(2,1)S(1)}, bf16[320,768]{1,0:T(8,128)(2,1)S(1)}, u32[]{:S(2)}, u32[]{:S(2)}) collective-permute-start(bf16[320,768]{1,0:T(8,128)(2,1)S(1)} %get-tuple-element.108), channel_id=1, source_target_pairs={{0,2},{1,3},{2,0},{3,1},{4,6},{5,7},{6,4},{7,5},{8,10},{9,11},{10,... | collective-permute-start | bytes 1474568 | tf_op jit(solution)/shard_map/ppermute | solution.py:43
  875.7 83.8 %collective-permute-start.21 = (bf16[320,768]{1,0:T(8,128)(2,1)}, bf16[320,768]{1,0:T(8,128)(2,1)}, u32[]{:S(2)}, u32[]{:S(2)}) collective-permute-start(bf16[320,768]{1,0:T(8,128)(2,1)} %slice.329), channel_id=1, source_target_pairs={{0,1},{1,0},{2,3},{3,2},{4,5},{5,4},{6,7},{7,6},{8,9},{9,8},{10,11... | collective-permute-start | bytes 1474568 | tf_op jit(solution)/shard_map/ppermute | solution.py:43
  876.1 21.8 %collective-permute-start.22 = (bf16[320,768]{1,0:T(8,128)(2,1)S(1)}, bf16[320,768]{1,0:T(8,128)(2,1)S(1)}, u32[]{:S(2)}, u32[]{:S(2)}) collective-permute-start(bf16[320,768]{1,0:T(8,128)(2,1)S(1)} %get-tuple-element.107), channel_id=1, source_target_pairs={{0,1},{1,0},{2,3},{3,2},{4,5},{5,4},{6,7},{7,6},{8,9},{9,8},{10,11... | collective-permute-start | bytes 1474568 | tf_op jit(solution)/shard_map/ppermute | solution.py:43
  878.0 81.5 %collective-permute-start.24 = (bf16[320,768]{1,0:T(8,128)(2,1)}, bf16[320,768]{1,0:T(8,128)(2,1)}, u32[]{:S(2)}, u32[]{:S(2)}) collective-permute-start(bf16[320,768]{1,0:T(8,128)(2,1)} %slice.333), channel_id=1, source_target_pairs={{0,2},{1,3},{2,0},{3,1},{4,6},{5,7},{6,4},{7,5},{8,10},{9,11},{10,... | collective-permute-start | bytes 1474568 | tf_op jit(solution)/shard_map/ppermute | solution.py:43
  878.4 4.4 collective-permute-start.31
  881.6 17.7 %copy-start.78 = (bf16[2,768]{1,0:T(2,128)(2,1)S(1)}, bf16[2,768]{1,0:T(2,128)(2,1)}, u32[]{:S(2)}) copy-start(bf16[2,768]{1,0:T(2,128)(2,1)} %param.21) | copy-start | bytes 9220
  881.6 18.3 %copy-start.80 = (bf16[2,768]{1,0:T(2,128)(2,1)S(1)}, bf16[2,768]{1,0:T(2,128)(2,1)}, u32[]{:S(2)}) copy-start(bf16[2,768]{1,0:T(2,128)(2,1)} %param.18) | copy-start | bytes 9220
  886.6 72.9 %collective-permute-start.26 = (bf16[320,768]{1,0:T(8,128)(2,1)}, bf16[320,768]{1,0:T(8,128)(2,1)}, u32[]{:S(2)}, u32[]{:S(2)}) collective-permute-start(bf16[320,768]{1,0:T(8,128)(2,1)} %add_convert_fusion.7), channel_id=1, source_target_pairs={{0,1},{1,0},{2,3},{3,2},{4,5},{5,4},{6,7},{7,6},{8,9},{9,8},{10,11... | collective-permute-start | bytes 1474568 | tf_op jit(solution)/shard_map/ppermute | solution.py:43
  898.8 60.7 %collective-permute-start.23 = (bf16[320,768]{1,0:T(8,128)(2,1)}, bf16[320,768]{1,0:T(8,128)(2,1)}, u32[]{:S(2)}, u32[]{:S(2)}) collective-permute-start(bf16[320,768]{1,0:T(8,128)(2,1)} %add_convert_fusion.8), channel_id=1, source_target_pairs={{0,2},{1,3},{2,0},{3,1},{4,6},{5,7},{6,4},{7,5},{8,10},{9,11},{10,... | collective-permute-start | bytes 1474568 | tf_op jit(solution)/shard_map/ppermute | solution.py:43
  (75 other events, 318.6 us)
Sparse Core Ops, SparseCore 0:
  10.5 30.2 all-gather.12
  42.7 25.7 all-gather.14
  70.9 34.5 all-gather.20
  107.8 34.5 all-gather.24
  144.1 58.8 all-gather.22
  204.7 58.8 all-gather.26
  533.4 49.5 reduce-scatter.12
  618.7 48.6 reduce-scatter.10
  671.4 48.2 reduce-scatter.8
  729.9 60.0 reduce-scatter.6
  793.5 76.4 reduce-scatter.16
  873.4 86.0 reduce-scatter.14
  962.1 57.1 all-reduce.4
  1020.7 10.6 all-gather.18
  1032.8 12.3 all-gather.16

commit v3 on v2

v3 whole, which is shorter than its diff:
```python
from types import SimpleNamespace

import jax
import jax.numpy as jnp
from jax import lax
from jax.experimental import pallas as pl
from jax.experimental.pallas import tpu as pltpu
from jax.sharding import PartitionSpec as P

HEAD_DIM = 64
BLK = 128
TRUNK = 8
PAIR = 2 * HEAD_DIM
EPS = 1e-06
NEG = -1000000000.0
BIG = 1 << 20
F32 = jnp.float32
BF16 = jnp.bfloat16
VMEM_LIMIT = 58 * 1024 * 1024
DP, EXPERT, TENSOR = "dp", "expert", "tensor"

NT = (((1,), (1,)), ((), ()))
TN = (((0,), (0,)), ((), ()))


def dot(a, b):
    return jnp.dot(a, b, preferred_element_type=F32)


def dot_nt(a, b):
    return lax.dot_general(a, b, NT, preferred_element_type=F32)


def dot_tn(a, b):
    return lax.dot_general(a, b, TN, preferred_element_type=F32)


def cost(macs, moved, trans=0):
    return pl.CostEstimate(flops=macs // 64, bytes_accessed=moved // 64, transcendentals=0)


def xperm(x, axis, k):
    n = lax.axis_size(axis)
    return lax.ppermute(x, axis, [(i, i ^ k) for i in range(n)])


def after(x, dep):
    return lax.optimization_barrier((x, dep))[0]


def sum_small(x):
    for axis in (DP, TENSOR, EXPERT):
        n = lax.axis_size(axis)
        k = 1
        while k < n:
            x = x + xperm(x, axis, k)
            k *= 2
    return x


def exchange(chunks):
    n = len(chunks)
    if n == 4:
        return [chunks[0]] + [xperm(chunks[k], EXPERT, k) for k in range(1, n)]
    out = lax.all_to_all(jnp.stack(chunks), EXPERT, split_axis=0, concat_axis=0, tiled=True)
    return [out[k] for k in range(n)]


def masked_pair(x):
    lane = lax.broadcasted_iota(jnp.int32, x.shape, 1)
    zero = jnp.zeros_like(x)
    return jnp.concatenate([jnp.where(lane < HEAD_DIM, x, zero), jnp.where(lane < HEAD_DIM, zero, x)], axis=0)


def attend_kernel(table, q_ref, k_ref, v_ref, out_ref, lse_ref, keys, values):
    pair = pl.program_id(0)
    blocks = k_ref.shape[0] // BLK
    mine = q_ref.shape[0] // BLK
    trunk = TRUNK * BLK
    for b in range(blocks):
        place = pl.ds(pl.multiple_of(table[b] * BLK, BLK), BLK)
        rows = pl.ds(b * BLK, BLK)
        keys[place, :] = k_ref[rows, :]
        values[place, pl.ds(0, PAIR)] = v_ref[rows, :]
    values[:, pl.ds(PAIR, PAIR)] = jnp.ones((blocks * BLK, PAIR), BF16)
    lane = lax.broadcasted_iota(jnp.int32, (BLK, PAIR), 1)
    for i in range(mine):
        at = blocks + 5 * i
        place_q, own, parent, base_own, base_parent = [table[at + j] for j in range(5)]
        rows = pl.ds(i * BLK, BLK)
        own_rows = pl.ds(pl.multiple_of(own * BLK, BLK), BLK)
        parent_rows = pl.ds(pl.multiple_of(parent * BLK, BLK), BLK)
        q = masked_pair(q_ref[rows, :] * jnp.asarray(HEAD_DIM ** -0.5, BF16))
        row = lax.broadcasted_iota(jnp.int32, (2 * BLK, 1), 0) % BLK
        pos_q = place_q + row
        s_trunk = dot_nt(q, keys[pl.ds(0, trunk), :])
        key_pos = lax.broadcasted_iota(jnp.int32, s_trunk.shape, 1)
        s_trunk = jnp.where(key_pos <= pos_q, s_trunk, NEG)
        s_parent = dot_nt(q, keys[parent_rows, :])
        col = lax.broadcasted_iota(jnp.int32, s_parent.shape, 1)
        s_parent = jnp.where(col + base_parent <= pos_q, s_parent, NEG)
        s_own = dot_nt(q, keys[own_rows, :])
        s_own = jnp.where(col + base_own <= pos_q, s_own, NEG)
        top = jnp.maximum(
            jnp.max(s_trunk, axis=1, keepdims=True),
            jnp.max(jnp.maximum(s_parent, s_own), axis=1, keepdims=True),
        )
        p_trunk = jnp.exp(s_trunk - top).astype(BF16)
        p_parent = jnp.exp(s_parent - top).astype(BF16)
        p_own = jnp.exp(s_own - top).astype(BF16)
        both = dot(p_trunk, values[pl.ds(0, trunk), :])
        both = both + dot(p_parent, values[parent_rows, :]) + dot(p_own, values[own_rows, :])
        total = both[:, PAIR:]
        heads = both[:, :PAIR] / total
        lse = top + jnp.log(total)
        out_ref[rows, :] = jnp.where(lane < HEAD_DIM, heads[:BLK], heads[BLK:]).astype(BF16)
        known = jnp.where(pair == 0, 0.0, lse_ref[rows, :])
        known = jnp.where(lane == 2 * pair, lse[:BLK], known)
        lse_ref[rows, :] = jnp.where(lane == 2 * pair + 1, lse[BLK:], known)


def attend(table, q, k, v):
    mine, width = q.shape
    rows = k.shape[0]
    pairs = width // PAIR
    column = lambda n: pl.BlockSpec((n, PAIR), lambda p, table: (0, p))
    return pl.pallas_call(
        attend_kernel,
        grid_spec=pltpu.PrefetchScalarGridSpec(
            num_scalar_prefetch=1,
            grid=(pairs,),
            in_specs=[column(mine), column(rows), column(rows)],
            out_specs=[column(mine), pl.BlockSpec((mine, PAIR), lambda p, table: (0, 0))],
            scratch_shapes=[pltpu.VMEM((rows, PAIR), BF16), pltpu.VMEM((rows, 2 * PAIR), BF16)],
        ),
        out_shape=[jax.ShapeDtypeStruct((mine, width), BF16), jax.ShapeDtypeStruct((mine, PAIR), F32)],
        compiler_params=pltpu.CompilerParams(vmem_limit_bytes=VMEM_LIMIT),
        cost_estimate=cost(mine * 1280 * width * 8, 4 * rows * width, mine * 1280 * width // HEAD_DIM),
        name="attend",
    )(table, q, k, v)


def attend_back_kernel(
    table, q_ref, k_ref, v_ref, do_ref, o_ref, lse_ref, dq_ref, dk_ref, dv_ref,
    keys, values, keys_t, dk_acc, dv_acc, lse_t,
):
    pair = pl.program_id(0)
    blocks = k_ref.shape[0] // BLK
    mine = q_ref.shape[0] // BLK
    trunk = TRUNK * BLK
    for b in range(blocks):
        place = pl.ds(pl.multiple_of(table[b] * BLK, BLK), BLK)
        rows = pl.ds(b * BLK, BLK)
        keys[place, :] = k_ref[rows, :]
        values[place, :] = v_ref[rows, :]
        keys_t[:, place] = k_ref[rows, :].T
    dk_acc[...] = jnp.zeros_like(dk_acc)
    dv_acc[...] = jnp.zeros_like(dv_acc)

    @pl.when(pair == 0)
    def _():
        for i in range(mine):
            turned = lse_ref[pl.ds(i * BLK, BLK), :].T
            for p in range(lse_t.shape[0]):
                lse_t[p, pl.ds(0, 2), pl.ds(i * BLK, BLK)] = turned[2 * p : 2 * p + 2]

    lane = lax.broadcasted_iota(jnp.int32, (BLK, PAIR), 1)
    scale = jnp.asarray(HEAD_DIM ** -0.5, BF16)
    for i in range(mine):
        at = blocks + 5 * i
        place_q, own, parent, base_own, base_parent = [table[at + j] for j in range(5)]
        rows = pl.ds(i * BLK, BLK)
        q = masked_pair(q_ref[rows, :] * scale)
        do = do_ref[rows, :]
        product = (do.astype(F32) * o_ref[rows, :].astype(F32)).T
        inner = jnp.concatenate(
            [
                jnp.sum(product[:HEAD_DIM], axis=0, keepdims=True),
                jnp.sum(product[HEAD_DIM:], axis=0, keepdims=True),
            ],
            axis=1,
        )
        do = masked_pair(do)
        lse = jnp.concatenate([lse_t[pair, pl.ds(0, 1), rows], lse_t[pair, pl.ds(1, 1), rows]], axis=1)
        pos_q = place_q + lax.broadcasted_iota(jnp.int32, (1, 2 * BLK), 1) % BLK
        dq_t = jnp.zeros((PAIR, 2 * BLK), F32)
        steps = [(j * 2 * BLK, 2 * BLK, j * 2 * BLK) for j in range(TRUNK // 2)]
        steps += [(pl.multiple_of(parent * BLK, BLK), BLK, base_parent)]
        steps += [(pl.multiple_of(own * BLK, BLK), BLK, base_own)]
        for start, size, base in steps:
            here = pl.ds(start, size)
            k_rows, v_rows = keys[here, :], values[here, :]
            scores = dot_nt(k_rows, q)
            key_pos = base + lax.broadcasted_iota(jnp.int32, (size, 1), 0)
            weights = jnp.exp(jnp.where(key_pos <= pos_q, scores - lse, NEG))
            d_weights = dot_nt(v_rows, do)
            d_scores = (weights * (d_weights - inner)).astype(BF16)
            dv_acc[here, :] += dot(weights.astype(BF16), do)
            dk_acc[here, :] += dot(d_scores, q)
            dq_t = dq_t + dot(keys_t[:, here], d_scores)
        dq = dq_t.T * (HEAD_DIM ** -0.5)
        dq_ref[rows, :] = jnp.where(lane < HEAD_DIM, dq[:BLK], dq[BLK:]).astype(BF16)
    for b in range(blocks):
        place = pl.ds(pl.multiple_of(table[b] * BLK, BLK), BLK)
        rows = pl.ds(b * BLK, BLK)
        dk_ref[rows, :] = dk_acc[place, :].astype(BF16)
        dv_ref[rows, :] = dv_acc[place, :].astype(BF16)


def attend_back(table, q, k, v, d_heads, heads, lse):
    mine, width = q.shape
    rows = k.shape[0]
    pairs = width // PAIR
    column = lambda n: pl.BlockSpec((n, PAIR), lambda p, table: (0, p))
    return pl.pallas_call(
        attend_back_kernel,
        grid_spec=pltpu.PrefetchScalarGridSpec(
            num_scalar_prefetch=1,
            grid=(pairs,),
            in_specs=[
                column(mine), column(rows), column(rows), column(mine), column(mine),
                pl.BlockSpec((mine, PAIR), lambda p, table: (0, 0)),
            ],
            out_specs=[column(mine), column(rows), column(rows)],
            scratch_shapes=[
                pltpu.VMEM((rows, PAIR), BF16),
                pltpu.VMEM((rows, PAIR), BF16),
                pltpu.VMEM((PAIR, rows), BF16),
                pltpu.VMEM((rows, PAIR), F32),
                pltpu.VMEM((rows, PAIR), F32),
                pltpu.VMEM((pairs, 8, mine), F32),
            ],
        ),
        out_shape=[
            jax.ShapeDtypeStruct((mine, width), BF16),
            jax.ShapeDtypeStruct((rows, width), BF16),
            jax.ShapeDtypeStruct((rows, width), BF16),
        ],
        compiler_params=pltpu.CompilerParams(vmem_limit_bytes=VMEM_LIMIT),
        cost_estimate=cost(mine * 1280 * width * 20, 8 * rows * width, mine * 1280 * width // HEAD_DIM),
        name="attend_back",
    )(table, q, k, v, d_heads, heads, lse)


GELU_C = 0.7978845608028654
GELU_A = 0.044715
CUTS = 4
MESH = pl.DeviceIdType.MESH
ANY = pl.BlockSpec(memory_space=pl.ANY)
VMEM = pl.BlockSpec(memory_space=pltpu.VMEM)


def low_shape(*dims):
    return jax.ShapeDtypeStruct(dims, BF16)


def low_vmem(*dims):
    return pltpu.VMEM(dims, BF16)


def run_kernel(body, ins, outs, scratch, identity, macs, near, far, **flags):
    scratch = dict(scratch, near=pltpu.SemaphoreType.DMA((near,)))
    params = dict(vmem_limit_bytes=VMEM_LIMIT)
    if far:
        scratch.update(send=pltpu.SemaphoreType.DMA((far,)), recv=pltpu.SemaphoreType.DMA((far,)))
        params.update(collective_id=identity, has_side_effects=True)
    names = [*ins, *outs, *scratch]

    def kernel(*refs):
        body(Moves(SimpleNamespace(**dict(zip(names, refs)))), **flags)

    results = pl.pallas_call(
        kernel,
        in_specs=[spec for _, spec in ins.values()],
        out_specs=[spec for _, spec in outs.values()],
        out_shape=[shape for shape, _ in outs.values()],
        scratch_shapes=list(scratch.values()),
        compiler_params=pltpu.CompilerParams(**params),
        cost_estimate=cost(macs, 0),
        name=body.__name__,
    )(*[value for value, _ in ins.values()])
    return SimpleNamespace(**dict(zip(outs, results)))


def xor_peer(index, k):
    if k == 1:
        return index + 1 - 2 * lax.rem(index, 2)
    if k == 2:
        return index + 2 - 4 * lax.rem(lax.div(index, 2), 2)
    return index + 3 - 2 * lax.rem(index, 4)


class Moves:
    def __init__(self, refs):
        self.refs, self.near, self.far, self.seen, self.left, self.sent = refs, 0, 0, set(), set(), []
        self.c, self.t, self.z = [lax.axis_index(axis) for axis in (DP, TENSOR, EXPERT)]
        self.x_peer, self.y_peer = [{TENSOR: xor_peer(self.t, k)} for k in (1, 2)]
        self.sibling = {DP: 1 - self.c}
        self.z_peers = [{EXPERT: xor_peer(self.z, k)} for k in (1, 2, 3)]

    def local(self, src, dst):
        copy = pltpu.make_async_copy(src, dst, self.refs.near.at[self.near])
        self.near += 1
        copy.start()
        return copy

    def remote(self, src, dst, device):
        copy = pltpu.make_async_remote_copy(
            src_ref=src, dst_ref=dst, send_sem=self.refs.send.at[self.far], recv_sem=self.refs.recv.at[self.far],
            device_id=device, device_id_type=MESH,
        )
        self.far += 1
        copy.start()
        self.sent.append(copy)
        return copy

    def need(self, *copies):
        for copy in copies:
            if id(copy) not in self.seen:
                self.seen.add(id(copy))
                copy.wait()

    def arrived(self, *copies):
        for copy in copies:
            if id(copy) not in self.seen:
                self.seen.add(id(copy))
                copy.wait_recv()

    def finish(self):
        self.gone(*self.sent)

    def gone(self, *copies):
        for copy in copies:
            if id(copy) not in self.left:
                self.left.add(id(copy))
                copy.wait_send()

    def greet(self, devices):
        barrier = pltpu.get_barrier_semaphore()
        for device in devices:
            pl.semaphore_signal(barrier, inc=1, device_id=device, device_id_type=MESH)
        return lambda: pl.semaphore_wait(barrier, len(devices))


def add_low(ref, *more):
    total = ref[...].astype(F32)
    for other in more:
        total = total + other[...].astype(F32)
    return total


class Scatter:
    def __init__(self, moves, pack, core_in, g_in, piece):
        self.moves, self.pack, self.core_in, self.g_in, self.piece = moves, pack, core_in, g_in, piece
        self.peers = core_in.shape[0]
        self.size = pack.shape[1] // 2
        c, t = moves.c, moves.t
        self.index = [t] + [xor_peer(t, k) for k in (1, 2, 3)]
        self.slots = [c * self.peers + i for i in self.index]
        self.flow = [dict(), dict()]

    def rows(self, h):
        return pl.ds(h * self.size, self.size)

    def sides(self, h):
        half = self.size // 2
        return pl.ds(h * self.size, half), pl.ds(h * self.size + half, half)

    def swap(self, h):
        m = self.moves
        there = pl.ds((1 - m.c) * self.peers, self.peers)
        self.flow[h][0] = m.remote(self.pack.at[there, self.rows(h)], self.core_in.at[:, self.rows(h)], m.sibling)

    def out(self, h):
        m, pack, slots, f = self.moves, self.pack, self.slots, self.flow[h]
        left, right = self.sides(h)
        m.arrived(f[0])
        for j in (3, 1, 2, 0):
            pack[slots[j], self.rows(h), :] = add_low(
                pack.at[slots[j], self.rows(h)], self.core_in.at[self.index[j], self.rows(h)]
            ).astype(BF16)
        f[1] = m.remote(pack.at[slots[3], left], self.g_in.at[h, 0], m.x_peer)
        f[2] = m.remote(pack.at[slots[3], right], self.g_in.at[h, 1], m.y_peer)
        f[3] = m.remote(pack.at[slots[1], left], self.g_in.at[h, 2], m.x_peer)
        f[4] = m.remote(pack.at[slots[2], right], self.g_in.at[h, 3], m.y_peer)

    def turn(self, h):
        m, pack, slots, f = self.moves, self.pack, self.slots, self.flow[h]
        left, right = self.sides(h)
        m.arrived(f[1])
        pack[slots[2], left, :] = add_low(pack.at[slots[2], left], self.g_in.at[h, 0]).astype(BF16)
        f[5] = m.remote(pack.at[slots[2], left], self.g_in.at[h, 4], m.y_peer)
        m.arrived(f[2])
        pack[slots[1], right, :] = add_low(pack.at[slots[1], right], self.g_in.at[h, 1]).astype(BF16)
        f[6] = m.remote(pack.at[slots[1], right], self.g_in.at[h, 5], m.x_peer)

    def end(self, h):
        f = self.flow[h]
        self.moves.arrived(f[3], f[4], f[5], f[6])
        for cut, a, b in zip(self.sides(h), (2, 3), (4, 5)):
            total = add_low(self.pack.at[self.slots[0], cut], self.g_in.at[h, a], self.g_in.at[h, b])
            self.piece[cut, :] = total.astype(BF16)


class Gather:
    def __init__(self, moves, pack):
        self.moves, self.pack = moves, pack
        self.half = pack.shape[1] // 2
        self.slots = [moves.c * (pack.shape[0] // 2) + i for i in [moves.t] + [xor_peer(moves.t, k) for k in (1, 2, 3)]]

    def out(self):
        own = self.pack.at[self.slots[0]]
        self.first = [self.moves.remote(own, own, device) for device in (self.moves.x_peer, self.moves.y_peer)]

    def turn(self):
        m = self.moves
        self.swaps, self.second = [], []
        for k, device in ((1, m.y_peer), (2, m.x_peer)):
            m.arrived(self.first[k - 1])
            piece = self.pack.at[self.slots[k], pl.ds((k - 1) * self.half, self.half)]
            self.second.append(m.remote(piece, piece, device))
            self.swap(k)

    def swap(self, k):
        whole = self.pack.at[self.slots[k]]
        self.swaps.append(self.moves.remote(whole, whole, self.moves.sibling))

    def end(self):
        self.moves.arrived(*self.second)
        self.swap(3)
        self.moves.arrived(*self.swaps)


def scatter_scratch(peers, half, width):
    return dict(
        pack_s=low_vmem(2 * peers, half, width), core_in=low_vmem(peers, half, width),
        g_in=low_vmem(2, 6, half // 4, width), piece=low_vmem(half, width),
    )


def one_hot(slot_row, k, size):
    index = lax.broadcasted_iota(jnp.int32, (size, slot_row.shape[1]), 0) + k * size
    return jnp.where(index == slot_row[...], 1.0, 0.0).astype(BF16)


def one_hot_turned(slot_col, k, size):
    index = lax.broadcasted_iota(jnp.int32, (slot_col.shape[0], size), 1) + k * size
    return jnp.where(index == slot_col[...], 1.0, 0.0).astype(BF16)


def combine(m, slot_col, source, copies, back, size):
    total = dot(one_hot_turned(slot_col, 0, size), source[pl.ds(0, size), :])
    for k in (1, 2, 3):
        m.arrived(copies[k])
        total = total + dot(one_hot_turned(slot_col, k, size), back[k - 1])
    return total.astype(BF16)


def expert_part(m, forward, backward, remote, hosted, reduces, fetches, experts):
    r = m.refs
    up, down, hidden, slope, rows, outs = r.up, r.down, r.hidden_s, r.slope_s, r.rows_s, r.outs_s
    count, width = rows.shape
    inner = up.shape[1]
    half = width // 2
    peers = inner // width
    size = count // CUTS
    tile = 256
    cuts = [pl.ds(k * size, size) for k in range(CUTS)]
    met = []
    if remote:
        met += m.z_peers
    if hosted or reduces:
        met += [m.x_peer, m.y_peer]
    if remote:
        met += [m.sibling]
    ready = m.greet(met) if met else None

    def up_at(c, t, start=0, rows=half):
        return up.at[pl.ds(pl.multiple_of(c * half + start, half // 2), rows), pl.ds(pl.multiple_of(t * width, width), width)]

    def down_at(c, t, start=0, rows=half):
        return down.at[pl.ds(pl.multiple_of(t * width + c * half + start, half // 2), rows)]

    loads, weight_loads = [], []
    if not remote:
        if forward:
            loads.append(m.local(r.x, rows))
        if backward:
            loads.append(m.local(r.g, r.d_s))
    if hosted:
        weight_loads.append(m.local(r.own_up, up.at[:, pl.ds(pl.multiple_of(m.t * width, width), width)]))
        weight_loads.append(m.local(r.own_down, down.at[pl.ds(pl.multiple_of(m.t * width, width), width)]))
    else:
        for t in range(peers):
            for c in range(2):
                weight_loads += [m.local(r.w.at[c, t, 0], up_at(c, t)), m.local(r.w.at[c, t, 1], down_at(c, t))]
    if backward and not forward:
        loads += [m.local(a, b) for a, b in ((r.rows, rows), (r.out, outs), (r.slope, slope), (r.hidden, hidden))]
    if ready:
        ready()

    def dispatch(source, target, stage):
        copies = {}
        x = source[...]
        for k in (2, 1, 3):
            stage[k - 1] = dot(one_hot(r.slot_row, k, size), x).astype(BF16)
            copies[k] = m.remote(stage.at[k - 1], target.at[cuts[k]], m.z_peers[k - 1])
        target[cuts[0], :] = dot(one_hot(r.slot_row, 0, size), x).astype(BF16)
        return copies

    def give_back(source, k):
        return m.remote(source.at[cuts[k]], r.back.at[k - 1], m.z_peers[k - 1])

    def forward_block(cut, at):
        u = dot(rows[cut, :], up[:, at])
        square = u * u
        gate = 0.5 + 0.5 * jnp.tanh(u * (GELU_C + (GELU_C * GELU_A) * square))
        value = u * gate
        hidden[cut, at] = value.astype(BF16)
        grow = gate + value * (1.0 - gate) * (2 * GELU_C + (6 * GELU_C * GELU_A) * square)
        slope[cut, at] = grow.astype(BF16)

    def forward_peer(cut, t):
        for col in range(0, width, tile):
            forward_block(cut, pl.ds(pl.multiple_of(t * width + col, tile), tile))

    def forward_down(cut):
        outs[cut, :] = dot(hidden[cut, :], down[...]).astype(BF16)

    def backward_chunk(cut):
        d = r.d_s[cut, :]
        for col in range(0, inner, tile):
            at = pl.ds(col, tile)
            d_hidden = dot_nt(d, down[at, :])
            slope[cut, at] = (d_hidden * slope[cut, at].astype(F32)).astype(BF16)
        x = rows[cut, :]
        logits = dot(x, r.route[...])
        lane = lax.broadcasted_iota(jnp.int32, logits.shape, 1)
        logits = jnp.where(lane < experts, logits, NEG)
        router = jnp.exp(logits - jnp.max(logits, axis=1, keepdims=True))
        router = router / jnp.sum(router, axis=1, keepdims=True)
        amount = jnp.sum(outs[cut, :].astype(F32) * d.astype(F32), axis=1, keepdims=True)
        d_log = (amount * (jnp.where(lane == m.z, 1.0, 0.0) - router)).astype(BF16)
        r.log_s[cut, :] = d_log
        d_rows = dot_nt(slope[cut, :], up[...]) + dot_nt(d_log, r.route[...])
        r.back_s[cut, :] = d_rows.astype(BF16)
        return jnp.sum(d_rows * x.astype(F32), axis=0, keepdims=True)

    sent_x = sent_d = None
    saves, returns = [], {}
    scatter = None
    if fetches:
        next_loads = [m.local(r.next_own.at[pl.ds(c * half, half)], r.next_s.at[c * peers + m.t]) for c in range(2)]
        fetch = Gather(m, r.next_s)
    if hosted:
        first = {}
        for k, device in ((1, m.x_peer), (2, m.y_peer)):
            mine = pl.ds(pl.multiple_of(m.c * half, half), half)
            first[k] = [m.remote(r.own_up.at[mine], up_at(m.c, m.t), device), m.remote(r.own_down.at[mine], down_at(m.c, m.t), device)]
    if reduces:
        scatter = Scatter(m, r.pack_s, r.core_in, r.g_in, r.piece)
        pack_load = m.local(r.pack, r.pack_s)
    if remote and forward:
        sent_x = dispatch(r.x, rows, r.stage_x)
    if remote and backward:
        sent_d = dispatch(r.g, r.d_s, r.stage_d)
    if reduces:
        m.need(pack_load)
        scatter.swap(0)
        scatter.swap(1)
    m.need(*loads, *weight_loads)
    if hosted:
        tens = [m.t] + [xor_peer(m.t, k) for k in (1, 2, 3)]
        onward, swaps = [], {}

        def pass_on(k, device, start):
            m.arrived(*first[k])
            for at in (up_at, down_at):
                piece = at(m.c, tens[k], start, half // 2)
                onward.append(m.remote(piece, piece, device))
            swap(k)

        def swap(k):
            swaps[k] = [m.remote(at(m.c, tens[k]), at(m.c, tens[k]), m.sibling) for at in (up_at, down_at)]

        forward_peer(cuts[0], tens[0])
        m.arrived(sent_x[1])
        forward_peer(cuts[1], tens[0])
        pass_on(1, m.y_peer, 0)
        pass_on(2, m.x_peer, half // 2)
        if fetches:
            m.need(*next_loads)
            fetch.out()
        m.arrived(sent_x[2])
        forward_peer(cuts[2], tens[0])
        m.arrived(sent_x[3])
        forward_peer(cuts[3], tens[0])
        for k in (1, 2, 3):
            if k == 3:
                m.arrived(*onward)
                swap(3)
            m.arrived(*swaps[k])
            for cut in cuts:
                forward_peer(cut, tens[k])
        if fetches:
            fetch.turn()
        for k in (2, 3, 1, 0):
            forward_down(cuts[k])
            if k and not backward:
                returns[k] = give_back(outs, k)
        if not backward:
            for c in range(2):
                for t in range(peers):
                    saves += [m.local(up_at(c, t), r.w.at[c, t, 0]), m.local(down_at(c, t), r.w.at[c, t, 1])]
        if fetches:
            fetch.end()
            saves.append(m.local(r.next_s, r.next_all))
    elif forward:
        for k in range(CUTS):
            if remote and k:
                m.arrived(sent_x[k])
            for t in range(peers):
                forward_peer(cuts[k], t)
            forward_down(cuts[k])
            if remote and k and not backward:
                returns[k] = give_back(outs, k)
    if forward:
        if not backward:
            saves += [m.local(hidden, r.hidden), m.local(slope, r.slope), m.local(rows, r.rows)]
        saves.append(m.local(outs, r.out))
    if backward:
        gain = jnp.zeros((1, width), F32)
        for k in range(CUTS):
            if remote and k:
                m.arrived(sent_d[k])
            gain = gain + backward_chunk(cuts[k])
            if remote and k:
                returns[k] = give_back(r.back_s, k)
            if reduces and k < 2:
                for h in range(2):
                    (scatter.out, scatter.turn)[k](h)
        if not remote:
            saves.append(m.local(r.back_s, r.result))
        if reduces:
            for h in range(2):
                scatter.end(h)
            saves.append(m.local(r.piece, r.summed))
        r.turned[...] = rows[...].T
        route = dot_tn(r.log_s[...], rows[...])
        pad = r.small.shape[0] - experts - 1
        r.small[...] = jnp.concatenate([route[:experts], gain, jnp.zeros((pad, width), F32)], axis=0)
        swapped = []
        if hosted:
            m.gone(*onward, *[copy for k in (1, 2, 3) for copy in swaps[k]])
        for t in range(peers):
            at = pl.ds(t * width, width)
            up[:, at] = dot(r.turned[...], slope[:, at]).astype(BF16)
            down[at, :] = dot_tn(hidden[:, at], r.d_s[...]).astype(BF16)
            if remote:
                swapped.append([m.remote(at(1 - m.c, t), r.grads_in.at[t, i], m.sibling) for i, at in enumerate((up_at, down_at))])
            else:
                for c in range(2):
                    saves += [m.local(up_at(c, t), r.grads.at[c, t, 0]), m.local(down_at(c, t), r.grads.at[c, t, 1])]
    if remote:
        if backward:
            for t in range(peers):
                for i, at in enumerate((up_at, down_at)):
                    m.arrived(swapped[t][i])
                    here = at(m.c, t)
                    here[...] = add_low(here, r.grads_in.at[t, i]).astype(BF16)
                    saves.append(m.local(here, r.grads.at[t, i]))
        r.result[...] = combine(m, r.slot_col, r.back_s if backward else outs, returns, r.back, size)
    m.finish()
    m.need(*saves)


def expert_call(plan, experts, count, w=None, own=None, x=None, g=None, kept=None, route=None, pack=None, fetch=None):
    slots = plan[0]
    forward, backward, remote, hosted, reduces = x is not None, g is not None, experts == CUTS, own is not None, pack is not None
    tokens, width = (x if forward else g).shape
    peers = lax.axis_size(TENSOR)
    half, inner = width // 2, peers * width
    w_shape = low_shape(2, peers, 2, half, width)
    data = VMEM if remote else ANY
    rows_shape, inner_shape = low_shape(count, width), low_shape(count, inner)
    ins, outs = {}, {}
    if hosted:
        ins.update(own_up=(own[0], ANY), own_down=(own[1], ANY))
        if not backward:
            outs.update(w=(w_shape, ANY))
    else:
        ins.update(w=(w, ANY))
    if remote:
        ins.update(slot_row=(slots[None, :], VMEM), slot_col=(slots[:, None], VMEM))
    if forward:
        ins.update(x=(x, data))
    if backward:
        ins.update(g=(g, data), route=(route, VMEM))
        if not forward:
            ins.update(rows=(kept.rows, ANY), out=(kept.out, ANY), hidden=(kept.hidden, ANY), slope=(kept.slope, ANY))
    if remote or backward:
        outs.update(result=(low_shape(tokens if remote else count, width), data))
    if forward:
        outs.update(out=(rows_shape, ANY))
        if not backward:
            outs.update(rows=(rows_shape, ANY), hidden=(inner_shape, ANY), slope=(inner_shape, ANY))
    if backward:
        outs.update(grads=(low_shape(peers, 2, half, width) if remote else w_shape, ANY), small=(jax.ShapeDtypeStruct((-(-(experts + 1) // 8) * 8, width), F32), VMEM))
    scratch = dict(
        up=low_vmem(width, inner), down=low_vmem(inner, width), hidden_s=low_vmem(count, inner), slope_s=low_vmem(count, inner),
        rows_s=low_vmem(count, width), outs_s=low_vmem(count, width),
    )
    if backward:
        scratch.update(
            d_s=low_vmem(count, width), back_s=low_vmem(count, width), log_s=low_vmem(count, BLK), turned=low_vmem(width, count)
        )
    if backward and remote:
        scratch.update(grads_in=low_vmem(peers, 2, half, width))
    if fetch is not None:
        ins.update(next_own=(fetch, ANY))
        outs.update(next_all=(low_shape(2 * peers, half, width), ANY))
        scratch.update(next_s=low_vmem(2 * peers, half, width))
    if reduces:
        ins.update(pack=(pack, ANY))
        outs.update(summed=(low_shape(half, width), ANY))
        scratch.update(scatter_scratch(peers, half, width))
    if remote:
        part = low_vmem(3, count // CUTS, width)
        scratch.update(back=part)
        if forward:
            scratch.update(stage_x=part)
        if backward:
            scratch.update(stage_d=part)
    return run_kernel(
        expert_part, ins, outs, scratch, forward + 2 * backward, count * width * inner, 48, 48 if remote else 0,
        forward=forward, backward=backward, remote=remote, hosted=hosted, reduces=reduces,
        fetches=fetch is not None, experts=experts,
    )


def experts_forward(plan, token_rows, experts, capacity, w, own, fetch):
    count = experts * capacity
    if experts == CUTS:
        got = expert_call(plan, experts, count, own=own, x=token_rows, fetch=fetch)
        return got.result, got
    got = expert_call(plan, experts, count, w=w, x=send_rows(plan[1], token_rows, experts, capacity))
    got.w = w
    return return_rows(plan[1], got.out, experts, capacity).astype(BF16), got


def experts_backward(plan, d_low, kept, route, experts, capacity, pack):
    count = experts * capacity
    if experts == CUTS:
        return expert_call(plan, experts, count, w=kept.w, g=d_low, kept=kept, route=route, pack=pack)
    d_sent = send_rows(plan[1], d_low, experts, capacity)
    got = expert_call(plan, experts, count, w=kept.w, g=d_sent, kept=kept, route=route)
    got.result = return_rows(plan[1], got.result, experts, capacity).astype(BF16)
    got.summed = scatter_all(pack)
    return got


def experts_both(w, own, plan, token_rows, d_low, route, experts, capacity):
    count = experts * capacity
    if experts == CUTS:
        return expert_call(plan, experts, count, own=own, x=token_rows, g=d_low, route=route)
    rows = send_rows(plan[1], token_rows, experts, capacity)
    d_sent = send_rows(plan[1], d_low, experts, capacity)
    got = expert_call(plan, experts, count, w=w, x=rows, g=d_sent, route=route)
    got.result = return_rows(plan[1], got.result, experts, capacity).astype(BF16)
    return got


def project_part(m, hosted):
    r = m.refs
    rows, w = r.n_s, r.w_s
    tokens = r.x.shape[0]
    peers = rows.shape[0] // tokens
    shard = w.shape[1] // peers
    c, t = m.c, m.t
    ready = m.greet([m.x_peer, m.y_peer] + ([m.sibling] if hosted else []))
    at = lambda index: pl.ds(pl.multiple_of(index * shard, shard), shard)
    first_load = m.local(r.x, rows.at[pl.ds(0, tokens)])
    loads = []
    if hosted:
        for i in range(4):
            loads.append(m.local(r.w.at[pl.ds(i * shard, shard)], w.at[i, at(t)]))
    else:
        for i in range(4):
            for j in range(peers):
                piece = r.w.at[i // 2, j, r.w.shape[2] - 1, pl.ds(i % 2 * shard, shard)]
                loads.append(m.local(piece, w.at[i, pl.ds(j * shard, shard)]))
    ready()
    half = tokens // 2
    m.need(first_load)
    cut = lambda j, part: pl.ds(j * tokens + part * half, half)

    def send(j, part, to, device):
        return m.remote(rows.at[cut(j, part)], rows.at[cut(to, part)], device)

    first, second, swaps, kept = {}, [], [], []
    if hosted:
        m.need(*loads)
        for h in range(2):
            mine = w.at[2 * c + h, at(t)]
            first[1, h] = m.remote(mine, mine, m.x_peer)
            first[2, h] = m.remote(mine, mine, m.y_peer)
    a_low, b_high = send(0, 0, 1, m.x_peer), send(0, 1, 2, m.y_peer)
    a_high, b_low = send(0, 1, 1, m.x_peer), send(0, 0, 2, m.y_peer)
    if hosted:
        for h in range(2):
            for k, onward, part in ((1, m.y_peer, 0), (2, m.x_peer, 1)):
                m.arrived(first[k, h])
                start = pl.multiple_of(xor_peer(t, k) * shard + part * (shard // 2), shard // 2)
                piece = w.at[2 * c + h, pl.ds(start, shard // 2)]
                second.append(m.remote(piece, piece, onward))
                whole = w.at[2 * c + h, at(xor_peer(t, k))]
                swaps.append(m.remote(whole, whole, m.sibling))
    m.arrived(a_low)
    c_low = send(1, 0, 3, m.y_peer)
    m.arrived(b_high)
    c_high = send(2, 1, 3, m.x_peer)
    if hosted:
        m.arrived(*second)
        for h in range(2):
            whole = w.at[2 * c + h, at(xor_peer(t, 3))]
            swaps.append(m.remote(whole, whole, m.sibling))
        m.arrived(*swaps)
    else:
        m.need(*loads)
    for i in range(4):
        kept.append(m.local(w.at[i], r.w_all.at[i]))

    def keys_values(start, size):
        here = pl.ds(start, size)
        x = rows[here, :]
        for i, near, far in ((1, r.k_s, r.k), (2, r.v_s, r.v)):
            near[here, :] = dot_nt(x, w[i]).astype(BF16)
            kept.append(m.local(near.at[here], far.at[here]))

    r.q_s[...] = dot_nt(rows[pl.ds(0, tokens), :], w[0]).astype(BF16)
    kept.append(m.local(r.q_s, r.q))
    keys_values(0, tokens)
    m.arrived(a_high)
    keys_values(tokens, tokens)
    m.arrived(b_low)
    keys_values(2 * tokens, tokens)
    m.arrived(c_low)
    keys_values(3 * tokens, half)
    m.arrived(c_high)
    keys_values(3 * tokens + half, half)
    kept.append(m.local(rows, r.n))
    m.finish()
    m.need(*kept)


def project(x, w, hosted, peers):
    tokens, width = x.shape
    every = peers * tokens
    outs = dict(
        q=(low_shape(tokens, width), ANY), k=(low_shape(every, width), ANY), v=(low_shape(every, width), ANY),
        n=(low_shape(every, width), ANY), w_all=(low_shape(4, width, width), ANY),
    )
    scratch = dict(
        n_s=low_vmem(every, width), w_s=low_vmem(4, width, width), q_s=low_vmem(tokens, width),
        k_s=low_vmem(every, width), v_s=low_vmem(every, width),
    )
    return run_kernel(
        project_part, dict(x=(x, ANY), w=(w, ANY)), outs, scratch, 6 + hosted, 9 * tokens * width * width, 40, 24, hosted=hosted
    )


def project_back_part(m, full, returns):
    r = m.refs
    tokens, width = r.dq_s.shape
    peers = r.dk_s.shape[0] // tokens
    shard = width // peers
    c, z = m.c, m.z
    local, remote, need, arrived = m.local, m.remote, m.need, m.arrived
    ready = m.greet([m.x_peer, m.y_peer] + ([m.sibling] if full else []) + (m.z_peers if full or returns else []))
    rows_of = lambda j: pl.ds(j * tokens, tokens)
    w = r.w_s
    weights_in = {i: local(r.w.at[i], w.at[i]) for i in (1, 2)}
    parts_in = {}
    for j in (3, 1, 2, 0):
        parts_in[j] = [local(a.at[rows_of(j)], b.at[rows_of(j)]) for a, b in ((r.dk, r.dk_s), (r.dv, r.dv_s))]
    above_in = local(r.above, r.above_s) if full else None
    rest_in = [local(a, b) for a, b in ((r.n, r.n_s), (r.dq, r.dq_s), (r.heads, r.heads_s), (r.d_att, r.d_att_s))]
    weights_in[0] = local(r.w.at[0], w.at[0])
    swaps_in = [local(e, r.e_s.at[l, c]) for l, e in enumerate((r.e0, r.e1))] if full else []
    ready()
    tops, ends = pl.ds(0, tokens // 2), pl.ds(tokens // 2, tokens // 2)

    def partial(j):
        at = rows_of(j)
        return dot(r.dk_s[at, :], w[1]) + dot(r.dv_s[at, :], w[2])

    over_x, over_y = {}, {}

    def rows_out(which):
        need(weights_in[1], weights_in[2])
        for j in which:
            stage = {1: r.p1, 2: r.p2, 3: r.p3}[j]
            need(*parts_in[j])
            stage[...] = partial(j).astype(BF16)
            if j != 2:
                over_x[j] = remote(stage.at[tops], r.row_in.at[j // 2], m.x_peer)
            if j != 1:
                over_y[j] = remote(stage.at[ends], r.row_in.at[2 + j // 3], m.y_peer)

    def rows_turn():
        arrived(over_x[3])
        r.p2[tops, :] = add_low(r.p2.at[tops], r.row_in.at[1]).astype(BF16)
        over_y[1] = remote(r.p2.at[tops], r.row_in.at[4], m.y_peer)
        arrived(over_y[3])
        r.p1[ends, :] = add_low(r.p1.at[ends], r.row_in.at[3]).astype(BF16)
        over_x[2] = remote(r.p1.at[ends], r.row_in.at[5], m.x_peer)

    def rows_own():
        need(*parts_in[0], weights_in[0], rest_in[1])
        r.dn[...] = partial(0) + dot(r.dq_s[...], w[0])

    def rows_end():
        for copy, slot, cut in ((over_x[1], 0, tops), (over_y[2], 2, ends), (over_y[1], 4, tops), (over_x[2], 5, ends)):
            arrived(copy)
            r.dn[cut, :] += r.row_in[slot].astype(F32)

    pack = r.pack_s
    part = lambda i: pl.ds(i % 2 * shard, shard)

    def weight_grad(i):
        need(*rest_in, weights_in[0], *[p for j in (3, 1, 2, 0) for p in parts_in[j]])
        if i == 0:
            g = dot_tn(r.dq_s[...], r.n_s[rows_of(0), :])
        elif i == 3:
            g = dot_tn(r.heads_s[...], r.d_att_s[...])
        else:
            g = dot_tn((r.dk_s if i == 1 else r.dv_s)[...], r.n_s[...])
        low = g.astype(BF16)
        for j in range(peers):
            pack[i // 2 * peers + j, part(i), :] = low[j * shard : (j + 1) * shard]
        return jnp.sum(g * w[i].astype(F32), axis=0, keepdims=True) if i < 3 else 0.0

    if not full:
        copies = {}
        if returns:
            size = r.out.shape[0] // CUTS
            out_in = local(r.out.at[pl.ds(0, size)], r.out_s)
            for k in (2, 3, 1):
                copies[k] = remote(r.out.at[pl.ds(k * size, size)], r.back.at[k - 1], m.z_peers[k - 1])
        rows_out((3, 1, 2))
        total = weight_grad(1)
        rows_turn()
        rows_own()
        total = total + weight_grad(2) + weight_grad(0) + weight_grad(3)
        r.att[...] = jnp.broadcast_to(total, r.att.shape)
        saved = local(pack, r.pack)
        if returns:
            need(out_in)
            r.result[...] = combine(m, r.slot_col, r.out_s, copies, r.back, size)
        rows_end()
        m.finish()
        need(saved)
        return

    mini = shard // 4
    at_z = lambda h, index: pl.ds(pl.multiple_of(h * shard + index * mini, mini), mini)
    both, z_in = r.both, r.z_in

    def z_out(source, layer, h):
        return [remote(source.at[at_z(h, xor_peer(z, k))], z_in.at[layer * 2 + h, k - 1], m.z_peers[k - 1]) for k in (1, 2, 3)]

    def z_sum(source, copies, layer, h):
        arrived(*copies)
        here = both.at[layer, c, at_z(h, z)]
        both[layer, c, at_z(h, z), :] = add_low(
            source.at[at_z(h, z)], *[z_in.at[layer * 2 + h, k] for k in range(3)]
        ).astype(BF16)
        return [remote(here, here, device) for device in m.z_peers]

    def core_out(copies, layer, h):
        arrived(*copies)
        here = both.at[layer, c, pl.ds(h * shard, shard)]
        return remote(here, here, m.sibling)

    scatter = Scatter(m, pack, r.core_in, r.g_in, r.piece)
    need(above_in)
    above = [z_out(r.above_s, 1, h) for h in range(2)]
    rows_out((3,))
    total = weight_grad(3) + weight_grad(1)
    scatter.swap(1)
    total = total + weight_grad(0) + weight_grad(2)
    scatter.swap(0)
    small_s, small_r = r.small_s, r.small_r
    row = lax.broadcasted_iota(jnp.int32, r.small.shape, 0)
    att_row = r.small_in.shape[0] // 2 - 1
    small_s[0] = jnp.where(row == att_row, total, r.small_in[...])
    small_1 = remote(small_s.at[0], small_r.at[0], m.sibling)
    scatter.out(1)
    scatter.out(0)
    above = [z_sum(r.above_s, above[h], 1, h) for h in range(2)]
    rows_out((1, 2))
    arrived(small_1)
    small_s[1] = small_s[0] + small_r[0]
    small_2 = remote(small_s.at[1], small_r.at[1], m.x_peer)
    scatter.turn(1)
    scatter.turn(0)
    rows_turn()
    above = [core_out(above[h], 1, h) for h in range(2)]
    need(*swaps_in)
    e_copies = [remote(r.e_s.at[l, c], r.e_s.at[l, c], m.sibling) for l in range(2)]
    rows_own()
    arrived(small_2)
    small_s[2] = small_s[1] + small_r[1]
    small_3 = remote(small_s.at[2], small_r.at[2], m.y_peer)
    scatter.end(1)
    piece_1 = z_out(r.piece, 0, 1)
    scatter.end(0)
    piece_0 = z_out(r.piece, 0, 0)
    arrived(small_3)
    small_s[3] = small_s[2] + small_r[2]
    last = [remote(small_s.at[3], small_r.at[2 + k], m.z_peers[k - 1]) for k in (1, 2, 3)]
    piece_1 = z_sum(r.piece, piece_1, 0, 1)
    piece_0 = z_sum(r.piece, piece_0, 0, 0)
    arrived(*above, *e_copies)
    saved = [local(both.at[1], r.g1), local(r.e_s, r.e)]
    piece_1 = core_out(piece_1, 0, 1)
    piece_0 = core_out(piece_0, 0, 0)
    rows_end()
    arrived(*last)
    r.small[...] = small_s[3] + small_r[3] + small_r[4] + small_r[5]
    arrived(piece_1, piece_0)
    saved.append(local(both.at[0], r.g0))
    m.finish()
    need(*saved)


def project_back(w, dq, dk, dv, normed_all, heads, d_att, above=None, small=None, swaps=None, out=None, slots=None):
    full, returns = above is not None, out is not None
    tokens, width = dq.shape
    rows = dk.shape[0]
    half = width // 2
    peers = rows // tokens
    shape = jax.ShapeDtypeStruct
    ins = dict(
        w=(w, ANY), dq=(dq, ANY), dk=(dk, ANY), dv=(dv, ANY), n=(normed_all, ANY), heads=(heads, ANY), d_att=(d_att, ANY),
    )
    outs = dict(dn=(shape((tokens, width), F32), VMEM))
    some, every = low_vmem(tokens, width), low_vmem(rows, width)
    scratch = dict(
        w_s=low_vmem(3, width, width), dq_s=some, dk_s=every, dv_s=every, n_s=every, heads_s=some, d_att_s=some,
        p1=some, p2=some, p3=some, row_in=low_vmem(6, tokens // 2, width),
    )
    if full:
        ins.update(above=(above, ANY), small_in=(small, VMEM), e0=(swaps[0], ANY), e1=(swaps[1], ANY))
        e_dims = (2, 2) + swaps[0].shape
        outs.update(
            g0=(low_shape(2, half, width), ANY), g1=(low_shape(2, half, width), ANY), e=(low_shape(*e_dims), ANY),
            small=(shape(small.shape, F32), VMEM),
        )
        scratch.update(
            scatter_scratch(peers, half, width), above_s=low_vmem(half, width), e_s=low_vmem(*e_dims),
            small_s=pltpu.VMEM((4,) + small.shape, F32), small_r=pltpu.VMEM((6,) + small.shape, F32),
            z_in=low_vmem(4, 3, half // 8, width), both=low_vmem(2, 2, half, width),
        )
    else:
        outs.update(pack=(low_shape(2 * peers, half, width), ANY), att=(shape((8, width), F32), VMEM))
        scratch.update(pack_s=low_vmem(2 * peers, half, width))
        if returns:
            ins.update(out=(out, ANY), slot_col=(slots[:, None], VMEM))
            outs.update(result=(low_shape(tokens, width), VMEM))
            size = out.shape[0] // CUTS
            scratch.update(out_s=low_vmem(size, width), back=low_vmem(3, size, width))
    return run_kernel(
        project_back_part, ins, outs, scratch, 4 + full, 4 * rows * width * width, 24, 64, full=full, returns=returns
    )


def inverse_rms(stream):
    return lax.rsqrt(jnp.mean(stream * stream, axis=-1, keepdims=True) + EPS)


def norm_backward(upstream, stream, inverse, gain):
    weighted = upstream * gain
    inner = jnp.mean(weighted * stream, axis=-1, keepdims=True)
    return inverse * weighted - stream * (inverse * inverse * inverse) * inner


def path_table(segment_ids, path_pos, parent_ids, peers):
    segment = segment_ids[::BLK].reshape(peers, -1)
    position = path_pos[::BLK].reshape(peers, -1)
    t = lax.axis_index(TENSOR)
    order = jnp.arange(peers, dtype=jnp.int32) ^ t
    match = order[:, None] == jnp.arange(peers, dtype=jnp.int32)[None, :]
    pick = lambda v: jnp.sum(jnp.where(match[:, :, None], v[None], 0), axis=1)
    segment, position = pick(segment), pick(position)
    place = jnp.where(segment == 0, position // BLK, segment + (TRUNK - 1))
    seg, pos, own = segment[0], position[0], place[0]
    names = jnp.arange(parent_ids.shape[-1], dtype=jnp.int32)
    parent = jnp.sum(jnp.where(seg[:, None] == names[None, :], parent_ids[0][None], 0), axis=1)
    leaf = (seg > 0) & (parent > 0)
    parent_place = jnp.where(leaf, parent + (TRUNK - 1), own)
    base_own = jnp.where(seg > 0, pos, BIG)
    base_parent = jnp.where(leaf, TRUNK * BLK, BIG)
    mine = jnp.stack([pos, own, parent_place, base_own, base_parent], axis=1)
    return jnp.concatenate([place.reshape(-1), mine.reshape(-1)]).astype(jnp.int32)


def dispatch_plan(route, experts, capacity):
    count = route.shape[0]
    chosen = route[:, None] == jnp.arange(experts, dtype=jnp.int32)[None, :]
    index = jnp.arange(count, dtype=jnp.int32)
    before = (index[None, :] < index[:, None]).astype(BF16)
    ranks = dot(before, chosen.astype(BF16)).astype(jnp.int32)
    rank = jnp.sum(jnp.where(chosen, ranks, 0), axis=1)
    to = route ^ lax.axis_index(EXPERT) if experts == 4 else route
    slot = to * capacity + rank
    table = slot[None, :] == jnp.arange(experts * capacity, dtype=jnp.int32)[:, None]
    return chosen, (slot, table.astype(BF16))


def send_rows(table, rows, experts, capacity):
    chunks = [
        dot(table[k * capacity : (k + 1) * capacity], rows).astype(BF16) for k in range(experts)
    ]
    return jnp.concatenate(exchange(chunks), axis=0)


def return_rows(table, results, experts, capacity):
    chunks = exchange([results[k * capacity : (k + 1) * capacity] for k in range(experts)])
    return dot_tn(table, jnp.concatenate(chunks, axis=0))


def own_half(x):
    half = x.shape[0] // 2
    return lax.dynamic_slice_in_dim(x, lax.axis_index(DP) * half, half, 0)


def gather_all(x):
    out = lax.all_gather(x, (DP, TENSOR), axis=0)
    return out.reshape((lax.axis_size(DP), lax.axis_size(TENSOR)) + x.shape)


def scatter_experts(x):
    if x.ndim == 4:
        return lax.psum_scatter(x, TENSOR, scatter_dimension=0, tiled=True)[0]
    return scatter_all(x)


def scatter_all(x):
    flat = x.reshape((-1,) + x.shape[2:])
    return lax.psum_scatter(flat, (DP, TENSOR), scatter_dimension=0, tiled=True)[0]


def pack_attention(w_mix, w_proj):
    width = w_mix.shape[0]
    return jnp.concatenate([w_mix.transpose(1, 2, 0).reshape(-1, width), w_proj], axis=0)


def pack_experts(w_up, w_back):
    return jnp.stack([own_half(w_up), own_half(w_back)])


def swap_cores(half):
    return lax.all_gather(half, DP, axis=0)


def body(
    hidden_in, route_ids, segment_ids, path_pos, parent_ids, norm_att, w_qkv, w_out, norm_ffn, w_route, w_in, w_down, cotangent,
):
    depth_total = w_qkv.shape[0]
    tokens, width = hidden_in.shape
    experts = w_route.shape[-1]
    capacity = 3 * tokens // (2 * experts)
    peers = lax.axis_size(TENSOR)
    shard = width // peers
    table = path_table(segment_ids, path_pos, parent_ids, peers)
    plans = [dispatch_plan(route_ids[d, :, 0], experts, capacity) for d in range(depth_total)]
    routes = [jnp.pad(w_route[d], ((0, 0), (0, BLK - experts))) for d in range(depth_total)]
    cotangent = cotangent.astype(F32)

    stream = hidden_in.astype(F32)
    kept = []
    packed = [pack_attention(w_qkv[d], w_out[d]) for d in range(depth_total)]
    own = [(w_in[d, 0], w_down[d, 0]) for d in range(depth_total)]
    weights = None
    for depth in range(depth_total):
        gain_att, gain_ffn = norm_att[depth].astype(F32), norm_ffn[depth].astype(F32)
        chosen, plan = plans[depth]
        last = depth + 1 == depth_total
        inverse_att = inverse_rms(stream)
        normed = (stream * inverse_att * gain_att).astype(BF16)
        proj = project(normed, packed[0] if depth == 0 else weights, depth == 0, peers)
        w_here = None if experts == CUTS else gather_all(pack_experts(*own[depth]))
        heads, lse = attend(table, proj.q, proj.k, proj.v)
        after_att = stream + dot(heads, proj.w_all[3])
        inverse_ffn = inverse_rms(after_att)
        token_rows = (after_att * inverse_ffn * gain_ffn).astype(BF16)
        router = jax.nn.softmax(dot(token_rows, w_route[depth]), axis=-1)
        gate = jnp.sum(jnp.where(chosen, router, 0.0), axis=1, keepdims=True)
        if last:
            d_low = (gate * cotangent).astype(BF16)
            held = experts_both(w_here, own[depth], plan, token_rows, d_low, routes[depth], experts, capacity)
            if experts != CUTS:
                back = return_rows(plan[1], held.out, experts, capacity).astype(BF16)
        else:
            back, held = experts_forward(plan, token_rows, experts, capacity, w_here, own[depth], packed[depth + 1])
            if experts == CUTS:
                weights = held.next_all.reshape((2, peers, 1) + held.next_all.shape[1:])
            else:
                weights = gather_all(own_half(packed[depth + 1]))[:, :, None]
        kept.append((stream, inverse_att, proj, heads, lse, after_att, inverse_ffn, gate, held))
        if not last:
            stream = after_att + gate * back.astype(F32)

    upstream = cotangent
    grads_e, grads_a, smalls = [None] * depth_total, [None] * depth_total, [None] * depth_total
    above = None
    for depth in reversed(range(depth_total)):
        stream, inverse_att, proj, heads, lse, after_att, inverse_ffn, gate, held = kept[depth]
        gain_att, gain_ffn = norm_att[depth].astype(F32), norm_ffn[depth].astype(F32)
        chosen, plan = plans[depth]
        last = depth + 1 == depth_total
        if not last:
            d_low = (gate * upstream).astype(BF16)
            held = experts_backward(plan, d_low, held, routes[depth], experts, capacity, above)
            above = held.summed
        dx1 = upstream + norm_backward(held.result.astype(F32), after_att, inverse_ffn, gain_ffn)
        d_att = dx1.astype(BF16)
        d_heads = dot_nt(d_att, proj.w_all[3]).astype(BF16)
        dq, dk, dv = attend_back(table, proj.q, proj.k, proj.v, d_heads, heads, lse)
        args = (proj.w_all, dq, dk, dv, proj.n, heads, d_att)
        if depth == 0 and experts == CUTS:
            grads_e[0] = scatter_experts(held.grads)
            lines = lambda n: jnp.zeros((n, width), F32)
            part = jnp.concatenate([held.small[: experts + 1], lines(3), smalls[1], lines(2)], axis=0)
            got = project_back(*args, above=above, small=part, swaps=grads_e)
            grads_a = [got.g0, got.g1]
            grads_e = [got.e[0], got.e[1]]
            total = got.small
            small = jnp.stack([
                jnp.concatenate([total[: experts + 1], total[7:8]], axis=0), total[8 : 8 + experts + 2]
            ])
        else:
            if last and experts == CUTS:
                got = project_back(*args, out=held.out, slots=plan[0])
                back = got.result
            else:
                got = project_back(*args)
            if last:
                hidden_out = (after_att + gate * back.astype(F32)).astype(BF16)
            if above is not None:
                grads_a[depth + 1] = swap_cores(lax.psum(above, EXPERT))
            above = got.pack.reshape((2, peers) + got.pack.shape[1:])
            if experts == CUTS:
                above = got.pack
            smalls[depth] = jnp.concatenate([held.small[: experts + 1], got.att[:1]], axis=0)
            grads_e[depth] = scatter_experts(after(held.grads, got.dn))
            if depth == 0:
                grads_a[0] = swap_cores(lax.psum(scatter_all(above), EXPERT))
                small = sum_small(jnp.stack(smalls))
                grads_e = [swap_cores(g) for g in grads_e]
        upstream = dx1 + norm_backward(got.dn, stream, inverse_att, gain_att)
    grad_up, grad_down = [
        jnp.stack([g[:, i].reshape(width, width) for g in grads_e])[:, None].astype(F32) for i in range(2)
    ]
    grads_a = jnp.stack([g.reshape(width, width) for g in grads_a]).astype(F32)
    grad_mix = grads_a[:, : 3 * shard].reshape(depth_total, 3, shard, width).transpose(0, 3, 1, 2)
    grad_out = grads_a[:, 3 * shard :]
    grad_route = small[:, :experts].transpose(0, 2, 1)
    grad_ffn = small[:, experts] / norm_ffn.astype(F32)
    grad_att = small[:, experts + 1] / norm_att.astype(F32)
    return (hidden_out, upstream, grad_att, grad_mix, grad_out, grad_ffn, grad_route, grad_up, grad_down)


def solution(mesh):
    in_specs = (
        P((DP, EXPERT, TENSOR), None),
        P(None, (DP, EXPERT, TENSOR), None),
        P((DP, EXPERT)),
        P((DP, EXPERT)),
        P((DP, EXPERT), None),
        P(),
        P(None, None, None, TENSOR),
        P(None, TENSOR, None),
        P(),
        P(),
        P(None, EXPERT, None, TENSOR),
        P(None, EXPERT, TENSOR, None),
        P((DP, EXPERT, TENSOR), None),
    )
    out_specs = (
        P((DP, EXPERT, TENSOR), None),
        P((DP, EXPERT, TENSOR), None),
        P(),
        P(None, None, None, TENSOR),
        P(None, TENSOR, None),
        P(),
        P(),
        P(None, EXPERT, None, TENSOR),
        P(None, EXPERT, TENSOR, None),
    )
    return jax.shard_map(body, mesh=mesh, in_specs=in_specs, out_specs=out_specs, check_vma=False)
```

time: 1070 us -> 740 us (0.69)
  waiting for transfers between devices: 357 us -> 5.85 us
  Pallas kernels: 375 us -> 635 us
  local copies, waits for them, and re-layouts: 111 us -> 23.8 us
  matrix products: 99 us -> 13.6 us
  starting transfers between devices: 50.7 us -> 0.08 us
    pallas_call x3 -> x7, Pallas kernels: 235 us -> 496 us  [run_kernel(): pl.pallas_call(kernel, in_specs=[spec for _, spec in ins.values()], out_s...]
    reduce_scatter x6 -> x0, waiting for transfers between devices: 136 us -> none  [scatter_all(): lax.psum_scatter(flat, ('dp', 'tensor'), scatter_dimension=0, tiled=True)[0]]
    ppermute x32 -> x0, waiting for transfers between devices: 89.2 us -> none  [xperm(): return lax.ppermute(x, axis, [(i, i ^ k) for i in range(n)])]
    all_gather x8 -> x0, waiting for transfers between devices: 76 us -> none  [the longest x6 69.1 us: gather_all(): out = lax.all_gather(x, ('dp', 'tensor'), axis=0)]
    psum x1 -> x0, waiting for transfers between devices: 54.6 us -> none  [body(): lax.psum((scatter_all(g_mix), scatter_all(g_o)), 'expert')]
    ppermute x32 -> x0, starting transfers between devices: 49.1 us -> none  [xperm(): return lax.ppermute(x, axis, [(i, i ^ k) for i in range(n)])]
    reshape x14 -> x0, local copies, waits for them, and re-layouts: 31.7 us -> none  [the longest x12 29.5 us: body(): g.astype(BF16).reshape(cores, half, peers, shard).transpose(0, 2, 1, 3)]
    dot_general x9 -> x0, matrix products: 31 us -> none  [dot_tn(): return lax.dot_general(a, b, TN, preferred_element_type=F32)]
  transfers between devices with their start and end apart: 47 -> 2, of which waited for: 25 -> 1; matrix products, arithmetic and copies ran while one was open for 21% -> 2% of each run, Pallas kernels for 21% -> 16%
where the time goes in v3:
time: 740 us; the launch traced here: 730 us
  Pallas kernels  635 us (86%)
  other arithmetic  37.1 us (5%)
  local copies, waits for them, and re-layouts  23.8 us (3%)
  between operations  14.8 us (2%)
  matrix products  13.6 us (2%)
    pallas_call x7, Pallas kernels, run_kernel(): pl.pallas_call(kernel, in_specs=[spec for _, spec in ins.values()], out_s...  496 us
    pallas_call x2, Pallas kernels, attend_back(): pl.pallas_call(attend_back_kernel, grid_spec=pltpu.PrefetchScalarGridSpec...  92.8 us
    pallas_call x2, Pallas kernels, attend(): pl.pallas_call(attend_kernel, grid_spec=pltpu.PrefetchScalarGridSpec(num_...  46.5 us
  transfers between devices with their start and end apart: 2, of which 1 were waited for; matrix products, arithmetic and copies ran while one was open for 2% of the time, Pallas kernels for 16%

profile of v3, /device:TPU:1, one launch (start us, length us, event | category | flops | bytes accessed | tf_op | source)
XLA Modules:
  0.0 730.3 jit_solution(14146710155761344669)
XLA Ops:
  7.3 0.9 slice.128
  8.3 0.8 slice.129
  9.4 0.7 slice_reduce_fusion
  10.7 0.7 bitcast_add_fusion
  11.4 1.3 bitcast_add_fusion.1
  12.7 0.8 select_reduce_fusion.2
  13.9 1.5 fusion.1
  15.6 0.9 copy-done.24
  16.5 0.6 pad_add_fusion.table
  17.2 1.2 fusion.3.refs_0_
  18.4 1.6 pad_maximum_fusion
  20.0 59.6 %project_part.2 = (bf16[640,768]{1,0:T(8,128)(2,1)}, bf16[2560,768]{1,0:T(8,128)(2,1)}, bf16[2560,768]{1,0:T(8,128)(2,1)}, bf16[2560,768]{1,0:T(8,128)(2,1)}, bf16[4,768,768]{2,1,0:T(8,128)(2,1)}) custom-call(bf16[640,768]{1,0:T(8,128)(2,1)} %fusion.3.refs_0_, bf16[768,768]{1,0:T(8,128)(2,1)} %get-tuple-element.160.refs_1_), custom_call_target="tpu_custom_call" | custom-call | flops 53084160 | tf_op jit(solution)/shard_map/project_part/pallas_call | solution.py:272
  79.5 23.3 %attend.2 = (bf16[640,768]{1,0:T(8,128)(2,1)}, f32[640,128]{1,0:T(8,128)}) custom-call(s32[45]{0:T(128)} %pad_add_fusion.table, bf16[640,768]{1,0:T(8,128)(2,1)} %get-tuple-element.54.q_ref, bf16[2560,768]{1,0:T(8,128)(2,1)} %get-tuple-element.55.k_ref, bf16[2560,768]{1,0:T(8,128)(2,1)} %get-tuple-element.56.v_ref), custom_call_target="tpu_custom_call" | custom-call | flops 78643200 | bytes 122880 | tf_op jit(solution)/shard_map/attend/pallas_call | solution.py:127
  102.9 2.6 multiply_reduce_fusion.5
  105.5 1.0 copy.48.refs_3_.refs_2_
  106.9 0.4 fusion.47
  107.3 0.5 copy-done.8
  107.8 0.8 copy-done.22
  108.6 3.9 slice_bitcast_fusion.2
  112.5 85.4 %expert_part.3 = (bf16[2,4,2,384,768]{4,3,2,1,0:T(8,128)(2,1)}, bf16[640,768]{1,0:T(8,128)(2,1)}, bf16[960,768]{1,0:T(8,128)(2,1)}, bf16[960,768]{1,0:T(8,128)(2...) custom-call(bf16[768,768]{1,0:T(8,128)(2,1)} %get-tuple-element.162.refs_0_, ...), custom_call_target="tpu_custom_call" | custom-call | flops 35389440 | tf_op jit(solution)/shard_map/expert_part/pallas_call | solution.py:272
  197.9 1.7 multiply_reduce_fusion.4
  199.6 1.2 multiply_convert_fusion.2.refs_0_
  200.8 34.3 %project_part.3 = (bf16[640,768]{1,0:T(8,128)(2,1)}, bf16[2560,768]{1,0:T(8,128)(2,1)}, bf16[2560,768]{1,0:T(8,128)(2,1)}, bf16[2560,768]{1,0:T(8,128)(2,1)}, bf16[4,768,768]{2,1,0:T(8,128)(2,1)}) custom-call(bf16[640,768]{1,0:T(8,128)(2,1)} %multiply_convert_fusion.2.refs_0_, bf16[2,4,1,384,768]{4,3,2,1,0:T(8,128)(2,1)} %bitcast.121), custom_call_target="tpu_custom_call" | custom-call | flops 53084160 | tf_op jit(solution)/shard_map/project_part/pallas_call | solution.py:272
  235.1 23.1 %attend.3 = (bf16[640,768]{1,0:T(8,128)(2,1)}, f32[640,128]{1,0:T(8,128)}) custom-call(s32[45]{0:T(128)} %pad_add_fusion.table, bf16[640,768]{1,0:T(8,128)(2,1)} %get-tuple-element.61.q_ref, bf16[2560,768]{1,0:T(8,128)(2,1)} %get-tuple-element.62.k_ref, bf16[2560,768]{1,0:T(8,128)(2,1)} %get-tuple-element.63.v_ref), custom_call_target="tpu_custom_call" | custom-call | flops 78643200 | bytes 122880 | tf_op jit(solution)/shard_map/attend/pallas_call | solution.py:127
  258.2 2.6 multiply_reduce_fusion.3
  261.1 0.4 fusion.48
  261.5 0.6 copy-done
  262.1 0.3 copy-done.7
  262.5 0.9 copy.50.refs_3_.refs_8_
  263.6 2.4 fusion.refs_5_
  265.9 0.7 pad.7.refs_6_
  266.7 113.1 %expert_part.4 = (bf16[640,768]{1,0:T(8,128)(2,1)}, bf16[960,768]{1,0:T(8,128)(2,1)}, bf16[4,2,384,768]{3,2,1,0:T(8,128)(2,1)}, f32[8,768]{1,0:T(8,128)}) custom-call(bf16[768,768]{1,0:T(8,128)(2,1)} %get-tuple-element.163.refs_0_, bf16[768,768]{1,0:T(8,128)(2,1)} %get-tuple-element.121.refs_1_, s32[1,640]{1,0:T(1,128)} %get-tuple-element.136.refs_2_, ...), custom_call_target="tpu_custom_call" | custom-call | flops 35389440 | tf_op jit(solution)/shard_map/expert_part/pallas_call | solution.py:272
  379.8 1.7 multiply_reduce_fusion.2
  381.6 0.6 fusion.41.refs_6_
  382.2 3.5 convolution_convert_fusion.1.do_ref
  385.8 46.2 %attend_back.2 = (bf16[640,768]{1,0:T(8,128)(2,1)}, bf16[2560,768]{1,0:T(8,128)(2,1)}, bf16[2560,768]{1,0:T(8,128)(2,1)}) custom-call(s32[45]{0:T(128)} %pad_add_fusion.table, bf16[640,768]{1,0:T(8,128)(2,1)} %get-tuple-element.61.q_ref, bf16[2560,768]{1,0:T(8,128)(2,1)} %get-tuple-element.62.k_ref, bf16[2560,768]{1,0:T(8,128)(2,1)} %get-tuple-element.63.v_ref, ...), custom_call_target="tpu_custom_call" | custom-call | flops 196608000 | bytes 245760 | tf_op jit(solution)/shard_map/attend_back/pallas_call | solution.py:215
  431.9 48.1 %project_back_part.2 = (f32[640,768]{1,0:T(8,128)}, bf16[8,384,768]{2,1,0:T(8,128)(2,1)}, f32[8,768]{1,0:T(8,128)}, bf16[640,768]{1,0:T(8,128)(2,1)}) custom-call(bf16[4,768,768]{2,1,0:T(8,128)(2,1)} %get-tuple-element.65.refs_0_, bf16[640,768]{1,0:T(8,128)(2,1)} %get-tuple-element.68.refs_1_, bf16[2560,768]{1,0:T(8,128)(2,1)} %get-tuple-element.69.refs_2_, ...), custom_call_target="tpu_custom_call" | custom-call | flops 94371840 | tf_op jit(solution)/shard_map/project_back_part/pallas_call | solution.py:272
  480.3 0.7 pad.8.refs_4_
  481.1 2.0 multiply_reduce_fusion.1
  483.7 4.1 multiply_convert_fusion
  487.9 69.3 %expert_part.5 = (bf16[640,768]{1,0:T(8,128)(2,1)}, bf16[4,2,384,768]{3,2,1,0:T(8,128)(2,1)}, f32[8,768]{1,0:T(8,128)}, bf16[384,768]{1,0:T(8,128)(2,1)}) custom-call(bf16[2,4,2,384,768]{4,3,2,1,0:T(8,128)(2,1)} %get-tuple-element.75.refs_0_, s32[1,640]{1,0:T(1,128)} %get-tuple-element.137.refs_2_.refs_1_, s32[640,1]{1,0:T(8,128)} %copy.48.refs_3_.refs_2_, ...), custom_call_target="tpu_custom_call" | custom-call | flops 35389440 | tf_op jit(solution)/shard_map/expert_part/pallas_call | solution.py:272
  557.2 0.9 slice.153
  558.1 1.2 concatenate.32.refs_8_
  559.4 1.7 multiply_reduce_fusion
  561.4 1.8 fusion.42
  563.3 3.5 convolution_convert_fusion.do_ref
  566.8 46.6 %attend_back.3 = (bf16[640,768]{1,0:T(8,128)(2,1)}, bf16[2560,768]{1,0:T(8,128)(2,1)}, bf16[2560,768]{1,0:T(8,128)(2,1)}) custom-call(s32[45]{0:T(128)} %pad_add_fusion.table, bf16[640,768]{1,0:T(8,128)(2,1)} %get-tuple-element.54.q_ref, bf16[2560,768]{1,0:T(8,128)(2,1)} %get-tuple-element.55.k_ref, bf16[2560,768]{1,0:T(8,128)(2,1)} %get-tuple-element.56.v_ref, ...), custom_call_target="tpu_custom_call" | custom-call | flops 196608000 | bytes 245760 | tf_op jit(solution)/shard_map/attend_back/pallas_call | solution.py:215
  613.5 5.8 reduce-scatter.7.cloned.1.call-done
  619.3 86.0 %project_back_part.3 = (f32[640,768]{1,0:T(8,128)}, bf16[2,384,768]{2,1,0:T(8,128)(2,1)}, bf16[2,384,768]{2,1,0:T(8,128)(2,1)}, bf16[2,2,2,384,768]{4,3,2,1,0:T(8,128)(2,1)}, f32[16,768]{1,0:T(8,128)}) custom-call(bf16[4,768,768]{2,1,0:T(8,128)(2,1)} %get-tuple-element.58.refs_0_, bf16[640,768]{1,0:T(8,128)(2,1)} %get-tuple-element.83.refs_1_, ...), custom_call_target="tpu_custom_call" | custom-call | flops 94371840 | tf_op jit(solution)/shard_map/project_back_part/pallas_call | solution.py:272
  705.3 0.9 slice.154
  706.2 0.7 slice.155
  707.0 0.7 slice_bitcast_fusion.8
  707.7 2.1 maximum_convert_fusion.3
  709.9 0.3 maximum_convert_fusion
  710.2 0.6 fusion.24
  710.8 1.4 copy-done.18
  712.2 0.3 slice_bitcast_fusion.1
  712.8 2.0 slice.168
  714.9 0.6 bitcast_divide_fusion
  715.5 0.6 bitcast_divide_fusion.1
  716.1 0.4 fusion.7
  716.4 2.5 maximum_convert_fusion.2
  718.9 2.5 maximum_convert_fusion.1
  721.4 1.8 fusion.6
  (103 shorter events, 4.4 us)
Async XLA Ops:
  7.2 8.3 %copy-start.23 = (bf16[2,768,3,192]{1,3,2,0:T(8,128)(2,1)S(1)}, bf16[2,768,3,192]{1,3,2,0:T(8,128)(2,1)}, u32[]{:S(2)}) copy-start(bf16[2,768,3,192]{1,3,2,0:T(8,128)(2,1)} %param.19) | copy-start | bytes 5308420
  7.2 606.3 %reduce-scatter.9.cloned.1.call-start = ((), (), s32[]{:S(2)}) async-start(), calls=%async_computation.3 | async-start | bytes 5898240
  15.4 1.1 copy-start.24
  15.4 1.7 copy-start.26
  15.5 1.7 copy-start.27
  15.5 1.7 copy-start.6
  102.9 3.7 copy-start.25
  105.5 1.7 copy-start.3
  106.6 2.0 copy-start.22
  106.8 0.9 copy-start.8
  112.5 85.4 %copy-start.4 = (f32[640,768]{1,0:T(8,128)S(1)}, f32[640,768]{1,0:T(8,128)}, u32[]{:S(2)}) copy-start(f32[640,768]{1,0:T(8,128)} %copy-done.3) | copy-start | bytes 5898244
  260.8 1.3 copy-start
  261.1 1.3 copy-start.7
  266.7 113.2 %copy-start.1 = (f32[640,768]{1,0:T(8,128)S(1)}, f32[640,768]{1,0:T(8,128)}, u32[]{:S(2)}) copy-start(f32[640,768]{1,0:T(8,128)} %copy-done) | copy-start | bytes 5898244
  379.8 1.7 copy-start.9
  379.8 1.8 copy-start.11
  382.2 3.5 copy-start.21
  480.1 139.2 %reduce-scatter.7.cloned.1.call-start = ((), (), s32[]{:S(2)}) async-start(), calls=%async_computation.2 | async-start | bytes 5898240
  481.1 2.1 copy-start.2
  481.1 2.4 copy-start.10
  481.1 2.7 copy-start.12
  557.2 0.9 copy-start.28
  557.2 0.9 copy-start.29
  557.2 2.2 copy-start.5
  559.4 1.8 copy-start.14
  559.4 2.1 copy-start.19
  563.3 3.5 copy-start.20
  705.3 4.5 copy-start.16
  705.3 4.5 copy-start.17
  709.8 2.3 copy-start.18
  712.8 3.2 copy-start.13
  718.9 2.5 copy-start.15
Sparse Core Ops, SparseCore 0:
  480.2 67.2 reduce-scatter.8
  557.3 61.8 reduce-scatter.6

commit v4 on v3

--- a/solution.py
+++ b/solution.py
@@ -72,8 +72,13 @@
     return jnp.concatenate([jnp.where(lane < HEAD_DIM, x, zero), jnp.where(lane < HEAD_DIM, zero, x)], axis=0)
 
 
-def attend_kernel(table, q_ref, k_ref, v_ref, out_ref, lse_ref, keys, values):
-    pair = pl.program_id(0)
+def path_spans(table, at, trunk):
+    own, parent, base_own, base_parent = [table[at + j] for j in range(1, 5)]
+    block = lambda place: pl.ds(pl.multiple_of(place * BLK, BLK), BLK)
+    return [(pl.ds(0, trunk), 0), (block(parent), base_parent), (block(own), base_own)]
+
+
+def attend_kernel(table, q_ref, k_ref, v_ref, out_ref, lse_ref, keys, values_t):
     blocks = k_ref.shape[0] // BLK
     mine = q_ref.shape[0] // BLK
     trunk = TRUNK * BLK
@@ -81,42 +86,39 @@
         place = pl.ds(pl.multiple_of(table[b] * BLK, BLK), BLK)
         rows = pl.ds(b * BLK, BLK)
         keys[place, :] = k_ref[rows, :]
-        values[place, pl.ds(0, PAIR)] = v_ref[rows, :]
-    values[:, pl.ds(PAIR, PAIR)] = jnp.ones((blocks * BLK, PAIR), BF16)
+        values_t[pl.ds(0, PAIR), place] = v_ref[rows, :].T
+    values_t[pl.ds(PAIR, 16), :] = jnp.ones((16, blocks * BLK), BF16)
     lane = lax.broadcasted_iota(jnp.int32, (BLK, PAIR), 1)
+
+    def scores_of(i):
+        at = blocks + 5 * i
+        q = masked_pair(q_ref[pl.ds(i * BLK, BLK), :] * jnp.asarray(HEAD_DIM ** -0.5, BF16))
+        pos_q = table[at] + lax.broadcasted_iota(jnp.int32, (1, 2 * BLK), 1) % BLK
+        parts = []
+        for here, base in path_spans(table, at, trunk):
+            scores = dot_nt(keys[here, :], q)
+            key_pos = base + lax.broadcasted_iota(jnp.int32, (here.size, 1), 0)
+            parts.append(jnp.where(key_pos <= pos_q, scores, NEG))
+        top = parts[0].max(axis=0, keepdims=True)
+        for part in parts[1:]:
+            top = jnp.maximum(top, part.max(axis=0, keepdims=True))
+        return parts, top
+
+    coming = scores_of(0)
     for i in range(mine):
-        at = blocks + 5 * i
-        place_q, own, parent, base_own, base_parent = [table[at + j] for j in range(5)]
+        parts, top = coming
+        if i + 1 < mine:
+            coming = scores_of(i + 1)
         rows = pl.ds(i * BLK, BLK)
-        own_rows = pl.ds(pl.multiple_of(own * BLK, BLK), BLK)
-        parent_rows = pl.ds(pl.multiple_of(parent * BLK, BLK), BLK)
-        q = masked_pair(q_ref[rows, :] * jnp.asarray(HEAD_DIM ** -0.5, BF16))
-        row = lax.broadcasted_iota(jnp.int32, (2 * BLK, 1), 0) % BLK
-        pos_q = place_q + row
-        s_trunk = dot_nt(q, keys[pl.ds(0, trunk), :])
-        key_pos = lax.broadcasted_iota(jnp.int32, s_trunk.shape, 1)
-        s_trunk = jnp.where(key_pos <= pos_q, s_trunk, NEG)
-        s_parent = dot_nt(q, keys[parent_rows, :])
-        col = lax.broadcasted_iota(jnp.int32, s_parent.shape, 1)
-        s_parent = jnp.where(col + base_parent <= pos_q, s_parent, NEG)
-        s_own = dot_nt(q, keys[own_rows, :])
-        s_own = jnp.where(col + base_own <= pos_q, s_own, NEG)
-        top = jnp.maximum(
-            jnp.max(s_trunk, axis=1, keepdims=True),
-            jnp.max(jnp.maximum(s_parent, s_own), axis=1, keepdims=True),
-        )
-        p_trunk = jnp.exp(s_trunk - top).astype(BF16)
-        p_parent = jnp.exp(s_parent - top).astype(BF16)
-        p_own = jnp.exp(s_own - top).astype(BF16)
-        both = dot(p_trunk, values[pl.ds(0, trunk), :])
-        both = both + dot(p_parent, values[parent_rows, :]) + dot(p_own, values[own_rows, :])
-        total = both[:, PAIR:]
-        heads = both[:, :PAIR] / total
+        both = jnp.zeros((PAIR + 16, 2 * BLK), F32)
+        for (here, _), part in zip(path_spans(table, blocks + 5 * i, trunk), parts):
+            both = both + dot(values_t[:, here], jnp.exp(part - top).astype(BF16))
+        total = both[PAIR : PAIR + 1]
+        heads = (both[:PAIR] / total).T
         lse = top + jnp.log(total)
         out_ref[rows, :] = jnp.where(lane < HEAD_DIM, heads[:BLK], heads[BLK:]).astype(BF16)
-        known = jnp.where(pair == 0, 0.0, lse_ref[rows, :])
-        known = jnp.where(lane == 2 * pair, lse[:BLK], known)
-        lse_ref[rows, :] = jnp.where(lane == 2 * pair + 1, lse[BLK:], known)
+        lse_ref[0, pl.ds(0, 1), rows] = lse[:, :BLK]
+        lse_ref[0, pl.ds(1, 1), rows] = lse[:, BLK:]
 
 
 def attend(table, q, k, v):
@@ -130,10 +132,10 @@
             num_scalar_prefetch=1,
             grid=(pairs,),
             in_specs=[column(mine), column(rows), column(rows)],
-            out_specs=[column(mine), pl.BlockSpec((mine, PAIR), lambda p, table: (0, 0))],
-            scratch_shapes=[pltpu.VMEM((rows, PAIR), BF16), pltpu.VMEM((rows, 2 * PAIR), BF16)],
+            out_specs=[column(mine), pl.BlockSpec((1, 8, mine), lambda p, table: (p, 0, 0))],
+            scratch_shapes=[pltpu.VMEM((rows, PAIR), BF16), pltpu.VMEM((PAIR + 16, rows), BF16)],
         ),
-        out_shape=[jax.ShapeDtypeStruct((mine, width), BF16), jax.ShapeDtypeStruct((mine, PAIR), F32)],
+        out_shape=[jax.ShapeDtypeStruct((mine, width), BF16), jax.ShapeDtypeStruct((pairs, 8, mine), F32)],
         compiler_params=pltpu.CompilerParams(vmem_limit_bytes=VMEM_LIMIT),
         cost_estimate=cost(mine * 1280 * width * 8, 4 * rows * width, mine * 1280 * width // HEAD_DIM),
         name="attend",
@@ -141,10 +143,8 @@
 
 
 def attend_back_kernel(
-    table, q_ref, k_ref, v_ref, do_ref, o_ref, lse_ref, dq_ref, dk_ref, dv_ref,
-    keys, values, keys_t, dk_acc, dv_acc, lse_t,
+    table, q_ref, k_ref, v_ref, do_ref, o_ref, lse_ref, dq_ref, dk_ref, dv_ref, keys, values, keys_t, dk_acc, dv_acc,
 ):
-    pair = pl.program_id(0)
     blocks = k_ref.shape[0] // BLK
     mine = q_ref.shape[0] // BLK
     trunk = TRUNK * BLK
@@ -156,50 +156,41 @@
         keys_t[:, place] = k_ref[rows, :].T
     dk_acc[...] = jnp.zeros_like(dk_acc)
     dv_acc[...] = jnp.zeros_like(dv_acc)
-
-    @pl.when(pair == 0)
-    def _():
-        for i in range(mine):
-            turned = lse_ref[pl.ds(i * BLK, BLK), :].T
-            for p in range(lse_t.shape[0]):
-                lse_t[p, pl.ds(0, 2), pl.ds(i * BLK, BLK)] = turned[2 * p : 2 * p + 2]
-
     lane = lax.broadcasted_iota(jnp.int32, (BLK, PAIR), 1)
-    scale = jnp.asarray(HEAD_DIM ** -0.5, BF16)
-    for i in range(mine):
+
+    def weights_of(i):
         at = blocks + 5 * i
-        place_q, own, parent, base_own, base_parent = [table[at + j] for j in range(5)]
         rows = pl.ds(i * BLK, BLK)
-        q = masked_pair(q_ref[rows, :] * scale)
+        q = masked_pair(q_ref[rows, :] * jnp.asarray(HEAD_DIM ** -0.5, BF16))
         do = do_ref[rows, :]
         product = (do.astype(F32) * o_ref[rows, :].astype(F32)).T
         inner = jnp.concatenate(
-            [
-                jnp.sum(product[:HEAD_DIM], axis=0, keepdims=True),
-                jnp.sum(product[HEAD_DIM:], axis=0, keepdims=True),
-            ],
-            axis=1,
+            [jnp.sum(product[:HEAD_DIM], axis=0, keepdims=True), jnp.sum(product[HEAD_DIM:], axis=0, keepdims=True)], axis=1
         )
         do = masked_pair(do)
-        lse = jnp.concatenate([lse_t[pair, pl.ds(0, 1), rows], lse_t[pair, pl.ds(1, 1), rows]], axis=1)
-        pos_q = place_q + lax.broadcasted_iota(jnp.int32, (1, 2 * BLK), 1) % BLK
+        lse = jnp.concatenate([lse_ref[0, pl.ds(0, 1), rows], lse_ref[0, pl.ds(1, 1), rows]], axis=1)
+        pos_q = table[at] + lax.broadcasted_iota(jnp.int32, (1, 2 * BLK), 1) % BLK
+        parts = []
+        for here, base in path_spans(table, at, trunk):
+            scores = dot_nt(keys[here, :], q)
+            key_pos = base + lax.broadcasted_iota(jnp.int32, (here.size, 1), 0)
+            weights = jnp.exp(jnp.where(key_pos <= pos_q, scores - lse, NEG))
+            d_weights = dot_nt(values[here, :], do)
+            parts.append((weights.astype(BF16), (weights * (d_weights - inner)).astype(BF16)))
+        return q, do, parts
+
+    coming = weights_of(0)
+    for i in range(mine):
+        q, do, parts = coming
+        if i + 1 < mine:
+            coming = weights_of(i + 1)
         dq_t = jnp.zeros((PAIR, 2 * BLK), F32)
-        steps = [(j * 2 * BLK, 2 * BLK, j * 2 * BLK) for j in range(TRUNK // 2)]
-        steps += [(pl.multiple_of(parent * BLK, BLK), BLK, base_parent)]
-        steps += [(pl.multiple_of(own * BLK, BLK), BLK, base_own)]
-        for start, size, base in steps:
-            here = pl.ds(start, size)
-            k_rows, v_rows = keys[here, :], values[here, :]
-            scores = dot_nt(k_rows, q)
-            key_pos = base + lax.broadcasted_iota(jnp.int32, (size, 1), 0)
-            weights = jnp.exp(jnp.where(key_pos <= pos_q, scores - lse, NEG))
-            d_weights = dot_nt(v_rows, do)
-            d_scores = (weights * (d_weights - inner)).astype(BF16)
-            dv_acc[here, :] += dot(weights.astype(BF16), do)
+        for (here, _), (weights, d_scores) in zip(path_spans(table, blocks + 5 * i, trunk), parts):
+            dv_acc[here, :] += dot(weights, do)
             dk_acc[here, :] += dot(d_scores, q)
             dq_t = dq_t + dot(keys_t[:, here], d_scores)
         dq = dq_t.T * (HEAD_DIM ** -0.5)
-        dq_ref[rows, :] = jnp.where(lane < HEAD_DIM, dq[:BLK], dq[BLK:]).astype(BF16)
+        dq_ref[pl.ds(i * BLK, BLK), :] = jnp.where(lane < HEAD_DIM, dq[:BLK], dq[BLK:]).astype(BF16)
     for b in range(blocks):
         place = pl.ds(pl.multiple_of(table[b] * BLK, BLK), BLK)
         rows = pl.ds(b * BLK, BLK)
@@ -219,7 +210,7 @@
             grid=(pairs,),
             in_specs=[
                 column(mine), column(rows), column(rows), column(mine), column(mine),
-                pl.BlockSpec((mine, PAIR), lambda p, table: (0, 0)),
+                pl.BlockSpec((1, 8, mine), lambda p, table: (p, 0, 0)),
             ],
             out_specs=[column(mine), column(rows), column(rows)],
             scratch_shapes=[
@@ -228,7 +219,6 @@
                 pltpu.VMEM((PAIR, rows), BF16),
                 pltpu.VMEM((rows, PAIR), F32),
                 pltpu.VMEM((rows, PAIR), F32),
-                pltpu.VMEM((pairs, 8, mine), F32),
             ],
         ),
         out_shape=[
@@ -352,11 +342,11 @@
 class Scatter:
     def __init__(self, moves, pack, core_in, g_in, piece):
         self.moves, self.pack, self.core_in, self.g_in, self.piece = moves, pack, core_in, g_in, piece
-        self.peers = core_in.shape[0]
+        self.peers = lax.axis_size(TENSOR)
         self.size = pack.shape[1] // 2
         c, t = moves.c, moves.t
         self.index = [t] + [xor_peer(t, k) for k in (1, 2, 3)]
-        self.slots = [c * self.peers + i for i in self.index]
+        self.slots = self.index if core_in is None else [c * self.peers + i for i in self.index]
         self.flow = [dict(), dict()]
 
     def rows(self, h):
@@ -374,11 +364,12 @@
     def out(self, h):
         m, pack, slots, f = self.moves, self.pack, self.slots, self.flow[h]
         left, right = self.sides(h)
-        m.arrived(f[0])
-        for j in (3, 1, 2, 0):
-            pack[slots[j], self.rows(h), :] = add_low(
-                pack.at[slots[j], self.rows(h)], self.core_in.at[self.index[j], self.rows(h)]
-            ).astype(BF16)
+        if self.core_in is not None:
+            m.arrived(f[0])
+            for j in (3, 1, 2, 0):
+                pack[slots[j], self.rows(h), :] = add_low(
+                    pack.at[slots[j], self.rows(h)], self.core_in.at[self.index[j], self.rows(h)]
+                ).astype(BF16)
         f[1] = m.remote(pack.at[slots[3], left], self.g_in.at[h, 0], m.x_peer)
         f[2] = m.remote(pack.at[slots[3], right], self.g_in.at[h, 1], m.y_peer)
         f[3] = m.remote(pack.at[slots[1], left], self.g_in.at[h, 2], m.x_peer)
@@ -402,6 +393,49 @@
             self.piece[cut, :] = total.astype(BF16)
 
 
+class ExpertScatter:
+    def __init__(self, moves, pack, own, keep, inbox):
+        self.m, self.pack, self.own, self.keep, self.inbox = moves, pack, own, keep, inbox
+        half = own.shape[1] // 2
+        self.left, self.right = pl.ds(0, half), pl.ds(half, half)
+        self.index = [moves.t] + [xor_peer(moves.t, k) for k in (1, 2, 3)]
+
+    def load(self):
+        p, i, m = self.pack, self.index, self.m
+        return [
+            m.local(p.at[i[0]], self.own),
+            m.local(p.at[i[2], :, self.left], self.keep.at[0]),
+            m.local(p.at[i[1], :, self.right], self.keep.at[1]),
+        ]
+
+    def out(self):
+        p, i, m = self.pack, self.index, self.m
+        self.flow = [
+            m.remote(p.at[i[3], :, self.left], self.inbox.at[0], m.x_peer),
+            m.remote(p.at[i[3], :, self.right], self.inbox.at[1], m.y_peer),
+            m.remote(p.at[i[1], :, self.left], self.inbox.at[2], m.x_peer),
+            m.remote(p.at[i[2], :, self.right], self.inbox.at[3], m.y_peer),
+        ]
+
+    def turn(self):
+        m = self.m
+        self.second = []
+        for n, device in enumerate((m.y_peer, m.x_peer)):
+            if self.flow:
+                m.arrived(self.flow[n])
+            self.keep[n] = add_low(self.keep.at[n], self.inbox.at[n]).astype(BF16)
+            self.second.append(m.remote(self.keep.at[n], self.inbox.at[4 + n], device))
+
+    def end(self):
+        self.m.arrived(*self.flow, *self.second)
+        for n, cut in enumerate((self.left, self.right)):
+            self.own[:, cut, :] = add_low(self.own.at[:, cut], self.inbox.at[2 + n], self.inbox.at[4 + n]).astype(BF16)
+
+
+def expert_scatter_scratch(half, width):
+    return dict(e_own=low_vmem(2, half, width), e_keep=low_vmem(2, 2, half // 2, width), e_in=low_vmem(6, 2, half // 2, width))
+
+
 class Gather:
     def __init__(self, moves, pack):
         self.moves, self.pack = moves, pack
@@ -431,6 +465,10 @@
         self.moves.arrived(*self.swaps)
 
 
+def attention_rows(r, depth, i):
+    return r.w_qkv.at[depth, i] if i < 3 else r.w_out.at[depth]
+
+
 def scatter_scratch(peers, half, width):
     return dict(
         pack_s=low_vmem(2 * peers, half, width), core_in=low_vmem(peers, half, width),
@@ -456,8 +494,10 @@
     return total.astype(BF16)
 
 
-def expert_part(m, forward, backward, remote, hosted, reduces, fetches, experts):
+def expert_part(m, forward, backward, remote, hosted, reduces, fetches, experts, depth):
     r = m.refs
+    if hosted:
+        own_up, own_down = r.w_in.at[depth, 0], r.w_down.at[depth, 0]
     up, down, hidden, slope, rows, outs = r.up, r.down, r.hidden_s, r.slope_s, r.rows_s, r.outs_s
     count, width = rows.shape
     inner = up.shape[1]
@@ -488,8 +528,8 @@
         if backward:
             loads.append(m.local(r.g, r.d_s))
     if hosted:
-        weight_loads.append(m.local(r.own_up, up.at[:, pl.ds(pl.multiple_of(m.t * width, width), width)]))
-        weight_loads.append(m.local(r.own_down, down.at[pl.ds(pl.multiple_of(m.t * width, width), width)]))
+        weight_loads.append(m.local(own_up, up.at[:, pl.ds(pl.multiple_of(m.t * width, width), width)]))
+        weight_loads.append(m.local(own_down, down.at[pl.ds(pl.multiple_of(m.t * width, width), width)]))
     else:
         for t in range(peers):
             for c in range(2):
@@ -550,16 +590,21 @@
     saves, returns = [], {}
     scatter = None
     if fetches:
-        next_loads = [m.local(r.next_own.at[pl.ds(c * half, half)], r.next_s.at[c * peers + m.t]) for c in range(2)]
+        shard = half // 2
+        next_loads = [
+            m.local(attention_rows(r, depth + 1, i), r.next_s.at[i // 2 * peers + m.t, pl.ds(i % 2 * shard, shard)]) for i in range(4)
+        ]
         fetch = Gather(m, r.next_s)
     if hosted:
         first = {}
         for k, device in ((1, m.x_peer), (2, m.y_peer)):
             mine = pl.ds(pl.multiple_of(m.c * half, half), half)
-            first[k] = [m.remote(r.own_up.at[mine], up_at(m.c, m.t), device), m.remote(r.own_down.at[mine], down_at(m.c, m.t), device)]
+            first[k] = [m.remote(own_up.at[mine], up_at(m.c, m.t), device), m.remote(own_down.at[mine], down_at(m.c, m.t), device)]
     if reduces:
         scatter = Scatter(m, r.pack_s, r.core_in, r.g_in, r.piece)
         pack_load = m.local(r.pack, r.pack_s)
+        e_scatter = ExpertScatter(m, r.e_pack, r.e_own, r.e_keep, r.e_in)
+        e_loads = e_scatter.load()
     if remote and forward:
         sent_x = dispatch(r.x, rows, r.stage_x)
     if remote and backward:
@@ -591,23 +636,21 @@
         if fetches:
             m.need(*next_loads)
             fetch.out()
-        m.arrived(sent_x[2])
-        forward_peer(cuts[2], tens[0])
-        m.arrived(sent_x[3])
-        forward_peer(cuts[3], tens[0])
+        m.arrived(sent_x[2], sent_x[3])
+        forward_peer(pl.ds(2 * size, 2 * size), tens[0])
         for k in (1, 2, 3):
             if k == 3:
                 m.arrived(*onward)
                 swap(3)
             m.arrived(*swaps[k])
-            for cut in cuts:
-                forward_peer(cut, tens[k])
+            forward_peer(pl.ds(0, count), tens[k])
         if fetches:
             fetch.turn()
-        for k in (2, 3, 1, 0):
-            forward_down(cuts[k])
-            if k and not backward:
-                returns[k] = give_back(outs, k)
+        for first_k in (2, 0):
+            forward_down(pl.ds(first_k * size, 2 * size))
+            for k in (first_k, first_k + 1):
+                if k and not backward:
+                    returns[k] = give_back(outs, k)
         if not backward:
             for c in range(2):
                 for t in range(peers):
@@ -636,15 +679,18 @@
             gain = gain + backward_chunk(cuts[k])
             if remote and k:
                 returns[k] = give_back(r.back_s, k)
-            if reduces and k < 2:
-                for h in range(2):
-                    (scatter.out, scatter.turn)[k](h)
+            if reduces and k == 0:
+                scatter.out(0)
+                scatter.out(1)
+                e_scatter.out()
+            if reduces and k == 2:
+                scatter.turn(0)
+                scatter.turn(1)
         if not remote:
             saves.append(m.local(r.back_s, r.result))
         if reduces:
-            for h in range(2):
-                scatter.end(h)
-            saves.append(m.local(r.piece, r.summed))
+            m.need(*e_loads)
+            e_scatter.turn()
         r.turned[...] = rows[...].T
         route = dot_tn(r.log_s[...], rows[...])
         pad = r.small.shape[0] - experts - 1
@@ -661,6 +707,11 @@
             else:
                 for c in range(2):
                     saves += [m.local(up_at(c, t), r.grads.at[c, t, 0]), m.local(down_at(c, t), r.grads.at[c, t, 1])]
+    if reduces:
+        for h in range(2):
+            scatter.end(h)
+        e_scatter.end()
+        saves += [m.local(r.piece, r.summed), m.local(r.e_own, r.e_summed)]
     if remote:
         if backward:
             for t in range(peers):
@@ -669,12 +720,16 @@
                     here = at(m.c, t)
                     here[...] = add_low(here, r.grads_in.at[t, i]).astype(BF16)
                     saves.append(m.local(here, r.grads.at[t, i]))
+            if reduces:
+                for i, at in enumerate((up_at, down_at)):
+                    for box, k, start in ((r.to_x.at[0], 3, 0), (r.to_x.at[1], 1, 0), (r.to_y.at[0], 3, 1), (r.to_y.at[1], 2, 1)):
+                        saves.append(m.local(at(m.c, xor_peer(m.t, k), start * (half // 2), half // 2), box.at[i]))
         r.result[...] = combine(m, r.slot_col, r.back_s if backward else outs, returns, r.back, size)
     m.finish()
     m.need(*saves)
 
 
-def expert_call(plan, experts, count, w=None, own=None, x=None, g=None, kept=None, route=None, pack=None, fetch=None):
+def expert_call(plan, experts, count, w=None, own=None, x=None, g=None, kept=None, route=None, pack=None, fetch=None, depth=0):
     slots = plan[0]
     forward, backward, remote, hosted, reduces = x is not None, g is not None, experts == CUTS, own is not None, pack is not None
     tokens, width = (x if forward else g).shape
@@ -685,7 +740,7 @@
     rows_shape, inner_shape = low_shape(count, width), low_shape(count, inner)
     ins, outs = {}, {}
     if hosted:
-        ins.update(own_up=(own[0], ANY), own_down=(own[1], ANY))
+        ins.update(w_in=(own[0], ANY), w_down=(own[1], ANY))
         if not backward:
             outs.update(w=(w_shape, ANY))
     else:
@@ -705,7 +760,8 @@
         if not backward:
             outs.update(rows=(rows_shape, ANY), hidden=(inner_shape, ANY), slope=(inner_shape, ANY))
     if backward:
-        outs.update(grads=(low_shape(peers, 2, half, width) if remote else w_shape, ANY), small=(jax.ShapeDtypeStruct((-(-(experts + 1) // 8) * 8, width), F32), VMEM))
+        outs.update(grads=(low_shape(peers, 2, half, width) if remote else w_shape, ANY))
+        outs.update(small=(jax.ShapeDtypeStruct((-(-(experts + 1) // 8) * 8, width), F32), VMEM))
     scratch = dict(
         up=low_vmem(width, inner), down=low_vmem(inner, width), hidden_s=low_vmem(count, inner), slope_s=low_vmem(count, inner),
         rows_s=low_vmem(count, width), outs_s=low_vmem(count, width),
@@ -717,13 +773,14 @@
     if backward and remote:
         scratch.update(grads_in=low_vmem(peers, 2, half, width))
     if fetch is not None:
-        ins.update(next_own=(fetch, ANY))
+        ins.update(w_qkv=(fetch[0], ANY), w_out=(fetch[1], ANY))
         outs.update(next_all=(low_shape(2 * peers, half, width), ANY))
         scratch.update(next_s=low_vmem(2 * peers, half, width))
     if reduces:
-        ins.update(pack=(pack, ANY))
-        outs.update(summed=(low_shape(half, width), ANY))
-        scratch.update(scatter_scratch(peers, half, width))
+        ins.update(pack=(pack[0], ANY), e_pack=(pack[1], ANY))
+        box = (low_shape(2, 2, half // 2, width), ANY)
+        outs.update(summed=(low_shape(half, width), ANY), e_summed=(low_shape(2, half, width), ANY), to_x=box, to_y=box)
+        scratch.update(scatter_scratch(peers, half, width), **expert_scatter_scratch(half, width))
     if remote:
         part = low_vmem(3, count // CUTS, width)
         scratch.update(back=part)
@@ -732,16 +789,16 @@
         if backward:
             scratch.update(stage_d=part)
     return run_kernel(
-        expert_part, ins, outs, scratch, forward + 2 * backward, count * width * inner, 48, 48 if remote else 0,
+        expert_part, ins, outs, scratch, forward + 2 * backward, count * width * inner, 64, 48 if remote else 0,
         forward=forward, backward=backward, remote=remote, hosted=hosted, reduces=reduces,
-        fetches=fetch is not None, experts=experts,
+        fetches=fetch is not None, experts=experts, depth=depth,
     )
 
 
-def experts_forward(plan, token_rows, experts, capacity, w, own, fetch):
+def experts_forward(plan, token_rows, experts, capacity, w, own, fetch, depth):
     count = experts * capacity
     if experts == CUTS:
-        got = expert_call(plan, experts, count, own=own, x=token_rows, fetch=fetch)
+        got = expert_call(plan, experts, count, own=own, x=token_rows, fetch=fetch, depth=depth)
         return got.result, got
     got = expert_call(plan, experts, count, w=w, x=send_rows(plan[1], token_rows, experts, capacity))
     got.w = w
@@ -759,10 +816,10 @@
     return got
 
 
-def experts_both(w, own, plan, token_rows, d_low, route, experts, capacity):
+def experts_both(w, own, plan, token_rows, d_low, route, experts, capacity, depth):
     count = experts * capacity
     if experts == CUTS:
-        return expert_call(plan, experts, count, own=own, x=token_rows, g=d_low, route=route)
+        return expert_call(plan, experts, count, own=own, x=token_rows, g=d_low, route=route, depth=depth)
     rows = send_rows(plan[1], token_rows, experts, capacity)
     d_sent = send_rows(plan[1], d_low, experts, capacity)
     got = expert_call(plan, experts, count, w=w, x=rows, g=d_sent, route=route)
@@ -783,7 +840,7 @@
     loads = []
     if hosted:
         for i in range(4):
-            loads.append(m.local(r.w.at[pl.ds(i * shard, shard)], w.at[i, at(t)]))
+            loads.append(m.local(attention_rows(r, 0, i), w.at[i, at(t)]))
     else:
         for i in range(4):
             for j in range(peers):
@@ -864,8 +921,9 @@
         n_s=low_vmem(every, width), w_s=low_vmem(4, width, width), q_s=low_vmem(tokens, width),
         k_s=low_vmem(every, width), v_s=low_vmem(every, width),
     )
+    given = dict(w_qkv=(w[0], ANY), w_out=(w[1], ANY)) if hosted else dict(w=(w, ANY))
     return run_kernel(
-        project_part, dict(x=(x, ANY), w=(w, ANY)), outs, scratch, 6 + hosted, 9 * tokens * width * width, 40, 24, hosted=hosted
+        project_part, dict(x=(x, ANY), **given), outs, scratch, 6 + hosted, 9 * tokens * width * width, 40, 24, hosted=hosted
     )
 
 
@@ -886,7 +944,13 @@
     above_in = local(r.above, r.above_s) if full else None
     rest_in = [local(a, b) for a, b in ((r.n, r.n_s), (r.dq, r.dq_s), (r.heads, r.heads_s), (r.d_att, r.d_att_s))]
     weights_in[0] = local(r.w.at[0], w.at[0])
-    swaps_in = [local(e, r.e_s.at[l, c]) for l, e in enumerate((r.e0, r.e1))] if full else []
+    swaps_in = []
+    if full:
+        e_scatter = ExpertScatter(m, r.e0, r.e_own, r.e_keep, r.e_in)
+        e_scatter.flow = []
+        e_loads = [local(a.at[n], r.e_in.at[2 * n + i]) for n in range(2) for i, a in enumerate((r.from_x, r.from_y))]
+        e_loads += e_scatter.load()
+        swaps_in = [local(r.e1.at[i], r.e_s.at[i, 1, c]) for i in range(2)]
     ready()
     tops, ends = pl.ds(0, tokens // 2), pl.ds(tokens // 2, tokens // 2)
 
@@ -896,16 +960,20 @@
 
     over_x, over_y = {}, {}
 
-    def rows_out(which):
+    stages = {1: r.p1, 2: r.p2, 3: r.p3}
+
+    def rows_part(*which):
         need(weights_in[1], weights_in[2])
         for j in which:
-            stage = {1: r.p1, 2: r.p2, 3: r.p3}[j]
             need(*parts_in[j])
-            stage[...] = partial(j).astype(BF16)
+            stages[j][...] = partial(j).astype(BF16)
+
+    def rows_send(*which):
+        for j in which:
             if j != 2:
-                over_x[j] = remote(stage.at[tops], r.row_in.at[j // 2], m.x_peer)
+                over_x[j] = remote(stages[j].at[tops], r.row_in.at[j // 2], m.x_peer)
             if j != 1:
-                over_y[j] = remote(stage.at[ends], r.row_in.at[2 + j // 3], m.y_peer)
+                over_y[j] = remote(stages[j].at[ends], r.row_in.at[2 + j // 3], m.y_peer)
 
     def rows_turn():
         arrived(over_x[3])
@@ -947,7 +1015,9 @@
             out_in = local(r.out.at[pl.ds(0, size)], r.out_s)
             for k in (2, 3, 1):
                 copies[k] = remote(r.out.at[pl.ds(k * size, size)], r.back.at[k - 1], m.z_peers[k - 1])
-        rows_out((3, 1, 2))
+        for j in (3, 1, 2):
+            rows_part(j)
+            rows_send(j)
         total = weight_grad(1)
         rows_turn()
         rows_own()
@@ -985,9 +1055,12 @@
     scatter = Scatter(m, pack, r.core_in, r.g_in, r.piece)
     need(above_in)
     above = [z_out(r.above_s, 1, h) for h in range(2)]
-    rows_out((3,))
+    rows_part(3)
+    rows_send(3)
     total = weight_grad(3) + weight_grad(1)
     scatter.swap(1)
+    need(*e_loads)
+    e_scatter.turn()
     total = total + weight_grad(0) + weight_grad(2)
     scatter.swap(0)
     small_s, small_r = r.small_s, r.small_r
@@ -995,41 +1068,47 @@
     att_row = r.small_in.shape[0] // 2 - 1
     small_s[0] = jnp.where(row == att_row, total, r.small_in[...])
     small_1 = remote(small_s.at[0], small_r.at[0], m.sibling)
+    above = [z_sum(r.above_s, above[h], 1, h) for h in range(2)]
+    arrived(small_1)
+    small_s[1] = small_s[0] + small_r[0]
+    small_2 = [remote(small_s.at[1], small_r.at[k], m.z_peers[k - 1]) for k in (1, 2, 3)]
     scatter.out(1)
     scatter.out(0)
-    above = [z_sum(r.above_s, above[h], 1, h) for h in range(2)]
-    rows_out((1, 2))
-    arrived(small_1)
-    small_s[1] = small_s[0] + small_r[0]
-    small_2 = remote(small_s.at[1], small_r.at[1], m.x_peer)
+    rows_part(1)
+    rows_part(2)
+    arrived(*small_2)
+    small_s[2] = small_s[1] + small_r[1] + small_r[2] + small_r[3]
     scatter.turn(1)
+    small_3 = remote(small_s.at[2], small_r.at[4], m.x_peer)
     scatter.turn(0)
-    rows_turn()
+    rows_send(1, 2)
     above = [core_out(above[h], 1, h) for h in range(2)]
     need(*swaps_in)
-    e_copies = [remote(r.e_s.at[l, c], r.e_s.at[l, c], m.sibling) for l in range(2)]
+    e_copies = [remote(r.e_s.at[i, 1, c], r.e_s.at[i, 1, c], m.sibling) for i in range(2)]
     rows_own()
-    arrived(small_2)
-    small_s[2] = small_s[1] + small_r[1]
-    small_3 = remote(small_s.at[2], small_r.at[2], m.y_peer)
     scatter.end(1)
     piece_1 = z_out(r.piece, 0, 1)
     scatter.end(0)
     piece_0 = z_out(r.piece, 0, 0)
     arrived(small_3)
-    small_s[3] = small_s[2] + small_r[2]
-    last = [remote(small_s.at[3], small_r.at[2 + k], m.z_peers[k - 1]) for k in (1, 2, 3)]
+    small_s[3] = small_s[2] + small_r[4]
+    rows_turn()
+    small_4 = remote(small_s.at[3], small_r.at[5], m.y_peer)
     piece_1 = z_sum(r.piece, piece_1, 0, 1)
     piece_0 = z_sum(r.piece, piece_0, 0, 0)
-    arrived(*above, *e_copies)
-    saved = [local(both.at[1], r.g1), local(r.e_s, r.e)]
+    e_scatter.end()
+    for i in range(2):
+        r.e_s[i, 0, c] = r.e_own[i]
+        e_copies.append(remote(r.e_s.at[i, 0, c], r.e_s.at[i, 0, c], m.sibling))
+    arrived(*e_copies)
+    saved = [local(r.e_s.at[0], r.e_up), local(r.e_s.at[1], r.e_down)]
     piece_1 = core_out(piece_1, 0, 1)
     piece_0 = core_out(piece_0, 0, 0)
     rows_end()
-    arrived(*last)
-    r.small[...] = small_s[3] + small_r[3] + small_r[4] + small_r[5]
-    arrived(piece_1, piece_0)
-    saved.append(local(both.at[0], r.g0))
+    arrived(*above, piece_1, piece_0)
+    saved.append(local(both, r.g))
+    arrived(small_4)
+    r.small[...] = small_s[3] + small_r[5]
     m.finish()
     need(*saved)
 
@@ -1051,14 +1130,11 @@
         p1=some, p2=some, p3=some, row_in=low_vmem(6, tokens // 2, width),
     )
     if full:
-        ins.update(above=(above, ANY), small_in=(small, VMEM), e0=(swaps[0], ANY), e1=(swaps[1], ANY))
-        e_dims = (2, 2) + swaps[0].shape
-        outs.update(
-            g0=(low_shape(2, half, width), ANY), g1=(low_shape(2, half, width), ANY), e=(low_shape(*e_dims), ANY),
-            small=(shape(small.shape, F32), VMEM),
-        )
+        ins.update(above=(above, ANY), small_in=(small, VMEM), e0=(swaps[0], ANY), e1=(swaps[1], ANY), from_x=(swaps[2], ANY), from_y=(swaps[3], ANY))
+        twice = (low_shape(2, 2, half, width), ANY)
+        outs.update(g=twice, e_up=twice, e_down=twice, small=(shape(small.shape, F32), VMEM))
         scratch.update(
-            scatter_scratch(peers, half, width), above_s=low_vmem(half, width), e_s=low_vmem(*e_dims),
+            scatter_scratch(peers, half, width), **expert_scatter_scratch(half, width), above_s=low_vmem(half, width), e_s=low_vmem(2, 2, 2, half, width),
             small_s=pltpu.VMEM((4,) + small.shape, F32), small_r=pltpu.VMEM((6,) + small.shape, F32),
             z_in=low_vmem(4, 3, half // 8, width), both=low_vmem(2, 2, half, width),
         )
@@ -1071,7 +1147,7 @@
             size = out.shape[0] // CUTS
             scratch.update(out_s=low_vmem(size, width), back=low_vmem(3, size, width))
     return run_kernel(
-        project_back_part, ins, outs, scratch, 4 + full, 4 * rows * width * width, 24, 64, full=full, returns=returns
+        project_back_part, ins, outs, scratch, 4 + full, 4 * rows * width * width, 32, 96, full=full, returns=returns
     )
 
 
@@ -1140,12 +1216,6 @@
     return out.reshape((lax.axis_size(DP), lax.axis_size(TENSOR)) + x.shape)
 
 
-def scatter_experts(x):
-    if x.ndim == 4:
-        return lax.psum_scatter(x, TENSOR, scatter_dimension=0, tiled=True)[0]
-    return scatter_all(x)
-
-
 def scatter_all(x):
     flat = x.reshape((-1,) + x.shape[2:])
     return lax.psum_scatter(flat, (DP, TENSOR), scatter_dimension=0, tiled=True)[0]
@@ -1180,8 +1250,8 @@
 
     stream = hidden_in.astype(F32)
     kept = []
-    packed = [pack_attention(w_qkv[d], w_out[d]) for d in range(depth_total)]
-    own = [(w_in[d, 0], w_down[d, 0]) for d in range(depth_total)]
+    turned = (w_qkv.transpose(0, 2, 3, 1), w_out)
+    own = (w_in, w_down)
     weights = None
     for depth in range(depth_total):
         gain_att, gain_ffn = norm_att[depth].astype(F32), norm_ffn[depth].astype(F32)
@@ -1189,8 +1259,8 @@
         last = depth + 1 == depth_total
         inverse_att = inverse_rms(stream)
         normed = (stream * inverse_att * gain_att).astype(BF16)
-        proj = project(normed, packed[0] if depth == 0 else weights, depth == 0, peers)
-        w_here = None if experts == CUTS else gather_all(pack_experts(*own[depth]))
+        proj = project(normed, turned if depth == 0 else weights, depth == 0, peers)
+        w_here = None if experts == CUTS else gather_all(pack_experts(w_in[depth, 0], w_down[depth, 0]))
         heads, lse = attend(table, proj.q, proj.k, proj.v)
         after_att = stream + dot(heads, proj.w_all[3])
         inverse_ffn = inverse_rms(after_att)
@@ -1199,15 +1269,15 @@
         gate = jnp.sum(jnp.where(chosen, router, 0.0), axis=1, keepdims=True)
         if last:
             d_low = (gate * cotangent).astype(BF16)
-            held = experts_both(w_here, own[depth], plan, token_rows, d_low, routes[depth], experts, capacity)
+            held = experts_both(w_here, own, plan, token_rows, d_low, routes[depth], experts, capacity, depth)
             if experts != CUTS:
                 back = return_rows(plan[1], held.out, experts, capacity).astype(BF16)
         else:
-            back, held = experts_forward(plan, token_rows, experts, capacity, w_here, own[depth], packed[depth + 1])
+            back, held = experts_forward(plan, token_rows, experts, capacity, w_here, own, turned, depth)
             if experts == CUTS:
                 weights = held.next_all.reshape((2, peers, 1) + held.next_all.shape[1:])
             else:
-                weights = gather_all(own_half(packed[depth + 1]))[:, :, None]
+                weights = gather_all(own_half(pack_attention(w_qkv[depth + 1], w_out[depth + 1])))[:, :, None]
         kept.append((stream, inverse_att, proj, heads, lse, after_att, inverse_ffn, gate, held))
         if not last:
             stream = after_att + gate * back.astype(F32)
@@ -1230,12 +1300,11 @@
         dq, dk, dv = attend_back(table, proj.q, proj.k, proj.v, d_heads, heads, lse)
         args = (proj.w_all, dq, dk, dv, proj.n, heads, d_att)
         if depth == 0 and experts == CUTS:
-            grads_e[0] = scatter_experts(held.grads)
+            swaps = (held.grads, held.e_summed, xperm(held.to_x, TENSOR, 1), xperm(held.to_y, TENSOR, 2))
             lines = lambda n: jnp.zeros((n, width), F32)
             part = jnp.concatenate([held.small[: experts + 1], lines(3), smalls[1], lines(2)], axis=0)
-            got = project_back(*args, above=above, small=part, swaps=grads_e)
-            grads_a = [got.g0, got.g1]
-            grads_e = [got.e[0], got.e[1]]
+            got = project_back(*args, above=above, small=part, swaps=swaps)
+            grads_a, grads_e = got.g, (got.e_up, got.e_down)
             total = got.small
             small = jnp.stack([
                 jnp.concatenate([total[: experts + 1], total[7:8]], axis=0), total[8 : 8 + experts + 2]
@@ -1252,18 +1321,18 @@
                 grads_a[depth + 1] = swap_cores(lax.psum(above, EXPERT))
             above = got.pack.reshape((2, peers) + got.pack.shape[1:])
             if experts == CUTS:
-                above = got.pack
+                above = (got.pack, held.grads)
+            else:
+                grads_e[depth] = scatter_all(after(held.grads, got.dn))
             smalls[depth] = jnp.concatenate([held.small[: experts + 1], got.att[:1]], axis=0)
-            grads_e[depth] = scatter_experts(after(held.grads, got.dn))
             if depth == 0:
                 grads_a[0] = swap_cores(lax.psum(scatter_all(above), EXPERT))
                 small = sum_small(jnp.stack(smalls))
-                grads_e = [swap_cores(g) for g in grads_e]
+                grads_e = jnp.stack([swap_cores(g) for g in grads_e]).transpose(2, 0, 1, 3, 4)
+                grads_a = jnp.stack(grads_a)
         upstream = dx1 + norm_backward(got.dn, stream, inverse_att, gain_att)
-    grad_up, grad_down = [
-        jnp.stack([g[:, i].reshape(width, width) for g in grads_e])[:, None].astype(F32) for i in range(2)
-    ]
-    grads_a = jnp.stack([g.reshape(width, width) for g in grads_a]).astype(F32)
+    grad_up, grad_down = [g.reshape(depth_total, 1, width, width).astype(F32) for g in grads_e]
+    grads_a = grads_a.reshape(depth_total, width, width).astype(F32)
     grad_mix = grads_a[:, : 3 * shard].reshape(depth_total, 3, shard, width).transpose(0, 3, 1, 2)
     grad_out = grads_a[:, 3 * shard :]
     grad_route = small[:, :experts].transpose(0, 2, 1)

time: 740 us -> 683 us (0.923)
  Pallas kernels: 635 us -> 605 us
  between operations: 14.8 us -> 1.51 us
    pallas_call x2, Pallas kernels: 92.8 us -> 62.4 us  [attend_back(): pl.pallas_call(attend_back_kernel, grid_spec=pltpu.PrefetchScalarGridSpec...]
    pallas_call x7, Pallas kernels: 496 us -> 504 us  [run_kernel(): pl.pallas_call(kernel, in_specs=[spec for _, spec in ins.values()], out_s...]
    pallas_call x2, Pallas kernels: 46.5 us -> 38.7 us  [attend(): pl.pallas_call(attend_kernel, grid_spec=pltpu.PrefetchScalarGridSpec(num_...]
  transfers between devices with their start and end apart: 2 -> 2, of which waited for: 1 -> 0; matrix products, arithmetic and copies ran while one was open for 2% -> 1% of each run, Pallas kernels for 16% -> 5%
where the time goes in v4:
time: 683 us; the launch traced here: 674 us
  Pallas kernels  605 us (89%)
  other arithmetic  34.7 us (5%)
  local copies, waits for them, and re-layouts  17.2 us (3%)
  matrix products  13.6 us (2%)
    pallas_call x7, Pallas kernels, run_kernel(): pl.pallas_call(kernel, in_specs=[spec for _, spec in ins.values()], out_s...  504 us
    pallas_call x2, Pallas kernels, attend_back(): pl.pallas_call(attend_back_kernel, grid_spec=pltpu.PrefetchScalarGridSpec...  62.4 us
    pallas_call x2, Pallas kernels, attend(): pl.pallas_call(attend_kernel, grid_spec=pltpu.PrefetchScalarGridSpec(num_...  38.7 us
  transfers between devices with their start and end apart: 2, of which 0 were waited for; matrix products, arithmetic and copies ran while one was open for 1% of the time, Pallas kernels for 5%

profile of v4, /device:TPU:1, one launch (start us, length us, event | category | flops | bytes accessed | tf_op | source)
XLA Modules:
  0.0 674.4 jit_solution(6437970878467187028)
XLA Ops:
  0.8 0.9 slice.87
  1.7 0.8 slice.86
  2.8 0.7 slice_reduce_fusion
  3.5 0.3 fusion.18
  3.8 0.3 fusion.19
  4.1 0.7 bitcast_add_fusion
  4.8 1.3 bitcast_add_fusion.1
  6.1 0.8 select_reduce_fusion.2
  7.4 1.5 fusion.1
  8.8 0.6 pad_add_fusion.table
  9.5 1.2 fusion.3.refs_0_
  10.7 59.5 %project_part.2 = (bf16[640,768]{1,0:T(8,128)(2,1)}, bf16[2560,768]{1,0:T(8,128)(2,1)}, bf16[2560,768]{1,0:T(8,128)(2,1)}, bf16[2560,768]{1,0:T(8,128)(2,1)}, bf16[4,768,768]{2,1,0:T(8,128)(2,1)}) custom-call(bf16[640,768]{1,0:T(8,128)(2,1)} %fusion.3.refs_0_, bf16[2,3,192,768]{3,2,1,0:T(8,128)(2,1)} %bitcast.100, bf16[2,192,768]{2,1,0:T(8,128)(2,1)} %refs_6_.1), custom_call_target="tpu_custom_call" | custom-call | flops 53084160 | tf_op jit(solution)/shard_map/project_part/pallas_call | solution.py:262
  70.3 19.4 %attend.2 = (bf16[640,768]{1,0:T(8,128)(2,1)}, f32[6,8,640]{2,1,0:T(8,128)}) custom-call(s32[45]{0:T(128)} %pad_add_fusion.table, bf16[640,768]{1,0:T(8,128)(2,1)} %get-tuple-element.56.q_ref, bf16[2560,768]{1,0:T(8,128)(2,1)} %get-tuple-element.57.k_ref, bf16[2560,768]{1,0:T(8,128)(2,1)} %get-tuple-element.58.v_ref), custom_call_target="tpu_custom_call" | custom-call | flops 78643200 | bytes 122880 | tf_op jit(solution)/shard_map/attend/pallas_call | solution.py:129
  89.7 2.6 multiply_reduce_fusion.5
  92.4 1.1 copy.47.refs_3_.refs_2_
  93.4 0.2 multiply_convert_fusion.3.refs_4_
  93.7 0.4 fusion.44
  94.2 0.5 copy-done.7
  94.6 87.9 %expert_part.3 = (bf16[2,4,2,384,768]{4,3,2,1,0:T(8,128)(2,1)}, bf16[640,768]{1,0:T(8,128)(2,1)}, bf16[960,768]{1,0:T(8,128)(2,1)}, bf16[960,768]{1,0:T(8,128)(2...) custom-call(bf16[2,1,768,768]{3,2,1,0:T(8,128)(2,1)} %refs_0_.3, ...), custom_call_target="tpu_custom_call" | custom-call | flops 35389440 | tf_op jit(solution)/shard_map/expert_part/pallas_call | solution.py:262
  182.6 1.7 multiply_reduce_fusion.4
  184.3 1.2 multiply_convert_fusion.2.refs_0_
  185.5 34.1 %project_part.3 = (bf16[640,768]{1,0:T(8,128)(2,1)}, bf16[2560,768]{1,0:T(8,128)(2,1)}, bf16[2560,768]{1,0:T(8,128)(2,1)}, bf16[2560,768]{1,0:T(8,128)(2,1)}, bf16[4,768,768]{2,1,0:T(8,128)(2,1)}) custom-call(bf16[640,768]{1,0:T(8,128)(2,1)} %multiply_convert_fusion.2.refs_0_, bf16[2,4,1,384,768]{4,3,2,1,0:T(8,128)(2,1)} %bitcast.102), custom_call_target="tpu_custom_call" | custom-call | flops 53084160 | tf_op jit(solution)/shard_map/project_part/pallas_call | solution.py:262
  219.6 19.2 %attend.3 = (bf16[640,768]{1,0:T(8,128)(2,1)}, f32[6,8,640]{2,1,0:T(8,128)}) custom-call(s32[45]{0:T(128)} %pad_add_fusion.table, bf16[640,768]{1,0:T(8,128)(2,1)} %get-tuple-element.63.q_ref, bf16[2560,768]{1,0:T(8,128)(2,1)} %get-tuple-element.64.k_ref, bf16[2560,768]{1,0:T(8,128)(2,1)} %get-tuple-element.65.v_ref), custom_call_target="tpu_custom_call" | custom-call | flops 78643200 | bytes 122880 | tf_op jit(solution)/shard_map/attend/pallas_call | solution.py:129
  238.8 2.6 multiply_reduce_fusion.3
  241.4 0.2 multiply_convert_fusion.1.refs_4_
  241.7 0.4 fusion.45
  242.0 0.6 copy-done
  242.7 0.3 copy-done.6
  243.0 0.9 copy.49.refs_3_.refs_8_
  244.1 2.4 fusion.refs_5_
  246.5 0.7 pad.7.refs_6_
  247.2 113.2 %expert_part.4 = (bf16[640,768]{1,0:T(8,128)(2,1)}, bf16[960,768]{1,0:T(8,128)(2,1)}, bf16[4,2,384,768]{3,2,1,0:T(8,128)(2,1)}, f32[8,768]{1,0:T(8,128)}) custom-call(bf16[2,1,768,768]{3,2,1,0:T(8,128)(2,1)} %refs_0_.3, bf16[2,1,768,768]{3,2,1,0:T(8,128)(2,1)} %refs_1_.3, s32[1,640]{1,0:T(1,128)} %get-tuple-element.162.refs_2_, ...), custom_call_target="tpu_custom_call" | custom-call | flops 35389440 | tf_op jit(solution)/shard_map/expert_part/pallas_call | solution.py:262
  360.4 1.7 multiply_reduce_fusion.2
  362.2 0.6 fusion.41.refs_6_
  362.8 3.6 convolution_convert_fusion.1.do_ref
  366.4 31.3 %attend_back.2 = (bf16[640,768]{1,0:T(8,128)(2,1)}, bf16[2560,768]{1,0:T(8,128)(2,1)}, bf16[2560,768]{1,0:T(8,128)(2,1)}) custom-call(s32[45]{0:T(128)} %pad_add_fusion.table, bf16[640,768]{1,0:T(8,128)(2,1)} %get-tuple-element.63.q_ref, bf16[2560,768]{1,0:T(8,128)(2,1)} %get-tuple-element.64.k_ref, bf16[2560,768]{1,0:T(8,128)(2,1)} %get-tuple-element.65.v_ref, ...), custom_call_target="tpu_custom_call" | custom-call | flops 196608000 | bytes 245760 | tf_op jit(solution)/shard_map/attend_back/pallas_call | solution.py:206
  397.7 48.2 %project_back_part.2 = (f32[640,768]{1,0:T(8,128)}, bf16[8,384,768]{2,1,0:T(8,128)(2,1)}, f32[8,768]{1,0:T(8,128)}, bf16[640,768]{1,0:T(8,128)(2,1)}) custom-call(bf16[4,768,768]{2,1,0:T(8,128)(2,1)} %get-tuple-element.67.refs_0_, bf16[640,768]{1,0:T(8,128)(2,1)} %get-tuple-element.70.refs_1_, bf16[2560,768]{1,0:T(8,128)(2,1)} %get-tuple-element.71.refs_2_, ...), custom_call_target="tpu_custom_call" | custom-call | flops 94371840 | tf_op jit(solution)/shard_map/project_back_part/pallas_call | solution.py:262
  446.0 1.8 multiply_reduce_fusion.1
  448.0 0.7 pad.8.refs_4_
  448.7 5.0 multiply_convert_fusion
  453.7 78.9 %expert_part.5 = (bf16[640,768]{1,0:T(8,128)(2,1)}, bf16[4,2,384,768]{3,2,1,0:T(8,128)(2,1)}, f32[8,768]{1,0:T(8,128)}, bf16[384,768]{1,0:T(8,128)(2,1)}, bf16[2...) custom-call(bf16[2,4,2,384,768]{4,3,2,1,0:T(8,128)(2,1)} %get-tuple-element.77.refs_0_, ...), custom_call_target="tpu_custom_call" | custom-call | flops 35389440 | tf_op jit(solution)/shard_map/expert_part/pallas_call | solution.py:262
  532.6 2.4 collective-permute-start
  535.1 0.7 slice.103
  535.9 2.0 concatenate.10.refs_8_
  537.8 1.7 multiply_reduce_fusion
  539.7 0.2 copy-done.12
  539.9 0.6 fusion.42
  540.5 3.5 convolution_convert_fusion.do_ref
  544.0 31.1 %attend_back.3 = (bf16[640,768]{1,0:T(8,128)(2,1)}, bf16[2560,768]{1,0:T(8,128)(2,1)}, bf16[2560,768]{1,0:T(8,128)(2,1)}) custom-call(s32[45]{0:T(128)} %pad_add_fusion.table, bf16[640,768]{1,0:T(8,128)(2,1)} %get-tuple-element.56.q_ref, bf16[2560,768]{1,0:T(8,128)(2,1)} %get-tuple-element.57.k_ref, bf16[2560,768]{1,0:T(8,128)(2,1)} %get-tuple-element.58.v_ref, ...), custom_call_target="tpu_custom_call" | custom-call | flops 196608000 | bytes 245760 | tf_op jit(solution)/shard_map/attend_back/pallas_call | solution.py:206
  575.1 82.0 %project_back_part.3 = (f32[640,768]{1,0:T(8,128)}, bf16[2,2,384,768]{3,2,1,0:T(8,128)(2,1)}, bf16[2,2,384,768]{3,2,1,0:T(8,128)(2,1)}, bf16[2,2,384,768]{3,2,1,0:T(8,128)(2,1)}, f32[16,768]{1,0:T(8,128)}) custom-call(bf16[4,768,768]{2,1,0:T(8,128)(2,1)} %get-tuple-element.60.refs_0_, bf16[640,768]{1,0:T(8,128)(2,1)} %get-tuple-element.86.refs_1_, ...), custom_call_target="tpu_custom_call" | custom-call | flops 94371840 | tf_op jit(solution)/shard_map/project_back_part/pallas_call | solution.py:262
  657.1 0.7 slice.104
  657.8 0.7 slice.105
  658.6 0.7 slice_bitcast_fusion
  659.3 2.0 bitcast_convert_fusion.2
  661.3 2.0 slice.112
  663.4 1.1 slice.113
  664.5 0.6 fusion.24
  665.1 0.4 copy-done.16
  665.5 2.5 bitcast_convert_fusion
  668.0 2.5 bitcast_convert_fusion.1
  670.6 0.6 bitcast_divide_fusion
  671.2 0.6 bitcast_divide_fusion.1
  671.8 0.4 fusion.7
  672.2 1.8 fusion.6
  (76 shorter events, 1.8 us)
Async XLA Ops:
  0.6 8.8 %copy-start.5 = (bf16[640,768]{1,0:T(8,128)(2,1)S(1)}, bf16[640,768]{1,0:T(8,128)(2,1)}, u32[]{:S(2)}) copy-start(bf16[640,768]{1,0:T(8,128)(2,1)} %param.13) | copy-start | bytes 2949124
  0.7 8.8 %copy-start.19 = (bf16[2,768]{1,0:T(2,128)(2,1)S(1)}, bf16[2,768]{1,0:T(2,128)(2,1)}, u32[]{:S(2)}) copy-start(bf16[2,768]{1,0:T(2,128)(2,1)} %param.18) | copy-start | bytes 9220
  0.7 8.8 %copy-start.18 = (bf16[2,768]{1,0:T(2,128)(2,1)S(1)}, bf16[2,768]{1,0:T(2,128)(2,1)}, u32[]{:S(2)}) copy-start(bf16[2,768]{1,0:T(2,128)(2,1)} %param.21) | copy-start | bytes 9220
  89.7 3.7 copy-start.17
  92.3 1.8 copy-start.2
  93.7 0.9 copy-start.7
  94.6 88.0 %copy-start.3 = (f32[640,768]{1,0:T(8,128)S(1)}, f32[640,768]{1,0:T(8,128)}, u32[]{:S(2)}) copy-start(f32[640,768]{1,0:T(8,128)} %copy-done.2) | copy-start | bytes 5898244
  241.4 1.3 copy-start
  241.6 1.3 copy-start.6
  247.2 113.2 %copy-start.1 = (f32[640,768]{1,0:T(8,128)S(1)}, f32[640,768]{1,0:T(8,128)}, u32[]{:S(2)}) copy-start(f32[640,768]{1,0:T(8,128)} %copy-done) | copy-start | bytes 5898244
  360.4 1.7 copy-start.8
  360.4 1.8 copy-start.9
  362.8 3.6 copy-start.13
  453.6 82.2 %copy-start.20 = (f32[8,768]{1,0:T(8,128)S(1)}, f32[8,768]{1,0:T(8,128)}, u32[]{:S(2)}) copy-start(f32[8,768]{1,0:T(8,128)} %get-tuple-element.92) | copy-start | bytes 73732
  453.6 84.2 %copy-start.4 = (f32[640,768]{1,0:T(8,128)S(1)}, f32[640,768]{1,0:T(8,128)}, u32[]{:S(2)}) copy-start(f32[640,768]{1,0:T(8,128)} %copy-done.2) | copy-start | bytes 5898244
  532.6 42.5 %collective-permute-start = (bf16[2,2,192,768]{3,2,1,0:T(8,128)(2,1)}, bf16[2,2,192,768]{3,2,1,0:T(8,128)(2,1)}, u32[]{:S(2)}, u32[]{:S(2)}) collective-permute-start(bf16[2,2,192,768]{3,2,1,0:T(8,128)(2,1)} %get-tuple-element.96), channel_id=1, source_target_pairs={{0,1},{1,0},{2,3},{3,2},{4,5},{5,4},{6,7},{7,6},{8,9},{9,8},{10,11... | collective-permute-start | bytes 3538952 | tf_op jit(solution)/shard_map/ppermute | solution.py:44
  535.0 40.1 %collective-permute-start.1 = (bf16[2,2,192,768]{3,2,1,0:T(8,128)(2,1)}, bf16[2,2,192,768]{3,2,1,0:T(8,128)(2,1)}, u32[]{:S(2)}, u32[]{:S(2)}) collective-permute-start(bf16[2,2,192,768]{3,2,1,0:T(8,128)(2,1)} %get-tuple-element.97), channel_id=1, source_target_pairs={{0,2},{1,3},{2,0},{3,1},{4,6},{5,7},{6,4},{7,5},{8,10},{9,11},{10,... | collective-permute-start | bytes 3538952 | tf_op jit(solution)/shard_map/ppermute | solution.py:44
  537.8 1.8 copy-start.10
  537.8 2.1 copy-start.12
  540.5 3.5 copy-start.14
  663.4 2.1 copy-start.16
  665.5 2.6 copy-start.15
  668.0 3.8 copy-start.11

commit v5 on v4

--- a/solution.py
+++ b/solution.py
@@ -289,12 +289,14 @@
         self.z_peers = [{EXPERT: xor_peer(self.z, k)} for k in (1, 2, 3)]
 
     def local(self, src, dst):
+        assert self.near < self.refs.near.shape[0]
         copy = pltpu.make_async_copy(src, dst, self.refs.near.at[self.near])
         self.near += 1
         copy.start()
         return copy
 
     def remote(self, src, dst, device):
+        assert self.far < self.refs.send.shape[0]
         copy = pltpu.make_async_remote_copy(
             src_ref=src, dst_ref=dst, send_sem=self.refs.send.at[self.far], recv_sem=self.refs.recv.at[self.far],
             device_id=device, device_id_type=MESH,
@@ -481,16 +483,11 @@
     return jnp.where(index == slot_row[...], 1.0, 0.0).astype(BF16)
 
 
-def one_hot_turned(slot_col, k, size):
-    index = lax.broadcasted_iota(jnp.int32, (slot_col.shape[0], size), 1) + k * size
-    return jnp.where(index == slot_col[...], 1.0, 0.0).astype(BF16)
-
-
-def combine(m, slot_col, source, copies, back, size):
-    total = dot(one_hot_turned(slot_col, 0, size), source[pl.ds(0, size), :])
+def combine(m, slot_row, source, copies, back, size):
+    total = dot_tn(one_hot(slot_row, 0, size), source[pl.ds(0, size), :])
     for k in (1, 2, 3):
         m.arrived(copies[k])
-        total = total + dot(one_hot_turned(slot_col, k, size), back[k - 1])
+        total = total + dot_tn(one_hot(slot_row, k, size), back[k - 1])
     return total.astype(BF16)
 
 
@@ -574,7 +571,7 @@
             d_hidden = dot_nt(d, down[at, :])
             slope[cut, at] = (d_hidden * slope[cut, at].astype(F32)).astype(BF16)
         x = rows[cut, :]
-        logits = dot(x, r.route[...])
+        logits = dot(x, r.route[depth])
         lane = lax.broadcasted_iota(jnp.int32, logits.shape, 1)
         logits = jnp.where(lane < experts, logits, NEG)
         router = jnp.exp(logits - jnp.max(logits, axis=1, keepdims=True))
@@ -582,7 +579,7 @@
         amount = jnp.sum(outs[cut, :].astype(F32) * d.astype(F32), axis=1, keepdims=True)
         d_log = (amount * (jnp.where(lane == m.z, 1.0, 0.0) - router)).astype(BF16)
         r.log_s[cut, :] = d_log
-        d_rows = dot_nt(slope[cut, :], up[...]) + dot_nt(d_log, r.route[...])
+        d_rows = dot_nt(slope[cut, :], up[...]) + dot_nt(d_log, r.route[depth])
         r.back_s[cut, :] = d_rows.astype(BF16)
         return jnp.sum(d_rows * x.astype(F32), axis=0, keepdims=True)
 
@@ -597,13 +594,15 @@
         fetch = Gather(m, r.next_s)
     if hosted:
         first = {}
-        for k, device in ((1, m.x_peer), (2, m.y_peer)):
-            mine = pl.ds(pl.multiple_of(m.c * half, half), half)
-            first[k] = [m.remote(own_up.at[mine], up_at(m.c, m.t), device), m.remote(own_down.at[mine], down_at(m.c, m.t), device)]
+        mine = pl.ds(pl.multiple_of(m.c * half, half), half)
+        for at, own in ((up_at, own_up), (down_at, own_down)):
+            for k, device in ((1, m.x_peer), (2, m.y_peer)):
+                first[at, k] = m.remote(own.at[mine], at(m.c, m.t), device)
     if reduces:
         scatter = Scatter(m, r.pack_s, r.core_in, r.g_in, r.piece)
         pack_load = m.local(r.pack, r.pack_s)
         e_scatter = ExpertScatter(m, r.e_pack, r.e_own, r.e_keep, r.e_in)
+        e_scatter.out()
         e_loads = e_scatter.load()
     if remote and forward:
         sent_x = dispatch(r.x, rows, r.stage_x)
@@ -616,38 +615,42 @@
     m.need(*loads, *weight_loads)
     if hosted:
         tens = [m.t] + [xor_peer(m.t, k) for k in (1, 2, 3)]
-        onward, swaps = [], {}
-
-        def pass_on(k, device, start):
-            m.arrived(*first[k])
-            for at in (up_at, down_at):
-                piece = at(m.c, tens[k], start, half // 2)
-                onward.append(m.remote(piece, piece, device))
-            swap(k)
-
-        def swap(k):
-            swaps[k] = [m.remote(at(m.c, tens[k]), at(m.c, tens[k]), m.sibling) for at in (up_at, down_at)]
+        onward, swaps = {up_at: [], down_at: []}, {}
+
+        def pass_on(at):
+            for k, device in ((1, m.y_peer), (2, m.x_peer)):
+                m.arrived(first[at, k])
+                piece = at(m.c, tens[k], (k - 1) * (half // 2), half // 2)
+                onward[at].append(m.remote(piece, piece, device))
+                swap(at, k)
+
+        def swap(at, k):
+            swaps[at, k] = m.remote(at(m.c, tens[k]), at(m.c, tens[k]), m.sibling)
 
         forward_peer(cuts[0], tens[0])
         m.arrived(sent_x[1])
         forward_peer(cuts[1], tens[0])
-        pass_on(1, m.y_peer, 0)
-        pass_on(2, m.x_peer, half // 2)
-        if fetches:
-            m.need(*next_loads)
-            fetch.out()
+        pass_on(up_at)
+        pass_on(down_at)
         m.arrived(sent_x[2], sent_x[3])
         forward_peer(pl.ds(2 * size, 2 * size), tens[0])
         for k in (1, 2, 3):
             if k == 3:
-                m.arrived(*onward)
-                swap(3)
-            m.arrived(*swaps[k])
-            forward_peer(pl.ds(0, count), tens[k])
+                m.arrived(*onward[up_at])
+                swap(up_at, 3)
+            m.arrived(swaps[up_at, k])
+            if k < 3:
+                forward_peer(pl.ds(0, count), tens[k])
+        m.arrived(*onward[down_at])
+        swap(down_at, 3)
         if fetches:
-            fetch.turn()
+            m.need(*next_loads)
+            fetch.out()
         for first_k in (2, 0):
-            forward_down(pl.ds(first_k * size, 2 * size))
+            pair = pl.ds(first_k * size, 2 * size)
+            forward_peer(pair, tens[3])
+            m.arrived(*[swaps[down_at, k] for k in (1, 2, 3)])
+            forward_down(pair)
             for k in (first_k, first_k + 1):
                 if k and not backward:
                     returns[k] = give_back(outs, k)
@@ -656,6 +659,7 @@
                 for t in range(peers):
                     saves += [m.local(up_at(c, t), r.w.at[c, t, 0]), m.local(down_at(c, t), r.w.at[c, t, 1])]
         if fetches:
+            fetch.turn()
             fetch.end()
             saves.append(m.local(r.next_s, r.next_all))
     elif forward:
@@ -682,7 +686,6 @@
             if reduces and k == 0:
                 scatter.out(0)
                 scatter.out(1)
-                e_scatter.out()
             if reduces and k == 2:
                 scatter.turn(0)
                 scatter.turn(1)
@@ -697,7 +700,7 @@
         r.small[...] = jnp.concatenate([route[:experts], gain, jnp.zeros((pad, width), F32)], axis=0)
         swapped = []
         if hosted:
-            m.gone(*onward, *[copy for k in (1, 2, 3) for copy in swaps[k]])
+            m.gone(*onward[up_at], *onward[down_at], *swaps.values())
         for t in range(peers):
             at = pl.ds(t * width, width)
             up[:, at] = dot(r.turned[...], slope[:, at]).astype(BF16)
@@ -724,7 +727,7 @@
                 for i, at in enumerate((up_at, down_at)):
                     for box, k, start in ((r.to_x.at[0], 3, 0), (r.to_x.at[1], 1, 0), (r.to_y.at[0], 3, 1), (r.to_y.at[1], 2, 1)):
                         saves.append(m.local(at(m.c, xor_peer(m.t, k), start * (half // 2), half // 2), box.at[i]))
-        r.result[...] = combine(m, r.slot_col, r.back_s if backward else outs, returns, r.back, size)
+        r.result[...] = combine(m, r.slot_row, r.back_s if backward else outs, returns, r.back, size)
     m.finish()
     m.need(*saves)
 
@@ -746,7 +749,7 @@
     else:
         ins.update(w=(w, ANY))
     if remote:
-        ins.update(slot_row=(slots[None, :], VMEM), slot_col=(slots[:, None], VMEM))
+        ins.update(slot_row=(slots[None, :], VMEM))
     if forward:
         ins.update(x=(x, data))
     if backward:
@@ -761,7 +764,7 @@
             outs.update(rows=(rows_shape, ANY), hidden=(inner_shape, ANY), slope=(inner_shape, ANY))
     if backward:
         outs.update(grads=(low_shape(peers, 2, half, width) if remote else w_shape, ANY))
-        outs.update(small=(jax.ShapeDtypeStruct((-(-(experts + 1) // 8) * 8, width), F32), VMEM))
+        outs.update(small=(jax.ShapeDtypeStruct((-(-(experts + 2) // 8) * 8, width), F32), VMEM))
     scratch = dict(
         up=low_vmem(width, inner), down=low_vmem(inner, width), hidden_s=low_vmem(count, inner), slope_s=low_vmem(count, inner),
         rows_s=low_vmem(count, width), outs_s=low_vmem(count, width),
@@ -805,12 +808,12 @@
     return return_rows(plan[1], got.out, experts, capacity).astype(BF16), got
 
 
-def experts_backward(plan, d_low, kept, route, experts, capacity, pack):
+def experts_backward(plan, d_low, kept, route, experts, capacity, pack, depth):
     count = experts * capacity
     if experts == CUTS:
-        return expert_call(plan, experts, count, w=kept.w, g=d_low, kept=kept, route=route, pack=pack)
+        return expert_call(plan, experts, count, w=kept.w, g=d_low, kept=kept, route=route, pack=pack, depth=depth)
     d_sent = send_rows(plan[1], d_low, experts, capacity)
-    got = expert_call(plan, experts, count, w=kept.w, g=d_sent, kept=kept, route=route)
+    got = expert_call(plan, experts, count, w=kept.w, g=d_sent, kept=kept, route=route, depth=depth)
     got.result = return_rows(plan[1], got.result, experts, capacity).astype(BF16)
     got.summed = scatter_all(pack)
     return got
@@ -822,7 +825,7 @@
         return expert_call(plan, experts, count, own=own, x=token_rows, g=d_low, route=route, depth=depth)
     rows = send_rows(plan[1], token_rows, experts, capacity)
     d_sent = send_rows(plan[1], d_low, experts, capacity)
-    got = expert_call(plan, experts, count, w=w, x=rows, g=d_sent, route=route)
+    got = expert_call(plan, experts, count, w=w, x=rows, g=d_sent, route=route, depth=depth)
     got.result = return_rows(plan[1], got.result, experts, capacity).astype(BF16)
     return got
 
@@ -862,7 +865,6 @@
             first[1, h] = m.remote(mine, mine, m.x_peer)
             first[2, h] = m.remote(mine, mine, m.y_peer)
     a_low, b_high = send(0, 0, 1, m.x_peer), send(0, 1, 2, m.y_peer)
-    a_high, b_low = send(0, 1, 1, m.x_peer), send(0, 0, 2, m.y_peer)
     if hosted:
         for h in range(2):
             for k, onward, part in ((1, m.y_peer, 0), (2, m.x_peer, 1)):
@@ -872,6 +874,7 @@
                 second.append(m.remote(piece, piece, onward))
                 whole = w.at[2 * c + h, at(xor_peer(t, k))]
                 swaps.append(m.remote(whole, whole, m.sibling))
+    a_high, b_low = send(0, 1, 1, m.x_peer), send(0, 0, 2, m.y_peer)
     m.arrived(a_low)
     c_low = send(1, 0, 3, m.y_peer)
     m.arrived(b_high)
@@ -901,6 +904,8 @@
     keys_values(tokens, tokens)
     m.arrived(b_low)
     keys_values(2 * tokens, tokens)
+    r.turned_s[...] = w[3].T
+    kept.append(m.local(r.turned_s, r.out_turned))
     m.arrived(c_low)
     keys_values(3 * tokens, half)
     m.arrived(c_high)
@@ -916,10 +921,11 @@
     outs = dict(
         q=(low_shape(tokens, width), ANY), k=(low_shape(every, width), ANY), v=(low_shape(every, width), ANY),
         n=(low_shape(every, width), ANY), w_all=(low_shape(4, width, width), ANY),
+        out_turned=(low_shape(width, width), ANY),
     )
     scratch = dict(
         n_s=low_vmem(every, width), w_s=low_vmem(4, width, width), q_s=low_vmem(tokens, width),
-        k_s=low_vmem(every, width), v_s=low_vmem(every, width),
+        k_s=low_vmem(every, width), v_s=low_vmem(every, width), turned_s=low_vmem(width, width),
     )
     given = dict(w_qkv=(w[0], ANY), w_out=(w[1], ANY)) if hosted else dict(w=(w, ANY))
     return run_kernel(
@@ -1026,7 +1032,7 @@
         saved = local(pack, r.pack)
         if returns:
             need(out_in)
-            r.result[...] = combine(m, r.slot_col, r.out_s, copies, r.back, size)
+            r.result[...] = combine(m, r.slot_row, r.out_s, copies, r.back, size)
         rows_end()
         m.finish()
         need(saved)
@@ -1106,7 +1112,12 @@
     piece_0 = core_out(piece_0, 0, 0)
     rows_end()
     arrived(*above, piece_1, piece_0)
-    saved.append(local(both, r.g))
+    for l in range(2):
+        saved += [
+            local(both.at[l, 0], r.g_mix.at[l, pl.ds(0, 2 * shard)]),
+            local(both.at[l, 1, pl.ds(0, shard)], r.g_mix.at[l, pl.ds(2 * shard, shard)]),
+            local(both.at[l, 1, pl.ds(shard, shard)], r.g_out.at[l]),
+        ]
     arrived(small_4)
     r.small[...] = small_s[3] + small_r[5]
     m.finish()
@@ -1132,7 +1143,10 @@
     if full:
         ins.update(above=(above, ANY), small_in=(small, VMEM), e0=(swaps[0], ANY), e1=(swaps[1], ANY), from_x=(swaps[2], ANY), from_y=(swaps[3], ANY))
         twice = (low_shape(2, 2, half, width), ANY)
-        outs.update(g=twice, e_up=twice, e_down=twice, small=(shape(small.shape, F32), VMEM))
+        outs.update(
+            g_mix=(low_shape(2, 3 * width // 4, width), ANY), g_out=(low_shape(2, width // 4, width), ANY), e_up=twice, e_down=twice,
+            small=(shape(small.shape, F32), VMEM),
+        )
         scratch.update(
             scatter_scratch(peers, half, width), **expert_scatter_scratch(half, width), above_s=low_vmem(half, width), e_s=low_vmem(2, 2, 2, half, width),
             small_s=pltpu.VMEM((4,) + small.shape, F32), small_r=pltpu.VMEM((6,) + small.shape, F32),
@@ -1142,12 +1156,12 @@
         outs.update(pack=(low_shape(2 * peers, half, width), ANY), att=(shape((8, width), F32), VMEM))
         scratch.update(pack_s=low_vmem(2 * peers, half, width))
         if returns:
-            ins.update(out=(out, ANY), slot_col=(slots[:, None], VMEM))
+            ins.update(out=(out, ANY), slot_row=(slots[None, :], VMEM))
             outs.update(result=(low_shape(tokens, width), VMEM))
             size = out.shape[0] // CUTS
             scratch.update(out_s=low_vmem(size, width), back=low_vmem(3, size, width))
     return run_kernel(
-        project_back_part, ins, outs, scratch, 4 + full, 4 * rows * width * width, 32, 96, full=full, returns=returns
+        project_back_part, ins, outs, scratch, 4 + full, 4 * rows * width * width, 40, 96, full=full, returns=returns
     )
 
 
@@ -1245,7 +1259,7 @@
     shard = width // peers
     table = path_table(segment_ids, path_pos, parent_ids, peers)
     plans = [dispatch_plan(route_ids[d, :, 0], experts, capacity) for d in range(depth_total)]
-    routes = [jnp.pad(w_route[d], ((0, 0), (0, BLK - experts))) for d in range(depth_total)]
+    routes = jnp.pad(w_route, ((0, 0), (0, 0), (0, BLK - experts)))
     cotangent = cotangent.astype(F32)
 
     stream = hidden_in.astype(F32)
@@ -1269,7 +1283,7 @@
         gate = jnp.sum(jnp.where(chosen, router, 0.0), axis=1, keepdims=True)
         if last:
             d_low = (gate * cotangent).astype(BF16)
-            held = experts_both(w_here, own, plan, token_rows, d_low, routes[depth], experts, capacity, depth)
+            held = experts_both(w_here, own, plan, token_rows, d_low, routes, experts, capacity, depth)
             if experts != CUTS:
                 back = return_rows(plan[1], held.out, experts, capacity).astype(BF16)
         else:
@@ -1292,23 +1306,20 @@
         last = depth + 1 == depth_total
         if not last:
             d_low = (gate * upstream).astype(BF16)
-            held = experts_backward(plan, d_low, held, routes[depth], experts, capacity, above)
+            held = experts_backward(plan, d_low, held, routes, experts, capacity, above, depth)
             above = held.summed
         dx1 = upstream + norm_backward(held.result.astype(F32), after_att, inverse_ffn, gain_ffn)
         d_att = dx1.astype(BF16)
-        d_heads = dot_nt(d_att, proj.w_all[3]).astype(BF16)
+        d_heads = dot(d_att, proj.out_turned).astype(BF16)
         dq, dk, dv = attend_back(table, proj.q, proj.k, proj.v, d_heads, heads, lse)
         args = (proj.w_all, dq, dk, dv, proj.n, heads, d_att)
         if depth == 0 and experts == CUTS:
             swaps = (held.grads, held.e_summed, xperm(held.to_x, TENSOR, 1), xperm(held.to_y, TENSOR, 2))
-            lines = lambda n: jnp.zeros((n, width), F32)
-            part = jnp.concatenate([held.small[: experts + 1], lines(3), smalls[1], lines(2)], axis=0)
+            part = jnp.concatenate([held.small, smalls[1]], axis=0)
             got = project_back(*args, above=above, small=part, swaps=swaps)
-            grads_a, grads_e = got.g, (got.e_up, got.e_down)
-            total = got.small
-            small = jnp.stack([
-                jnp.concatenate([total[: experts + 1], total[7:8]], axis=0), total[8 : 8 + experts + 2]
-            ])
+            grads_e = (got.e_up, got.e_down)
+            grad_mix, grad_out = got.g_mix.astype(F32), got.g_out.astype(F32)
+            small = got.small.reshape(depth_total, -1, width)
         else:
             if last and experts == CUTS:
                 got = project_back(*args, out=held.out, slots=plan[0])
@@ -1324,20 +1335,20 @@
                 above = (got.pack, held.grads)
             else:
                 grads_e[depth] = scatter_all(after(held.grads, got.dn))
-            smalls[depth] = jnp.concatenate([held.small[: experts + 1], got.att[:1]], axis=0)
+            line = lax.broadcasted_iota(jnp.int32, held.small.shape, 0)
+            smalls[depth] = jnp.where(line == held.small.shape[0] - 1, got.att[:1], held.small)
             if depth == 0:
                 grads_a[0] = swap_cores(lax.psum(scatter_all(above), EXPERT))
                 small = sum_small(jnp.stack(smalls))
                 grads_e = jnp.stack([swap_cores(g) for g in grads_e]).transpose(2, 0, 1, 3, 4)
-                grads_a = jnp.stack(grads_a)
+                grads_a = jnp.stack(grads_a).reshape(depth_total, width, width).astype(F32)
+                grad_mix, grad_out = grads_a[:, : 3 * shard], grads_a[:, 3 * shard :]
         upstream = dx1 + norm_backward(got.dn, stream, inverse_att, gain_att)
     grad_up, grad_down = [g.reshape(depth_total, 1, width, width).astype(F32) for g in grads_e]
-    grads_a = grads_a.reshape(depth_total, width, width).astype(F32)
-    grad_mix = grads_a[:, : 3 * shard].reshape(depth_total, 3, shard, width).transpose(0, 3, 1, 2)
-    grad_out = grads_a[:, 3 * shard :]
+    grad_mix = grad_mix.reshape(depth_total, 3, shard, width).transpose(0, 3, 1, 2)
     grad_route = small[:, :experts].transpose(0, 2, 1)
     grad_ffn = small[:, experts] / norm_ffn.astype(F32)
-    grad_att = small[:, experts + 1] / norm_att.astype(F32)
+    grad_att = small[:, -1] / norm_att.astype(F32)
     return (hidden_out, upstream, grad_att, grad_mix, grad_out, grad_ffn, grad_route, grad_up, grad_down)
 
 

time: 683 us -> 654 us (0.958)
  Pallas kernels: 605 us -> 586 us
    pallas_call x7, Pallas kernels: 504 us -> 485 us  [run_kernel(): pl.pallas_call(kernel, in_specs=[spec for _, spec in ins.values()], out_s...]
    dot_general x2 -> x0, matrix products: 7.1 us -> none  [dot_nt(): return lax.dot_general(a, b, NT, preferred_element_type=F32)]
where the time goes in v5:
time: 654 us; the launch traced here: 647 us
  Pallas kernels  586 us (90%)
  other arithmetic  35.9 us (5%)
  local copies, waits for them, and re-layouts  11.3 us (2%)
  matrix products  10.3 us (2%)
    pallas_call x7, Pallas kernels, run_kernel(): pl.pallas_call(kernel, in_specs=[spec for _, spec in ins.values()], out_s...  485 us
    pallas_call x2, Pallas kernels, attend_back(): pl.pallas_call(attend_back_kernel, grid_spec=pltpu.PrefetchScalarGridSpec...  62.5 us
    pallas_call x2, Pallas kernels, attend(): pl.pallas_call(attend_kernel, grid_spec=pltpu.PrefetchScalarGridSpec(num_...  38.8 us
  transfers between devices with their start and end apart: 2, of which 0 were waited for; matrix products, arithmetic and copies ran while one was open for 1% of the time, Pallas kernels for 5%

profile of v5, /device:TPU:1, one launch (start us, length us, event | category | flops | bytes accessed | tf_op | source)
XLA Modules:
  0.0 647.0 jit_solution(17299164728191446531)
XLA Ops:
  0.7 0.8 slice.61
  1.5 0.1 broadcast_in_dim.115
  1.6 0.8 slice.62
  2.4 0.1 broadcast_in_dim.118
  2.5 0.1 select_reduce_fusion.1
  2.7 0.8 select_reduce_fusion.2
  3.6 0.1 copy.26
  3.9 0.1 eq.80
  3.9 1.5 fusion.1
  5.4 0.6 pad_add_fusion.table
  6.0 0.8 convert_reduce_fusion
  6.8 2.4 fusion.3.refs_0_
  9.3 59.6 %project_part.2 = (bf16[640,768]{1,0:T(8,128)(2,1)}, bf16[2560,768]{1,0:T(8,128)(2,1)}, bf16[2560,768]{1,0:T(8,128)(2,1)}, bf16[2560,768]{1,0:T(8,128)(2,1)}, bf...) custom-call(bf16[640,768]{1,0:T(8,128)(2,1)} %fusion.3.refs_0_, bf16[2,3,192,768]{3,2,1,0:T(8,128)(2,1)} %bitcast.85, ...), custom_call_target="tpu_custom_call" | custom-call | flops 53084160 | tf_op jit(solution)/shard_map/project_part/pallas_call | solution.py:262
  68.9 19.5 %attend.2 = (bf16[640,768]{1,0:T(8,128)(2,1)}, f32[6,8,640]{2,1,0:T(8,128)}) custom-call(s32[45]{0:T(128)} %pad_add_fusion.table, bf16[640,768]{1,0:T(8,128)(2,1)} %get-tuple-element.59.q_ref, bf16[2560,768]{1,0:T(8,128)(2,1)} %get-tuple-element.60.k_ref, bf16[2560,768]{1,0:T(8,128)(2,1)} %get-tuple-element.61.v_ref), custom_call_target="tpu_custom_call" | custom-call | flops 78643200 | bytes 122880 | tf_op jit(solution)/shard_map/attend/pallas_call | solution.py:129
  88.4 2.6 multiply_reduce_fusion.5
  91.1 0.3 fusion.18
  91.4 0.3 fusion.19
  91.7 1.0 copy.27
  92.7 0.2 multiply_convert_fusion.3.refs_3_
  92.9 0.4 fusion.39
  93.3 0.6 bitcast_add_fusion
  93.9 85.5 %expert_part.3 = (bf16[2,4,2,384,768]{4,3,2,1,0:T(8,128)(2,1)}, bf16[640,768]{1,0:T(8,128)(2,1)}, bf16[960,768]{1,0:T(8,128)(2,1)}, bf16[960,768]{1,0:T(8,128)(2...) custom-call(bf16[2,1,768,768]{3,2,1,0:T(8,128)(2,1)} %refs_0_.3, ...), custom_call_target="tpu_custom_call" | custom-call | flops 35389440 | tf_op jit(solution)/shard_map/expert_part/pallas_call | solution.py:262
  179.5 1.7 multiply_reduce_fusion.4
  181.2 1.2 multiply_convert_fusion.2.refs_0_
  182.4 37.8 %project_part.3 = (bf16[640,768]{1,0:T(8,128)(2,1)}, bf16[2560,768]{1,0:T(8,128)(2,1)}, bf16[2560,768]{1,0:T(8,128)(2,1)}, bf16[2560,768]{1,0:T(8,128)(2,1)}, bf...) custom-call(bf16[640,768]{1,0:T(8,128)(2,1)} %multiply_convert_fusion.2.refs_0_, bf16[2,4,1,384,768]{4,3,2,1,0:T(8,128)(2,1)} %bitcast.87), custom_call_target="tpu_custom_call" | custom-call | flops 53084160 | tf_op jit(solution)/shard_map/project_part/pallas_call | solution.py:262
  220.2 19.2 %attend.3 = (bf16[640,768]{1,0:T(8,128)(2,1)}, f32[6,8,640]{2,1,0:T(8,128)}) custom-call(s32[45]{0:T(128)} %pad_add_fusion.table, bf16[640,768]{1,0:T(8,128)(2,1)} %get-tuple-element.66.q_ref, bf16[2560,768]{1,0:T(8,128)(2,1)} %get-tuple-element.67.k_ref, bf16[2560,768]{1,0:T(8,128)(2,1)} %get-tuple-element.68.v_ref), custom_call_target="tpu_custom_call" | custom-call | flops 78643200 | bytes 122880 | tf_op jit(solution)/shard_map/attend/pallas_call | solution.py:129
  239.4 2.6 multiply_reduce_fusion.3
  242.0 0.2 multiply_convert_fusion.1.refs_3_
  242.2 0.9 copy-done.3
  243.2 0.4 fusion.40
  243.6 1.2 fusion.refs_4_
  244.8 0.8 pad.4.refs_5_.refs_3_
  245.6 109.5 %expert_part.4 = (bf16[640,768]{1,0:T(8,128)(2,1)}, bf16[960,768]{1,0:T(8,128)(2,1)}, bf16[4,2,384,768]{3,2,1,0:T(8,128)(2,1)}, f32[8,768]{1,0:T(8,128)}) custom-call(bf16[2,1,768,768]{3,2,1,0:T(8,128)(2,1)} %refs_0_.3, bf16[2,1,768,768]{3,2,1,0:T(8,128)(2,1)} %refs_1_.3, s32[1,640]{1,0:T(1,128)} %get-tuple-element.146.refs_2_.refs_8_, ...), custom_call_target="tpu_custom_call" | custom-call | flops 35389440 | tf_op jit(solution)/shard_map/expert_part/pallas_call | solution.py:262
  355.1 1.7 multiply_reduce_fusion.2
  356.8 0.1 copy-done.7
  356.9 0.6 fusion.36.refs_6_
  357.5 0.7 copy-done.26
  358.2 1.9 convolution_convert_fusion.1.do_ref
  360.1 31.3 %attend_back.2 = (bf16[640,768]{1,0:T(8,128)(2,1)}, bf16[2560,768]{1,0:T(8,128)(2,1)}, bf16[2560,768]{1,0:T(8,128)(2,1)}) custom-call(s32[45]{0:T(128)} %pad_add_fusion.table, bf16[640,768]{1,0:T(8,128)(2,1)} %get-tuple-element.66.q_ref, bf16[2560,768]{1,0:T(8,128)(2,1)} %get-tuple-element.67.k_ref, bf16[2560,768]{1,0:T(8,128)(2,1)} %get-tuple-element.68.v_ref, ...), custom_call_target="tpu_custom_call" | custom-call | flops 196608000 | bytes 245760 | tf_op jit(solution)/shard_map/attend_back/pallas_call | solution.py:206
  391.4 42.4 %project_back_part.2 = (f32[640,768]{1,0:T(8,128)}, bf16[8,384,768]{2,1,0:T(8,128)(2,1)}, f32[8,768]{1,0:T(8,128)}, bf16[640,768]{1,0:T(8,128)(2,1)}) custom-call(bf16[4,768,768]{2,1,0:T(8,128)(2,1)} %get-tuple-element.70.refs_0_, bf16[640,768]{1,0:T(8,128)(2,1)} %get-tuple-element.74.refs_1_, bf16[2560,768]{1,0:T(8,128)(2,1)} %get-tuple-element.75.refs_2_, ...), custom_call_target="tpu_custom_call" | custom-call | flops 94371840 | tf_op jit(solution)/shard_map/project_back_part/pallas_call | solution.py:262
  433.8 2.0 multiply_reduce_fusion.1
  435.9 0.7 copy-done.9
  436.5 3.8 multiply_convert_fusion
  440.4 66.6 %expert_part.5 = (bf16[640,768]{1,0:T(8,128)(2,1)}, bf16[4,2,384,768]{3,2,1,0:T(8,128)(2,1)}, f32[8,768]{1,0:T(8,128)}, bf16[384,768]{1,0:T(8,128)(2,1)}, bf16[2...) custom-call(bf16[2,4,2,384,768]{4,3,2,1,0:T(8,128)(2,1)} %get-tuple-element.81.refs_0_, ...), custom_call_target="tpu_custom_call" | custom-call | flops 35389440 | tf_op jit(solution)/shard_map/expert_part/pallas_call | solution.py:262
  507.1 1.7 collective-permute-start
  508.8 1.5 multiply_reduce_fusion
  510.4 0.6 fusion.37
  511.0 0.7 copy-done.25
  511.6 1.9 convolution_convert_fusion.do_ref
  513.5 31.2 %attend_back.3 = (bf16[640,768]{1,0:T(8,128)(2,1)}, bf16[2560,768]{1,0:T(8,128)(2,1)}, bf16[2560,768]{1,0:T(8,128)(2,1)}) custom-call(s32[45]{0:T(128)} %pad_add_fusion.table, bf16[640,768]{1,0:T(8,128)(2,1)} %get-tuple-element.59.q_ref, bf16[2560,768]{1,0:T(8,128)(2,1)} %get-tuple-element.60.k_ref, bf16[2560,768]{1,0:T(8,128)(2,1)} %get-tuple-element.61.v_ref, ...), custom_call_target="tpu_custom_call" | custom-call | flops 196608000 | bytes 245760 | tf_op jit(solution)/shard_map/attend_back/pallas_call | solution.py:206
  544.7 0.8 slice_reduce_fusion
  545.6 0.6 pad_maximum_fusion.refs_8_
  546.2 83.5 %project_back_part.3 = (f32[640,768]{1,0:T(8,128)}, bf16[2,576,768]{2,1,0:T(8,128)(2,1)}, bf16[2,192,768]{2,1,0:T(8,128)(2,1)}, bf16[2,2,384,768]{3,2,1,0:T(8,12...) custom-call(bf16[4,768,768]{2,1,0:T(8,128)(2,1)} %get-tuple-element.63.refs_0_, ...), custom_call_target="tpu_custom_call" | custom-call | flops 94371840 | tf_op jit(solution)/shard_map/project_back_part/pallas_call | solution.py:262
  629.7 1.4 slice_bitcast_fusion
  631.1 0.9 fusion.38
  632.0 4.4 bitcast_convert_fusion
  636.4 2.5 bitcast_convert_fusion.1
  639.0 2.1 convert_bitcast_fusion
  641.1 1.0 copy-done.11
  642.1 0.3 fusion.7
  642.4 1.1 convert_element_type.133
  643.5 0.6 bitcast_divide_fusion
  644.1 0.6 bitcast_divide_fusion.1
  644.7 1.8 fusion.6
  (77 shorter events, 0.9 us)
Async XLA Ops:
  68.8 19.6 %copy-start = (bf16[640,768]{1,0:T(8,128)(2,1)S(1)}, bf16[640,768]{1,0:T(8,128)(2,1)}, u32[]{:S(2)}) copy-start(bf16[640,768]{1,0:T(8,128)(2,1)} %param.13) | copy-start | bytes 2949124
  88.4 2.6 copy-start.24
  88.4 3.3 copy-start.19
  92.9 1.1 copy-start.2
  242.0 1.7 copy-start.4
  242.2 0.9 copy-start.3
  243.2 1.6 copy-start.17
  355.1 1.7 copy-start.5
  355.1 1.8 copy-start.7
  356.9 1.3 copy-start.26
  357.5 2.5 copy-start.12
  433.8 2.0 copy-start.6
  433.8 2.1 copy-start.8
  433.8 2.7 copy-start.9
  507.0 3.3 copy-start.10
  507.0 3.3 copy-start.13
  507.1 39.2 %collective-permute-start = (bf16[2,2,192,768]{3,2,1,0:T(8,128)(2,1)}, bf16[2,2,192,768]{3,2,1,0:T(8,128)(2,1)}, u32[]{:S(2)}, u32[]{:S(2)}) collective-permute-start(bf16[2,2,192,768]{3,2,1,0:T(8,128)(2,1)} %get-tuple-element.101), channel_id=1, source_target_pairs={{0,1},{1,0},{2,3},{3,2},{4,5},{5,4},{6,7},{7,6},{8,9},{9,8},{10,11... | collective-permute-start | bytes 3538952 | tf_op jit(solution)/shard_map/ppermute | solution.py:44
  508.7 37.5 %collective-permute-start.1 = (bf16[2,2,192,768]{3,2,1,0:T(8,128)(2,1)}, bf16[2,2,192,768]{3,2,1,0:T(8,128)(2,1)}, u32[]{:S(2)}, u32[]{:S(2)}) collective-permute-start(bf16[2,2,192,768]{3,2,1,0:T(8,128)(2,1)} %get-tuple-element.102), channel_id=1, source_target_pairs={{0,2},{1,3},{2,0},{3,1},{4,6},{5,7},{6,4},{7,5},{8,10},{9,11},{10,... | collective-permute-start | bytes 3538952 | tf_op jit(solution)/shard_map/ppermute | solution.py:44
  510.4 1.3 copy-start.25
  510.9 2.6 copy-start.14
  513.5 32.0 %copy-start.22 = (f32[8,768]{1,0:T(8,128)S(1)}, f32[8,768]{1,0:T(8,128)}, u32[]{:S(2)}) copy-start(f32[8,768]{1,0:T(8,128)} %get-tuple-element.98) | copy-start | bytes 73732
  513.5 32.1 %copy-start.23 = (f32[8,768]{1,0:T(8,128)S(1)}, f32[8,768]{1,0:T(8,128)}, u32[]{:S(2)}) copy-start(f32[8,768]{1,0:T(8,128)} %get-tuple-element.96) | copy-start | bytes 73732
  632.0 4.4 copy-start.15
  636.4 2.6 copy-start.16
  638.9 2.1 copy-start.1
  638.9 3.1 copy-start.11
  641.1 1.4 copy-start.18
  642.1 1.4 copy-start.20
  642.1 2.0 copy-start.21

commit v6 on v5

--- a/solution.py
+++ b/solution.py
@@ -1176,8 +1176,9 @@
 
 
 def path_table(segment_ids, path_pos, parent_ids, peers):
-    segment = segment_ids[::BLK].reshape(peers, -1)
-    position = path_pos[::BLK].reshape(peers, -1)
+    front = jnp.arange(BLK, dtype=jnp.int32) == 0
+    head = lambda v: jnp.sum(jnp.where(front, v.reshape(-1, BLK), 0), axis=1).reshape(peers, -1)
+    segment, position = head(segment_ids), head(path_pos)
     t = lax.axis_index(TENSOR)
     order = jnp.arange(peers, dtype=jnp.int32) ^ t
     match = order[:, None] == jnp.arange(peers, dtype=jnp.int32)[None, :]
@@ -1195,17 +1196,22 @@
     return jnp.concatenate([place.reshape(-1), mine.reshape(-1)]).astype(jnp.int32)
 
 
-def dispatch_plan(route, experts, capacity):
-    count = route.shape[0]
-    chosen = route[:, None] == jnp.arange(experts, dtype=jnp.int32)[None, :]
+def dispatch_plans(routes, experts, capacity):
+    layers, count = routes.shape
+    names = jnp.arange(experts, dtype=jnp.int32)
+    chosen = routes[:, :, None] == names[None, None, :]
     index = jnp.arange(count, dtype=jnp.int32)
     before = (index[None, :] < index[:, None]).astype(BF16)
-    ranks = dot(before, chosen.astype(BF16)).astype(jnp.int32)
-    rank = jnp.sum(jnp.where(chosen, ranks, 0), axis=1)
-    to = route ^ lax.axis_index(EXPERT) if experts == 4 else route
-    slot = to * capacity + rank
-    table = slot[None, :] == jnp.arange(experts * capacity, dtype=jnp.int32)[:, None]
-    return chosen, (slot, table.astype(BF16))
+    every = jnp.concatenate([chosen[d] for d in range(layers)], axis=1)
+    ranks = jnp.where(every, dot(before, every.astype(BF16)), 0.0)
+    plans = []
+    for d in range(layers):
+        rank = jnp.sum(ranks[:, d * experts : (d + 1) * experts], axis=1).astype(jnp.int32)
+        to = routes[d] ^ lax.axis_index(EXPERT) if experts == CUTS else routes[d]
+        slot = to * capacity + rank
+        table = slot[None, :] == jnp.arange(experts * capacity, dtype=jnp.int32)[:, None]
+        plans.append((chosen[d], (slot, table.astype(BF16))))
+    return plans
 
 
 def send_rows(table, rows, experts, capacity):
@@ -1258,7 +1264,7 @@
     peers = lax.axis_size(TENSOR)
     shard = width // peers
     table = path_table(segment_ids, path_pos, parent_ids, peers)
-    plans = [dispatch_plan(route_ids[d, :, 0], experts, capacity) for d in range(depth_total)]
+    plans = dispatch_plans(route_ids[:, :, 0], experts, capacity)
     routes = jnp.pad(w_route, ((0, 0), (0, 0), (0, BLK - experts)))
     cotangent = cotangent.astype(F32)
 

time: 654 us -> 655 us (level)
  no operation moved by 1% of the time
where the time goes in v6:
time: 655 us; the launch traced here: 651 us
  Pallas kernels  591 us (90%)
  other arithmetic  36.8 us (6%)
  matrix products  9.96 us (2%)
  local copies, waits for them, and re-layouts  9.67 us (1%)
    pallas_call x7, Pallas kernels, run_kernel(): pl.pallas_call(kernel, in_specs=[spec for _, spec in ins.values()], out_s...  490 us
    pallas_call x2, Pallas kernels, attend_back(): pl.pallas_call(attend_back_kernel, grid_spec=pltpu.PrefetchScalarGridSpec...  62.6 us
    pallas_call x2, Pallas kernels, attend(): pl.pallas_call(attend_kernel, grid_spec=pltpu.PrefetchScalarGridSpec(num_...  38.8 us
  transfers between devices with their start and end apart: 2, of which 0 were waited for; matrix products, arithmetic and copies ran while one was open for 1% of the time, Pallas kernels for 5%

profile of v6, /device:TPU:1, one launch (start us, length us, event | category | flops | bytes accessed | tf_op | source)
XLA Modules:
  0.0 650.8 jit_solution(17812937667547339098)
XLA Ops:
  0.7 0.8 fusion.18
  1.5 0.1 broadcast_in_dim.125
  1.7 0.1 select_reduce_fusion.1
  1.9 0.1 reduce_sum.177
  2.0 0.8 select_reduce_fusion.2
  2.8 0.1 copy.26
  3.1 0.1 eq.75
  3.2 1.5 fusion.1
  4.7 0.6 pad_add_fusion.table
  5.3 0.8 convert_reduce_fusion
  6.1 2.4 fusion.3.refs_0_
  8.5 59.6 %project_part.2 = (bf16[640,768]{1,0:T(8,128)(2,1)}, bf16[2560,768]{1,0:T(8,128)(2,1)}, bf16[2560,768]{1,0:T(8,128)(2,1)}, bf16[2560,768]{1,0:T(8,128)(2,1)}, bf...) custom-call(bf16[640,768]{1,0:T(8,128)(2,1)} %fusion.3.refs_0_, bf16[2,3,192,768]{3,2,1,0:T(8,128)(2,1)} %bitcast.104, ...), custom_call_target="tpu_custom_call" | custom-call | flops 53084160 | tf_op jit(solution)/shard_map/project_part/pallas_call | solution.py:262
  68.1 19.5 %attend.2 = (bf16[640,768]{1,0:T(8,128)(2,1)}, f32[6,8,640]{2,1,0:T(8,128)}) custom-call(s32[45]{0:T(128)} %pad_add_fusion.table, bf16[640,768]{1,0:T(8,128)(2,1)} %get-tuple-element.59.q_ref, bf16[2560,768]{1,0:T(8,128)(2,1)} %get-tuple-element.60.k_ref, bf16[2560,768]{1,0:T(8,128)(2,1)} %get-tuple-element.61.v_ref), custom_call_target="tpu_custom_call" | custom-call | flops 78643200 | bytes 122880 | tf_op jit(solution)/shard_map/attend/pallas_call | solution.py:129
  87.7 2.6 multiply_reduce_fusion.5
  90.3 0.3 fusion.13
  90.7 1.0 copy.27
  91.7 0.2 multiply_convert_fusion.3.refs_3_
  91.9 0.4 fusion.37
  92.4 0.6 bitcast_add_fusion
  93.0 85.5 %expert_part.3 = (bf16[2,4,2,384,768]{4,3,2,1,0:T(8,128)(2,1)}, bf16[640,768]{1,0:T(8,128)(2,1)}, bf16[960,768]{1,0:T(8,128)(2,1)}, bf16[960,768]{1,0:T(8,128)(2...) custom-call(bf16[2,1,768,768]{3,2,1,0:T(8,128)(2,1)} %refs_0_.3, ...), custom_call_target="tpu_custom_call" | custom-call | flops 35389440 | tf_op jit(solution)/shard_map/expert_part/pallas_call | solution.py:262
  178.4 1.7 multiply_reduce_fusion.4
  180.1 1.2 multiply_convert_fusion.2.refs_0_
  181.3 37.8 %project_part.3 = (bf16[640,768]{1,0:T(8,128)(2,1)}, bf16[2560,768]{1,0:T(8,128)(2,1)}, bf16[2560,768]{1,0:T(8,128)(2,1)}, bf16[2560,768]{1,0:T(8,128)(2,1)}, bf...) custom-call(bf16[640,768]{1,0:T(8,128)(2,1)} %multiply_convert_fusion.2.refs_0_, bf16[2,4,1,384,768]{4,3,2,1,0:T(8,128)(2,1)} %bitcast.106), custom_call_target="tpu_custom_call" | custom-call | flops 53084160 | tf_op jit(solution)/shard_map/project_part/pallas_call | solution.py:262
  219.2 19.2 %attend.3 = (bf16[640,768]{1,0:T(8,128)(2,1)}, f32[6,8,640]{2,1,0:T(8,128)}) custom-call(s32[45]{0:T(128)} %pad_add_fusion.table, bf16[640,768]{1,0:T(8,128)(2,1)} %get-tuple-element.66.q_ref, bf16[2560,768]{1,0:T(8,128)(2,1)} %get-tuple-element.67.k_ref, bf16[2560,768]{1,0:T(8,128)(2,1)} %get-tuple-element.68.v_ref), custom_call_target="tpu_custom_call" | custom-call | flops 78643200 | bytes 122880 | tf_op jit(solution)/shard_map/attend/pallas_call | solution.py:129
  238.4 2.6 multiply_reduce_fusion.3
  241.0 0.2 multiply_convert_fusion.1.refs_3_
  241.2 0.9 copy-done.3
  242.2 0.4 fusion.38
  242.6 1.2 fusion.refs_4_
  243.8 0.8 pad.4.refs_5_.refs_3_
  244.6 109.1 %expert_part.4 = (bf16[640,768]{1,0:T(8,128)(2,1)}, bf16[960,768]{1,0:T(8,128)(2,1)}, bf16[4,2,384,768]{3,2,1,0:T(8,128)(2,1)}, f32[8,768]{1,0:T(8,128)}) custom-call(bf16[2,1,768,768]{3,2,1,0:T(8,128)(2,1)} %refs_0_.3, bf16[2,1,768,768]{3,2,1,0:T(8,128)(2,1)} %refs_1_.3, s32[1,640]{1,0:T(1,128)} %get-tuple-element.148.refs_2_.refs_8_, ...), custom_call_target="tpu_custom_call" | custom-call | flops 35389440 | tf_op jit(solution)/shard_map/expert_part/pallas_call | solution.py:262
  353.7 1.7 multiply_reduce_fusion.2
  355.4 0.1 copy-done.7
  355.5 0.6 fusion.34.refs_6_
  356.1 0.6 copy-done.26
  356.8 1.9 convolution_convert_fusion.1.do_ref
  358.7 31.3 %attend_back.2 = (bf16[640,768]{1,0:T(8,128)(2,1)}, bf16[2560,768]{1,0:T(8,128)(2,1)}, bf16[2560,768]{1,0:T(8,128)(2,1)}) custom-call(s32[45]{0:T(128)} %pad_add_fusion.table, bf16[640,768]{1,0:T(8,128)(2,1)} %get-tuple-element.66.q_ref, bf16[2560,768]{1,0:T(8,128)(2,1)} %get-tuple-element.67.k_ref, bf16[2560,768]{1,0:T(8,128)(2,1)} %get-tuple-element.68.v_ref, ...), custom_call_target="tpu_custom_call" | custom-call | flops 196608000 | bytes 245760 | tf_op jit(solution)/shard_map/attend_back/pallas_call | solution.py:206
  390.0 41.3 %project_back_part.2 = (f32[640,768]{1,0:T(8,128)}, bf16[8,384,768]{2,1,0:T(8,128)(2,1)}, f32[8,768]{1,0:T(8,128)}, bf16[640,768]{1,0:T(8,128)(2,1)}) custom-call(bf16[4,768,768]{2,1,0:T(8,128)(2,1)} %get-tuple-element.70.refs_0_, bf16[640,768]{1,0:T(8,128)(2,1)} %get-tuple-element.74.refs_1_, bf16[2560,768]{1,0:T(8,128)(2,1)} %get-tuple-element.75.refs_2_, ...), custom_call_target="tpu_custom_call" | custom-call | flops 94371840 | tf_op jit(solution)/shard_map/project_back_part/pallas_call | solution.py:262
  431.3 2.0 multiply_reduce_fusion.1
  433.3 0.1 copy-done.8
  433.4 0.7 copy-done.9
  434.0 3.8 multiply_convert_fusion
  437.9 67.5 %expert_part.5 = (bf16[640,768]{1,0:T(8,128)(2,1)}, bf16[4,2,384,768]{3,2,1,0:T(8,128)(2,1)}, f32[8,768]{1,0:T(8,128)}, bf16[384,768]{1,0:T(8,128)(2,1)}, bf16[2...) custom-call(bf16[2,4,2,384,768]{4,3,2,1,0:T(8,128)(2,1)} %get-tuple-element.81.refs_0_, ...), custom_call_target="tpu_custom_call" | custom-call | flops 35389440 | tf_op jit(solution)/shard_map/expert_part/pallas_call | solution.py:262
  505.4 0.5 collective-permute-start
  505.9 1.1 collective-permute-start.1
  506.9 1.5 multiply_reduce_fusion
  508.5 0.6 fusion.35
  509.1 0.7 copy-done.25
  509.8 1.9 convolution_convert_fusion.do_ref
  511.6 31.2 %attend_back.3 = (bf16[640,768]{1,0:T(8,128)(2,1)}, bf16[2560,768]{1,0:T(8,128)(2,1)}, bf16[2560,768]{1,0:T(8,128)(2,1)}) custom-call(s32[45]{0:T(128)} %pad_add_fusion.table, bf16[640,768]{1,0:T(8,128)(2,1)} %get-tuple-element.59.q_ref, bf16[2560,768]{1,0:T(8,128)(2,1)} %get-tuple-element.60.k_ref, bf16[2560,768]{1,0:T(8,128)(2,1)} %get-tuple-element.61.v_ref, ...), custom_call_target="tpu_custom_call" | custom-call | flops 196608000 | bytes 245760 | tf_op jit(solution)/shard_map/attend_back/pallas_call | solution.py:206
  542.9 0.8 slice_reduce_fusion.2
  543.7 0.6 pad_maximum_fusion.refs_8_
  544.4 89.2 %project_back_part.3 = (f32[640,768]{1,0:T(8,128)}, bf16[2,576,768]{2,1,0:T(8,128)(2,1)}, bf16[2,192,768]{2,1,0:T(8,128)(2,1)}, bf16[2,2,384,768]{3,2,1,0:T(8,12...) custom-call(bf16[4,768,768]{2,1,0:T(8,128)(2,1)} %get-tuple-element.63.refs_0_, ...), custom_call_target="tpu_custom_call" | custom-call | flops 94371840 | tf_op jit(solution)/shard_map/project_back_part/pallas_call | solution.py:262
  633.6 1.4 slice_bitcast_fusion
  635.0 0.9 fusion.36
  635.9 4.4 bitcast_convert_fusion
  640.2 2.5 bitcast_convert_fusion.1
  642.8 2.1 convert_bitcast_fusion
  644.9 1.0 copy-done.11
  645.9 0.3 fusion.7
  646.3 1.1 convert_element_type.153
  647.4 0.6 bitcast_divide_fusion
  648.0 0.6 bitcast_divide_fusion.1
  648.6 1.8 fusion.6
  (81 shorter events, 0.8 us)
Async XLA Ops:
  68.1 19.6 %copy-start = (bf16[640,768]{1,0:T(8,128)(2,1)S(1)}, bf16[640,768]{1,0:T(8,128)(2,1)}, u32[]{:S(2)}) copy-start(bf16[640,768]{1,0:T(8,128)(2,1)} %param.13) | copy-start | bytes 2949124
  87.7 2.6 copy-start.24
  87.7 3.0 copy-start.19
  91.9 1.1 copy-start.2
  241.0 1.7 copy-start.4
  241.2 0.9 copy-start.3
  242.2 1.6 copy-start.17
  353.7 1.7 copy-start.5
  353.7 1.8 copy-start.7
  355.5 1.3 copy-start.26
  356.1 2.5 copy-start.12
  431.3 2.0 copy-start.6
  431.3 2.1 copy-start.8
  431.3 2.7 copy-start.9
  505.4 3.1 copy-start.10
  505.4 3.1 copy-start.13
  505.4 39.0 %collective-permute-start = (bf16[2,2,192,768]{3,2,1,0:T(8,128)(2,1)}, bf16[2,2,192,768]{3,2,1,0:T(8,128)(2,1)}, u32[]{:S(2)}, u32[]{:S(2)}) collective-permute-start(bf16[2,2,192,768]{3,2,1,0:T(8,128)(2,1)} %get-tuple-element.101), channel_id=1, source_target_pairs={{0,1},{1,0},{2,3},{3,2},{4,5},{5,4},{6,7},{7,6},{8,9},{9,8},{10,11... | collective-permute-start | bytes 3538952 | tf_op jit(solution)/shard_map/ppermute | solution.py:44
  505.9 38.5 %collective-permute-start.1 = (bf16[2,2,192,768]{3,2,1,0:T(8,128)(2,1)}, bf16[2,2,192,768]{3,2,1,0:T(8,128)(2,1)}, u32[]{:S(2)}, u32[]{:S(2)}) collective-permute-start(bf16[2,2,192,768]{3,2,1,0:T(8,128)(2,1)} %get-tuple-element.102), channel_id=1, source_target_pairs={{0,2},{1,3},{2,0},{3,1},{4,6},{5,7},{6,4},{7,5},{8,10},{9,11},{10,... | collective-permute-start | bytes 3538952 | tf_op jit(solution)/shard_map/ppermute | solution.py:44
  508.5 1.3 copy-start.25
  509.1 2.6 copy-start.14
  511.6 32.0 %copy-start.22 = (f32[8,768]{1,0:T(8,128)S(1)}, f32[8,768]{1,0:T(8,128)}, u32[]{:S(2)}) copy-start(f32[8,768]{1,0:T(8,128)} %get-tuple-element.98) | copy-start | bytes 73732
  511.6 32.1 %copy-start.23 = (f32[8,768]{1,0:T(8,128)S(1)}, f32[8,768]{1,0:T(8,128)}, u32[]{:S(2)}) copy-start(f32[8,768]{1,0:T(8,128)} %get-tuple-element.96) | copy-start | bytes 73732
  635.9 4.4 copy-start.15
  640.2 2.6 copy-start.16
  642.8 2.1 copy-start.1
  642.8 3.1 copy-start.11
  644.9 1.4 copy-start.18
  645.9 1.4 copy-start.20
  645.9 2.0 copy-start.21
